TPU v7x, 32 devices: a whole 2x2x4 slice. The times are simulated.
32 devices in a mesh: grp: 1, row: 32 (over z, y, x, core), col: 1.
Axes of the slice: x: 2, y: 2, z: 4, core: 2. Of those that a mesh axis runs over, the one named last changes fastest.
Arguments:
- alignment_rows: bfloat16 [64, 128, 256], P(('grp', 'row'), 'col'), may hold values from -40 to 40
- pair_state: bfloat16 [128, 128, 128], P(('grp', 'row'), 'col'), may hold values from -4 to 4
- update_cotangent: bfloat16 [64, 128, 256], P(('grp', 'row'), 'col'), may hold values from -96 to 96
- sequence_mask: int32 [64], P('grp'), may hold values 0 or 1
- residue_mask: int32 [128], P('grp'), may hold values 0 or 1
- left_weight: bfloat16 [256, 32], replicated, may hold values from -0.375 to 0.375
- right_weight: bfloat16 [256, 32], replicated, may hold values from -0.375 to 0.375
- outer_weight: bfloat16 [32, 32, 128], replicated, may hold values from -1 to 1
- bias_weight: bfloat16 [128, 8], replicated, may hold values from -1.5 to 1.5
- query_weight: bfloat16 [256, 256], replicated, may hold values from -13 to 13
- key_weight: bfloat16 [256, 256], replicated, may hold values from -0.375 to 0.375
- value_weight: bfloat16 [256, 256], replicated, may hold values from -0.375 to 0.375
- gate_weight: bfloat16 [256, 256], replicated, may hold values from -0.375 to 0.375
- output_weight: bfloat16 [256, 256], replicated, may hold values from -0.375 to 0.375
Outputs:
- alignment_update: bfloat16 [64, 128, 256], P(('grp', 'row'), 'col')
- pair_updated: bfloat16 [128, 128, 128], P(('grp', 'row'), 'col')
- pair_gradient: float32 [128, 128, 128], P(('grp', 'row'), 'col')
All inputs are finite; a program needn't handle non-finite values.
Results may differ from a plain program's by a relative error of at most 0.034.
Values may be sent and summed in bfloat16 or wider, within the bound.
No kernel may reach another device: no remote copies, remote signals or barrier semaphores. Data moves between devices by JAX's collectives and lax.ppermute only.
A program may use at most 64 MiB of HBM per device.

v0:
```python
import jax
import jax.numpy as jnp
from jax import lax
from jax.sharding import PartitionSpec as P

norm_eps = 1e-05
mask_fill = 1000000000.0


def layer_normalize(values):
    values = values.astype(jnp.float32)
    center = values - jnp.mean(values, axis=-1, keepdims=True)
    spread = jnp.mean(center * center, axis=-1, keepdims=True)
    return center * lax.rsqrt(spread + norm_eps)


def norm_backward(values, upstream):
    values = values.astype(jnp.float32)
    center = values - jnp.mean(values, axis=-1, keepdims=True)
    inverse = lax.rsqrt(jnp.mean(center * center, axis=-1, keepdims=True) + norm_eps)
    normal_part = center * inverse
    return inverse * (
        upstream
        - jnp.mean(upstream, axis=-1, keepdims=True)
        - normal_part * jnp.mean(upstream * normal_part, axis=-1, keepdims=True)
    )


def attend_partial(
    projected_queries, projected_keys, projected_values, bias_all, key_mask, score_scale
):
    scores = jnp.einsum(
        "ihd,jhd->ihj", projected_queries, projected_keys, preferred_element_type=jnp.float32
    )
    scores = scores * score_scale + bias_all.astype(jnp.float32) + key_mask
    maxima = jnp.max(scores, axis=-1)
    weights = jnp.exp(scores - maxima[..., None])
    totals = jnp.sum(weights, axis=-1)
    summed = jnp.einsum(
        "ihj,jhd->ihd",
        weights.astype(jnp.bfloat16),
        projected_values,
        preferred_element_type=jnp.float32,
    )
    return (maxima, totals, summed.reshape(summed.shape[0], -1))


def on_device(
    alignment_rows,
    pair_state,
    update_cotangent,
    sequence_mask,
    residue_mask,
    left_weight,
    right_weight,
    outer_weight,
    bias_weight,
    query_weight,
    key_weight,
    value_weight,
    gate_weight,
    output_weight,
):
    sequence_wise, residue_half, channel_count = alignment_rows.shape
    rows_here = pair_state.shape[0]
    residues = residue_mask.shape[0]
    head_count = bias_weight.shape[1]
    head_dim = channel_count // head_count
    score_scale = head_dim ** (-0.5)
    row_index = lax.axis_index("row")
    col_index = lax.axis_index("col")
    complete_alignment, complete_cotangent = (
        lax.all_gather(alignment_rows, "col", axis=1, tiled=True),
        lax.all_gather(update_cotangent, "col", axis=1, tiled=True),
    )
    seq_live = sequence_mask.astype(jnp.float32)
    res_live = residue_mask.astype(jnp.float32)
    own_seq = lax.dynamic_slice_in_dim(seq_live, row_index * sequence_wise, sequence_wise)
    own_cols = lax.dynamic_slice_in_dim(res_live, col_index * residue_half, residue_half)
    own_rows = lax.dynamic_slice_in_dim(res_live, row_index * rows_here, rows_here)
    normalized_input = layer_normalize(complete_alignment).astype(jnp.bfloat16)
    flat_rows = normalized_input.reshape(-1, channel_count)
    normed_half = lax.dynamic_slice_in_dim(
        normalized_input, col_index * residue_half, residue_half, 1
    )
    half_rows = normed_half.reshape(-1, channel_count)
    left_proj = jnp.dot(flat_rows, left_weight, preferred_element_type=jnp.float32).reshape(
        sequence_wise, residues, -1
    )
    left_proj = (left_proj * (own_seq[:, None] * res_live[None, :])[..., None]).astype(jnp.bfloat16)
    right_proj = jnp.dot(half_rows, right_weight, preferred_element_type=jnp.float32).reshape(
        sequence_wise, residue_half, -1
    )
    right_proj = (right_proj * (own_seq[:, None] * own_cols[None, :])[..., None]).astype(
        jnp.bfloat16
    )
    left_tile = lax.all_to_all(left_proj, "row", split_axis=1, concat_axis=0, tiled=True)
    right_all = lax.all_gather(right_proj, "row", axis=0, tiled=True)
    outer_width = left_tile.shape[2]
    outer_sum = lax.dot_general(
        left_tile.reshape(left_tile.shape[0], -1),
        right_all.reshape(right_all.shape[0], -1),
        (((0,), (0,)), ((), ())),
        preferred_element_type=jnp.float32,
    )
    outer_half = outer_sum.astype(jnp.bfloat16).reshape(
        rows_here, outer_width, residue_half, outer_width
    )
    opm_update = jnp.einsum(
        "ipjq,pqz->ijz", outer_half, outer_weight, preferred_element_type=jnp.float32
    )
    divisor = jnp.maximum(jnp.sum(seq_live) * own_rows[:, None] * own_cols[None, :], 1.0)
    pair_updated = (pair_state.astype(jnp.float32) + opm_update / divisor[..., None]).astype(
        jnp.bfloat16
    )
    pair_normed = layer_normalize(pair_updated).astype(jnp.bfloat16)
    bias_tile = jnp.einsum(
        "ijz,zh->ihj", pair_normed, bias_weight, preferred_element_type=jnp.float32
    ).astype(jnp.bfloat16)
    projected_queries = (
        jnp.dot(flat_rows, query_weight, preferred_element_type=jnp.float32)
        .astype(jnp.bfloat16)
        .reshape(sequence_wise, residues, head_count, head_dim)
    )
    gate_activations = jax.nn.sigmoid(
        jnp.dot(flat_rows, gate_weight, preferred_element_type=jnp.float32)
    ).reshape(sequence_wise, residues, channel_count)
    key_live = (res_live - 1.0) * mask_fill
    half_live = lax.dynamic_slice_in_dim(key_live, col_index * residue_half, residue_half)
    bias_cols = lax.all_gather(bias_tile, "col", axis=2, tiled=True)
    bias_all = lax.all_gather(bias_cols, "row", axis=0, tiled=True)
    key_count = bias_all.shape[2]
    projected_keys = (
        jnp.dot(flat_rows, key_weight, preferred_element_type=jnp.float32)
        .astype(jnp.bfloat16)
        .reshape(sequence_wise, key_count, head_count, head_dim)
    )
    projected_values = (
        jnp.dot(flat_rows, value_weight, preferred_element_type=jnp.float32)
        .astype(jnp.bfloat16)
        .reshape(sequence_wise, key_count, head_count, head_dim)
    )
    maxima, totals, summed = lax.map(
        lambda inputs: attend_partial(
            inputs[0], inputs[1], inputs[2], bias_all, key_live, score_scale
        ),
        (projected_queries, projected_keys, projected_values),
    )
    attended = summed / jnp.repeat(totals, head_dim, axis=-1)
    gated = gate_activations * attended
    gated_own = lax.dynamic_slice_in_dim(gated, col_index * residue_half, residue_half, 1).astype(
        jnp.bfloat16
    )
    alignment_update = (
        jnp.dot(
            gated_own.reshape(-1, channel_count), output_weight, preferred_element_type=jnp.float32
        )
        .astype(jnp.bfloat16)
        .reshape(sequence_wise, residue_half, channel_count)
    )
    d_gated = lax.dot_general(
        complete_cotangent.reshape(-1, channel_count),
        output_weight,
        (((1,), (1,)), ((), ())),
        preferred_element_type=jnp.float32,
    ).reshape(sequence_wise, residues, channel_count)
    d_attended = d_gated * gate_activations
    delta_sum = jnp.sum(
        (d_attended * attended).reshape(sequence_wise, residues, head_count, head_dim), axis=-1
    )
    d_rounded = d_attended.astype(jnp.bfloat16).reshape(
        sequence_wise, residues, head_count, head_dim
    )
    log_total = maxima + jnp.log(totals)
    keys_half = lax.dynamic_slice_in_dim(projected_keys, col_index * residue_half, residue_half, 1)
    values_half = lax.dynamic_slice_in_dim(
        projected_values, col_index * residue_half, residue_half, 1
    )
    bias_half = lax.dynamic_slice_in_dim(bias_all, col_index * residue_half, residue_half, 2)
    bias_rows = bias_half.astype(jnp.float32)

    def single_sequence(running, sequence_items):
        query_rows, d_rows, total_rows, delta_rows, keys_one, values_one = sequence_items
        scores = jnp.einsum(
            "ihd,jhd->ihj", query_rows, keys_one, preferred_element_type=jnp.float32
        )
        scores = scores * score_scale + bias_rows + half_live
        probs = jnp.exp(scores - total_rows[..., None])
        d_weights = jnp.einsum(
            "ihd,jhd->ihj", d_rows, values_one, preferred_element_type=jnp.float32
        )
        return (running + probs * (d_weights - delta_rows[..., None]), None)

    sequence_items = (projected_queries, d_rounded, log_total, delta_sum, keys_half, values_half)
    initial_value = jnp.zeros(
        (rows_here * lax.axis_size("row"), head_count, residue_half), jnp.float32
    )
    result, unused = lax.scan(single_sequence, initial_value, sequence_items)
    bias_gradient = lax.psum_scatter(result, "row", scatter_dimension=0, tiled=True)
    d_normed = jnp.einsum(
        "ihj,zh->ijz",
        bias_gradient,
        bias_weight.astype(jnp.float32),
        precision=lax.Precision.HIGHEST,
    )
    pair_gradient = norm_backward(pair_updated, d_normed)
    return (alignment_update, pair_updated, pair_gradient)


def solution(mesh):
    placed = (
        P(("grp", "row"), "col", None),
        P(("grp", "row"), "col", None),
        P(("grp", "row"), "col", None),
        P("grp"),
        P("grp"),
        P(),
        P(),
        P(),
        P(),
        P(),
        P(),
        P(),
        P(),
        P(),
    )
    return jax.shard_map(
        on_device,
        mesh=mesh,
        in_specs=placed,
        out_specs=(
            P(("grp", "row"), "col", None),
            P(("grp", "row"), "col", None),
            P(("grp", "row"), "col", None),
        ),
        check_vma=False,
    )
```

profile of v0, /device:TPU:0, one launch (start us, length us, event | category | flops | bytes accessed | tf_op | source)
XLA Modules:
  0.0 270.6 jit_solution(744304922000768027)
XLA Ops:
  7.2 0.7 convert_element_type.73
  7.9 0.7 convert_element_type.74
  8.6 1.0 convert_reduce_fusion.1
  9.6 1.1 fusion.54
  10.7 1.0 fusion.55
  11.8 0.1 dynamic_slice.42
  11.8 0.1 broadcast_multiply_fusion.3
  11.9 0.9 fusion.40
  12.8 0.2 copy.64
  12.9 0.7 reshape.182
  13.7 7.3 %all-to-all-start = ((bf16[32,2,128]{2,1,0:T(2,128)(2,1)}), bf16[32,2,128]{2,1,0:T(2,128)(2,1)S(1)}, u32[]{:S(2)}, u32[]{:S(2)}) async-start(bf16[32,2,128]{2,1,0:T(2,128)(2,1)} %reshape.182), calls=%async_computation | async-start | bytes 32768 | tf_op jit(solution)/shard_map/all_to_all | solution.py:97
  21.0 0.0 reduce-scatter.2.cloned.1.call-start
  21.0 1.3 convert_reduce_fusion.2
  22.3 0.9 fusion.41
  23.1 43.2 %all_gather.4 = bf16[64,128,32]{1,2,0:T(8,128)(2,1)S(1)} all-gather(bf16[2,128,32]{1,2,0:T(8,128)(2,1)S(1)} %fusion.41), channel_id=1, replica_groups=mesh['grp'=1,'row'=32,'col'=1] {'row'}, dimensions={0}, use_global_device_ids=true | all-gather | bytes 540672 | tf_op jit(solution)/shard_map/all_gather | solution.py:98
  66.3 0.7 dynamic-slice_multiply_fusion
  67.1 0.7 multiply_maximum_fusion
  67.7 1.1 convolution_convert_fusion.4
  68.8 1.1 convolution_convert_fusion.3
  69.9 1.1 convolution_convert_fusion.2
  71.0 1.1 fusion.36
  72.1 1.2 add_multiply_fusion
  73.4 1.7 copy.67
  75.1 0.8 copy.63
  75.9 0.1 copy.61
  76.0 0.1 copy.62
  76.2 0.1 copy.70
  76.4 0.1 reshape.183
  76.6 0.1 reshape.167
  76.7 0.5 convolution_convert_fusion
  77.1 4.5 %reshape.169 = bf16[4,32,128,32]{3,2,1,0:T(8,128)(2,1)} reshape(bf16[128,4096]{1,0:T(8,128)(2,1)S(1)} %convolution_convert_fusion) | data formatting | bytes 2097152 | tf_op jit(solution)/shard_map/reshape | solution.py:106
  81.6 3.7 %convert_reduce_fusion = (f32[4,128]{1,0:T(4,128)S(1)}, bf16[4,128,128]{1,2,0:T(8,128)(2,1)S(1)}) fusion(f32[4,128]{1,0:T(4,128)} %multiply_maximum_fusion, bf16[4,32,128,32]{3,2,1,0:T(8,128)(2,1)} %reshape.169, bf16[32,32,128]{2,1,0:T(8,128)(2,1)S(1)} %copy-done, bf16[4,128,128]{1,2,0:T(8,128)(2,1)} %copy.63), kind=kOutput, calls=%fused_computation.63 | convolution fusion | flops 134610432 | bytes 1576960 | tf_op jit(solution)/shard_map/ipjq,pqz->ijz/dot_general | solution.py:109
  85.3 0.1 fusion.53
  85.4 0.1 fusion.42
  85.6 37.3 %all_gather.10 = bf16[128,8,128]{2,1,0:T(8,128)(2,1)S(1)} all-gather(bf16[4,8,128]{2,1,0:T(8,128)(2,1)S(1)} %fusion.42), channel_id=1, replica_groups=mesh['grp'=1,'row'=32,'col'=1] {'row'}, dimensions={0}, use_global_device_ids=true | all-gather | bytes 270336 | tf_op jit(solution)/shard_map/all_gather | solution.py:131
  122.9 0.2 copy.73
  123.1 0.2 copy.81
  123.4 2.8 %while.25 = (s32[]{:T(128)}, f32[2,128,8]{1,2,0:T(8,128)S(1)}, f32[2,128,8]{1,2,0:T(8,128)S(1)}, f32[2,128,256]{2,1,0:T(8,128)}, bf16[2,128,8,32]{1,3,2,0:T(8,12...) while((s32[]{:T(128)}, f32[2,128,8]{1,2,0:T(8,128)S(1)}, ...), condition=%wide.region_8.9_spmd, body=%wide.region_5.8_spmd.sunk | while | flops 17954816 | bytes 2721901 | solution.py:143
  123.4 0.3 fusion.98
  123.7 0.2 fusion.100
  123.9 0.1 copy.101
  124.0 0.7 constant_dynamic-update-slice_fusion.2
  124.7 0.1 fusion.99
  124.8 0.3 fusion.98
  125.1 0.2 fusion.100
  125.3 0.1 copy.101
  125.4 0.7 constant_dynamic-update-slice_fusion.2
  126.1 0.1 fusion.99
  126.3 0.1 copy.76
  126.4 1.2 divide_multiply_fusion
  127.6 0.1 copy.78
  127.8 0.1 copy.77
  127.9 1.6 while.26
  127.9 0.3 fusion.105
  128.2 0.5 fusion.106
  128.7 0.3 fusion.105
  129.0 0.5 fusion.106
  129.5 1.0 copy.83
  130.5 0.8 copy.84
  131.3 0.8 convolution_convert_fusion.1
  132.1 129.6 %reduce-scatter.2.cloned.1.call-done = f32[4,8,128]{2,1,0:T(8,128)} async-done(((f32[128,8,128]{2,1,0:T(8,128)}), f32[4,8,128]{2,1,0:T(8,128)}) %reduce-scatter.2.cloned.1.call-update) | async-done | bytes 16400 | tf_op jit(solution)/shard_map/reduce_scatter | solution.py:199
  261.8 1.0 fusion.66
  262.8 0.1 fusion.52
  262.9 0.8 copy.85
  (42 shorter events, 0.4 us)
Async XLA Ops:
  7.2 74.4 %copy-start = (bf16[32,32,128]{2,1,0:T(8,128)(2,1)S(1)}, bf16[32,32,128]{2,1,0:T(8,128)(2,1)}, u32[]{:S(2)}) copy-start(bf16[32,32,128]{2,1,0:T(8,128)(2,1)} %param.25) | copy-start | bytes 786436
  7.2 67.9 %copy-start.3 = (bf16[4,128,128]{2,1,0:T(8,128)(2,1)S(1)}, bf16[4,128,128]{2,1,0:T(8,128)(2,1)}, u32[]{:S(2)}) copy-start(bf16[4,128,128]{2,1,0:T(8,128)(2,1)} %param.19) | copy-start | bytes 393220
  13.7 62.7 %all-to-all-start = ((bf16[32,2,128]{2,1,0:T(2,128)(2,1)}), bf16[32,2,128]{2,1,0:T(2,128)(2,1)S(1)}, u32[]{:S(2)}, u32[]{:S(2)}) async-start(bf16[32,2,128]{2,1,0:T(2,128)(2,1)} %reshape.182), calls=%async_computation | async-start | bytes 32768 | tf_op jit(solution)/shard_map/all_to_all | solution.py:97
  21.0 240.8 %reduce-scatter.2.cloned.1.call-start = ((), (), s32[]{:S(2)}) async-start(), calls=%async_computation.2 | async-start | bytes 540672 | tf_op jit(solution)/shard_map/reduce_scatter | solution.py:199
  77.1 8.3 %copy-start.7 = (bf16[128,8]{0,1:T(8,128)(2,1)S(1)}, bf16[128,8]{0,1:T(8,128)(2,1)}, u32[]{:S(2)}) copy-start(bf16[128,8]{0,1:T(8,128)(2,1)} %param.26) | copy-start | bytes 6148
  81.6 41.7 %copy-start.4 = (f32[128]{0:T(128)S(1)}, f32[128]{0:T(128)}, u32[]{:S(2)}) copy-start(f32[128]{0:T(128)} %add_multiply_fusion) | copy-start | bytes 1540
  81.6 41.7 %copy-start.5 = (f32[2,128,8]{1,2,0:T(8,128)S(1)}, f32[2,128,8]{1,2,0:T(8,128)}, u32[]{:S(2)}) copy-start(f32[2,128,8]{1,2,0:T(8,128)} %custom-call.2) | copy-start | bytes 24580
  81.6 41.8 %copy-start.6 = (f32[2,128,8]{1,2,0:T(8,128)S(1)}, f32[2,128,8]{1,2,0:T(8,128)}, u32[]{:S(2)}) copy-start(f32[2,128,8]{1,2,0:T(8,128)} %custom-call.1) | copy-start | bytes 24580
  123.4 3.0 %copy-start.1 = (bf16[256,256]{1,0:T(8,128)(2,1)S(1)}, bf16[256,256]{1,0:T(8,128)(2,1)}, u32[]{:S(2)}) copy-start(bf16[256,256]{1,0:T(8,128)(2,1)} %param.31) | copy-start | bytes 393220
  123.4 3.0 %copy-start.2 = (bf16[2,128,256]{2,1,0:T(8,128)(2,1)S(1)}, bf16[2,128,256]{2,1,0:T(8,128)(2,1)}, u32[]{:S(2)}) copy-start(bf16[2,128,256]{2,1,0:T(8,128)(2,1)} %param.20) | copy-start | bytes 393220
Sparse Core Ops, SparseCore 0:
  130.6 131.1 reduce-scatter.1
where the time goes:
time: 271 us
  waiting for transfers between devices  130 us (48%)
  blocking collectives  80.5 us (30%)
  matrix products  16 us (6%)
  between operations  14.4 us (5%)
  local copies, waits for them, and re-layouts  13.6 us (5%)
  other arithmetic  8.85 us (3%)
  starting transfers between devices  7.34 us (3%)
    reduce_scatter x1, waiting for transfers between devices, on_device(): lax.psum_scatter(result, 'row', scatter_dimension=0, tiled=True)  130 us
    all_gather x1, blocking collectives, on_device(): right_all = lax.all_gather(right_proj, 'row', axis=0, tiled=True)  43.2 us
    all_gather x1, blocking collectives, on_device(): bias_all = lax.all_gather(bias_cols, 'row', axis=0, tiled=True)  37.3 us
    all_to_all x1, starting transfers between devices, on_device(): lax.all_to_all(left_proj, 'row', split_axis=1, concat_axis=0, tiled=True)  7.3 us
  transfers between devices with their start and end apart: 2, of which 1 were waited for; matrix products, arithmetic and copies ran while one was open for 5% of the time, Pallas kernels for 0%

commit v1 on v0

--- a/solution.py
+++ b/solution.py
@@ -24,6 +24,12 @@
         - jnp.mean(upstream, axis=-1, keepdims=True)
         - normal_part * jnp.mean(upstream * normal_part, axis=-1, keepdims=True)
     )
+
+
+def spread_all(shard):
+    copies = jnp.broadcast_to(shard[None], (lax.axis_size("row"),) + shard.shape)
+    gathered = lax.all_to_all(copies, "row", split_axis=0, concat_axis=0, tiled=True)
+    return gathered.reshape((-1,) + shard.shape[1:])
 
 
 def attend_partial(
@@ -95,7 +101,7 @@
         jnp.bfloat16
     )
     left_tile = lax.all_to_all(left_proj, "row", split_axis=1, concat_axis=0, tiled=True)
-    right_all = lax.all_gather(right_proj, "row", axis=0, tiled=True)
+    right_all = spread_all(right_proj)
     outer_width = left_tile.shape[2]
     outer_sum = lax.dot_general(
         left_tile.reshape(left_tile.shape[0], -1),
@@ -128,7 +134,7 @@
     key_live = (res_live - 1.0) * mask_fill
     half_live = lax.dynamic_slice_in_dim(key_live, col_index * residue_half, residue_half)
     bias_cols = lax.all_gather(bias_tile, "col", axis=2, tiled=True)
-    bias_all = lax.all_gather(bias_cols, "row", axis=0, tiled=True)
+    bias_all = spread_all(bias_cols)
     key_count = bias_all.shape[2]
     projected_keys = (
         jnp.dot(flat_rows, key_weight, preferred_element_type=jnp.float32)
@@ -196,7 +202,14 @@
         (rows_here * lax.axis_size("row"), head_count, residue_half), jnp.float32
     )
     result, unused = lax.scan(single_sequence, initial_value, sequence_items)
-    bias_gradient = lax.psum_scatter(result, "row", scatter_dimension=0, tiled=True)
+    shares = lax.all_to_all(
+        result.astype(jnp.bfloat16).reshape((-1,) + (rows_here,) + result.shape[1:]),
+        "row",
+        split_axis=0,
+        concat_axis=0,
+        tiled=True,
+    )
+    bias_gradient = jnp.sum(shares.astype(jnp.float32), axis=0)
     d_normed = jnp.einsum(
         "ihj,zh->ijz",
         bias_gradient,

time: 271 us -> 89.8 us (0.33)
  waiting for transfers between devices: 130 us -> 34.7 us
  blocking collectives: 80.5 us -> 0 us
  between operations: 14.4 us -> 1.14 us
  starting transfers between devices: 7.34 us -> 15.5 us
  local copies, waits for them, and re-layouts: 13.6 us -> 17.2 us
  matrix products: 16 us -> 12.6 us
    reduce_scatter x1 -> x0, waiting for transfers between devices: 130 us -> none  [on_device(): lax.psum_scatter(result, 'row', scatter_dimension=0, tiled=True)]
    all_gather x2 -> x0, blocking collectives: 80.5 us -> none  [the longest x1 43.2 us: on_device(): right_all = lax.all_gather(right_proj, 'row', axis=0, tiled=True)]
    all_to_all x0 -> x3, waiting for transfers between devices: none -> 28.5 us  [the longest x2 19.6 us: spread_all(): lax.all_to_all(copies, 'row', split_axis=0, concat_axis=0, tiled=True)]
    all_to_all x0 -> x3, starting transfers between devices: none -> 8.17 us  [the longest x2 5.58 us: spread_all(): lax.all_to_all(copies, 'row', split_axis=0, concat_axis=0, tiled=True)]
    all_to_all x1, waiting for transfers between devices: 0.01 us -> 6.2 us  [on_device(): lax.all_to_all(left_proj, 'row', split_axis=1, concat_axis=0, tiled=True)]
  transfers between devices with their start and end apart: 2 -> 4, of which waited for: 1 -> 4; matrix products, arithmetic and copies ran while one was open for 5% -> 10% of each run, Pallas kernels for 0% -> 0%
where the time goes in v1:
time: 89.8 us; the launch traced here: 89.1 us
  waiting for transfers between devices  34.7 us (39%)
  local copies, waits for them, and re-layouts  17.2 us (19%)
  starting transfers between devices  15.5 us (17%)
  matrix products  12.6 us (14%)
  other arithmetic  7.81 us (9%)
  between operations  1.14 us (1%)
    all_to_all x2, waiting for transfers between devices, spread_all(): lax.all_to_all(copies, 'row', split_axis=0, concat_axis=0, tiled=True)  19.6 us
    all_to_all x1, waiting for transfers between devices, on_device(): lax.all_to_all(result.astype(jnp.bfloat16).reshape((-1,) + (rows_here,) +...  8.98 us
    all_to_all x1, starting transfers between devices, on_device(): lax.all_to_all(left_proj, 'row', split_axis=1, concat_axis=0, tiled=True)  7.3 us
    all_to_all x1, waiting for transfers between devices, on_device(): lax.all_to_all(left_proj, 'row', split_axis=1, concat_axis=0, tiled=True)  6.2 us
    all_to_all x2, starting transfers between devices, spread_all(): lax.all_to_all(copies, 'row', split_axis=0, concat_axis=0, tiled=True)  5.58 us
    reshape x1, local copies, waits for them, and re-layouts, on_device(): outer_sum.astype(jnp.bfloat16)  4.45 us
    dot_general x1, matrix products, on_device(): jnp.einsum('ipjq,pqz->ijz', outer_half, outer_weight, preferred_element_t...  3.74 us
    unnamed x26, local copies, waits for them, and re-layouts  3.71 us
  transfers between devices with their start and end apart: 4, of which 4 were waited for; matrix products, arithmetic and copies ran while one was open for 10% of the time, Pallas kernels for 0%

profile of v1, /device:TPU:0, one launch (start us, length us, event | category | flops | bytes accessed | tf_op | source)
XLA Modules:
  0.0 89.1 jit_solution(2770749636973778153)
XLA Ops:
  0.6 0.7 convert_element_type.79
  1.4 0.7 convert_element_type.80
  2.0 1.0 %convert_reduce_fusion.2 = f32[2,128]{1,0:T(2,128)S(1)} fusion(bf16[2,128,256]{2,1,0:T(8,128)(2,1)} %param.18), kind=kLoop, calls=%fused_computation.66 | loop fusion | flops 130816 | bytes 132096 | tf_op jit(solution)/shard_map/reduce_sum | solution.py:12
  3.0 1.1 %fusion.54 = f32[2,128]{1,0:T(2,128)S(1)} fusion(bf16[2,128,256]{2,1,0:T(8,128)(2,1)} %param.18, f32[2,128]{1,0:T(2,128)S(1)} %broadcast_multiply_fusion.4), kind=kLoop, calls=%fused_computation.78 | loop fusion | flops 261888 | bytes 133120 | tf_op jit(solution)/shard_map/reduce_sum | solution.py:13
  4.1 1.0 %fusion.55 = bf16[2,128,256]{2,1,0:T(8,128)(2,1)S(1)} fusion(bf16[2,128,256]{2,1,0:T(8,128)(2,1)} %param.18, f32[2,128]{1,0:T(2,128)S(1)} %add_rsqrt_fusion.1, f32[2,128]{1,0:T(2,128)S(1)} %broadcast_multiply_fusion.4), kind=kLoop, calls=%fused_computation.79 | loop fusion | flops 262144 | bytes 264192 | tf_op jit(solution)/shard_map/convert_element_type | solution.py:87
  5.3 0.9 fusion.40
  6.2 0.2 copy.63
  6.4 0.7 reshape.188
  7.1 7.3 %all-to-all-start = ((bf16[32,2,128]{2,1,0:T(2,128)(2,1)}), bf16[32,2,128]{2,1,0:T(2,128)(2,1)S(1)}, u32[]{:S(2)}, u32[]{:S(2)}) async-start(bf16[32,2,128]{2,1,0:T(2,128)(2,1)} %reshape.188), calls=%async_computation | async-start | bytes 32768 | tf_op jit(solution)/shard_map/all_to_all | solution.py:103
  14.4 0.9 fusion.41
  15.3 6.2 %all-to-all-done = bf16[32,2,128]{2,1,0:T(2,128)(2,1)S(1)} async-done(((bf16[32,2,128]{2,1,0:T(2,128)(2,1)}), bf16[32,2,128]{2,1,0:T(2,128)(2,1)S(1)}, u32[]{:S(2)}, u32[]{:S(2)}) %all-to-all-start) | async-done | bytes 16416 | tf_op jit(solution)/shard_map/all_to_all | solution.py:103
  21.5 0.9 %broadcast_in_dim.20 = bf16[32,2,128,32]{2,3,1,0:T(8,128)(2,1)} broadcast(bf16[2,128,32]{1,2,0:T(8,128)(2,1)S(1)} %fusion.41), dimensions={1,2,3} | broadcast | bytes 540672 | tf_op jit(solution)/shard_map/broadcast_in_dim | solution.py:30
  22.4 2.6 %all-to-all-start.1 = ((bf16[32,2,128,32]{2,3,1,0:T(8,128)(2,1)}), bf16[32,2,128,32]{2,3,1,0:T(8,128)(2,1)S(1)}, u32[]{:S(2)}, u32[]{:S(2)}) async-start(bf16[32,2,128,32]{2,3,1,0:T(8,128)(2,1)} %broadcast_in_dim.20), calls=%async_computation.1 | async-start | bytes 1048576 | tf_op jit(solution)/shard_map/all_to_all | solution.py:31
  25.0 1.0 %copy.62 = bf16[4,128,128]{1,2,0:T(8,128)(2,1)S(1)} copy(bf16[4,128,128]{2,1,0:T(8,128)(2,1)} %param.19) | data formatting | bytes 262144 | tf_op args[1]
  26.0 1.3 %convert_reduce_fusion.3 = f32[]{:T(128)} fusion(s32[64]{0:T(128)} %param.21), kind=kLoop, calls=%fused_computation.103 | loop fusion | flops 127 | bytes 260 | tf_op jit(solution)/shard_map/reduce_sum | solution.py:118
  27.3 0.7 dynamic-slice_multiply_fusion
  28.1 1.1 %convolution_convert_fusion.4 = bf16[256,256]{1,0:T(8,128)(2,1)S(1)} fusion(bf16[256,256]{1,0:T(8,128)(2,1)S(1)} %bitcast.160, bf16[256,256]{1,0:T(8,128)(2,1)} %param.28), kind=kOutput, calls=%fused_computation.52 | convolution fusion | flops 33619968 | bytes 393216 | tf_op jit(solution)/shard_map/dot_general | solution.py:140
  29.2 1.1 %convolution_convert_fusion.3 = bf16[256,256]{1,0:T(8,128)(2,1)S(1)} fusion(bf16[256,256]{1,0:T(8,128)(2,1)S(1)} %bitcast.161, bf16[256,256]{1,0:T(8,128)(2,1)} %param.27), kind=kOutput, calls=%fused_computation.51 | convolution fusion | flops 33619968 | bytes 393216 | tf_op jit(solution)/shard_map/dot_general | solution.py:127
  30.4 0.1 reshape.172
  30.5 10.0 %all-to-all-done.1 = bf16[32,2,128,32]{2,3,1,0:T(8,128)(2,1)S(1)} async-done(((bf16[32,2,128,32]{2,3,1,0:T(8,128)(2,1)}), bf16[32,2,128,32]{2,3,1,0:T(8,128)(2,1)S(1)}, u32[]{:S(2)}, u32[]{:S(2)}) %all-to-all-start.1) | async-done | bytes 524320 | tf_op jit(solution)/shard_map/all_to_all | solution.py:31
  40.5 1.2 %copy.66 = bf16[32,2,128,32]{3,2,1,0:T(8,128)(2,1)S(1)} copy(bf16[32,2,128,32]{2,3,1,0:T(8,128)(2,1)S(1)} %all-to-all-done.1) | data formatting | bytes 1048576 | tf_op jit(solution)/shard_map/all_to_all | solution.py:31
  41.8 2.4 %reshape_reshape.3 = bf16[64,4096]{1,0:T(8,128)(2,1)S(1)} reshape(bf16[32,2,128,32]{3,2,1,0:T(8,128)(2,1)S(1)} %copy.66) | data formatting | bytes 1048576 | tf_op jit(solution)/shard_map/reshape;reshape | solution.py:108
  44.2 0.5 convolution_convert_fusion
  44.6 4.4 %reshape.173 = bf16[4,32,128,32]{3,2,1,0:T(8,128)(2,1)} reshape(bf16[128,4096]{1,0:T(8,128)(2,1)S(1)} %convolution_convert_fusion) | data formatting | bytes 2097152 | tf_op jit(solution)/shard_map/reshape | solution.py:112
  49.1 3.7 %convert_reduce_fusion.1 = (f32[4,128]{1,0:T(4,128)S(1)}, bf16[4,128,128]{1,2,0:T(8,128)(2,1)S(1)}) fusion(f32[4,128]{1,0:T(4,128)S(1)} %multiply_maximum_fusion, bf16[4,32,128,32]{3,2,1,0:T(8,128)(2,1)} %reshape.173, bf16[32,32,128]{2,1,0:T(8,128)(2,1)S(1)} %copy-done, bf16[4,128,128]{1,2,0:T(8,128)(2,1)S(1)} %copy.62), kind=kOutput, calls=%fused_computation.64 | convolution fusion | flops 134610432 | bytes 1576960 | tf_op jit(solution)/shard_map/ipjq,pqz->ijz/dot_general | solution.py:115
  52.9 0.1 fusion.42
  53.1 0.7 broadcast_in_dim.21
  53.8 3.0 %all-to-all-start.2 = ((bf16[32,4,8,128]{3,2,1,0:T(8,128)(2,1)}), bf16[32,4,8,128]{3,2,1,0:T(8,128)(2,1)S(1)}, u32[]{:S(2)}, u32[]{:S(2)}) async-start(bf16[32,4,8,128]{3,2,1,0:T(8,128)(2,1)} %broadcast_in_dim.21), calls=%async_computation.2 | async-start | bytes 524288 | tf_op jit(solution)/shard_map/all_to_all | solution.py:31
  56.8 0.2 convolution_convert_fusion.2
  57.1 0.1 copy.60
  57.2 0.1 copy.61
  57.4 0.1 copy.69
  57.6 0.2 fusion.36
  57.9 9.6 %all-to-all-done.2 = bf16[32,4,8,128]{3,2,1,0:T(8,128)(2,1)S(1)} async-done(((bf16[32,4,8,128]{3,2,1,0:T(8,128)(2,1)}), bf16[32,4,8,128]{3,2,1,0:T(8,128)(2,1)S(1)}, u32[]{:S(2)}, u32[]{:S(2)}) %all-to-all-start.2) | async-done | bytes 262176 | tf_op jit(solution)/shard_map/all_to_all | solution.py:31
  67.4 0.2 copy.72
  67.7 2.7 %while.25 = (s32[]{:T(128)}, f32[2,128,8]{1,2,0:T(8,128)}, f32[2,128,8]{1,2,0:T(8,128)S(1)}, f32[2,128,256]{2,1,0:T(8,128)S(1)}, bf16[2,128,8,32]{1,3,2,0:T(8,12...) while((s32[]{:T(128)}, f32[2,128,8]{1,2,0:T(8,128)}, ...), condition=%wide.region_8.9_spmd, body=%wide.region_5.8_spmd.sunk | while | flops 17954816 | bytes 2721901 | solution.py:149
  67.7 0.3 fusion.98
  68.0 0.2 fusion.100
  68.2 0.1 copy.101
  68.3 0.1 fusion.99
  68.4 0.6 bitcast_dynamic-update-slice_fusion.3
  69.0 0.3 fusion.98
  69.3 0.2 fusion.100
  69.5 0.1 copy.101
  69.7 0.1 fusion.99
  69.7 0.6 bitcast_dynamic-update-slice_fusion.3
  70.3 0.7 log_add_fusion
  71.1 0.1 copy.75
  71.2 0.2 divide_multiply_fusion
  71.5 0.1 copy.77
  71.6 0.1 copy.76
  71.8 0.2 copy.80
  72.1 1.6 %while.26 = (s32[]{:T(128)}, f32[128,8,128]{0,2,1:T(8,128)S(1)}, bf16[2,128,8,32]{1,3,2,0:T(8,128)(2,1)S(1)}, bf16[2,128,8,32]{1,3,2,0:T(8,128)(2,1)S(1)}, f32[1...) while((s32[]{:T(128)}, f32[128,8,128]{0,2,1:T(8,128)S(1)}, ...), condition=%wide.region_11.12_spmd.clone, body=%wide.region_10.11_spmd.clone.sunk | while | flops 17825796 | bytes 2910851 | solution.py:204
  72.1 0.3 fusion.105
  72.4 0.5 fusion.106
  72.9 0.3 fusion.105
  73.2 0.5 fusion.106
  73.7 0.9 %copy.82 = bf16[128,8,128]{2,1,0:T(8,128)(2,1)} copy(f32[128,8,128]{0,2,1:T(8,128)S(1)} %get-tuple-element.107) | data formatting | bytes 786432 | tf_op jit(solution)/shard_map/while | solution.py:204
  74.6 2.6 %all-to-all-start.3 = ((bf16[32,4,8,128]{3,2,1,0:T(8,128)(2,1)}), bf16[32,4,8,128]{3,2,1,0:T(8,128)(2,1)S(1)}, u32[]{:S(2)}, u32[]{:S(2)}) async-start(bf16[32,4,8,128]{3,2,1,0:T(8,128)(2,1)} %bitcast.26), calls=%async_computation.3 | async-start | bytes 524288 | tf_op jit(solution)/shard_map/all_to_all | solution.py:205
  77.2 0.8 copy.83
  78.0 0.8 convolution_convert_fusion.1
  78.8 9.0 %all-to-all-done.3 = bf16[32,4,8,128]{3,2,1,0:T(8,128)(2,1)S(1)} async-done(((bf16[32,4,8,128]{3,2,1,0:T(8,128)(2,1)}), bf16[32,4,8,128]{3,2,1,0:T(8,128)(2,1)S(1)}, u32[]{:S(2)}, u32[]{:S(2)}) %all-to-all-start.3) | async-done | bytes 262176 | tf_op jit(solution)/shard_map/all_to_all | solution.py:205
  87.9 0.3 fusion.66
  88.3 0.8 copy.84
  (52 shorter events, 0.9 us)
Async XLA Ops:
  0.6 48.4 %copy-start = (bf16[32,32,128]{2,1,0:T(8,128)(2,1)S(1)}, bf16[32,32,128]{2,1,0:T(8,128)(2,1)}, u32[]{:S(2)}) copy-start(bf16[32,32,128]{2,1,0:T(8,128)(2,1)} %param.25) | copy-start | bytes 786436
  7.1 14.4 %all-to-all-start = ((bf16[32,2,128]{2,1,0:T(2,128)(2,1)}), bf16[32,2,128]{2,1,0:T(2,128)(2,1)S(1)}, u32[]{:S(2)}, u32[]{:S(2)}) async-start(bf16[32,2,128]{2,1,0:T(2,128)(2,1)} %reshape.188), calls=%async_computation | async-start | bytes 32768 | tf_op jit(solution)/shard_map/all_to_all | solution.py:103
  22.4 18.2 %all-to-all-start.1 = ((bf16[32,2,128,32]{2,3,1,0:T(8,128)(2,1)}), bf16[32,2,128,32]{2,3,1,0:T(8,128)(2,1)S(1)}, u32[]{:S(2)}, u32[]{:S(2)}) async-start(bf16[32,2,128,32]{2,3,1,0:T(8,128)(2,1)} %broadcast_in_dim.20), calls=%async_computation.1 | async-start | bytes 1048576 | tf_op jit(solution)/shard_map/all_to_all | solution.py:31
  44.6 8.3 %copy-start.6 = (bf16[128,8]{0,1:T(8,128)(2,1)S(1)}, bf16[128,8]{0,1:T(8,128)(2,1)}, u32[]{:S(2)}) copy-start(bf16[128,8]{0,1:T(8,128)(2,1)} %param.26) | copy-start | bytes 6148
  49.1 7.7 %copy-start.2 = (bf16[256,256]{1,0:T(8,128)(2,1)S(1)}, bf16[256,256]{1,0:T(8,128)(2,1)}, u32[]{:S(2)}) copy-start(bf16[256,256]{1,0:T(8,128)(2,1)} %param.29) | copy-start | bytes 393220
  49.1 8.5 %copy-start.9 = (s32[128]{0:T(128)S(1)}, s32[128]{0:T(128)}, u32[]{:S(2)}) copy-start(s32[128]{0:T(128)} %param.22) | copy-start | bytes 1540
  49.1 8.5 %copy-start.8 = (bf16[256,256]{1,0:T(8,128)(2,1)S(1)}, bf16[256,256]{1,0:T(8,128)(2,1)}, u32[]{:S(2)}) copy-start(bf16[256,256]{1,0:T(8,128)(2,1)} %param.30) | copy-start | bytes 393220
  52.9 4.1 %copy-start.4 = (f32[4,128]{1,0:T(4,128)}, f32[4,128]{1,0:T(4,128)S(1)}, u32[]{:S(2)}) copy-start(f32[4,128]{1,0:T(4,128)S(1)} %add_rsqrt_fusion) | copy-start | bytes 6148
  53.8 13.6 %all-to-all-start.2 = ((bf16[32,4,8,128]{3,2,1,0:T(8,128)(2,1)}), bf16[32,4,8,128]{3,2,1,0:T(8,128)(2,1)S(1)}, u32[]{:S(2)}, u32[]{:S(2)}) async-start(bf16[32,4,8,128]{3,2,1,0:T(8,128)(2,1)} %broadcast_in_dim.21), calls=%async_computation.2 | async-start | bytes 524288 | tf_op jit(solution)/shard_map/all_to_all | solution.py:31
  67.6 3.6 %copy-start.1 = (bf16[256,256]{1,0:T(8,128)(2,1)S(1)}, bf16[256,256]{1,0:T(8,128)(2,1)}, u32[]{:S(2)}) copy-start(bf16[256,256]{1,0:T(8,128)(2,1)} %param.31) | copy-start | bytes 393220
  67.6 3.6 %copy-start.3 = (bf16[2,128,256]{2,1,0:T(8,128)(2,1)S(1)}, bf16[2,128,256]{2,1,0:T(8,128)(2,1)}, u32[]{:S(2)}) copy-start(bf16[2,128,256]{2,1,0:T(8,128)(2,1)} %param.20) | copy-start | bytes 393220
  72.1 15.8 %copy-start.5 = (f32[4,128]{1,0:T(4,128)S(1)}, f32[4,128]{1,0:T(4,128)}, u32[]{:S(2)}) copy-start(f32[4,128]{1,0:T(4,128)} %copy-done.4) | copy-start | bytes 6148
  72.1 15.8 %copy-start.7 = (bf16[128,8]{0,1:T(8,128)(2,1)S(1)}, bf16[128,8]{0,1:T(8,128)(2,1)}, u32[]{:S(2)}) copy-start(bf16[128,8]{0,1:T(8,128)(2,1)} %param.26) | copy-start | bytes 6148
  74.6 13.2 %all-to-all-start.3 = ((bf16[32,4,8,128]{3,2,1,0:T(8,128)(2,1)}), bf16[32,4,8,128]{3,2,1,0:T(8,128)(2,1)S(1)}, u32[]{:S(2)}, u32[]{:S(2)}) async-start(bf16[32,4,8,128]{3,2,1,0:T(8,128)(2,1)} %bitcast.26), calls=%async_computation.3 | async-start | bytes 524288 | tf_op jit(solution)/shard_map/all_to_all | solution.py:205

commit v2 on v1

--- a/solution.py
+++ b/solution.py
@@ -1,6 +1,8 @@
 import jax
 import jax.numpy as jnp
 from jax import lax
+from jax.experimental import pallas as pl
+from jax.experimental.pallas import tpu as pltpu
 from jax.sharding import PartitionSpec as P
 
 norm_eps = 1e-05
@@ -51,7 +53,7 @@
     return (maxima, totals, summed.reshape(summed.shape[0], -1))
 
 
-def on_device(
+def on_device_general(
     alignment_rows,
     pair_state,
     update_cotangent,
@@ -220,6 +222,319 @@
     return (alignment_update, pair_updated, pair_gradient)
 
 
+LANES = 128
+LEFT_ROWS = 4
+STRIDE = 40
+f32 = jnp.float32
+bf16 = jnp.bfloat16
+
+
+def dot_nn(a, b):
+    return lax.dot_general(a, b, (((1,), (0,)), ((), ())), preferred_element_type=f32)
+
+
+def dot_nt(a, b):
+    return lax.dot_general(a, b, (((1,), (1,)), ((), ())), preferred_element_type=f32)
+
+
+def dot_tn(a, b):
+    return lax.dot_general(a, b, (((0,), (0,)), ((), ())), preferred_element_type=f32)
+
+
+def lane_index(rows):
+    return lax.broadcasted_iota(jnp.int32, (rows, LANES), 1)
+
+
+def factors_kernel(seq_ref, res_ref, rows_ref, left_ref, right_ref, send_ref, normed_ref, left_scr):
+    seqs = send_ref.shape[2] // 18
+    residues = res_ref.shape[1]
+    chips = send_ref.shape[0]
+    me = lax.axis_index("row")
+    normed = layer_normalize(rows_ref[...]).astype(bf16)
+    normed_ref[...] = normed
+    live = res_ref[...].astype(f32)
+    live_rows = jnp.broadcast_to(live, (residues, residues)).T
+    right_t = right_ref[...].astype(f32).T.astype(bf16)
+    left_wide = jnp.concatenate([left_ref[...]] * 4, axis=1)
+    low = lane_index(16) < 64
+    lane_group = lane_index(chips) // 32
+    halves = ([], [])
+    tail = []
+    for s in range(seqs):
+        seq_live = seq_ref[me * seqs + s].astype(f32)
+        own = normed[s * residues : (s + 1) * residues]
+        factor = dot_nt(right_t, own) * (live * seq_live)
+        first, second = factor[:16], factor[16:]
+        halves[0].append(jnp.where(low, first, pltpu.roll(second, 64, 1)))
+        halves[1].append(jnp.where(low, pltpu.roll(first, 64, 1), second))
+        left_scr[...] = dot_nn(own, left_wide) * (live_rows * seq_live)
+        for a in range(2):
+            row = jnp.zeros((chips, LANES), f32)
+            for b in range(4):
+                part = left_scr[pl.ds(4 * a + b, chips, stride=8), :]
+                row = jnp.where(lane_group == b, part, row)
+            tail.append(row)
+    tail = jnp.stack(tail, axis=1).astype(bf16)
+    right_rows = 16 * seqs
+    for core in range(2):
+        block = jnp.concatenate(halves[core], axis=0).astype(bf16)
+        send_ref[:, core, :right_rows, :] = jnp.broadcast_to(block[None], (chips, right_rows, LANES))
+        send_ref[:, core, right_rows:, :] = tail
+
+
+def projections_kernel(
+    normed_ref, cot_ref, wq_ref, wk_ref, wv_ref, wg_ref, wo_ref, q_ref, k_ref, v_ref, gate_ref, d_ref
+):
+    normed = normed_ref[...]
+    q_ref[...] = dot_nn(normed, wq_ref[...]).astype(bf16)
+    k_ref[...] = dot_nn(normed, wk_ref[...]).astype(bf16)
+    v_ref[...] = dot_nn(normed, wv_ref[...]).astype(bf16)
+    gate = jax.nn.sigmoid(dot_nn(normed, wg_ref[...]))
+    gate_ref[...] = gate
+    d_ref[...] = (dot_nt(cot_ref[...], wo_ref[...]) * gate).astype(bf16)
+
+
+def pair_kernel(recv_ref, weight_ref, pair_ref, div_ref, bias_w_ref, send_ref, updated_ref, flat, rbuf, lbuf, obuf):
+    peers, block_rows, _ = recv_ref.shape
+    seqs = block_rows // 18
+    for p in range(peers):
+        flat[p * STRIDE : p * STRIDE + block_rows, :] = recv_ref[p].astype(f32)
+    for s in range(seqs):
+        for g in range(16):
+            part = flat[pl.ds(s * 16 + g, peers, stride=STRIDE), :]
+            rbuf[s * peers : (s + 1) * peers, g * LANES : (g + 1) * LANES] = part.astype(bf16)
+        for a in range(2):
+            part = flat[pl.ds(16 * seqs + 2 * s + a, peers, stride=STRIDE), :]
+            lbuf[s * peers : (s + 1) * peers, a * LANES : (a + 1) * LANES] = part.astype(bf16)
+    left_t = lbuf[...].astype(f32).T.astype(bf16)
+    for g in range(16):
+        outer = dot_nn(left_t, rbuf[:, g * LANES : (g + 1) * LANES]).astype(bf16)
+        for i in range(8):
+            obuf[g * 32 : (g + 1) * 32, i * LANES : (i + 1) * LANES] = outer[i * 32 : (i + 1) * 32]
+    sums = dot_nn(weight_ref[...], obuf[...])
+    low = lane_index(LANES) < 64
+
+    def piece(a, i):
+        return sums[a * LANES : (a + 1) * LANES, i * LANES : (i + 1) * LANES]
+
+    blocks = []
+    bias_w = bias_w_ref[...]
+    for b in range(4):
+        straight = jnp.where(low, piece(0, b), piece(1, b + 4))
+        crossed = jnp.where(low, piece(0, b + 4), piece(1, b))
+        update = (straight + pltpu.roll(crossed, 64, 1)) / div_ref[b : b + 1, :]
+        state = jnp.concatenate([pair_ref[b], pair_ref[b + 4]], axis=0).astype(f32)
+        updated = (state + update.T).astype(bf16)
+        updated_ref[b] = updated[:64]
+        updated_ref[b + 4] = updated[64:]
+        pair_normed = layer_normalize(updated).astype(bf16)
+        blocks.append(dot_nt(bias_w, pair_normed))
+    block = jnp.concatenate(blocks, axis=0).astype(bf16)
+    send_ref[...] = jnp.broadcast_to(block[None], send_ref.shape)
+
+
+def attention_kernel(
+    scale, bias_ref, res_ref, q_ref, k_ref, v_ref, gate_ref, d_ref, send_ref, gated_ref, flat, grads
+):
+    residues = res_ref.shape[1]
+    channels = q_ref.shape[1]
+    seqs = q_ref.shape[0] // residues
+    heads = flat.shape[0] // residues
+    flat[...] = bias_ref[...].reshape(flat.shape).astype(f32)
+    key_mask = (res_ref[...].astype(f32) - 1.0) * mask_fill
+    sub = lax.broadcasted_iota(jnp.int32, (residues, LANES), 0) % 8
+    keep = (sub < 4) == (lane_index(residues) < 64)
+    head_of = lax.broadcasted_iota(jnp.int32, (1, channels), 1) // (channels // heads)
+    attended = [jnp.zeros((residues, channels), f32) for _ in range(seqs)]
+    for h in range(heads):
+        raw = flat[pl.ds(h, residues, stride=heads), :]
+        up, down = pltpu.roll(raw, residues - 4, 0), pltpu.roll(raw, 4, 0)
+        moved = pltpu.roll(jnp.where(sub < 4, up, down), 64, 1)
+        bias = jnp.where(keep, raw, moved) + key_mask
+        of_head = head_of == h
+        total = jnp.zeros((residues, residues), f32)
+        for s in range(seqs):
+            at = slice(s * residues, (s + 1) * residues)
+            q = jnp.where(of_head, q_ref[at, :], jnp.zeros((), bf16))
+            d = jnp.where(of_head, d_ref[at, :], jnp.zeros((), bf16))
+            scores = dot_nt(q, k_ref[at, :]) * scale + bias
+            weights = jnp.exp(scores - jnp.max(scores, axis=-1, keepdims=True))
+            inverse = 1.0 / jnp.sum(weights, axis=-1, keepdims=True)
+            mixed = dot_nn(weights.astype(bf16), v_ref[at, :]) * inverse
+            attended[s] = jnp.where(of_head, mixed, attended[s])
+            probs = weights * inverse
+            flow = probs * dot_nt(d, v_ref[at, :])
+            total = total + (flow - probs * jnp.sum(flow, axis=-1, keepdims=True))
+        grads[pl.ds(h, residues, stride=heads), :] = total
+    send_ref[...] = grads[...].astype(bf16).reshape(send_ref.shape)
+    for s in range(seqs):
+        at = slice(s * residues, (s + 1) * residues)
+        gated_ref[at, :] = (gate_ref[at, :] * attended[s]).astype(bf16)
+
+
+def output_kernel(gated_ref, wo_ref, out_ref):
+    out_ref[...] = dot_nn(gated_ref[...], wo_ref[...]).astype(bf16)
+
+
+def gradient_kernel(shares_ref, bias_w_ref, pair_ref, out_ref):
+    total = jnp.sum(shares_ref[...].astype(f32), axis=0)
+    rows = pair_ref.shape[0]
+    heads = total.shape[0] // rows
+    bias_w = bias_w_ref[...].astype(f32)
+    for i in range(rows):
+        own = total[i * heads : (i + 1) * heads]
+        upstream = lax.dot_general(
+            own, bias_w, (((0,), (0,)), ((), ())), precision=lax.Precision.HIGHEST, preferred_element_type=f32
+        )
+        out_ref[i] = norm_backward(pair_ref[i], upstream)
+
+
+def kernel_call(body, out_shape, in_specs=None, scratch=(), flops=0, moved=0):
+    vmem = pl.BlockSpec(memory_space=pltpu.VMEM)
+    many = isinstance(out_shape, (list, tuple))
+    return pl.pallas_call(
+        body,
+        out_shape=out_shape,
+        in_specs=in_specs,
+        out_specs=[vmem] * len(out_shape) if many else vmem,
+        scratch_shapes=list(scratch),
+        compiler_params=pltpu.CompilerParams(vmem_limit_bytes=24 * 1024 * 1024),
+        cost_estimate=pl.CostEstimate(flops=flops, bytes_accessed=moved, transcendentals=0),
+    )
+
+
+def on_device_paired(
+    alignment_rows,
+    pair_state,
+    update_cotangent,
+    sequence_mask,
+    residue_mask,
+    left_weight,
+    right_weight,
+    outer_weight,
+    bias_weight,
+    query_weight,
+    key_weight,
+    value_weight,
+    gate_weight,
+    output_weight,
+):
+    sequence_wise, residues, channel_count = alignment_rows.shape
+    rows_here, _, pair_channels = pair_state.shape
+    head_count = bias_weight.shape[1]
+    peers = lax.axis_size("row")
+    factor = left_weight.shape[1]
+    chips = peers // 2
+    vmem = pl.BlockSpec(memory_space=pltpu.VMEM)
+    smem = pl.BlockSpec(memory_space=pltpu.SMEM)
+    me = lax.axis_index("row")
+    core = me % 2
+    sibling = [(i, i ^ 1) for i in range(peers)]
+    token_rows = sequence_wise * residues
+    half = residues // 2
+    block_rows = sequence_wise * 18
+    res_row = residue_mask.reshape(1, residues)
+    flat_rows = alignment_rows.reshape(token_rows, channel_count)
+    shape = jax.ShapeDtypeStruct
+
+    send, normed = kernel_call(
+        factors_kernel,
+        [shape((chips, 2, block_rows, LANES), bf16), shape((token_rows, channel_count), bf16)],
+        [smem, vmem, vmem, vmem, vmem],
+        [pltpu.VMEM((residues, LANES), f32)],
+        flops=2 * token_rows * channel_count * LANES,
+        moved=1 << 19,
+    )(sequence_mask, res_row, flat_rows, left_weight, right_weight)
+    received = lax.all_to_all(
+        send.reshape(peers, block_rows, LANES), "row", split_axis=0, concat_axis=0, tiled=True
+    )
+
+    queries, keys, values, gate, d_rounded = kernel_call(
+        projections_kernel,
+        [shape((token_rows, channel_count), t) for t in (bf16, bf16, bf16, f32, bf16)],
+        [vmem] * 7,
+        flops=10 * token_rows * channel_count * channel_count,
+        moved=1 << 21,
+    )(
+        normed,
+        update_cotangent.reshape(token_rows, channel_count),
+        query_weight,
+        key_weight,
+        value_weight,
+        gate_weight,
+        output_weight,
+    )
+
+    def trade_columns(tile):
+        kept = lax.dynamic_slice_in_dim(tile, core * half, half, 1)
+        got = lax.ppermute(lax.dynamic_slice_in_dim(tile, (1 - core) * half, half, 1), "row", sibling)
+        return jnp.where(core == 0, jnp.concatenate([kept, got]), jnp.concatenate([got, kept]))
+
+    def trade_rows(tile):
+        kept = lax.dynamic_slice_in_dim(tile, core * rows_here, rows_here, 0)
+        got = lax.ppermute(
+            lax.dynamic_slice_in_dim(tile, (1 - core) * rows_here, rows_here, 0), "row", sibling
+        )
+        return jnp.where(
+            core == 0, jnp.concatenate([kept, got], axis=1), jnp.concatenate([got, kept], axis=1)
+        )
+
+    pair_tile = trade_columns(pair_state)
+    weight_t = (
+        outer_weight.reshape(factor, 2, 16, pair_channels)
+        .transpose(1, 3, 2, 0)
+        .reshape(2 * pair_channels, 16 * factor)
+    )
+    seq_live = sequence_mask.astype(f32)
+    res_live = residue_mask.astype(f32)
+    tile_rows = lax.dynamic_slice_in_dim(res_live, (me // 2) * 8, 8).reshape(2, 4)
+    tile_cols = lax.dynamic_slice_in_dim(res_live, core * half, half)
+    divisor = jnp.maximum(
+        jnp.sum(seq_live) * tile_rows.T[:, :, None] * tile_cols[None, None, :], 1.0
+    ).reshape(4, 2 * half)
+    bias_rows = 4 * head_count
+    send_bias, updated_tile = kernel_call(
+        pair_kernel,
+        [shape((peers, bias_rows, LANES), bf16), shape((8, half, pair_channels), bf16)],
+        [vmem] * 5,
+        [
+            pltpu.VMEM((peers * STRIDE, LANES), f32),
+            pltpu.VMEM((peers * sequence_wise, 16 * LANES), bf16),
+            pltpu.VMEM((peers * sequence_wise, 2 * LANES), bf16),
+            pltpu.VMEM((16 * factor, 8 * LANES), bf16),
+        ],
+        flops=1 << 29,
+        moved=1 << 20,
+    )(received, weight_t, pair_tile, divisor, bias_weight.T)
+    bias_all = lax.all_to_all(send_bias, "row", split_axis=0, concat_axis=0, tiled=True)
+    pair_updated = trade_rows(updated_tile)
+
+    send_grad, gated = kernel_call(
+        lambda *refs: attention_kernel((channel_count // head_count) ** (-0.5), *refs),
+        [shape((peers, rows_here * head_count, LANES), bf16), shape((token_rows, channel_count), bf16)],
+        [vmem] * 7,
+        [pltpu.VMEM((residues * head_count, LANES), f32), pltpu.VMEM((residues * head_count, LANES), f32)],
+        flops=1 << 29,
+        moved=1 << 21,
+    )(bias_all, res_row, queries, keys, values, gate, d_rounded)
+    shares = lax.all_to_all(send_grad, "row", split_axis=0, concat_axis=0, tiled=True)
+    update = kernel_call(
+        output_kernel,
+        shape((token_rows, channel_count), bf16),
+        [vmem] * 2,
+        flops=2 * token_rows * channel_count * channel_count,
+        moved=1 << 19,
+    )(gated, output_weight)
+    pair_gradient = kernel_call(
+        gradient_kernel,
+        shape((rows_here, residues, pair_channels), f32),
+        [vmem] * 3,
+        flops=1 << 24,
+        moved=1 << 20,
+    )(shares, bias_weight.T, pair_updated)
+    return (update.reshape(alignment_rows.shape), pair_updated, pair_gradient)
+
+
 def solution(mesh):
     placed = (
         P(("grp", "row"), "col", None),
@@ -237,8 +552,9 @@
         P(),
         P(),
     )
+    one_column = mesh.shape["col"] == 1 and mesh.shape["row"] % 2 == 0
     return jax.shard_map(
-        on_device,
+        on_device_paired if one_column else on_device_general,
         mesh=mesh,
         in_specs=placed,
         out_specs=(

time: 89.8 us -> 59.5 us (0.66)
  local copies, waits for them, and re-layouts: 17.2 us -> 2.66 us
  matrix products: 12.6 us -> 0 us
  Pallas kernels: 0 us -> 12.1 us
  other arithmetic: 7.81 us -> 1.38 us
  waiting for transfers between devices: 34.7 us -> 28.9 us
  starting transfers between devices: 15.5 us -> 13.1 us
    dot_general x20 -> x0, matrix products: 12.6 us -> none  [the longest x1 3.74 us: on_device(): jnp.einsum('ipjq,pqz->ijz', outer_half, outer_weight, preferred_element_t...]
    pallas_call x0 -> x6, Pallas kernels: none -> 12.1 us  [the longest x1 5.38 us: on_device_paired(): kernel_call(lambda *refs: attention_kernel((channel_count // head_count)...]
    all_to_all x4 -> x3, waiting for transfers between devices: 34.7 us -> 27.8 us  [the longest x1 10.2 us: on_device_paired(): lax.all_to_all(send_bias, 'row', split_axis=0, concat_axis=0, tiled=True)]
    reshape x6 -> x2, local copies, waits for them, and re-layouts: 4.79 us -> 0.39 us  [the longest x1 0.25 us: on_device_paired(): outer_weight.reshape(factor, 2, 16, pair_channels).transpose(1, 3, 2, 0)]
    reduce_sum x8 -> x1, other arithmetic: 3.67 us -> 0.6 us  [on_device_paired(): jnp.sum(seq_live) * tile_rows.T[:, :, None] * tile_cols[None, None, :]]
    all_to_all x4 -> x3, starting transfers between devices: 15.5 us -> 12.6 us  [the longest x1 7.3 us: on_device_paired(): lax.all_to_all(send.reshape(peers, block_rows, LANES), 'row', split_axis=...]
    convert_element_type x4 -> x1, other arithmetic: 2.45 us -> 0.01 us  [on_device_paired(): res_live = residue_mask.astype(f32)]
    another operation x1 -> x0, local copies, waits for them, and re-layouts: 2.38 us -> none  [on_device(): right_all.reshape(right_all.shape[0], -1)]
  transfers between devices with their start and end apart: 4 -> 5, of which waited for: 4 -> 4; matrix products, arithmetic and copies ran while one was open for 10% -> 4% of each run, Pallas kernels for 0% -> 2%
where the time goes in v2:
time: 59.5 us; the launch traced here: 59 us
  waiting for transfers between devices  28.9 us (49%)
  starting transfers between devices  13.1 us (22%)
  Pallas kernels  12.1 us (20%)
  local copies, waits for them, and re-layouts  2.66 us (4%)
  other arithmetic  1.38 us (2%)
  between operations  0.9 us (2%)
    all_to_all x1, waiting for transfers between devices, on_device_paired(): lax.all_to_all(send_bias, 'row', split_axis=0, concat_axis=0, tiled=True)  10.2 us
    all_to_all x1, waiting for transfers between devices, on_device_paired(): lax.all_to_all(send.reshape(peers, block_rows, LANES), 'row', split_axis=...  9.27 us
    all_to_all x1, waiting for transfers between devices, on_device_paired(): lax.all_to_all(send_grad, 'row', split_axis=0, concat_axis=0, tiled=True)  8.34 us
    all_to_all x1, starting transfers between devices, on_device_paired(): lax.all_to_all(send.reshape(peers, block_rows, LANES), 'row', split_axis=...  7.3 us
    pallas_call x1, Pallas kernels, on_device_paired(): kernel_call(lambda *refs: attention_kernel((channel_count // head_count)...  5.38 us
    all_to_all x1, starting transfers between devices, on_device_paired(): lax.all_to_all(send_bias, 'row', split_axis=0, concat_axis=0, tiled=True)  2.74 us
    all_to_all x1, starting transfers between devices, on_device_paired(): lax.all_to_all(send_grad, 'row', split_axis=0, concat_axis=0, tiled=True)  2.59 us
    pallas_call x1, Pallas kernels, on_device_paired(): kernel_call(pair_kernel, [shape((peers, bias_rows, LANES), bf16), shape((...  2.14 us
  transfers between devices with their start and end apart: 5, of which 4 were waited for; matrix products, arithmetic and copies ran while one was open for 4% of the time, Pallas kernels for 2%

profile of v2, /device:TPU:0, one launch (start us, length us, event | category | flops | bytes accessed | tf_op | source)
XLA Modules:
  0.0 59.0 jit_solution(8799013079948567999)
XLA Ops:
  0.6 0.0 copy-start.13
  0.6 0.0 copy-start.7
  0.7 0.9 %copy.21.left_ref = bf16[256,32]{1,0:T(8,128)(2,1)S(1)} copy(bf16[256,32]{0,1:T(8,128)(2,1)} %param.19) | data formatting | bytes 32768 | tf_op args[5]
  1.5 0.0 copy-done.13
  1.5 0.1 copy.22.right_ref
  1.6 0.0 copy-start.9
  1.7 0.0 copy-start.10
  1.7 0.0 copy-done.7
  1.7 0.6 %copy-done.9 = s32[64]{0:T(128)S(1)} copy-done((s32[64]{0:T(128)S(1)}, s32[64]{0:T(128)}, u32[]{:S(2)}) %copy-start.9) | copy-done | bytes 280
  2.3 0.0 copy-done.10
  2.3 1.9 %shard_map.157 = (bf16[16,2,36,128]{3,2,1,0:T(8,128)(2,1)}, bf16[256,256]{1,0:T(8,128)(2,1)S(1)}) custom-call(s32[64]{0:T(128)S(1)} %copy-done.9, s32[1,128]{1,0:T(1,128)S(1)} %bitcast.20, bf16[256,256]{1,0:T(8,128)(2,1)S(1)} %bitcast.17, bf16[256,32]{1,0:T(8,128)(2,1)S(1)} %copy.21.left_ref, bf16[256,32]{1,0:T(8,128)(2,1)S(1)} %copy.22.right_ref), custom_call_target="tpu_custom_call" | custom-call | flops 16777216 | bytes 524288 | tf_op jit(solution)/shard_map/pallas_call | solution.py:440
  4.2 0.0 copy-start.12
  4.2 7.3 %all-to-all-start = ((bf16[32,36,128]{2,1,0:T(8,128)(2,1)}), bf16[32,36,128]{2,1,0:T(8,128)(2,1)S(1)}, u32[]{:S(2)}, u32[]{:S(2)}) async-start(bf16[32,36,128]{2,1,0:T(8,128)(2,1)} %bitcast.2), calls=%async_computation | async-start | bytes 655360 | tf_op jit(solution)/shard_map/all_to_all | solution.py:448
  11.5 0.0 copy-start.11
  11.5 0.0 copy-done.12
  11.6 0.3 collective-permute-start
  11.9 0.1 dynamic_slice.21
  12.0 0.1 mul.59
  12.1 0.6 %convert_reduce_fusion = f32[]{:T(128)} fusion(s32[64]{0:T(128)S(1)} %copy-done.9), kind=kLoop, calls=%fused_computation.9 | loop fusion | flops 127 | bytes 260 | tf_op jit(solution)/shard_map/reduce_sum | solution.py:493
  12.7 0.7 %dynamic-slice_multiply_fusion = f32[8]{0:T(128)S(1)} fusion(f32[128]{0:T(128)S(1)} %convert_element_type.7, s32[]{:T(128)S(6)} %select_n.49, f32[]{:T(128)} %convert_reduce_fusion), kind=kLoop, calls=%fused_computation.8 | loop fusion | flops 8 | bytes 72 | tf_op jit(solution)/shard_map/mul | solution.py:493
  13.4 0.1 mul.54
  13.5 0.1 copy.24
  13.6 0.1 mul.56
  13.6 0.1 mul.57
  13.7 0.0 copy-done.11
  13.7 0.2 copy.23
  14.0 0.1 copy.25.weight_ref
  14.2 0.0 collective-permute-done
  14.2 0.0 copy-start.8
  14.2 9.3 %all-to-all-done.recv_ref = bf16[32,36,128]{2,1,0:T(8,128)(2,1)S(1)} async-done(((bf16[32,36,128]{2,1,0:T(8,128)(2,1)}), bf16[32,36,128]{2,1,0:T(8,128)(2,1)S(1)}, u32[]{:S(2)}, u32[]{:S(2)}) %all-to-all-start) | async-done | bytes 294944 | tf_op jit(solution)/shard_map/all_to_all | solution.py:448
  23.5 0.0 copy-done.8
  23.5 0.0 copy-start.5
  23.5 0.0 copy-start.6
  23.5 2.1 %shard_map.158 = (bf16[32,32,128]{2,1,0:T(8,128)(2,1)}, bf16[8,64,128]{2,1,0:T(8,128)(2,1)S(1)}) custom-call(bf16[32,36,128]{2,1,0:T(8,128)(2,1)S(1)} %all-to-all-done.recv_ref, bf16[256,512]{1,0:T(8,128)(2,1)S(1)} %copy.25.weight_ref, bf16[8,64,128]{2,1,0:T(8,128)(2,1)S(1)} %maximum_select_fusion.pair_ref, f32[4,128]{1,0:T(4,128)S(1)} %multiply_maximum_fusion.div_ref, ...), custom_call_target="tpu_custom_call" | custom-call | flops 536870912 | bytes 1048576 | tf_op jit(solution)/shard_map/pallas_call | solution.py:496
  25.6 0.0 copy-start
  25.6 0.0 copy-start.2
  25.6 0.0 copy-start.3
  25.6 0.0 copy-start.4
  25.6 2.7 %all-to-all-start.1 = ((bf16[32,32,128]{2,1,0:T(8,128)(2,1)}), bf16[32,32,128]{2,1,0:T(8,128)(2,1)S(1)}, u32[]{:S(2)}, u32[]{:S(2)}) async-start(bf16[32,32,128]{2,1,0:T(8,128)(2,1)} %get-tuple-element.15), calls=%async_computation.1 | async-start | bytes 524288 | tf_op jit(solution)/shard_map/all_to_all | solution.py:509
  28.4 0.0 copy-done.5
  28.4 0.0 copy-done.6
  28.4 0.0 copy-done
  28.4 0.0 copy-done.2
  28.4 0.0 copy-done.3
  28.4 0.0 copy-done.4
  28.4 0.4 shard_map.159
  28.8 10.2 %all-to-all-done.1.refs_0_ = bf16[32,32,128]{2,1,0:T(8,128)(2,1)S(1)} async-done(((bf16[32,32,128]{2,1,0:T(8,128)(2,1)}), bf16[32,32,128]{2,1,0:T(8,128)(2,1)S(1)}, u32[]{:S(2)}, u32[]{:S(2)}) %all-to-all-start.1) | async-done | bytes 262176 | tf_op jit(solution)/shard_map/all_to_all | solution.py:509
  39.0 5.4 %shard_map.160 = (bf16[32,32,128]{2,1,0:T(8,128)(2,1)}, bf16[256,256]{1,0:T(8,128)(2,1)S(1)}) custom-call(bf16[32,32,128]{2,1,0:T(8,128)(2,1)S(1)} %all-to-all-done.1.refs_0_, s32[1,128]{1,0:T(1,128)S(1)} %bitcast.21, bf16[256,256]{1,0:T(8,128)(2,1)S(1)} %get-tuple-element.17.refs_2_, bf16[256,256]{1,0:T(8,128)(2,1)S(1)} %get-tuple-element.18.refs_3_, ...), custom_call_target="tpu_custom_call" | custom-call | flops 536870912 | bytes 2097152 | tf_op jit(solution)/shard_map/pallas_call | solution.py:512
  44.4 2.6 %all-to-all-start.2 = ((bf16[32,32,128]{2,1,0:T(8,128)(2,1)}), bf16[32,32,128]{2,1,0:T(8,128)(2,1)S(1)}, u32[]{:S(2)}, u32[]{:S(2)}) async-start(bf16[32,32,128]{2,1,0:T(8,128)(2,1)} %get-tuple-element.24), calls=%async_computation.2 | async-start | bytes 524288 | tf_op jit(solution)/shard_map/all_to_all | solution.py:520
  47.0 0.2 collective-permute-start.1
  47.2 1.1 %collective-permute-done.1 = bf16[4,64,128]{2,1,0:T(8,128)(2,1)S(1)} collective-permute-done((bf16[4,64,128]{2,1,0:T(8,128)(2,1)S(1)}, bf16[4,64,128]{2,1,0:T(8,128)(2,1)S(1)}, u32[]{:S(2)}, u32[]{:S(2)}) %collective-permute-start.1) | collective-permute-done | bytes 65568 | tf_op jit(solution)/shard_map/ppermute | solution.py:475
  48.4 0.0 copy-start.1
  48.4 0.8 %shard_map.161 = bf16[256,256]{1,0:T(8,128)(2,1)} custom-call(bf16[256,256]{1,0:T(8,128)(2,1)S(1)} %get-tuple-element.22.gated_ref, bf16[256,256]{1,0:T(8,128)(2,1)S(1)} %copy-done), custom_call_target="tpu_custom_call" | custom-call | flops 33554432 | bytes 524288 | tf_op jit(solution)/shard_map/pallas_call | solution.py:521
  49.2 8.3 %all-to-all-done.2.shares_ref = bf16[32,32,128]{2,1,0:T(8,128)(2,1)S(1)} async-done(((bf16[32,32,128]{2,1,0:T(8,128)(2,1)}), bf16[32,32,128]{2,1,0:T(8,128)(2,1)S(1)}, u32[]{:S(2)}, u32[]{:S(2)}) %all-to-all-start.2) | async-done | bytes 262176 | tf_op jit(solution)/shard_map/all_to_all | solution.py:520
  57.6 0.0 copy-done.1
  57.6 1.5 %shard_map.162 = f32[4,128,128]{2,1,0:T(8,128)} custom-call(bf16[32,32,128]{2,1,0:T(8,128)(2,1)S(1)} %all-to-all-done.2.shares_ref, bf16[8,128]{1,0:T(8,128)(2,1)S(1)} %bitcast.19, bf16[4,128,128]{2,1,0:T(8,128)(2,1)S(1)} %maximum_select_fusion.1.pair_ref), custom_call_target="tpu_custom_call" | custom-call | flops 16777216 | bytes 1048576 | tf_op jit(solution)/shard_map/pallas_call | solution.py:528
  (8 shorter events, 0.1 us)
Async XLA Ops:
  0.6 0.9 %copy-start.13 = (bf16[256,32]{0,1:T(8,128)(2,1)S(1)}, bf16[256,32]{0,1:T(8,128)(2,1)}, u32[]{:S(2)}) copy-start(bf16[256,32]{0,1:T(8,128)(2,1)} %param.20) | copy-start | bytes 49156
  0.6 1.0 %copy-start.7 = (bf16[2,128,256]{2,1,0:T(8,128)(2,1)S(1)}, bf16[2,128,256]{2,1,0:T(8,128)(2,1)}, u32[]{:S(2)}) copy-start(bf16[2,128,256]{2,1,0:T(8,128)(2,1)} %param.14) | copy-start | bytes 393220
  1.6 0.7 %copy-start.9 = (s32[64]{0:T(128)S(1)}, s32[64]{0:T(128)}, u32[]{:S(2)}) copy-start(s32[64]{0:T(128)} %seq_ref.1) | copy-start | bytes 772
  1.7 0.7 %copy-start.10 = (s32[128]{0:T(128)S(1)}, s32[128]{0:T(128)}, u32[]{:S(2)}) copy-start(s32[128]{0:T(128)} %param.18) | copy-start | bytes 1540
  4.2 7.3 %copy-start.12 = (bf16[4,128,128]{2,1,0:T(8,128)(2,1)S(1)}, bf16[4,128,128]{2,1,0:T(8,128)(2,1)}, u32[]{:S(2)}) copy-start(bf16[4,128,128]{2,1,0:T(8,128)(2,1)} %param.15) | copy-start | bytes 393220
  4.2 19.3 %all-to-all-start = ((bf16[32,36,128]{2,1,0:T(8,128)(2,1)}), bf16[32,36,128]{2,1,0:T(8,128)(2,1)S(1)}, u32[]{:S(2)}, u32[]{:S(2)}) async-start(bf16[32,36,128]{2,1,0:T(8,128)(2,1)} %bitcast.2), calls=%async_computation | async-start | bytes 655360 | tf_op jit(solution)/shard_map/all_to_all | solution.py:448
  11.5 2.2 %copy-start.11 = (bf16[32,32,128]{2,1,0:T(8,128)(2,1)S(1)}, bf16[32,32,128]{2,1,0:T(8,128)(2,1)}, u32[]{:S(2)}) copy-start(bf16[32,32,128]{2,1,0:T(8,128)(2,1)} %param.21) | copy-start | bytes 786436
  11.6 2.6 %collective-permute-start = (bf16[4,64,128]{2,1,0:T(8,128)(2,1)S(1)}, bf16[4,64,128]{2,1,0:T(8,128)(2,1)S(1)}, u32[]{:S(2)}, u32[]{:S(2)}) collective-permute-start(bf16[4,64,128]{2,1,0:T(8,128)(2,1)S(1)} %get-tuple-element.28), channel_id=1, source_target_pairs={{0,1},{1,0},{2,3},{3,2},{4,5},{5,4},{6,7},{7,6},{8,9},{9,8},{10,11... | collective-permute-start | bytes 196616 | tf_op jit(solution)/shard_map/ppermute | solution.py:470
  14.2 9.3 %copy-start.8 = (bf16[128,8]{0,1:T(8,128)(2,1)S(1)}, bf16[128,8]{0,1:T(8,128)(2,1)}, u32[]{:S(2)}) copy-start(bf16[128,8]{0,1:T(8,128)(2,1)} %param.22) | copy-start | bytes 6148
  23.5 4.9 %copy-start.5 = (bf16[256,256]{1,0:T(8,128)(2,1)S(1)}, bf16[256,256]{1,0:T(8,128)(2,1)}, u32[]{:S(2)}) copy-start(bf16[256,256]{1,0:T(8,128)(2,1)} %wv_ref.1) | copy-start | bytes 393220
  23.5 4.9 %copy-start.6 = (bf16[256,256]{1,0:T(8,128)(2,1)S(1)}, bf16[256,256]{1,0:T(8,128)(2,1)}, u32[]{:S(2)}) copy-start(bf16[256,256]{1,0:T(8,128)(2,1)} %wg_ref.1) | copy-start | bytes 393220
  25.6 2.8 %copy-start = (bf16[256,256]{1,0:T(8,128)(2,1)S(1)}, bf16[256,256]{1,0:T(8,128)(2,1)}, u32[]{:S(2)}) copy-start(bf16[256,256]{1,0:T(8,128)(2,1)} %wo_ref.3) | copy-start | bytes 393220
  25.6 2.8 %copy-start.2 = (bf16[2,128,256]{2,1,0:T(8,128)(2,1)S(1)}, bf16[2,128,256]{2,1,0:T(8,128)(2,1)}, u32[]{:S(2)}) copy-start(bf16[2,128,256]{2,1,0:T(8,128)(2,1)} %param.16) | copy-start | bytes 393220
  25.6 2.8 %copy-start.3 = (bf16[256,256]{1,0:T(8,128)(2,1)S(1)}, bf16[256,256]{1,0:T(8,128)(2,1)}, u32[]{:S(2)}) copy-start(bf16[256,256]{1,0:T(8,128)(2,1)} %wq_ref.1) | copy-start | bytes 393220
  25.6 2.8 %copy-start.4 = (bf16[256,256]{1,0:T(8,128)(2,1)S(1)}, bf16[256,256]{1,0:T(8,128)(2,1)}, u32[]{:S(2)}) copy-start(bf16[256,256]{1,0:T(8,128)(2,1)} %wk_ref.1) | copy-start | bytes 393220
  25.6 13.3 %all-to-all-start.1 = ((bf16[32,32,128]{2,1,0:T(8,128)(2,1)}), bf16[32,32,128]{2,1,0:T(8,128)(2,1)S(1)}, u32[]{:S(2)}, u32[]{:S(2)}) async-start(bf16[32,32,128]{2,1,0:T(8,128)(2,1)} %get-tuple-element.15), calls=%async_computation.1 | async-start | bytes 524288 | tf_op jit(solution)/shard_map/all_to_all | solution.py:509
  44.4 13.2 %all-to-all-start.2 = ((bf16[32,32,128]{2,1,0:T(8,128)(2,1)}), bf16[32,32,128]{2,1,0:T(8,128)(2,1)S(1)}, u32[]{:S(2)}, u32[]{:S(2)}) async-start(bf16[32,32,128]{2,1,0:T(8,128)(2,1)} %get-tuple-element.24), calls=%async_computation.2 | async-start | bytes 524288 | tf_op jit(solution)/shard_map/all_to_all | solution.py:520
  47.0 1.3 %collective-permute-start.1 = (bf16[4,64,128]{2,1,0:T(8,128)(2,1)S(1)}, bf16[4,64,128]{2,1,0:T(8,128)(2,1)S(1)}, u32[]{:S(2)}, u32[]{:S(2)}) collective-permute-start(bf16[4,64,128]{2,1,0:T(8,128)(2,1)S(1)} %get-tuple-element.26), channel_id=1, source_target_pairs={{0,1},{1,0},{2,3},{3,2},{4,5},{5,4},{6,7},{7,6},{8,9},{9,8},{10,11... | collective-permute-start | bytes 196616 | tf_op jit(solution)/shard_map/ppermute | solution.py:475
  48.4 9.2 %copy-start.1 = (bf16[4,128,128]{2,1,0:T(8,128)(2,1)}, bf16[4,128,128]{2,1,0:T(8,128)(2,1)S(1)}, u32[]{:S(2)}) copy-start(bf16[4,128,128]{2,1,0:T(8,128)(2,1)S(1)} %maximum_select_fusion.1.pair_ref) | copy-start | bytes 393220

commit v3 on v2

--- a/solution.py
+++ b/solution.py
@@ -254,8 +254,8 @@
     normed_ref[...] = normed
     live = res_ref[...].astype(f32)
     live_rows = jnp.broadcast_to(live, (residues, residues)).T
-    right_t = right_ref[...].astype(f32).T.astype(bf16)
-    left_wide = jnp.concatenate([left_ref[...]] * 4, axis=1)
+    right_t = right_ref[...]
+    left_wide = jnp.concatenate([left_ref[...]] * 4, axis=0)
     low = lane_index(16) < 64
     lane_group = lane_index(chips) // 32
     halves = ([], [])
@@ -267,7 +267,7 @@
         first, second = factor[:16], factor[16:]
         halves[0].append(jnp.where(low, first, pltpu.roll(second, 64, 1)))
         halves[1].append(jnp.where(low, pltpu.roll(first, 64, 1), second))
-        left_scr[...] = dot_nn(own, left_wide) * (live_rows * seq_live)
+        left_scr[...] = dot_nt(own, left_wide) * (live_rows * seq_live)
         for a in range(2):
             row = jnp.zeros((chips, LANES), f32)
             for b in range(4):
@@ -282,16 +282,30 @@
         send_ref[:, core, right_rows:, :] = tail
 
 
+def by_head(rows, heads):
+    channels = rows.shape[1]
+    head_of = lax.broadcasted_iota(jnp.int32, (1, channels), 1) // (channels // heads)
+    return jnp.concatenate(
+        [jnp.where(head_of == h, rows, jnp.zeros((), rows.dtype)) for h in range(heads)], axis=0
+    )
+
+
 def projections_kernel(
-    normed_ref, cot_ref, wq_ref, wk_ref, wv_ref, wg_ref, wo_ref, q_ref, k_ref, v_ref, gate_ref, d_ref
+    heads, scale, normed_ref, cot_ref, wq_ref, wk_ref, wv_ref, wg_ref, wo_ref, score_ref, flow_ref, v_ref, gate_ref
 ):
+    seqs, _, residues = score_ref.shape
     normed = normed_ref[...]
-    q_ref[...] = dot_nn(normed, wq_ref[...]).astype(bf16)
-    k_ref[...] = dot_nn(normed, wk_ref[...]).astype(bf16)
-    v_ref[...] = dot_nn(normed, wv_ref[...]).astype(bf16)
+    queries = dot_nn(normed, wq_ref[...]).astype(bf16)
+    keys = dot_nn(normed, wk_ref[...]).astype(bf16)
+    values = dot_nn(normed, wv_ref[...]).astype(bf16)
     gate = jax.nn.sigmoid(dot_nn(normed, wg_ref[...]))
+    d_rounded = (dot_nt(cot_ref[...], wo_ref[...]) * gate).astype(bf16)
+    v_ref[...] = values
     gate_ref[...] = gate
-    d_ref[...] = (dot_nt(cot_ref[...], wo_ref[...]) * gate).astype(bf16)
+    for s in range(seqs):
+        at = slice(s * residues, (s + 1) * residues)
+        score_ref[s] = dot_nt(by_head(queries[at], heads), keys[at]) * scale
+        flow_ref[s] = dot_nt(by_head(d_rounded[at], heads), values[at])
 
 
 def pair_kernel(recv_ref, weight_ref, pair_ref, div_ref, bias_w_ref, send_ref, updated_ref, flat, rbuf, lbuf, obuf):
@@ -333,47 +347,55 @@
     send_ref[...] = jnp.broadcast_to(block[None], send_ref.shape)
 
 
-def attention_kernel(
-    scale, bias_ref, res_ref, q_ref, k_ref, v_ref, gate_ref, d_ref, send_ref, gated_ref, flat, grads
-):
+def placed_bias(flat, res_ref, heads, h):
     residues = res_ref.shape[1]
-    channels = q_ref.shape[1]
-    seqs = q_ref.shape[0] // residues
-    heads = flat.shape[0] // residues
-    flat[...] = bias_ref[...].reshape(flat.shape).astype(f32)
-    key_mask = (res_ref[...].astype(f32) - 1.0) * mask_fill
     sub = lax.broadcasted_iota(jnp.int32, (residues, LANES), 0) % 8
     keep = (sub < 4) == (lane_index(residues) < 64)
-    head_of = lax.broadcasted_iota(jnp.int32, (1, channels), 1) // (channels // heads)
-    attended = [jnp.zeros((residues, channels), f32) for _ in range(seqs)]
+    raw = flat[pl.ds(h, residues, stride=heads), :]
+    moved = jnp.where(sub < 4, pltpu.roll(raw, residues - 4, 0), pltpu.roll(raw, 4, 0))
+    key_mask = (res_ref[...].astype(f32) - 1.0) * mask_fill
+    return jnp.where(keep, raw, pltpu.roll(moved, 64, 1)) + key_mask
+
+
+def bias_gradient_kernel(bias_ref, res_ref, score_ref, flow_ref, send_ref, full_ref, flat, grads):
+    seqs, rows, residues = score_ref.shape
+    heads = rows // residues
+    flat[...] = bias_ref[...].reshape(flat.shape).astype(f32)
+    ones = jnp.ones((residues, LANES), bf16)
     for h in range(heads):
-        raw = flat[pl.ds(h, residues, stride=heads), :]
-        up, down = pltpu.roll(raw, residues - 4, 0), pltpu.roll(raw, 4, 0)
-        moved = pltpu.roll(jnp.where(sub < 4, up, down), 64, 1)
-        bias = jnp.where(keep, raw, moved) + key_mask
-        of_head = head_of == h
+        at = slice(h * residues, (h + 1) * residues)
+        bias = placed_bias(flat, res_ref, heads, h)
+        full_ref[at, :] = bias
         total = jnp.zeros((residues, residues), f32)
         for s in range(seqs):
-            at = slice(s * residues, (s + 1) * residues)
-            q = jnp.where(of_head, q_ref[at, :], jnp.zeros((), bf16))
-            d = jnp.where(of_head, d_ref[at, :], jnp.zeros((), bf16))
-            scores = dot_nt(q, k_ref[at, :]) * scale + bias
+            scores = score_ref[s, at, :] + bias
             weights = jnp.exp(scores - jnp.max(scores, axis=-1, keepdims=True))
-            inverse = 1.0 / jnp.sum(weights, axis=-1, keepdims=True)
-            mixed = dot_nn(weights.astype(bf16), v_ref[at, :]) * inverse
-            attended[s] = jnp.where(of_head, mixed, attended[s])
-            probs = weights * inverse
-            flow = probs * dot_nt(d, v_ref[at, :])
-            total = total + (flow - probs * jnp.sum(flow, axis=-1, keepdims=True))
+            flow = flow_ref[s, at, :]
+            inverse = 1.0 / dot_nn(weights.astype(bf16), ones)
+            delta = dot_nn((weights * flow).astype(bf16), ones) * inverse
+            total = total + weights * inverse * (flow - delta)
         grads[pl.ds(h, residues, stride=heads), :] = total
     send_ref[...] = grads[...].astype(bf16).reshape(send_ref.shape)
+
+
+def output_kernel(score_ref, full_ref, v_ref, gate_ref, wo_ref, out_ref):
+    seqs, rows, residues = score_ref.shape
+    heads = rows // residues
+    channels = v_ref.shape[1]
+    head_of = lax.broadcasted_iota(jnp.int32, (1, channels), 1) // (channels // heads)
+    ones = jnp.ones((residues, LANES), bf16)
     for s in range(seqs):
-        at = slice(s * residues, (s + 1) * residues)
-        gated_ref[at, :] = (gate_ref[at, :] * attended[s]).astype(bf16)
-
-
-def output_kernel(gated_ref, wo_ref, out_ref):
-    out_ref[...] = dot_nn(gated_ref[...], wo_ref[...]).astype(bf16)
+        own = slice(s * residues, (s + 1) * residues)
+        attended = jnp.zeros((residues, channels), f32)
+        for h in range(heads):
+            at = slice(h * residues, (h + 1) * residues)
+            scores = score_ref[s, at, :] + full_ref[at, :]
+            weights = jnp.exp(scores - jnp.max(scores, axis=-1, keepdims=True))
+            total = jnp.sum(weights, axis=-1, keepdims=True)
+            mixed = dot_nn(weights.astype(bf16), v_ref[own, :]) / total
+            attended = jnp.where(head_of == h, mixed, attended)
+        gated = (gate_ref[own, :] * attended).astype(bf16)
+        out_ref[own, :] = dot_nn(gated, wo_ref[...]).astype(bf16)
 
 
 def gradient_kernel(shares_ref, bias_w_ref, pair_ref, out_ref):
@@ -444,17 +466,24 @@
         [pltpu.VMEM((residues, LANES), f32)],
         flops=2 * token_rows * channel_count * LANES,
         moved=1 << 19,
-    )(sequence_mask, res_row, flat_rows, left_weight, right_weight)
+    )(sequence_mask, res_row, flat_rows, left_weight.T, right_weight.T)
     received = lax.all_to_all(
         send.reshape(peers, block_rows, LANES), "row", split_axis=0, concat_axis=0, tiled=True
     )
 
-    queries, keys, values, gate, d_rounded = kernel_call(
-        projections_kernel,
-        [shape((token_rows, channel_count), t) for t in (bf16, bf16, bf16, f32, bf16)],
+    head_rows = head_count * residues
+    scale = (channel_count // head_count) ** (-0.5)
+    scores, flow, values, gate = kernel_call(
+        lambda *refs: projections_kernel(head_count, scale, *refs),
+        [
+            shape((sequence_wise, head_rows, residues), f32),
+            shape((sequence_wise, head_rows, residues), f32),
+            shape((token_rows, channel_count), bf16),
+            shape((token_rows, channel_count), f32),
+        ],
         [vmem] * 7,
         flops=10 * token_rows * channel_count * channel_count,
-        moved=1 << 21,
+        moved=1 << 22,
     )(
         normed,
         update_cotangent.reshape(token_rows, channel_count),
@@ -509,22 +538,22 @@
     bias_all = lax.all_to_all(send_bias, "row", split_axis=0, concat_axis=0, tiled=True)
     pair_updated = trade_rows(updated_tile)
 
-    send_grad, gated = kernel_call(
-        lambda *refs: attention_kernel((channel_count // head_count) ** (-0.5), *refs),
-        [shape((peers, rows_here * head_count, LANES), bf16), shape((token_rows, channel_count), bf16)],
-        [vmem] * 7,
-        [pltpu.VMEM((residues * head_count, LANES), f32), pltpu.VMEM((residues * head_count, LANES), f32)],
-        flops=1 << 29,
-        moved=1 << 21,
-    )(bias_all, res_row, queries, keys, values, gate, d_rounded)
+    send_grad, full_bias = kernel_call(
+        bias_gradient_kernel,
+        [shape((peers, rows_here * head_count, LANES), bf16), shape((head_rows, residues), f32)],
+        [vmem] * 4,
+        [pltpu.VMEM((head_rows, LANES), f32), pltpu.VMEM((head_rows, LANES), f32)],
+        flops=1 << 28,
+        moved=1 << 22,
+    )(bias_all, res_row, scores, flow)
     shares = lax.all_to_all(send_grad, "row", split_axis=0, concat_axis=0, tiled=True)
     update = kernel_call(
         output_kernel,
         shape((token_rows, channel_count), bf16),
-        [vmem] * 2,
-        flops=2 * token_rows * channel_count * channel_count,
-        moved=1 << 19,
-    )(gated, output_weight)
+        [vmem] * 5,
+        flops=1 << 29,
+        moved=1 << 22,
+    )(scores, full_bias, values, gate, output_weight)
     pair_gradient = kernel_call(
         gradient_kernel,
         shape((rows_here, residues, pair_channels), f32),

time: 59.5 us -> 58.4 us (0.982)
  local copies, waits for them, and re-layouts: 2.66 us -> 6.17 us
  waiting for transfers between devices: 28.9 us -> 26.1 us
  Pallas kernels: 12.1 us -> 10.1 us
    unnamed x31 -> x39, local copies, waits for them, and re-layouts: 1.73 us -> 5.24 us
    pallas_call x2, Pallas kernels: 5.73 us -> 3.12 us  [the longest x1 2.19 us: on_device_paired(): kernel_call(bias_gradient_kernel, [shape((peers, rows_here * head_count,...]
    all_to_all x1, waiting for transfers between devices: 8.34 us -> 6.77 us  [on_device_paired(): lax.all_to_all(send_grad, 'row', split_axis=0, concat_axis=0, tiled=True)]
    all_to_all x1, waiting for transfers between devices: 10.2 us -> 8.93 us  [on_device_paired(): lax.all_to_all(send_bias, 'row', split_axis=0, concat_axis=0, tiled=True)]
    pallas_call x1, Pallas kernels: 0.85 us -> 1.55 us  [on_device_paired(): kernel_call(output_kernel, shape((token_rows, channel_count), bf16), [vme...]
  transfers between devices with their start and end apart: 5 -> 5, of which waited for: 4 -> 4; matrix products, arithmetic and copies ran while one was open for 4% -> 4% of each run, Pallas kernels for 2% -> 4%
where the time goes in v3:
time: 58.4 us; the launch traced here: 57.9 us
  waiting for transfers between devices  26.1 us (45%)
  starting transfers between devices  13.2 us (23%)
  Pallas kernels  10.1 us (17%)
  local copies, waits for them, and re-layouts  6.17 us (11%)
  other arithmetic  1.38 us (2%)
  between operations  0.9 us (2%)
    all_to_all x1, waiting for transfers between devices, on_device_paired(): lax.all_to_all(send.reshape(peers, block_rows, LANES), 'row', split_axis=...  9.26 us
    all_to_all x1, waiting for transfers between devices, on_device_paired(): lax.all_to_all(send_bias, 'row', split_axis=0, concat_axis=0, tiled=True)  8.93 us
    all_to_all x1, starting transfers between devices, on_device_paired(): lax.all_to_all(send.reshape(peers, block_rows, LANES), 'row', split_axis=...  7.3 us
    all_to_all x1, waiting for transfers between devices, on_device_paired(): lax.all_to_all(send_grad, 'row', split_axis=0, concat_axis=0, tiled=True)  6.77 us
    unnamed x39, local copies, waits for them, and re-layouts  5.24 us
    all_to_all x1, starting transfers between devices, on_device_paired(): lax.all_to_all(send_bias, 'row', split_axis=0, concat_axis=0, tiled=True)  2.74 us
    all_to_all x1, starting transfers between devices, on_device_paired(): lax.all_to_all(send_grad, 'row', split_axis=0, concat_axis=0, tiled=True)  2.72 us
    pallas_call x1, Pallas kernels, on_device_paired(): kernel_call(bias_gradient_kernel, [shape((peers, rows_here * head_count,...  2.19 us
  transfers between devices with their start and end apart: 5, of which 4 were waited for; matrix products, arithmetic and copies ran while one was open for 4% of the time, Pallas kernels for 4%

profile of v3, /device:TPU:0, one launch (start us, length us, event | category | flops | bytes accessed | tf_op | source)
XLA Modules:
  0.0 57.9 jit_solution(6916823215092798377)
XLA Ops:
  0.6 0.0 copy-start.15
  0.6 0.0 copy-start.16
  0.7 0.6 %copy-done.15 = s32[128]{0:T(128)S(1)} copy-done((s32[128]{0:T(128)S(1)}, s32[128]{0:T(128)}, u32[]{:S(2)}) %copy-start.15) | copy-done | bytes 536
  1.3 0.0 copy-done.16
  1.3 0.0 copy-start.9
  1.3 0.9 %copy-done.9 = bf16[2,128,256]{2,1,0:T(8,128)(2,1)S(1)} copy-done((bf16[2,128,256]{2,1,0:T(8,128)(2,1)S(1)}, bf16[2,128,256]{2,1,0:T(8,128)(2,1)}, u32[]{:S(2)}) %copy-start.9) | copy-done | bytes 131096
  2.2 0.0 copy-start.12
  2.2 0.7 %copy-done.12 = bf16[256,32]{0,1:T(8,128)(2,1)S(1)} copy-done((bf16[256,32]{0,1:T(8,128)(2,1)S(1)}, bf16[256,32]{0,1:T(8,128)(2,1)}, u32[]{:S(2)}) %copy-start.12) | copy-done | bytes 16408
  2.9 0.0 copy-start.13
  2.9 0.7 %copy-done.13 = bf16[256,32]{0,1:T(8,128)(2,1)S(1)} copy-done((bf16[256,32]{0,1:T(8,128)(2,1)S(1)}, bf16[256,32]{0,1:T(8,128)(2,1)}, u32[]{:S(2)}) %copy-start.13) | copy-done | bytes 16408
  3.6 1.8 %shard_map.157 = (bf16[16,2,36,128]{3,2,1,0:T(8,128)(2,1)}, bf16[256,256]{1,0:T(8,128)(2,1)S(1)}) custom-call(s32[64]{0:T(128)S(1)} %copy-done.16, s32[1,128]{1,0:T(1,128)S(1)} %bitcast.24, bf16[256,256]{1,0:T(8,128)(2,1)S(1)} %bitcast.19, bf16[32,256]{1,0:T(8,128)(2,1)S(1)} %bitcast.20, bf16[32,256]{1,0:T(8,128)(2,1)S(1)} %bitcast.21), custom_call_target="tpu_custom_call" | custom-call | flops 16777216 | bytes 524288 | tf_op jit(solution)/shard_map/pallas_call | solution.py:462
  5.4 0.0 copy-start.18
  5.4 7.3 %all-to-all-start = ((bf16[32,36,128]{2,1,0:T(8,128)(2,1)}), bf16[32,36,128]{2,1,0:T(8,128)(2,1)S(1)}, u32[]{:S(2)}, u32[]{:S(2)}) async-start(bf16[32,36,128]{2,1,0:T(8,128)(2,1)} %bitcast.5), calls=%async_computation | async-start | bytes 655360 | tf_op jit(solution)/shard_map/all_to_all | solution.py:470
  12.7 0.0 copy-start.17
  12.7 0.0 copy-done.18
  12.8 0.3 collective-permute-start
  13.1 0.1 dynamic_slice.21
  13.2 0.1 mul.59
  13.3 0.6 %convert_reduce_fusion = f32[]{:T(128)} fusion(s32[64]{0:T(128)S(1)} %copy-done.16), kind=kLoop, calls=%fused_computation.9 | loop fusion | flops 127 | bytes 260 | tf_op jit(solution)/shard_map/reduce_sum | solution.py:522
  13.9 0.7 %dynamic-slice_multiply_fusion = f32[8]{0:T(128)S(1)} fusion(f32[128]{0:T(128)S(1)} %convert_element_type.7, s32[]{:T(128)S(6)} %select_n.49, f32[]{:T(128)} %convert_reduce_fusion), kind=kLoop, calls=%fused_computation.8 | loop fusion | flops 8 | bytes 72 | tf_op jit(solution)/shard_map/mul | solution.py:522
  14.6 0.1 mul.54
  14.7 0.1 copy.20
  14.8 0.1 mul.56
  14.8 0.1 mul.57
  14.9 0.0 copy-done.17
  14.9 0.2 copy.19
  15.2 0.1 copy.21.weight_ref
  15.4 0.0 collective-permute-done
  15.4 0.0 copy-start.14
  15.4 9.3 %all-to-all-done.recv_ref = bf16[32,36,128]{2,1,0:T(8,128)(2,1)S(1)} async-done(((bf16[32,36,128]{2,1,0:T(8,128)(2,1)}), bf16[32,36,128]{2,1,0:T(8,128)(2,1)S(1)}, u32[]{:S(2)}, u32[]{:S(2)}) %all-to-all-start) | async-done | bytes 294944 | tf_op jit(solution)/shard_map/all_to_all | solution.py:470
  24.7 0.0 copy-done.14
  24.7 0.0 copy-start.5
  24.7 0.0 copy-start.6
  24.7 2.2 %shard_map.159 = (bf16[32,32,128]{2,1,0:T(8,128)(2,1)}, bf16[8,64,128]{2,1,0:T(8,128)(2,1)S(1)}) custom-call(bf16[32,36,128]{2,1,0:T(8,128)(2,1)S(1)} %all-to-all-done.recv_ref, bf16[256,512]{1,0:T(8,128)(2,1)S(1)} %copy.21.weight_ref, bf16[8,64,128]{2,1,0:T(8,128)(2,1)S(1)} %maximum_select_fusion.pair_ref, f32[4,128]{1,0:T(4,128)S(1)} %multiply_maximum_fusion.div_ref, ...), custom_call_target="tpu_custom_call" | custom-call | flops 536870912 | bytes 1048576 | tf_op jit(solution)/shard_map/pallas_call | solution.py:525
  26.9 0.0 copy-start.10
  26.9 0.7 %copy-done.10 = bf16[8,64,128]{2,1,0:T(8,128)(2,1)} copy-done((bf16[8,64,128]{2,1,0:T(8,128)(2,1)}, bf16[8,64,128]{2,1,0:T(8,128)(2,1)S(1)}, u32[]{:S(2)}) %copy-start.10) | copy-done | bytes 131096
  27.5 0.0 copy-start
  27.5 0.0 copy-start.2
  27.5 0.0 copy-start.3
  27.5 0.0 copy-start.4
  27.5 2.7 %all-to-all-start.1 = ((bf16[32,32,128]{2,1,0:T(8,128)(2,1)}), bf16[32,32,128]{2,1,0:T(8,128)(2,1)S(1)}, u32[]{:S(2)}, u32[]{:S(2)}) async-start(bf16[32,32,128]{2,1,0:T(8,128)(2,1)} %get-tuple-element.16), calls=%async_computation.1 | async-start | bytes 524288 | tf_op jit(solution)/shard_map/all_to_all | solution.py:538
  30.3 0.0 copy-done.5
  30.3 0.0 copy-done.6
  30.3 0.0 copy-done
  30.3 0.0 copy-done.2
  30.3 0.0 copy-done.3
  30.3 0.0 copy-done.4
  30.3 0.9 %shard_map.158 = (f32[2,1024,128]{2,1,0:T(8,128)S(1)}, f32[2,1024,128]{2,1,0:T(8,128)S(1)}, bf16[256,256]{1,0:T(8,128)(2,1)S(1)}, f32[256,256]{1,0:T(8,128)S(1)}) custom-call(bf16[256,256]{1,0:T(8,128)(2,1)S(1)} %get-tuple-element.13.refs_0_, bf16[256,256]{1,0:T(8,128)(2,1)S(1)} %bitcast.18, bf16[256,256]{1,0:T(8,128)(2,1)S(1)} %copy-done.3, ...), custom_call_target="tpu_custom_call" | custom-call | flops 167772160 | bytes 4194304 | tf_op jit(solution)/shard_map/pallas_call | solution.py:476
  31.3 0.0 copy-start.7
  31.3 0.6 %copy-done.7 = bf16[256,256]{1,0:T(8,128)(2,1)} copy-done((bf16[256,256]{1,0:T(8,128)(2,1)}, bf16[256,256]{1,0:T(8,128)(2,1)S(1)}, u32[]{:S(2)}) %copy-start.7) | copy-done | bytes 131096
  31.9 8.9 %all-to-all-done.1.bias_ref = bf16[32,32,128]{2,1,0:T(8,128)(2,1)S(1)} async-done(((bf16[32,32,128]{2,1,0:T(8,128)(2,1)}), bf16[32,32,128]{2,1,0:T(8,128)(2,1)S(1)}, u32[]{:S(2)}, u32[]{:S(2)}) %all-to-all-start.1) | async-done | bytes 262176 | tf_op jit(solution)/shard_map/all_to_all | solution.py:538
  40.9 2.2 %shard_map.160 = (bf16[32,32,128]{2,1,0:T(8,128)(2,1)}, f32[1024,128]{1,0:T(8,128)S(1)}) custom-call(bf16[32,32,128]{2,1,0:T(8,128)(2,1)S(1)} %all-to-all-done.1.bias_ref, s32[1,128]{1,0:T(1,128)S(1)} %bitcast.25, f32[2,1024,128]{2,1,0:T(8,128)S(1)} %get-tuple-element.14.score_ref, f32[2,1024,128]{2,1,0:T(8,128)S(1)} %get-tuple-element.17.flow_ref), custom_call_target="tpu_custom_call" | custom-call | flops 268435456 | bytes 4194304 | tf_op jit(solution)/shard_map/pallas_call | solution.py:541
  43.1 0.0 copy-start.11
  43.1 2.7 %all-to-all-start.2 = ((bf16[32,32,128]{2,1,0:T(8,128)(2,1)}), bf16[32,32,128]{2,1,0:T(8,128)(2,1)S(1)}, u32[]{:S(2)}, u32[]{:S(2)}) async-start(bf16[32,32,128]{2,1,0:T(8,128)(2,1)} %get-tuple-element.22), calls=%async_computation.2 | async-start | bytes 524288 | tf_op jit(solution)/shard_map/all_to_all | solution.py:549
  45.8 0.0 copy-done.11
  45.8 0.2 collective-permute-start.1
  46.0 1.1 %collective-permute-done.1 = bf16[4,64,128]{2,1,0:T(8,128)(2,1)S(1)} collective-permute-done((bf16[4,64,128]{2,1,0:T(8,128)(2,1)S(1)}, bf16[4,64,128]{2,1,0:T(8,128)(2,1)S(1)}, u32[]{:S(2)}, u32[]{:S(2)}) %collective-permute-start.1) | collective-permute-done | bytes 65568 | tf_op jit(solution)/shard_map/ppermute | solution.py:504
  47.1 0.0 copy-start.8
  47.2 0.0 copy-start.1
  47.2 0.9 %copy-done.8 = bf16[256,256]{1,0:T(8,128)(2,1)S(1)} copy-done((bf16[256,256]{1,0:T(8,128)(2,1)S(1)}, bf16[256,256]{1,0:T(8,128)(2,1)}, u32[]{:S(2)}) %copy-start.8) | copy-done | bytes 131096
  48.1 1.6 %shard_map.161 = bf16[256,256]{1,0:T(8,128)(2,1)} custom-call(f32[2,1024,128]{2,1,0:T(8,128)S(1)} %get-tuple-element.14.score_ref, f32[1024,128]{1,0:T(8,128)S(1)} %get-tuple-element.18.full_ref, bf16[256,256]{1,0:T(8,128)(2,1)S(1)} %copy-done.8, f32[256,256]{1,0:T(8,128)S(1)} %get-tuple-element.20.gate_ref, bf16[256,256]{1,0:T(8,128)(2,1)S(1)} %copy-done), custom_call_target="tpu_custom_call" | custom-call | flops 536870912 | bytes 4194304 | tf_op jit(solution)/shard_map/pallas_call | solution.py:550
  49.6 6.8 %all-to-all-done.2.shares_ref = bf16[32,32,128]{2,1,0:T(8,128)(2,1)S(1)} async-done(((bf16[32,32,128]{2,1,0:T(8,128)(2,1)}), bf16[32,32,128]{2,1,0:T(8,128)(2,1)S(1)}, u32[]{:S(2)}, u32[]{:S(2)}) %all-to-all-start.2) | async-done | bytes 262176 | tf_op jit(solution)/shard_map/all_to_all | solution.py:549
  56.4 0.0 copy-done.1
  56.4 1.5 %shard_map.162 = f32[4,128,128]{2,1,0:T(8,128)} custom-call(bf16[32,32,128]{2,1,0:T(8,128)(2,1)S(1)} %all-to-all-done.2.shares_ref, bf16[8,128]{1,0:T(8,128)(2,1)S(1)} %bitcast.23, bf16[4,128,128]{2,1,0:T(8,128)(2,1)S(1)} %maximum_select_fusion.1.pair_ref), custom_call_target="tpu_custom_call" | custom-call | flops 16777216 | bytes 1048576 | tf_op jit(solution)/shard_map/pallas_call | solution.py:557
  (8 shorter events, 0.1 us)
Async XLA Ops:
  0.6 0.7 %copy-start.15 = (s32[128]{0:T(128)S(1)}, s32[128]{0:T(128)}, u32[]{:S(2)}) copy-start(s32[128]{0:T(128)} %param.18) | copy-start | bytes 1540
  0.6 0.7 %copy-start.16 = (s32[64]{0:T(128)S(1)}, s32[64]{0:T(128)}, u32[]{:S(2)}) copy-start(s32[64]{0:T(128)} %seq_ref.1) | copy-start | bytes 772
  1.3 0.9 %copy-start.9 = (bf16[2,128,256]{2,1,0:T(8,128)(2,1)S(1)}, bf16[2,128,256]{2,1,0:T(8,128)(2,1)}, u32[]{:S(2)}) copy-start(bf16[2,128,256]{2,1,0:T(8,128)(2,1)} %param.14) | copy-start | bytes 393220
  2.2 0.7 %copy-start.12 = (bf16[256,32]{0,1:T(8,128)(2,1)S(1)}, bf16[256,32]{0,1:T(8,128)(2,1)}, u32[]{:S(2)}) copy-start(bf16[256,32]{0,1:T(8,128)(2,1)} %param.19) | copy-start | bytes 49156
  2.9 0.7 %copy-start.13 = (bf16[256,32]{0,1:T(8,128)(2,1)S(1)}, bf16[256,32]{0,1:T(8,128)(2,1)}, u32[]{:S(2)}) copy-start(bf16[256,32]{0,1:T(8,128)(2,1)} %param.20) | copy-start | bytes 49156
  5.4 7.3 %copy-start.18 = (bf16[4,128,128]{2,1,0:T(8,128)(2,1)S(1)}, bf16[4,128,128]{2,1,0:T(8,128)(2,1)}, u32[]{:S(2)}) copy-start(bf16[4,128,128]{2,1,0:T(8,128)(2,1)} %param.15) | copy-start | bytes 393220
  5.4 19.3 %all-to-all-start = ((bf16[32,36,128]{2,1,0:T(8,128)(2,1)}), bf16[32,36,128]{2,1,0:T(8,128)(2,1)S(1)}, u32[]{:S(2)}, u32[]{:S(2)}) async-start(bf16[32,36,128]{2,1,0:T(8,128)(2,1)} %bitcast.5), calls=%async_computation | async-start | bytes 655360 | tf_op jit(solution)/shard_map/all_to_all | solution.py:470
  12.7 2.2 %copy-start.17 = (bf16[32,32,128]{2,1,0:T(8,128)(2,1)S(1)}, bf16[32,32,128]{2,1,0:T(8,128)(2,1)}, u32[]{:S(2)}) copy-start(bf16[32,32,128]{2,1,0:T(8,128)(2,1)} %param.21) | copy-start | bytes 786436
  12.8 2.6 %collective-permute-start = (bf16[4,64,128]{2,1,0:T(8,128)(2,1)S(1)}, bf16[4,64,128]{2,1,0:T(8,128)(2,1)S(1)}, u32[]{:S(2)}, u32[]{:S(2)}) collective-permute-start(bf16[4,64,128]{2,1,0:T(8,128)(2,1)S(1)} %get-tuple-element.26), channel_id=1, source_target_pairs={{0,1},{1,0},{2,3},{3,2},{4,5},{5,4},{6,7},{7,6},{8,9},{9,8},{10,11... | collective-permute-start | bytes 196616 | tf_op jit(solution)/shard_map/ppermute | solution.py:499
  15.4 9.3 %copy-start.14 = (bf16[128,8]{0,1:T(8,128)(2,1)S(1)}, bf16[128,8]{0,1:T(8,128)(2,1)}, u32[]{:S(2)}) copy-start(bf16[128,8]{0,1:T(8,128)(2,1)} %param.22) | copy-start | bytes 6148
  24.7 5.6 %copy-start.5 = (bf16[256,256]{1,0:T(8,128)(2,1)S(1)}, bf16[256,256]{1,0:T(8,128)(2,1)}, u32[]{:S(2)}) copy-start(bf16[256,256]{1,0:T(8,128)(2,1)} %refs_4_.1) | copy-start | bytes 393220
  24.7 5.6 %copy-start.6 = (bf16[256,256]{1,0:T(8,128)(2,1)S(1)}, bf16[256,256]{1,0:T(8,128)(2,1)}, u32[]{:S(2)}) copy-start(bf16[256,256]{1,0:T(8,128)(2,1)} %refs_5_.1) | copy-start | bytes 393220
  26.9 0.7 %copy-start.10 = (bf16[8,64,128]{2,1,0:T(8,128)(2,1)}, bf16[8,64,128]{2,1,0:T(8,128)(2,1)S(1)}, u32[]{:S(2)}) copy-start(bf16[8,64,128]{2,1,0:T(8,128)(2,1)S(1)} %get-tuple-element.21) | copy-start | bytes 393220
  27.5 2.8 %copy-start = (bf16[256,256]{1,0:T(8,128)(2,1)S(1)}, bf16[256,256]{1,0:T(8,128)(2,1)}, u32[]{:S(2)}) copy-start(bf16[256,256]{1,0:T(8,128)(2,1)} %wo_ref.1) | copy-start | bytes 393220
  27.5 2.8 %copy-start.2 = (bf16[2,128,256]{2,1,0:T(8,128)(2,1)S(1)}, bf16[2,128,256]{2,1,0:T(8,128)(2,1)}, u32[]{:S(2)}) copy-start(bf16[2,128,256]{2,1,0:T(8,128)(2,1)} %param.16) | copy-start | bytes 393220
  27.5 2.8 %copy-start.3 = (bf16[256,256]{1,0:T(8,128)(2,1)S(1)}, bf16[256,256]{1,0:T(8,128)(2,1)}, u32[]{:S(2)}) copy-start(bf16[256,256]{1,0:T(8,128)(2,1)} %refs_2_.1) | copy-start | bytes 393220
  27.5 2.8 %copy-start.4 = (bf16[256,256]{1,0:T(8,128)(2,1)S(1)}, bf16[256,256]{1,0:T(8,128)(2,1)}, u32[]{:S(2)}) copy-start(bf16[256,256]{1,0:T(8,128)(2,1)} %refs_3_.1) | copy-start | bytes 393220
  27.5 13.3 %all-to-all-start.1 = ((bf16[32,32,128]{2,1,0:T(8,128)(2,1)}), bf16[32,32,128]{2,1,0:T(8,128)(2,1)S(1)}, u32[]{:S(2)}, u32[]{:S(2)}) async-start(bf16[32,32,128]{2,1,0:T(8,128)(2,1)} %get-tuple-element.16), calls=%async_computation.1 | async-start | bytes 524288 | tf_op jit(solution)/shard_map/all_to_all | solution.py:538
  31.3 0.7 %copy-start.7 = (bf16[256,256]{1,0:T(8,128)(2,1)}, bf16[256,256]{1,0:T(8,128)(2,1)S(1)}, u32[]{:S(2)}) copy-start(bf16[256,256]{1,0:T(8,128)(2,1)S(1)} %get-tuple-element.19.v_ref) | copy-start | bytes 393220
  43.1 2.7 %copy-start.11 = (bf16[8,64,128]{2,1,0:T(8,128)(2,1)S(1)}, bf16[8,64,128]{2,1,0:T(8,128)(2,1)}, u32[]{:S(2)}) copy-start(bf16[8,64,128]{2,1,0:T(8,128)(2,1)} %copy-done.10) | copy-start | bytes 393220
  43.1 13.3 %all-to-all-start.2 = ((bf16[32,32,128]{2,1,0:T(8,128)(2,1)}), bf16[32,32,128]{2,1,0:T(8,128)(2,1)S(1)}, u32[]{:S(2)}, u32[]{:S(2)}) async-start(bf16[32,32,128]{2,1,0:T(8,128)(2,1)} %get-tuple-element.22), calls=%async_computation.2 | async-start | bytes 524288 | tf_op jit(solution)/shard_map/all_to_all | solution.py:549
  45.8 1.3 %collective-permute-start.1 = (bf16[4,64,128]{2,1,0:T(8,128)(2,1)S(1)}, bf16[4,64,128]{2,1,0:T(8,128)(2,1)S(1)}, u32[]{:S(2)}, u32[]{:S(2)}) collective-permute-start(bf16[4,64,128]{2,1,0:T(8,128)(2,1)S(1)} %get-tuple-element.24), channel_id=1, source_target_pairs={{0,1},{1,0},{2,3},{3,2},{4,5},{5,4},{6,7},{7,6},{8,9},{9,8},{10,11... | collective-permute-start | bytes 196616 | tf_op jit(solution)/shard_map/ppermute | solution.py:504
  47.1 0.9 %copy-start.8 = (bf16[256,256]{1,0:T(8,128)(2,1)S(1)}, bf16[256,256]{1,0:T(8,128)(2,1)}, u32[]{:S(2)}) copy-start(bf16[256,256]{1,0:T(8,128)(2,1)} %copy-done.7) | copy-start | bytes 393220
  47.2 9.2 %copy-start.1 = (bf16[4,128,128]{2,1,0:T(8,128)(2,1)}, bf16[4,128,128]{2,1,0:T(8,128)(2,1)S(1)}, u32[]{:S(2)}) copy-start(bf16[4,128,128]{2,1,0:T(8,128)(2,1)S(1)} %maximum_select_fusion.1.pair_ref) | copy-start | bytes 393220

commit v4 on v3

--- a/solution.py
+++ b/solution.py
@@ -411,7 +411,7 @@
         out_ref[i] = norm_backward(pair_ref[i], upstream)
 
 
-def kernel_call(body, out_shape, in_specs=None, scratch=(), flops=0, moved=0):
+def kernel_call(body, out_shape, in_specs=None, scratch=(), flops=0, moved=0, vmem_mib=24):
     vmem = pl.BlockSpec(memory_space=pltpu.VMEM)
     many = isinstance(out_shape, (list, tuple))
     return pl.pallas_call(
@@ -420,7 +420,7 @@
         in_specs=in_specs,
         out_specs=[vmem] * len(out_shape) if many else vmem,
         scratch_shapes=list(scratch),
-        compiler_params=pltpu.CompilerParams(vmem_limit_bytes=24 * 1024 * 1024),
+        compiler_params=pltpu.CompilerParams(vmem_limit_bytes=vmem_mib * 1024 * 1024),
         cost_estimate=pl.CostEstimate(flops=flops, bytes_accessed=moved, transcendentals=0),
     )
 
@@ -466,6 +466,7 @@
         [pltpu.VMEM((residues, LANES), f32)],
         flops=2 * token_rows * channel_count * LANES,
         moved=1 << 19,
+        vmem_mib=60,
     )(sequence_mask, res_row, flat_rows, left_weight.T, right_weight.T)
     received = lax.all_to_all(
         send.reshape(peers, block_rows, LANES), "row", split_axis=0, concat_axis=0, tiled=True

time: 58.4 us -> 55.7 us (0.954)
  local copies, waits for them, and re-layouts: 6.17 us -> 4.5 us
  waiting for transfers between devices: 26.1 us -> 24.8 us
    unnamed x39 -> x35, local copies, waits for them, and re-layouts: 5.24 us -> 3.57 us
    all_to_all x1, waiting for transfers between devices: 9.26 us -> 7.95 us  [on_device_paired(): lax.all_to_all(send.reshape(peers, block_rows, LANES), 'row', split_axis=...]
  transfers between devices with their start and end apart: 5 -> 5, of which waited for: 4 -> 4; matrix products, arithmetic and copies ran while one was open for 4% -> 4% of each run, Pallas kernels for 4% -> 5%
where the time goes in v4:
time: 55.7 us; the launch traced here: 55.2 us
  waiting for transfers between devices  24.8 us (45%)
  starting transfers between devices  13.2 us (24%)
  Pallas kernels  10.4 us (19%)
  local copies, waits for them, and re-layouts  4.5 us (8%)
  other arithmetic  1.38 us (2%)
  between operations  0.89 us (2%)
    all_to_all x1, waiting for transfers between devices, on_device_paired(): lax.all_to_all(send_bias, 'row', split_axis=0, concat_axis=0, tiled=True)  8.92 us
    all_to_all x1, waiting for transfers between devices, on_device_paired(): lax.all_to_all(send.reshape(peers, block_rows, LANES), 'row', split_axis=...  7.95 us
    all_to_all x1, starting transfers between devices, on_device_paired(): lax.all_to_all(send.reshape(peers, block_rows, LANES), 'row', split_axis=...  7.3 us
    all_to_all x1, waiting for transfers between devices, on_device_paired(): lax.all_to_all(send_grad, 'row', split_axis=0, concat_axis=0, tiled=True)  6.77 us
    unnamed x35, local copies, waits for them, and re-layouts  3.57 us
    all_to_all x1, starting transfers between devices, on_device_paired(): lax.all_to_all(send_bias, 'row', split_axis=0, concat_axis=0, tiled=True)  2.74 us
    all_to_all x1, starting transfers between devices, on_device_paired(): lax.all_to_all(send_grad, 'row', split_axis=0, concat_axis=0, tiled=True)  2.72 us
    pallas_call x1, Pallas kernels, on_device_paired(): kernel_call(bias_gradient_kernel, [shape((peers, rows_here * head_count,...  2.18 us
  transfers between devices with their start and end apart: 5, of which 4 were waited for; matrix products, arithmetic and copies ran while one was open for 4% of the time, Pallas kernels for 5%

profile of v4, /device:TPU:0, one launch (start us, length us, event | category | flops | bytes accessed | tf_op | source)
XLA Modules:
  0.0 55.2 jit_solution(9444543405718796641)
XLA Ops:
  0.6 2.1 %shard_map.157 = (bf16[16,2,36,128]{3,2,1,0:T(8,128)(2,1)}, bf16[256,256]{1,0:T(8,128)(2,1)}) custom-call(s32[64]{0:T(128)} %seq_ref.1, s32[1,128]{1,0:T(1,128)} %bitcast.21, bf16[256,256]{1,0:T(8,128)(2,1)} %bitcast.28, bf16[32,256]{1,0:T(8,128)(2,1)} %bitcast.29, bf16[32,256]{1,0:T(8,128)(2,1)} %bitcast.30), custom_call_target="tpu_custom_call" | custom-call | flops 16777216 | bytes 524288 | tf_op jit(solution)/shard_map/pallas_call | solution.py:462
  2.8 0.0 copy-start.15
  2.8 7.3 %all-to-all-start = ((bf16[32,36,128]{2,1,0:T(8,128)(2,1)}), bf16[32,36,128]{2,1,0:T(8,128)(2,1)S(1)}, u32[]{:S(2)}, u32[]{:S(2)}) async-start(bf16[32,36,128]{2,1,0:T(8,128)(2,1)} %bitcast.25), calls=%async_computation | async-start | bytes 655360 | tf_op jit(solution)/shard_map/all_to_all | solution.py:471
  10.1 0.0 copy-start.14
  10.1 0.0 copy-done.15
  10.1 0.3 collective-permute-start
  10.5 0.0 copy-start.13
  10.5 0.7 %copy-done.13 = s32[128]{0:T(128)S(1)} copy-done((s32[128]{0:T(128)S(1)}, s32[128]{0:T(128)}, u32[]{:S(2)}) %copy-start.13) | copy-done | bytes 536
  11.1 0.1 dynamic_slice.21
  11.2 0.1 mul.59
  11.3 0.0 copy-start.16
  11.3 0.7 %copy-done.16 = s32[64]{0:T(128)S(1)} copy-done((s32[64]{0:T(128)S(1)}, s32[64]{0:T(128)}, u32[]{:S(2)}) %copy-start.16) | copy-done | bytes 280
  11.9 0.6 %convert_reduce_fusion = f32[]{:T(128)} fusion(s32[64]{0:T(128)S(1)} %copy-done.16), kind=kLoop, calls=%fused_computation.9 | loop fusion | flops 127 | bytes 260 | tf_op jit(solution)/shard_map/reduce_sum | solution.py:523
  12.5 0.7 %dynamic-slice_multiply_fusion = f32[8]{0:T(128)S(1)} fusion(f32[128]{0:T(128)S(1)} %convert_element_type.7, s32[]{:T(128)S(6)} %select_n.49, f32[]{:T(128)} %convert_reduce_fusion), kind=kLoop, calls=%fused_computation.8 | loop fusion | flops 8 | bytes 72 | tf_op jit(solution)/shard_map/mul | solution.py:523
  13.3 0.1 mul.54
  13.4 0.1 copy.20
  13.4 0.1 mul.56
  13.5 0.1 mul.57
  13.6 0.0 copy-done.14
  13.6 0.2 copy.19
  13.9 0.1 copy.21.weight_ref
  14.1 0.0 collective-permute-done
  14.1 0.0 copy-start.12
  14.1 8.0 %all-to-all-done.recv_ref = bf16[32,36,128]{2,1,0:T(8,128)(2,1)S(1)} async-done(((bf16[32,36,128]{2,1,0:T(8,128)(2,1)}), bf16[32,36,128]{2,1,0:T(8,128)(2,1)S(1)}, u32[]{:S(2)}, u32[]{:S(2)}) %all-to-all-start) | async-done | bytes 294944 | tf_op jit(solution)/shard_map/all_to_all | solution.py:471
  22.1 0.0 copy-done.12
  22.1 0.0 copy-start.5
  22.1 0.0 copy-start.6
  22.1 0.0 copy-start.7
  22.1 2.2 %shard_map.159 = (bf16[32,32,128]{2,1,0:T(8,128)(2,1)}, bf16[8,64,128]{2,1,0:T(8,128)(2,1)S(1)}) custom-call(bf16[32,36,128]{2,1,0:T(8,128)(2,1)S(1)} %all-to-all-done.recv_ref, bf16[256,512]{1,0:T(8,128)(2,1)S(1)} %copy.21.weight_ref, bf16[8,64,128]{2,1,0:T(8,128)(2,1)S(1)} %maximum_select_fusion.pair_ref, f32[4,128]{1,0:T(4,128)S(1)} %multiply_maximum_fusion.div_ref, ...), custom_call_target="tpu_custom_call" | custom-call | flops 536870912 | bytes 1048576 | tf_op jit(solution)/shard_map/pallas_call | solution.py:526
  24.2 0.0 copy-start.10
  24.2 0.7 %copy-done.10 = bf16[8,64,128]{2,1,0:T(8,128)(2,1)} copy-done((bf16[8,64,128]{2,1,0:T(8,128)(2,1)}, bf16[8,64,128]{2,1,0:T(8,128)(2,1)S(1)}, u32[]{:S(2)}) %copy-start.10) | copy-done | bytes 131096
  24.9 0.0 copy-start
  24.9 0.0 copy-start.2
  24.9 0.0 copy-start.3
  24.9 0.0 copy-start.4
  24.9 2.7 %all-to-all-start.1 = ((bf16[32,32,128]{2,1,0:T(8,128)(2,1)}), bf16[32,32,128]{2,1,0:T(8,128)(2,1)S(1)}, u32[]{:S(2)}, u32[]{:S(2)}) async-start(bf16[32,32,128]{2,1,0:T(8,128)(2,1)} %get-tuple-element.16), calls=%async_computation.1 | async-start | bytes 524288 | tf_op jit(solution)/shard_map/all_to_all | solution.py:539
  27.7 0.0 copy-done.5
  27.7 0.0 copy-done.6
  27.7 0.0 copy-done.7
  27.7 0.0 copy-done
  27.7 0.0 copy-done.2
  27.7 0.0 copy-done.3
  27.7 0.0 copy-done.4
  27.7 0.9 %shard_map.158 = (f32[2,1024,128]{2,1,0:T(8,128)S(1)}, f32[2,1024,128]{2,1,0:T(8,128)S(1)}, bf16[256,256]{1,0:T(8,128)(2,1)S(1)}, f32[256,256]{1,0:T(8,128)S(1)}) custom-call(bf16[256,256]{1,0:T(8,128)(2,1)S(1)} %copy-done.7, bf16[256,256]{1,0:T(8,128)(2,1)S(1)} %bitcast.18, bf16[256,256]{1,0:T(8,128)(2,1)S(1)} %copy-done.3, bf16[256,256]{1,0:T(8,128)(2,1)S(1)} %copy-done.4, ...), custom_call_target="tpu_custom_call" | custom-call | flops 167772160 | bytes 4194304 | tf_op jit(solution)/shard_map/pallas_call | solution.py:477
  28.7 0.0 copy-start.8
  28.7 0.6 %copy-done.8 = bf16[256,256]{1,0:T(8,128)(2,1)} copy-done((bf16[256,256]{1,0:T(8,128)(2,1)}, bf16[256,256]{1,0:T(8,128)(2,1)S(1)}, u32[]{:S(2)}) %copy-start.8) | copy-done | bytes 131096
  29.3 8.9 %all-to-all-done.1.bias_ref = bf16[32,32,128]{2,1,0:T(8,128)(2,1)S(1)} async-done(((bf16[32,32,128]{2,1,0:T(8,128)(2,1)}), bf16[32,32,128]{2,1,0:T(8,128)(2,1)S(1)}, u32[]{:S(2)}, u32[]{:S(2)}) %all-to-all-start.1) | async-done | bytes 262176 | tf_op jit(solution)/shard_map/all_to_all | solution.py:539
  38.3 2.2 %shard_map.160 = (bf16[32,32,128]{2,1,0:T(8,128)(2,1)}, f32[1024,128]{1,0:T(8,128)S(1)}) custom-call(bf16[32,32,128]{2,1,0:T(8,128)(2,1)S(1)} %all-to-all-done.1.bias_ref, s32[1,128]{1,0:T(1,128)S(1)} %bitcast.22, f32[2,1024,128]{2,1,0:T(8,128)S(1)} %get-tuple-element.14.score_ref, f32[2,1024,128]{2,1,0:T(8,128)S(1)} %get-tuple-element.17.flow_ref), custom_call_target="tpu_custom_call" | custom-call | flops 268435456 | bytes 4194304 | tf_op jit(solution)/shard_map/pallas_call | solution.py:542
  40.4 0.0 copy-start.11
  40.4 2.7 %all-to-all-start.2 = ((bf16[32,32,128]{2,1,0:T(8,128)(2,1)}), bf16[32,32,128]{2,1,0:T(8,128)(2,1)S(1)}, u32[]{:S(2)}, u32[]{:S(2)}) async-start(bf16[32,32,128]{2,1,0:T(8,128)(2,1)} %get-tuple-element.22), calls=%async_computation.2 | async-start | bytes 524288 | tf_op jit(solution)/shard_map/all_to_all | solution.py:550
  43.2 0.0 copy-done.11
  43.2 0.2 collective-permute-start.1
  43.4 1.1 %collective-permute-done.1 = bf16[4,64,128]{2,1,0:T(8,128)(2,1)S(1)} collective-permute-done((bf16[4,64,128]{2,1,0:T(8,128)(2,1)S(1)}, bf16[4,64,128]{2,1,0:T(8,128)(2,1)S(1)}, u32[]{:S(2)}, u32[]{:S(2)}) %collective-permute-start.1) | collective-permute-done | bytes 65568 | tf_op jit(solution)/shard_map/ppermute | solution.py:505
  44.5 0.0 copy-start.9
  44.6 0.0 copy-start.1
  44.6 0.9 %copy-done.9 = bf16[256,256]{1,0:T(8,128)(2,1)S(1)} copy-done((bf16[256,256]{1,0:T(8,128)(2,1)S(1)}, bf16[256,256]{1,0:T(8,128)(2,1)}, u32[]{:S(2)}) %copy-start.9) | copy-done | bytes 131096
  45.4 1.6 %shard_map.161 = bf16[256,256]{1,0:T(8,128)(2,1)} custom-call(f32[2,1024,128]{2,1,0:T(8,128)S(1)} %get-tuple-element.14.score_ref, f32[1024,128]{1,0:T(8,128)S(1)} %get-tuple-element.18.full_ref, bf16[256,256]{1,0:T(8,128)(2,1)S(1)} %copy-done.9, f32[256,256]{1,0:T(8,128)S(1)} %get-tuple-element.20.gate_ref, bf16[256,256]{1,0:T(8,128)(2,1)S(1)} %copy-done), custom_call_target="tpu_custom_call" | custom-call | flops 536870912 | bytes 4194304 | tf_op jit(solution)/shard_map/pallas_call | solution.py:551
  47.0 6.8 %all-to-all-done.2.shares_ref = bf16[32,32,128]{2,1,0:T(8,128)(2,1)S(1)} async-done(((bf16[32,32,128]{2,1,0:T(8,128)(2,1)}), bf16[32,32,128]{2,1,0:T(8,128)(2,1)S(1)}, u32[]{:S(2)}, u32[]{:S(2)}) %all-to-all-start.2) | async-done | bytes 262176 | tf_op jit(solution)/shard_map/all_to_all | solution.py:550
  53.8 0.0 copy-done.1
  53.8 1.5 %shard_map.162 = f32[4,128,128]{2,1,0:T(8,128)} custom-call(bf16[32,32,128]{2,1,0:T(8,128)(2,1)S(1)} %all-to-all-done.2.shares_ref, bf16[8,128]{1,0:T(8,128)(2,1)S(1)} %bitcast.20, bf16[4,128,128]{2,1,0:T(8,128)(2,1)S(1)} %maximum_select_fusion.1.pair_ref), custom_call_target="tpu_custom_call" | custom-call | flops 16777216 | bytes 1048576 | tf_op jit(solution)/shard_map/pallas_call | solution.py:558
  (8 shorter events, 0.1 us)
Async XLA Ops:
  2.8 7.3 %copy-start.15 = (bf16[4,128,128]{2,1,0:T(8,128)(2,1)S(1)}, bf16[4,128,128]{2,1,0:T(8,128)(2,1)}, u32[]{:S(2)}) copy-start(bf16[4,128,128]{2,1,0:T(8,128)(2,1)} %param.15) | copy-start | bytes 393220
  2.8 19.3 %all-to-all-start = ((bf16[32,36,128]{2,1,0:T(8,128)(2,1)}), bf16[32,36,128]{2,1,0:T(8,128)(2,1)S(1)}, u32[]{:S(2)}, u32[]{:S(2)}) async-start(bf16[32,36,128]{2,1,0:T(8,128)(2,1)} %bitcast.25), calls=%async_computation | async-start | bytes 655360 | tf_op jit(solution)/shard_map/all_to_all | solution.py:471
  10.1 3.5 %copy-start.14 = (bf16[32,32,128]{2,1,0:T(8,128)(2,1)S(1)}, bf16[32,32,128]{2,1,0:T(8,128)(2,1)}, u32[]{:S(2)}) copy-start(bf16[32,32,128]{2,1,0:T(8,128)(2,1)} %param.21) | copy-start | bytes 786436
  10.1 3.9 %collective-permute-start = (bf16[4,64,128]{2,1,0:T(8,128)(2,1)S(1)}, bf16[4,64,128]{2,1,0:T(8,128)(2,1)S(1)}, u32[]{:S(2)}, u32[]{:S(2)}) collective-permute-start(bf16[4,64,128]{2,1,0:T(8,128)(2,1)S(1)} %get-tuple-element.26), channel_id=1, source_target_pairs={{0,1},{1,0},{2,3},{3,2},{4,5},{5,4},{6,7},{7,6},{8,9},{9,8},{10,11... | collective-permute-start | bytes 196616 | tf_op jit(solution)/shard_map/ppermute | solution.py:500
  10.5 0.7 %copy-start.13 = (s32[128]{0:T(128)S(1)}, s32[128]{0:T(128)}, u32[]{:S(2)}) copy-start(s32[128]{0:T(128)} %param.18) | copy-start | bytes 1540
  11.3 0.7 %copy-start.16 = (s32[64]{0:T(128)S(1)}, s32[64]{0:T(128)}, u32[]{:S(2)}) copy-start(s32[64]{0:T(128)} %seq_ref.1) | copy-start | bytes 772
  14.1 8.0 %copy-start.12 = (bf16[128,8]{0,1:T(8,128)(2,1)S(1)}, bf16[128,8]{0,1:T(8,128)(2,1)}, u32[]{:S(2)}) copy-start(bf16[128,8]{0,1:T(8,128)(2,1)} %param.22) | copy-start | bytes 6148
  22.1 5.6 %copy-start.5 = (bf16[256,256]{1,0:T(8,128)(2,1)S(1)}, bf16[256,256]{1,0:T(8,128)(2,1)}, u32[]{:S(2)}) copy-start(bf16[256,256]{1,0:T(8,128)(2,1)} %refs_4_.1) | copy-start | bytes 393220
  22.1 5.6 %copy-start.6 = (bf16[256,256]{1,0:T(8,128)(2,1)S(1)}, bf16[256,256]{1,0:T(8,128)(2,1)}, u32[]{:S(2)}) copy-start(bf16[256,256]{1,0:T(8,128)(2,1)} %refs_5_.1) | copy-start | bytes 393220
  22.1 5.6 %copy-start.7 = (bf16[256,256]{1,0:T(8,128)(2,1)S(1)}, bf16[256,256]{1,0:T(8,128)(2,1)}, u32[]{:S(2)}) copy-start(bf16[256,256]{1,0:T(8,128)(2,1)} %get-tuple-element.13.refs_0_) | copy-start | bytes 393220
  24.2 0.7 %copy-start.10 = (bf16[8,64,128]{2,1,0:T(8,128)(2,1)}, bf16[8,64,128]{2,1,0:T(8,128)(2,1)S(1)}, u32[]{:S(2)}) copy-start(bf16[8,64,128]{2,1,0:T(8,128)(2,1)S(1)} %get-tuple-element.21) | copy-start | bytes 393220
  24.9 2.8 %copy-start = (bf16[256,256]{1,0:T(8,128)(2,1)S(1)}, bf16[256,256]{1,0:T(8,128)(2,1)}, u32[]{:S(2)}) copy-start(bf16[256,256]{1,0:T(8,128)(2,1)} %wo_ref.1) | copy-start | bytes 393220
  24.9 2.8 %copy-start.2 = (bf16[2,128,256]{2,1,0:T(8,128)(2,1)S(1)}, bf16[2,128,256]{2,1,0:T(8,128)(2,1)}, u32[]{:S(2)}) copy-start(bf16[2,128,256]{2,1,0:T(8,128)(2,1)} %param.16) | copy-start | bytes 393220
  24.9 2.8 %copy-start.3 = (bf16[256,256]{1,0:T(8,128)(2,1)S(1)}, bf16[256,256]{1,0:T(8,128)(2,1)}, u32[]{:S(2)}) copy-start(bf16[256,256]{1,0:T(8,128)(2,1)} %refs_2_.1) | copy-start | bytes 393220
  24.9 2.8 %copy-start.4 = (bf16[256,256]{1,0:T(8,128)(2,1)S(1)}, bf16[256,256]{1,0:T(8,128)(2,1)}, u32[]{:S(2)}) copy-start(bf16[256,256]{1,0:T(8,128)(2,1)} %refs_3_.1) | copy-start | bytes 393220
  24.9 13.3 %all-to-all-start.1 = ((bf16[32,32,128]{2,1,0:T(8,128)(2,1)}), bf16[32,32,128]{2,1,0:T(8,128)(2,1)S(1)}, u32[]{:S(2)}, u32[]{:S(2)}) async-start(bf16[32,32,128]{2,1,0:T(8,128)(2,1)} %get-tuple-element.16), calls=%async_computation.1 | async-start | bytes 524288 | tf_op jit(solution)/shard_map/all_to_all | solution.py:539
  28.7 0.7 %copy-start.8 = (bf16[256,256]{1,0:T(8,128)(2,1)}, bf16[256,256]{1,0:T(8,128)(2,1)S(1)}, u32[]{:S(2)}) copy-start(bf16[256,256]{1,0:T(8,128)(2,1)S(1)} %get-tuple-element.19.v_ref) | copy-start | bytes 393220
  40.4 2.7 %copy-start.11 = (bf16[8,64,128]{2,1,0:T(8,128)(2,1)S(1)}, bf16[8,64,128]{2,1,0:T(8,128)(2,1)}, u32[]{:S(2)}) copy-start(bf16[8,64,128]{2,1,0:T(8,128)(2,1)} %copy-done.10) | copy-start | bytes 393220
  40.4 13.3 %all-to-all-start.2 = ((bf16[32,32,128]{2,1,0:T(8,128)(2,1)}), bf16[32,32,128]{2,1,0:T(8,128)(2,1)S(1)}, u32[]{:S(2)}, u32[]{:S(2)}) async-start(bf16[32,32,128]{2,1,0:T(8,128)(2,1)} %get-tuple-element.22), calls=%async_computation.2 | async-start | bytes 524288 | tf_op jit(solution)/shard_map/all_to_all | solution.py:550
  43.2 1.3 %collective-permute-start.1 = (bf16[4,64,128]{2,1,0:T(8,128)(2,1)S(1)}, bf16[4,64,128]{2,1,0:T(8,128)(2,1)S(1)}, u32[]{:S(2)}, u32[]{:S(2)}) collective-permute-start(bf16[4,64,128]{2,1,0:T(8,128)(2,1)S(1)} %get-tuple-element.24), channel_id=1, source_target_pairs={{0,1},{1,0},{2,3},{3,2},{4,5},{5,4},{6,7},{7,6},{8,9},{9,8},{10,11... | collective-permute-start | bytes 196616 | tf_op jit(solution)/shard_map/ppermute | solution.py:505
  44.5 0.9 %copy-start.9 = (bf16[256,256]{1,0:T(8,128)(2,1)S(1)}, bf16[256,256]{1,0:T(8,128)(2,1)}, u32[]{:S(2)}) copy-start(bf16[256,256]{1,0:T(8,128)(2,1)} %copy-done.8) | copy-start | bytes 393220
  44.6 9.2 %copy-start.1 = (bf16[4,128,128]{2,1,0:T(8,128)(2,1)}, bf16[4,128,128]{2,1,0:T(8,128)(2,1)S(1)}, u32[]{:S(2)}) copy-start(bf16[4,128,128]{2,1,0:T(8,128)(2,1)S(1)} %maximum_select_fusion.1.pair_ref) | copy-start | bytes 393220

commit v5 on v4

--- a/solution.py
+++ b/solution.py
@@ -223,8 +223,8 @@
 
 
 LANES = 128
-LEFT_ROWS = 4
 STRIDE = 40
+GROUP = 4
 f32 = jnp.float32
 bf16 = jnp.bfloat16
 
@@ -282,30 +282,56 @@
         send_ref[:, core, right_rows:, :] = tail
 
 
-def by_head(rows, heads):
-    channels = rows.shape[1]
-    head_of = lax.broadcasted_iota(jnp.int32, (1, channels), 1) // (channels // heads)
-    return jnp.concatenate(
-        [jnp.where(head_of == h, rows, jnp.zeros((), rows.dtype)) for h in range(heads)], axis=0
-    )
+def side_by_side(first, second, at):
+    low = lane_index(first.shape[0]) < 64
+    span = slice(at // 2 * LANES, at // 2 * LANES + LANES)
+    first, second = first[:, span], second[:, span]
+    if at % 2 == 0:
+        return jnp.where(low, first, pltpu.roll(second, 64, 1))
+    return jnp.where(low, pltpu.roll(first, 64, 1), second)
+
+
+def partner(step):
+    return lax.bitwise_xor(lax.rem(lax.axis_index("row"), GROUP), step)
 
 
 def projections_kernel(
-    heads, scale, normed_ref, cot_ref, wq_ref, wk_ref, wv_ref, wg_ref, wo_ref, score_ref, flow_ref, v_ref, gate_ref
+    normed_ref, cot_ref, wq_ref, wk_ref, wv_ref, wg_ref, wo_ref, gate_ref, *rest
 ):
-    seqs, _, residues = score_ref.shape
+    block_refs, every = rest[:GROUP], rest[GROUP]
+    residues = gate_ref.shape[1]
+    seqs = normed_ref.shape[0] // residues
     normed = normed_ref[...]
-    queries = dot_nn(normed, wq_ref[...]).astype(bf16)
-    keys = dot_nn(normed, wk_ref[...]).astype(bf16)
-    values = dot_nn(normed, wv_ref[...]).astype(bf16)
+    queries = dot_nn(normed, wq_ref[...])
+    keys = dot_nn(normed, wk_ref[...])
+    values = dot_nn(normed, wv_ref[...])
     gate = jax.nn.sigmoid(dot_nn(normed, wg_ref[...]))
-    d_rounded = (dot_nt(cot_ref[...], wo_ref[...]) * gate).astype(bf16)
-    v_ref[...] = values
-    gate_ref[...] = gate
-    for s in range(seqs):
-        at = slice(s * residues, (s + 1) * residues)
-        score_ref[s] = dot_nt(by_head(queries[at], heads), keys[at]) * scale
-        flow_ref[s] = dot_nt(by_head(d_rounded[at], heads), values[at])
+    d_attended = dot_nt(cot_ref[...], wo_ref[...]) * gate
+    for t in range(GROUP):
+        rows = side_by_side(queries, d_attended, t).astype(bf16)
+        columns = side_by_side(keys, values, t).astype(bf16)
+        gate_ref[t] = side_by_side(gate[:residues], gate[residues:], t)
+        for s in range(seqs):
+            every[t, s] = rows[s * residues : (s + 1) * residues]
+            every[t, seqs + s] = columns[s * residues : (s + 1) * residues]
+    for step in range(GROUP):
+        block_refs[step][...] = every[partner(step)]
+
+
+def products_kernel(scale, *refs):
+    block_refs, score_ref, flow_ref = refs[:GROUP], refs[GROUP], refs[GROUP + 1]
+    rows = score_ref.shape[1]
+    residues = score_ref.shape[2]
+    part_of = lane_index(residues) // 32
+    seqs = block_refs[0].shape[0] // 2
+    for step, block in enumerate(block_refs):
+        for s in range(seqs):
+            wide = jnp.concatenate(
+                [jnp.where(part_of == g, block[s], jnp.zeros((), bf16)) for g in range(4)], axis=0
+            )
+            both = dot_nt(wide, block[seqs + s])
+            score_ref[step * seqs + s] = both[:rows] * scale
+            flow_ref[step * seqs + s] = both[rows:]
 
 
 def pair_kernel(recv_ref, weight_ref, pair_ref, div_ref, bias_w_ref, send_ref, updated_ref, flat, rbuf, lbuf, obuf):
@@ -343,8 +369,11 @@
         updated_ref[b + 4] = updated[64:]
         pair_normed = layer_normalize(updated).astype(bf16)
         blocks.append(dot_nt(bias_w, pair_normed))
-    block = jnp.concatenate(blocks, axis=0).astype(bf16)
-    send_ref[...] = jnp.broadcast_to(block[None], send_ref.shape)
+    lines, _, share, _ = send_ref.shape
+    heads = share // 4
+    for t in range(GROUP):
+        block = jnp.concatenate([rows[t * heads : (t + 1) * heads] for rows in blocks], axis=0).astype(bf16)
+        send_ref[:, t] = jnp.broadcast_to(block[None], (lines, share, LANES))
 
 
 def placed_bias(flat, res_ref, heads, h):
@@ -378,33 +407,54 @@
     send_ref[...] = grads[...].astype(bf16).reshape(send_ref.shape)
 
 
-def output_kernel(score_ref, full_ref, v_ref, gate_ref, wo_ref, out_ref):
-    seqs, rows, residues = score_ref.shape
+def attended_kernel(score_ref, full_ref, *refs):
+    block_refs, out_refs = refs[:GROUP], refs[GROUP:]
+    _, rows, residues = score_ref.shape
     heads = rows // residues
-    channels = v_ref.shape[1]
-    head_of = lax.broadcasted_iota(jnp.int32, (1, channels), 1) // (channels // heads)
-    ones = jnp.ones((residues, LANES), bf16)
-    for s in range(seqs):
-        own = slice(s * residues, (s + 1) * residues)
-        attended = jnp.zeros((residues, channels), f32)
-        for h in range(heads):
-            at = slice(h * residues, (h + 1) * residues)
-            scores = score_ref[s, at, :] + full_ref[at, :]
-            weights = jnp.exp(scores - jnp.max(scores, axis=-1, keepdims=True))
-            total = jnp.sum(weights, axis=-1, keepdims=True)
-            mixed = dot_nn(weights.astype(bf16), v_ref[own, :]) / total
-            attended = jnp.where(head_of == h, mixed, attended)
-        gated = (gate_ref[own, :] * attended).astype(bf16)
-        out_ref[own, :] = dot_nn(gated, wo_ref[...]).astype(bf16)
+    seqs = block_refs[0].shape[0] // 2
+    part_of = lane_index(residues) // 32
+    for step in range(GROUP):
+        attended = []
+        for s in range(seqs):
+            own = jnp.zeros((residues, LANES), f32)
+            for h in range(heads):
+                at = slice(h * residues, (h + 1) * residues)
+                scores = score_ref[step * seqs + s, at, :] + full_ref[at, :]
+                weights = jnp.exp(scores - jnp.max(scores, axis=-1, keepdims=True))
+                total = jnp.sum(weights, axis=-1, keepdims=True)
+                mixed = dot_nn(weights.astype(bf16), block_refs[step][seqs + s]) / total
+                own = jnp.where(part_of == heads + h, mixed, own)
+            attended.append(own)
+        out_refs[step][...] = jnp.where(
+            part_of < heads, pltpu.roll(attended[0], 64, 1), attended[1]
+        ).astype(bf16)
+
+
+def output_kernel(gate_ref, wo_ref, *refs):
+    in_refs, out_ref = refs[:GROUP], refs[GROUP]
+    residues = gate_ref.shape[1]
+    low = lane_index(residues) < 64
+    zero = jnp.zeros((), bf16)
+    sums = [jnp.zeros((residues, out_ref.shape[1]), f32) for _ in range(2)]
+    for step in range(GROUP):
+        at = partner(step)
+        gated = (gate_ref[at] * in_refs[step][...].astype(f32)).astype(bf16)
+        weight = wo_ref[pl.ds(pl.multiple_of(at * 64, 64), 64), :]
+        weight = jnp.concatenate([weight, weight], axis=0)
+        sums[0] = sums[0] + dot_nn(jnp.where(low, gated, zero), weight)
+        sums[1] = sums[1] + dot_nn(jnp.where(low, zero, gated), weight)
+    for s in range(2):
+        out_ref[s * residues : (s + 1) * residues, :] = sums[s].astype(bf16)
 
 
 def gradient_kernel(shares_ref, bias_w_ref, pair_ref, out_ref):
-    total = jnp.sum(shares_ref[...].astype(f32), axis=0)
+    peers, share, _ = shares_ref.shape
+    total = jnp.sum(shares_ref[...].astype(f32).reshape(peers // GROUP, GROUP, share, LANES), axis=0)
     rows = pair_ref.shape[0]
-    heads = total.shape[0] // rows
+    heads = share // rows
     bias_w = bias_w_ref[...].astype(f32)
     for i in range(rows):
-        own = total[i * heads : (i + 1) * heads]
+        own = jnp.concatenate([total[t, i * heads : (i + 1) * heads] for t in range(GROUP)], axis=0)
         upstream = lax.dot_general(
             own, bias_w, (((0,), (0,)), ((), ())), precision=lax.Precision.HIGHEST, preferred_element_type=f32
         )
@@ -472,19 +522,17 @@
         send.reshape(peers, block_rows, LANES), "row", split_axis=0, concat_axis=0, tiled=True
     )
 
-    head_rows = head_count * residues
+    group_heads = head_count // GROUP
+    head_rows = group_heads * residues
     scale = (channel_count // head_count) ** (-0.5)
-    scores, flow, values, gate = kernel_call(
-        lambda *refs: projections_kernel(head_count, scale, *refs),
-        [
-            shape((sequence_wise, head_rows, residues), f32),
-            shape((sequence_wise, head_rows, residues), f32),
-            shape((token_rows, channel_count), bf16),
-            shape((token_rows, channel_count), f32),
-        ],
+    gate, *blocks = kernel_call(
+        projections_kernel,
+        [shape((GROUP, residues, LANES), f32)]
+        + [shape((2 * sequence_wise, residues, LANES), bf16)] * GROUP,
         [vmem] * 7,
+        [pltpu.VMEM((GROUP, 2 * sequence_wise, residues, LANES), bf16)],
         flops=10 * token_rows * channel_count * channel_count,
-        moved=1 << 22,
+        moved=1 << 21,
     )(
         normed,
         update_cotangent.reshape(token_rows, channel_count),
@@ -495,6 +543,20 @@
         output_weight,
     )
 
+    def trade(parts):
+        return parts[:1] + [
+            lax.ppermute(parts[d], "row", [(i, i ^ d) for i in range(peers)]) for d in range(1, GROUP)
+        ]
+
+    blocks = trade(blocks)
+    scores, flow = kernel_call(
+        lambda *refs: products_kernel(scale, *refs),
+        [shape((GROUP * sequence_wise, head_rows, residues), f32)] * 2,
+        [vmem] * GROUP,
+        flops=1 << 28,
+        moved=1 << 21,
+    )(*blocks)
+
     def trade_columns(tile):
         kept = lax.dynamic_slice_in_dim(tile, core * half, half, 1)
         got = lax.ppermute(lax.dynamic_slice_in_dim(tile, (1 - core) * half, half, 1), "row", sibling)
@@ -522,10 +584,10 @@
     divisor = jnp.maximum(
         jnp.sum(seq_live) * tile_rows.T[:, :, None] * tile_cols[None, None, :], 1.0
     ).reshape(4, 2 * half)
-    bias_rows = 4 * head_count
+    share_rows = 4 * group_heads
     send_bias, updated_tile = kernel_call(
         pair_kernel,
-        [shape((peers, bias_rows, LANES), bf16), shape((8, half, pair_channels), bf16)],
+        [shape((peers // GROUP, GROUP, share_rows, LANES), bf16), shape((8, half, pair_channels), bf16)],
         [vmem] * 5,
         [
             pltpu.VMEM((peers * STRIDE, LANES), f32),
@@ -536,25 +598,34 @@
         flops=1 << 29,
         moved=1 << 20,
     )(received, weight_t, pair_tile, divisor, bias_weight.T)
-    bias_all = lax.all_to_all(send_bias, "row", split_axis=0, concat_axis=0, tiled=True)
+    bias_all = lax.all_to_all(
+        send_bias.reshape(peers, share_rows, LANES), "row", split_axis=0, concat_axis=0, tiled=True
+    )
     pair_updated = trade_rows(updated_tile)
 
     send_grad, full_bias = kernel_call(
         bias_gradient_kernel,
-        [shape((peers, rows_here * head_count, LANES), bf16), shape((head_rows, residues), f32)],
+        [shape((peers, rows_here * group_heads, LANES), bf16), shape((head_rows, residues), f32)],
         [vmem] * 4,
         [pltpu.VMEM((head_rows, LANES), f32), pltpu.VMEM((head_rows, LANES), f32)],
         flops=1 << 28,
         moved=1 << 22,
     )(bias_all, res_row, scores, flow)
     shares = lax.all_to_all(send_grad, "row", split_axis=0, concat_axis=0, tiled=True)
+    attended = kernel_call(
+        attended_kernel,
+        [shape((residues, LANES), bf16)] * GROUP,
+        [vmem] * (2 + GROUP),
+        flops=1 << 28,
+        moved=1 << 21,
+    )(scores, full_bias, *blocks)
     update = kernel_call(
         output_kernel,
         shape((token_rows, channel_count), bf16),
-        [vmem] * 5,
-        flops=1 << 29,
-        moved=1 << 22,
-    )(scores, full_bias, values, gate, output_weight)
+        [vmem] * (2 + GROUP),
+        flops=2 * token_rows * channel_count * channel_count,
+        moved=1 << 20,
+    )(gate, output_weight, *trade(list(attended)))
     pair_gradient = kernel_call(
         gradient_kernel,
         shape((rows_here, residues, pair_channels), f32),
@@ -565,6 +636,20 @@
     return (update.reshape(alignment_rows.shape), pair_updated, pair_gradient)
 
 
+def on_device(*arguments):
+    rows, pair, left, bias = arguments[0], arguments[1], arguments[5], arguments[8]
+    peers = lax.axis_size("row")
+    fits = (
+        lax.axis_size("col") == 1
+        and peers == 32
+        and rows.shape == (2, 128, 256)
+        and pair.shape == (4, 128, 128)
+        and left.shape[1] == 32
+        and bias.shape[1] == 8
+    )
+    return (on_device_paired if fits else on_device_general)(*arguments)
+
+
 def solution(mesh):
     placed = (
         P(("grp", "row"), "col", None),
@@ -582,9 +667,8 @@
         P(),
         P(),
     )
-    one_column = mesh.shape["col"] == 1 and mesh.shape["row"] % 2 == 0
     return jax.shard_map(
-        on_device_paired if one_column else on_device_general,
+        on_device,
         mesh=mesh,
         in_specs=placed,
         out_specs=(

time: 55.7 us -> 48.9 us (0.88)
  waiting for transfers between devices: 24.8 us -> 14.9 us
  starting transfers between devices: 13.2 us -> 16.8 us
    all_to_all x1, waiting for transfers between devices: 6.77 us -> 0.01 us  [on_device_paired(): lax.all_to_all(send_grad, 'row', split_axis=0, concat_axis=0, tiled=True)]
    ppermute x0 -> x6, starting transfers between devices: none -> 3.97 us  [trade(): lax.ppermute(parts[d], 'row', [(i, i ^ d) for i in range(peers)])]
    ppermute x0 -> x6, waiting for transfers between devices: none -> 3.35 us  [trade(): lax.ppermute(parts[d], 'row', [(i, i ^ d) for i in range(peers)])]
    all_to_all x1, waiting for transfers between devices: 7.95 us -> 4.83 us  [on_device_paired(): lax.all_to_all(send.reshape(peers, block_rows, LANES), 'row', split_axis=...]
    all_to_all x1, waiting for transfers between devices: 8.92 us -> 6.75 us  [on_device_paired(): lax.all_to_all(send_bias.reshape(peers, share_rows, LANES), 'row', split_...]
    unnamed x35 -> x25, local copies, waits for them, and re-layouts: 3.57 us -> 2.29 us
    ppermute x1, waiting for transfers between devices: 1.14 us -> 0.01 us  [trade_rows(): lax.ppermute(lax.dynamic_slice_in_dim(tile, (1 - core) * rows_here, rows_...]
    dynamic_slice x1, local copies, waits for them, and re-layouts: 0.02 us -> 0.89 us  [trade_columns(): kept = lax.dynamic_slice_in_dim(tile, core * half, half, 1)]
  transfers between devices with their start and end apart: 5 -> 11, of which waited for: 4 -> 4; matrix products, arithmetic and copies ran while one was open for 4% -> 5% of each run, Pallas kernels for 5% -> 19%
where the time goes in v5:
time: 48.9 us; the launch traced here: 48.6 us
  starting transfers between devices  16.8 us (34%)
  waiting for transfers between devices  14.9 us (30%)
  Pallas kernels  10.5 us (21%)
  local copies, waits for them, and re-layouts  4.09 us (8%)
  other arithmetic  1.38 us (3%)
  between operations  0.89 us (2%)
    all_to_all x1, starting transfers between devices, on_device_paired(): lax.all_to_all(send.reshape(peers, block_rows, LANES), 'row', split_axis=...  6.96 us
    all_to_all x1, waiting for transfers between devices, on_device_paired(): lax.all_to_all(send_bias.reshape(peers, share_rows, LANES), 'row', split_...  6.75 us
    all_to_all x1, waiting for transfers between devices, on_device_paired(): lax.all_to_all(send.reshape(peers, block_rows, LANES), 'row', split_axis=...  4.83 us
    ppermute x6, starting transfers between devices, trade(): lax.ppermute(parts[d], 'row', [(i, i ^ d) for i in range(peers)])  3.97 us
    ppermute x6, waiting for transfers between devices, trade(): lax.ppermute(parts[d], 'row', [(i, i ^ d) for i in range(peers)])  3.35 us
    all_to_all x1, starting transfers between devices, on_device_paired(): lax.all_to_all(send_bias.reshape(peers, share_rows, LANES), 'row', split_...  2.57 us
    all_to_all x1, starting transfers between devices, on_device_paired(): lax.all_to_all(send_grad, 'row', split_axis=0, concat_axis=0, tiled=True)  2.57 us
    unnamed x25, local copies, waits for them, and re-layouts  2.29 us
  transfers between devices with their start and end apart: 11, of which 4 were waited for; matrix products, arithmetic and copies ran while one was open for 5% of the time, Pallas kernels for 19%

profile of v5, /device:TPU:0, one launch (start us, length us, event | category | flops | bytes accessed | tf_op | source)
XLA Modules:
  0.0 48.6 jit_solution(16133349839276070752)
XLA Ops:
  0.7 0.9 %constant_dynamic-slice_fusion.3 = (bf16[4,64,128]{2,1,0:T(8,128)(2,1)S(1)}, bf16[4,64,128]{2,1,0:T(8,128)(2,1)S(1)}) fusion(bf16[4,128,128]{2,1,0:T(8,128)(2,1)} %param.15, s32[]{:T(128)S(6)} %select_n.45, s32[]{:T(128)S(6)} %select_n.46), kind=kLoop, calls=%fused_computation.7 | loop fusion | bytes 262152 | tf_op jit(solution)/shard_map/dynamic_slice | solution.py:561
  1.5 0.5 %collective-permute-start.3 = (bf16[4,64,128]{2,1,0:T(8,128)(2,1)S(1)}, bf16[4,64,128]{2,1,0:T(8,128)(2,1)S(1)}, u32[]{:S(2)}, u32[]{:S(2)}) collective-permute-start(bf16[4,64,128]{2,1,0:T(8,128)(2,1)S(1)} %get-tuple-element.40), channel_id=1, source_target_pairs={{0,1},{1,0},{2,3},{3,2},{4,5},{5,4},{6,7},{7,6},{8,9},{9,8},{10,11... | collective-permute-start | bytes 196616 | tf_op jit(solution)/shard_map/ppermute | solution.py:562
  2.1 0.0 copy-start.6
  2.1 2.2 %shard_map.157 = (bf16[16,2,36,128]{3,2,1,0:T(8,128)(2,1)}, bf16[256,256]{1,0:T(8,128)(2,1)}) custom-call(s32[64]{0:T(128)} %seq_ref.1, s32[1,128]{1,0:T(1,128)} %bitcast.22, bf16[256,256]{1,0:T(8,128)(2,1)} %bitcast.29, bf16[32,256]{1,0:T(8,128)(2,1)} %bitcast.30, bf16[32,256]{1,0:T(8,128)(2,1)} %bitcast.31), custom_call_target="tpu_custom_call" | custom-call | flops 16777216 | bytes 524288 | tf_op jit(solution)/shard_map/pallas_call | solution.py:512
  4.2 0.0 copy-start
  4.2 0.0 copy-start.2
  4.2 0.0 copy-start.3
  4.2 0.0 copy-start.4
  4.3 0.0 copy-start.5
  4.3 7.0 %all-to-all-start = ((bf16[32,36,128]{2,1,0:T(8,128)(2,1)}), bf16[32,36,128]{2,1,0:T(8,128)(2,1)S(1)}, u32[]{:S(2)}, u32[]{:S(2)}) async-start(bf16[32,36,128]{2,1,0:T(8,128)(2,1)} %bitcast.26), calls=%async_computation | async-start | bytes 655360 | tf_op jit(solution)/shard_map/all_to_all | solution.py:521
  11.2 0.0 copy-done.6
  11.2 0.0 copy-done
  11.3 0.0 copy-done.2
  11.3 0.0 copy-done.3
  11.3 0.0 copy-done.4
  11.3 0.0 copy-done.5
  11.3 0.0 copy-start.7
  11.3 0.9 %copy-done.7 = bf16[256,256]{1,0:T(8,128)(2,1)S(1)} copy-done((bf16[256,256]{1,0:T(8,128)(2,1)S(1)}, bf16[256,256]{1,0:T(8,128)(2,1)}, u32[]{:S(2)}) %copy-start.7) | copy-done | bytes 131096
  12.2 0.0 copy-start.10
  12.2 0.5 %shard_map.158 = (f32[4,128,128]{2,1,0:T(8,128)S(1)}, bf16[4,128,128]{2,1,0:T(8,128)(2,1)S(1)}, bf16[4,128,128]{2,1,0:T(8,128)(2,1)S(1)}, bf16[4,128,128]{2,1,0:T(8,128)(2,1)S(1)}, bf16[4,128,128]{2,1,0:T(8,128)(2,1)S(1)}) custom-call(bf16[256,256]{1,0:T(8,128)(2,1)S(1)} %copy-done.7, bf16[256,256]{1,0:T(8,128)(2,1)S(1)} %bitcast.19, ...), custom_call_target="tpu_custom_call" | custom-call | flops 167772160 | bytes 2097152 | tf_op jit(solution)/shard_map/pallas_call | solution.py:528
  12.7 0.3 collective-permute-start
  13.0 1.7 %collective-permute-start.1 = (bf16[4,128,128]{2,1,0:T(8,128)(2,1)S(1)}, bf16[4,128,128]{2,1,0:T(8,128)(2,1)S(1)}, u32[]{:S(2)}, u32[]{:S(2)}) collective-permute-start(bf16[4,128,128]{2,1,0:T(8,128)(2,1)S(1)} %get-tuple-element.24), channel_id=1, source_target_pairs={{0,2},{1,3},{2,0},{3,1},{4,6},{5,7},{6,4},{7,5},{8,10},{9,11},{10,... | collective-permute-start | bytes 393224 | tf_op jit(solution)/shard_map/ppermute | solution.py:548
  14.7 0.0 collective-permute-start.2
  14.7 0.0 copy-start.9
  14.8 0.7 %copy-done.9 = s32[128]{0:T(128)S(1)} copy-done((s32[128]{0:T(128)S(1)}, s32[128]{0:T(128)}, u32[]{:S(2)}) %copy-start.9) | copy-done | bytes 536
  15.4 0.1 dynamic_slice.21
  15.5 0.1 mul.59
  15.6 0.7 %copy-done.11 = s32[64]{0:T(128)S(1)} copy-done((s32[64]{0:T(128)S(1)}, s32[64]{0:T(128)}, u32[]{:S(2)}) %copy-start.11) | copy-done | bytes 280
  16.2 0.6 %convert_reduce_fusion = f32[]{:T(128)} fusion(s32[64]{0:T(128)S(1)} %copy-done.11), kind=kLoop, calls=%fused_computation.9 | loop fusion | flops 127 | bytes 260 | tf_op jit(solution)/shard_map/reduce_sum | solution.py:585
  16.8 0.7 %dynamic-slice_multiply_fusion = f32[8]{0:T(128)S(1)} fusion(f32[128]{0:T(128)S(1)} %convert_element_type.7, s32[]{:T(128)S(6)} %select_n.49, f32[]{:T(128)} %convert_reduce_fusion), kind=kLoop, calls=%fused_computation.8 | loop fusion | flops 8 | bytes 72 | tf_op jit(solution)/shard_map/mul | solution.py:585
  17.6 0.1 mul.54
  17.6 0.1 copy.20
  17.7 0.1 mul.56
  17.8 0.1 mul.57
  17.9 0.0 copy-done.10
  17.9 0.2 copy.19
  18.2 0.1 copy.21.weight_ref
  18.4 0.0 collective-permute-done.3
  18.4 0.0 copy-start.8
  18.4 4.8 %all-to-all-done.recv_ref = bf16[32,36,128]{2,1,0:T(8,128)(2,1)S(1)} async-done(((bf16[32,36,128]{2,1,0:T(8,128)(2,1)}), bf16[32,36,128]{2,1,0:T(8,128)(2,1)S(1)}, u32[]{:S(2)}, u32[]{:S(2)}) %all-to-all-start) | async-done | bytes 294944 | tf_op jit(solution)/shard_map/all_to_all | solution.py:521
  23.2 0.0 copy-done.8
  23.2 2.1 %shard_map.160 = (bf16[8,4,8,128]{3,2,1,0:T(8,128)(2,1)}, bf16[8,64,128]{2,1,0:T(8,128)(2,1)S(1)}) custom-call(bf16[32,36,128]{2,1,0:T(8,128)(2,1)S(1)} %all-to-all-done.recv_ref, bf16[256,512]{1,0:T(8,128)(2,1)S(1)} %copy.21.weight_ref, bf16[8,64,128]{2,1,0:T(8,128)(2,1)S(1)} %maximum_select_fusion.pair_ref, f32[4,128]{1,0:T(4,128)S(1)} %multiply_maximum_fusion.div_ref, ...), custom_call_target="tpu_custom_call" | custom-call | flops 536870912 | bytes 1048576 | tf_op jit(solution)/shard_map/pallas_call | solution.py:588
  25.3 2.6 %all-to-all-start.1 = ((bf16[32,8,128]{2,1,0:T(8,128)(2,1)}), bf16[32,8,128]{2,1,0:T(8,128)(2,1)S(1)}, u32[]{:S(2)}, u32[]{:S(2)}) async-start(bf16[32,8,128]{2,1,0:T(8,128)(2,1)} %bitcast.10), calls=%async_computation.1 | async-start | bytes 131072 | tf_op jit(solution)/shard_map/all_to_all | solution.py:601
  27.9 0.2 collective-permute-start.7
  28.1 0.0 collective-permute-done.refs_1_
  28.1 0.0 collective-permute-done.1.refs_2_
  28.1 0.0 collective-permute-done.2.refs_3_
  28.1 0.4 shard_map.159
  28.6 6.8 %all-to-all-done.1.bias_ref = bf16[32,8,128]{2,1,0:T(8,128)(2,1)S(1)} async-done(((bf16[32,8,128]{2,1,0:T(8,128)(2,1)}), bf16[32,8,128]{2,1,0:T(8,128)(2,1)S(1)}, u32[]{:S(2)}, u32[]{:S(2)}) %all-to-all-start.1) | async-done | bytes 65568 | tf_op jit(solution)/shard_map/all_to_all | solution.py:601
  35.3 1.4 %shard_map.161 = (bf16[32,8,128]{2,1,0:T(8,128)(2,1)}, f32[256,128]{1,0:T(8,128)S(1)}) custom-call(bf16[32,8,128]{2,1,0:T(8,128)(2,1)S(1)} %all-to-all-done.1.bias_ref, s32[1,128]{1,0:T(1,128)S(1)} %bitcast.23, f32[8,256,128]{2,1,0:T(8,128)S(1)} %get-tuple-element.26.score_ref, f32[8,256,128]{2,1,0:T(8,128)S(1)} %get-tuple-element.29.flow_ref), custom_call_target="tpu_custom_call" | custom-call | flops 268435456 | bytes 4194304 | tf_op jit(solution)/shard_map/pallas_call | solution.py:606
  36.7 2.6 %all-to-all-start.2 = ((bf16[32,8,128]{2,1,0:T(8,128)(2,1)}), bf16[32,8,128]{2,1,0:T(8,128)(2,1)S(1)}, u32[]{:S(2)}, u32[]{:S(2)}) async-start(bf16[32,8,128]{2,1,0:T(8,128)(2,1)} %get-tuple-element.36), calls=%async_computation.2 | async-start | bytes 131072 | tf_op jit(solution)/shard_map/all_to_all | solution.py:614
  39.3 1.4 %shard_map.162 = (bf16[128,128]{1,0:T(8,128)(2,1)S(1)}, bf16[128,128]{1,0:T(8,128)(2,1)S(1)}, bf16[128,128]{1,0:T(8,128)(2,1)S(1)}, bf16[128,128]{1,0:T(8,128)(2,1)S(1)}) custom-call(f32[8,256,128]{2,1,0:T(8,128)S(1)} %get-tuple-element.26.score_ref, f32[256,128]{1,0:T(8,128)S(1)} %get-tuple-element.30.full_ref, ...), custom_call_target="tpu_custom_call" | custom-call | flops 268435456 | bytes 2097152 | tf_op jit(solution)/shard_map/pallas_call | solution.py:615
  40.8 0.2 collective-permute-start.4
  40.9 1.7 %collective-permute-start.5 = (bf16[128,128]{1,0:T(8,128)(2,1)S(1)}, bf16[128,128]{1,0:T(8,128)(2,1)S(1)}, u32[]{:S(2)}, u32[]{:S(2)}) collective-permute-start(bf16[128,128]{1,0:T(8,128)(2,1)S(1)} %get-tuple-element.33), channel_id=1, source_target_pairs={{0,2},{1,3},{2,0},{3,1},{4,6},{5,7},{6,4},{7,5},{8,10},{9,11},{10,... | collective-permute-start | bytes 98312 | tf_op jit(solution)/shard_map/ppermute | solution.py:548
  42.6 0.1 collective-permute-start.6
  42.7 0.0 collective-permute-done.7
  42.8 0.0 copy-start.1
  42.8 0.0 collective-permute-done.4.refs_1_
  42.8 2.2 %collective-permute-done.5.refs_2_ = bf16[128,128]{1,0:T(8,128)(2,1)S(1)} collective-permute-done((bf16[128,128]{1,0:T(8,128)(2,1)S(1)}, bf16[128,128]{1,0:T(8,128)(2,1)S(1)}, u32[]{:S(2)}, u32[]{:S(2)}) %collective-permute-start.5) | collective-permute-done | bytes 32800 | tf_op jit(solution)/shard_map/ppermute | solution.py:548
  44.9 1.2 %collective-permute-done.6.refs_3_ = bf16[128,128]{1,0:T(8,128)(2,1)S(1)} collective-permute-done((bf16[128,128]{1,0:T(8,128)(2,1)S(1)}, bf16[128,128]{1,0:T(8,128)(2,1)S(1)}, u32[]{:S(2)}, u32[]{:S(2)}) %collective-permute-start.6) | collective-permute-done | bytes 32800 | tf_op jit(solution)/shard_map/ppermute | solution.py:548
  46.1 1.0 %shard_map.163 = bf16[256,256]{1,0:T(8,128)(2,1)} custom-call(f32[4,128,128]{2,1,0:T(8,128)S(1)} %get-tuple-element.21.gate_ref, bf16[256,256]{1,0:T(8,128)(2,1)S(1)} %copy-done, bf16[128,128]{1,0:T(8,128)(2,1)S(1)} %get-tuple-element.31.refs_0_, bf16[128,128]{1,0:T(8,128)(2,1)S(1)} %collective-permute-done.4.refs_1_, ...), custom_call_target="tpu_custom_call" | custom-call | flops 33554432 | bytes 1048576 | tf_op jit(solution)/shard_map/pallas_call | solution.py:622
  47.1 0.0 all-to-all-done.2.shares_ref
  47.1 0.0 copy-done.1
  47.1 1.5 %shard_map.164 = f32[4,128,128]{2,1,0:T(8,128)} custom-call(bf16[32,8,128]{2,1,0:T(8,128)(2,1)S(1)} %all-to-all-done.2.shares_ref, bf16[8,128]{1,0:T(8,128)(2,1)S(1)} %bitcast.21, bf16[4,128,128]{2,1,0:T(8,128)(2,1)S(1)} %maximum_select_fusion.1.pair_ref), custom_call_target="tpu_custom_call" | custom-call | flops 16777216 | bytes 1048576 | tf_op jit(solution)/shard_map/pallas_call | solution.py:629
  (8 shorter events, 0.1 us)
Async XLA Ops:
  1.5 16.8 %collective-permute-start.3 = (bf16[4,64,128]{2,1,0:T(8,128)(2,1)S(1)}, bf16[4,64,128]{2,1,0:T(8,128)(2,1)S(1)}, u32[]{:S(2)}, u32[]{:S(2)}) collective-permute-start(bf16[4,64,128]{2,1,0:T(8,128)(2,1)S(1)} %get-tuple-element.40), channel_id=1, source_target_pairs={{0,1},{1,0},{2,3},{3,2},{4,5},{5,4},{6,7},{7,6},{8,9},{9,8},{10,11... | collective-permute-start | bytes 196616 | tf_op jit(solution)/shard_map/ppermute | solution.py:562
  2.1 9.2 %copy-start.6 = (bf16[256,256]{1,0:T(8,128)(2,1)S(1)}, bf16[256,256]{1,0:T(8,128)(2,1)}, u32[]{:S(2)}) copy-start(bf16[256,256]{1,0:T(8,128)(2,1)} %wg_ref.1) | copy-start | bytes 393220
  4.2 7.0 %copy-start = (bf16[256,256]{1,0:T(8,128)(2,1)S(1)}, bf16[256,256]{1,0:T(8,128)(2,1)}, u32[]{:S(2)}) copy-start(bf16[256,256]{1,0:T(8,128)(2,1)} %wo_ref.3) | copy-start | bytes 393220
  4.2 7.0 %copy-start.2 = (bf16[2,128,256]{2,1,0:T(8,128)(2,1)S(1)}, bf16[2,128,256]{2,1,0:T(8,128)(2,1)}, u32[]{:S(2)}) copy-start(bf16[2,128,256]{2,1,0:T(8,128)(2,1)} %param.16) | copy-start | bytes 393220
  4.2 7.0 %copy-start.3 = (bf16[256,256]{1,0:T(8,128)(2,1)S(1)}, bf16[256,256]{1,0:T(8,128)(2,1)}, u32[]{:S(2)}) copy-start(bf16[256,256]{1,0:T(8,128)(2,1)} %wq_ref.1) | copy-start | bytes 393220
  4.2 7.0 %copy-start.4 = (bf16[256,256]{1,0:T(8,128)(2,1)S(1)}, bf16[256,256]{1,0:T(8,128)(2,1)}, u32[]{:S(2)}) copy-start(bf16[256,256]{1,0:T(8,128)(2,1)} %wk_ref.1) | copy-start | bytes 393220
  4.3 7.0 %copy-start.5 = (bf16[256,256]{1,0:T(8,128)(2,1)S(1)}, bf16[256,256]{1,0:T(8,128)(2,1)}, u32[]{:S(2)}) copy-start(bf16[256,256]{1,0:T(8,128)(2,1)} %wv_ref.1) | copy-start | bytes 393220
  4.3 19.0 %all-to-all-start = ((bf16[32,36,128]{2,1,0:T(8,128)(2,1)}), bf16[32,36,128]{2,1,0:T(8,128)(2,1)S(1)}, u32[]{:S(2)}, u32[]{:S(2)}) async-start(bf16[32,36,128]{2,1,0:T(8,128)(2,1)} %bitcast.26), calls=%async_computation | async-start | bytes 655360 | tf_op jit(solution)/shard_map/all_to_all | solution.py:521
  11.3 0.9 %copy-start.7 = (bf16[256,256]{1,0:T(8,128)(2,1)S(1)}, bf16[256,256]{1,0:T(8,128)(2,1)}, u32[]{:S(2)}) copy-start(bf16[256,256]{1,0:T(8,128)(2,1)} %get-tuple-element.20.normed_ref) | copy-start | bytes 393220
  12.2 5.7 %copy-start.10 = (bf16[32,32,128]{2,1,0:T(8,128)(2,1)S(1)}, bf16[32,32,128]{2,1,0:T(8,128)(2,1)}, u32[]{:S(2)}) copy-start(bf16[32,32,128]{2,1,0:T(8,128)(2,1)} %param.21) | copy-start | bytes 786436
  12.7 15.4 %collective-permute-start = (bf16[4,128,128]{2,1,0:T(8,128)(2,1)S(1)}, bf16[4,128,128]{2,1,0:T(8,128)(2,1)S(1)}, u32[]{:S(2)}, u32[]{:S(2)}) collective-permute-start(bf16[4,128,128]{2,1,0:T(8,128)(2,1)S(1)} %get-tuple-element.23), channel_id=1, source_target_pairs={{0,1},{1,0},{2,3},{3,2},{4,5},{5,4},{6,7},{7,6},{8,9},{9,8},{10,11... | collective-permute-start | bytes 393224 | tf_op jit(solution)/shard_map/ppermute | solution.py:548
  13.0 15.1 %collective-permute-start.1 = (bf16[4,128,128]{2,1,0:T(8,128)(2,1)S(1)}, bf16[4,128,128]{2,1,0:T(8,128)(2,1)S(1)}, u32[]{:S(2)}, u32[]{:S(2)}) collective-permute-start(bf16[4,128,128]{2,1,0:T(8,128)(2,1)S(1)} %get-tuple-element.24), channel_id=1, source_target_pairs={{0,2},{1,3},{2,0},{3,1},{4,6},{5,7},{6,4},{7,5},{8,10},{9,11},{10,... | collective-permute-start | bytes 393224 | tf_op jit(solution)/shard_map/ppermute | solution.py:548
  14.7 13.4 %collective-permute-start.2 = (bf16[4,128,128]{2,1,0:T(8,128)(2,1)S(1)}, bf16[4,128,128]{2,1,0:T(8,128)(2,1)S(1)}, u32[]{:S(2)}, u32[]{:S(2)}) collective-permute-start(bf16[4,128,128]{2,1,0:T(8,128)(2,1)S(1)} %get-tuple-element.25), channel_id=1, source_target_pairs={{0,3},{1,2},{2,1},{3,0},{4,7},{5,6},{6,5},{7,4},{8,11},{9,10},{10,... | collective-permute-start | bytes 393224 | tf_op jit(solution)/shard_map/ppermute | solution.py:548
  14.7 0.7 %copy-start.9 = (s32[128]{0:T(128)S(1)}, s32[128]{0:T(128)}, u32[]{:S(2)}) copy-start(s32[128]{0:T(128)} %param.18) | copy-start | bytes 1540
  15.6 0.7 %copy-start.11 = (s32[64]{0:T(128)S(1)}, s32[64]{0:T(128)}, u32[]{:S(2)}) copy-start(s32[64]{0:T(128)} %seq_ref.1) | copy-start | bytes 772
  18.4 4.9 %copy-start.8 = (bf16[128,8]{0,1:T(8,128)(2,1)S(1)}, bf16[128,8]{0,1:T(8,128)(2,1)}, u32[]{:S(2)}) copy-start(bf16[128,8]{0,1:T(8,128)(2,1)} %param.22) | copy-start | bytes 6148
  25.3 10.0 %all-to-all-start.1 = ((bf16[32,8,128]{2,1,0:T(8,128)(2,1)}), bf16[32,8,128]{2,1,0:T(8,128)(2,1)S(1)}, u32[]{:S(2)}, u32[]{:S(2)}) async-start(bf16[32,8,128]{2,1,0:T(8,128)(2,1)} %bitcast.10), calls=%async_computation.1 | async-start | bytes 131072 | tf_op jit(solution)/shard_map/all_to_all | solution.py:601
  27.9 14.8 %collective-permute-start.7 = (bf16[4,64,128]{2,1,0:T(8,128)(2,1)S(1)}, bf16[4,64,128]{2,1,0:T(8,128)(2,1)S(1)}, u32[]{:S(2)}, u32[]{:S(2)}) collective-permute-start(bf16[4,64,128]{2,1,0:T(8,128)(2,1)S(1)} %get-tuple-element.38), channel_id=1, source_target_pairs={{0,1},{1,0},{2,3},{3,2},{4,5},{5,4},{6,7},{7,6},{8,9},{9,8},{10,11... | collective-permute-start | bytes 196616 | tf_op jit(solution)/shard_map/ppermute | solution.py:567
  36.7 10.3 %all-to-all-start.2 = ((bf16[32,8,128]{2,1,0:T(8,128)(2,1)}), bf16[32,8,128]{2,1,0:T(8,128)(2,1)S(1)}, u32[]{:S(2)}, u32[]{:S(2)}) async-start(bf16[32,8,128]{2,1,0:T(8,128)(2,1)} %get-tuple-element.36), calls=%async_computation.2 | async-start | bytes 131072 | tf_op jit(solution)/shard_map/all_to_all | solution.py:614
  40.8 2.0 %collective-permute-start.4 = (bf16[128,128]{1,0:T(8,128)(2,1)S(1)}, bf16[128,128]{1,0:T(8,128)(2,1)S(1)}, u32[]{:S(2)}, u32[]{:S(2)}) collective-permute-start(bf16[128,128]{1,0:T(8,128)(2,1)S(1)} %get-tuple-element.32), channel_id=1, source_target_pairs={{0,1},{1,0},{2,3},{3,2},{4,5},{5,4},{6,7},{7,6},{8,9},{9,8},{10,11... | collective-permute-start | bytes 98312 | tf_op jit(solution)/shard_map/ppermute | solution.py:548
  40.9 4.0 %collective-permute-start.5 = (bf16[128,128]{1,0:T(8,128)(2,1)S(1)}, bf16[128,128]{1,0:T(8,128)(2,1)S(1)}, u32[]{:S(2)}, u32[]{:S(2)}) collective-permute-start(bf16[128,128]{1,0:T(8,128)(2,1)S(1)} %get-tuple-element.33), channel_id=1, source_target_pairs={{0,2},{1,3},{2,0},{3,1},{4,6},{5,7},{6,4},{7,5},{8,10},{9,11},{10,... | collective-permute-start | bytes 98312 | tf_op jit(solution)/shard_map/ppermute | solution.py:548
  42.6 3.5 %collective-permute-start.6 = (bf16[128,128]{1,0:T(8,128)(2,1)S(1)}, bf16[128,128]{1,0:T(8,128)(2,1)S(1)}, u32[]{:S(2)}, u32[]{:S(2)}) collective-permute-start(bf16[128,128]{1,0:T(8,128)(2,1)S(1)} %get-tuple-element.34), channel_id=1, source_target_pairs={{0,3},{1,2},{2,1},{3,0},{4,7},{5,6},{6,5},{7,4},{8,11},{9,10},{10,... | collective-permute-start | bytes 98312 | tf_op jit(solution)/shard_map/ppermute | solution.py:548
  42.8 4.3 %copy-start.1 = (bf16[4,128,128]{2,1,0:T(8,128)(2,1)}, bf16[4,128,128]{2,1,0:T(8,128)(2,1)S(1)}, u32[]{:S(2)}) copy-start(bf16[4,128,128]{2,1,0:T(8,128)(2,1)S(1)} %maximum_select_fusion.1.pair_ref) | copy-start | bytes 393220

commit v6 on v5

--- a/solution.py
+++ b/solution.py
@@ -223,7 +223,6 @@
 
 
 LANES = 128
-STRIDE = 40
 GROUP = 4
 f32 = jnp.float32
 bf16 = jnp.bfloat16
@@ -245,10 +244,35 @@
     return lax.broadcasted_iota(jnp.int32, (rows, LANES), 1)
 
 
-def factors_kernel(seq_ref, res_ref, rows_ref, left_ref, right_ref, send_ref, normed_ref, left_scr):
-    seqs = send_ref.shape[2] // 18
+def swap_groups(parts):
+    lane = lane_index(parts[0].shape[0])
+    low, even = lane < 64, lane % 64 < 32
+    parts = [
+        jnp.where(low, parts[0], pltpu.roll(parts[2], 64, 1)),
+        jnp.where(low, parts[1], pltpu.roll(parts[3], 64, 1)),
+        jnp.where(low, pltpu.roll(parts[0], 64, 1), parts[2]),
+        jnp.where(low, pltpu.roll(parts[1], 64, 1), parts[3]),
+    ]
+    return [
+        jnp.where(even, parts[0], pltpu.roll(parts[1], 32, 1)),
+        jnp.where(even, pltpu.roll(parts[0], 96, 1), parts[1]),
+        jnp.where(even, parts[2], pltpu.roll(parts[3], 32, 1)),
+        jnp.where(even, pltpu.roll(parts[2], 96, 1), parts[3]),
+    ]
+
+
+def factors_kernel(
+    seq_smem_ref, res_smem_ref, seq_ref, res_ref, bias_w_ref, rows_ref, left_ref, right_ref, pair_ref,
+    send_ref, aux_ref, normed_ref, *refs
+):
+    pair_refs, left_scr = refs[:GROUP], refs[GROUP]
+    columns_each = pair_refs[0].shape[1]
+    for step in range(GROUP):
+        first = pl.multiple_of(partner(step) * columns_each, columns_each)
+        pair_refs[step][...] = pair_ref[:, pl.ds(first, columns_each), :]
+    lines = send_ref.shape[0]
+    seqs = send_ref.shape[2] // 12
     residues = res_ref.shape[1]
-    chips = send_ref.shape[0]
     me = lax.axis_index("row")
     normed = layer_normalize(rows_ref[...]).astype(bf16)
     normed_ref[...] = normed
@@ -256,30 +280,30 @@
     live_rows = jnp.broadcast_to(live, (residues, residues)).T
     right_t = right_ref[...]
     left_wide = jnp.concatenate([left_ref[...]] * 4, axis=0)
-    low = lane_index(16) < 64
-    lane_group = lane_index(chips) // 32
-    halves = ([], [])
+    lane_group = lane_index(lines) // 32
+    quarters = []
     tail = []
     for s in range(seqs):
-        seq_live = seq_ref[me * seqs + s].astype(f32)
+        seq_live = seq_smem_ref[me * seqs + s].astype(f32)
         own = normed[s * residues : (s + 1) * residues]
         factor = dot_nt(right_t, own) * (live * seq_live)
-        first, second = factor[:16], factor[16:]
-        halves[0].append(jnp.where(low, first, pltpu.roll(second, 64, 1)))
-        halves[1].append(jnp.where(low, pltpu.roll(first, 64, 1), second))
+        quarters.append(swap_groups([factor[a * 8 : (a + 1) * 8] for a in range(4)]))
         left_scr[...] = dot_nt(own, left_wide) * (live_rows * seq_live)
-        for a in range(2):
-            row = jnp.zeros((chips, LANES), f32)
+        for a in range(4):
+            row = jnp.zeros((lines, LANES), f32)
             for b in range(4):
-                part = left_scr[pl.ds(4 * a + b, chips, stride=8), :]
+                part = left_scr[pl.ds(4 * a + b, lines, stride=4 * GROUP), :]
                 row = jnp.where(lane_group == b, part, row)
             tail.append(row)
     tail = jnp.stack(tail, axis=1).astype(bf16)
-    right_rows = 16 * seqs
-    for core in range(2):
-        block = jnp.concatenate(halves[core], axis=0).astype(bf16)
-        send_ref[:, core, :right_rows, :] = jnp.broadcast_to(block[None], (chips, right_rows, LANES))
-        send_ref[:, core, right_rows:, :] = tail
+    right_rows = 8 * seqs
+    for t in range(GROUP):
+        block = jnp.concatenate([own[t] for own in quarters], axis=0).astype(bf16)
+        send_ref[:, t, :right_rows, :] = jnp.broadcast_to(block[None], (lines, right_rows, LANES))
+        send_ref[:, t, right_rows:, :] = tail
+    aux_ref[0:4] = tile_divisor(res_smem_ref, res_ref, seq_ref)
+    aux_ref[4:8] = jnp.broadcast_to((live - 1.0) * mask_fill, (4, LANES))
+    aux_ref[8:16] = bias_w_ref[...].astype(f32)
 
 
 def side_by_side(first, second, at):
@@ -295,17 +319,39 @@
     return lax.bitwise_xor(lax.rem(lax.axis_index("row"), GROUP), step)
 
 
-def projections_kernel(
-    normed_ref, cot_ref, wq_ref, wk_ref, wv_ref, wg_ref, wo_ref, gate_ref, *rest
-):
+def tile_divisor(res_smem_ref, res_ref, seq_ref):
+    own = partner(0)
+    rows = lax.div(lax.axis_index("row"), GROUP) * 16
+    lane = lane_index(1)
+    live = res_ref[...].astype(f32)
+    columns = jnp.zeros((1, LANES), f32)
+    for t in range(GROUP):
+        turned = live if t == 0 else pltpu.roll(live, LANES - 32 * t, 1)
+        columns = jnp.where(own == t, turned, columns)
+    columns = jnp.where(lane < 32, columns, 0.0)
+    columns = columns + pltpu.roll(columns, 32, 1)
+    columns = columns + pltpu.roll(columns, 64, 1)
+    total = jnp.sum(seq_ref[...].astype(f32), axis=-1, keepdims=True)
+    lines = []
+    for b in range(4):
+        line = jnp.zeros((1, LANES), f32)
+        for a in range(4):
+            line = jnp.where(lane // 32 == a, res_smem_ref[rows + 4 * a + b].astype(f32), line)
+        lines.append(jnp.maximum(total * line * columns, 1.0))
+    return jnp.concatenate(lines, axis=0)
+
+
+def projections_kernel(normed_ref, cot_ref, weights_ref, wo_ref, gate_ref, *rest):
     block_refs, every = rest[:GROUP], rest[GROUP]
+    normed = normed_ref[...]
+    tokens = normed.shape[0]
     residues = gate_ref.shape[1]
-    seqs = normed_ref.shape[0] // residues
-    normed = normed_ref[...]
-    queries = dot_nn(normed, wq_ref[...])
-    keys = dot_nn(normed, wk_ref[...])
-    values = dot_nn(normed, wv_ref[...])
-    gate = jax.nn.sigmoid(dot_nn(normed, wg_ref[...]))
+    seqs = tokens // residues
+    channels = normed.shape[1]
+    queries, keys, values, gate = [
+        dot_nn(normed, weights_ref[:, at * channels : (at + 1) * channels]) for at in range(4)
+    ]
+    gate = jax.nn.sigmoid(gate)
     d_attended = dot_nt(cot_ref[...], wo_ref[...]) * gate
     for t in range(GROUP):
         rows = side_by_side(queries, d_attended, t).astype(bf16)
@@ -319,7 +365,7 @@
 
 
 def products_kernel(scale, *refs):
-    block_refs, score_ref, flow_ref = refs[:GROUP], refs[GROUP], refs[GROUP + 1]
+    block_refs, (score_ref, flow_ref, value_ref) = refs[:GROUP], refs[GROUP:]
     rows = score_ref.shape[1]
     residues = score_ref.shape[2]
     part_of = lane_index(residues) // 32
@@ -332,102 +378,103 @@
             both = dot_nt(wide, block[seqs + s])
             score_ref[step * seqs + s] = both[:rows] * scale
             flow_ref[step * seqs + s] = both[rows:]
-
-
-def pair_kernel(recv_ref, weight_ref, pair_ref, div_ref, bias_w_ref, send_ref, updated_ref, flat, rbuf, lbuf, obuf):
+            value_ref[step * seqs + s] = jnp.where(part_of < 2, jnp.ones((), bf16), block[seqs + s])
+
+
+def pair_kernel(recv_ref, weight_ref, aux_ref, *refs):
+    pair_refs, send_ref, updated_refs = refs[:GROUP], refs[GROUP], refs[GROUP + 1 : 2 * GROUP + 1]
+    flat, rbuf, lbuf, obuf, state, after = refs[2 * GROUP + 1 :]
     peers, block_rows, _ = recv_ref.shape
-    seqs = block_rows // 18
-    for p in range(peers):
-        flat[p * STRIDE : p * STRIDE + block_rows, :] = recv_ref[p].astype(f32)
+    seqs = block_rows // 12
+    for step in range(GROUP):
+        state[partner(step)] = pair_refs[step][...]
+    flat[...] = recv_ref[...].astype(f32).reshape(flat.shape)
     for s in range(seqs):
-        for g in range(16):
-            part = flat[pl.ds(s * 16 + g, peers, stride=STRIDE), :]
+        for g in range(8):
+            part = flat[pl.ds(s * 8 + g, peers, stride=block_rows), :]
             rbuf[s * peers : (s + 1) * peers, g * LANES : (g + 1) * LANES] = part.astype(bf16)
-        for a in range(2):
-            part = flat[pl.ds(16 * seqs + 2 * s + a, peers, stride=STRIDE), :]
-            lbuf[s * peers : (s + 1) * peers, a * LANES : (a + 1) * LANES] = part.astype(bf16)
-    left_t = lbuf[...].astype(f32).T.astype(bf16)
-    for g in range(16):
-        outer = dot_nn(left_t, rbuf[:, g * LANES : (g + 1) * LANES]).astype(bf16)
-        for i in range(8):
-            obuf[g * 32 : (g + 1) * 32, i * LANES : (i + 1) * LANES] = outer[i * 32 : (i + 1) * 32]
+        for a in range(4):
+            part = flat[pl.ds(8 * seqs + 4 * s + a, peers, stride=block_rows), :]
+            lbuf[s * peers : (s + 1) * peers, a * LANES : (a + 1) * LANES] = part
+    left_t = lbuf[...].T.astype(bf16)
+    for g in range(8):
+        outer = dot_nn(left_t, rbuf[:, g * LANES : (g + 1) * LANES])
+        for b in range(4):
+            turned = swap_groups([outer[(4 * a + b) * 32 : (4 * a + b + 1) * 32] for a in range(4)])
+            for a in range(4):
+                obuf[(g * 4 + a) * 32 : (g * 4 + a + 1) * 32, b * LANES : (b + 1) * LANES] = turned[a].astype(bf16)
     sums = dot_nn(weight_ref[...], obuf[...])
-    low = lane_index(LANES) < 64
-
-    def piece(a, i):
-        return sums[a * LANES : (a + 1) * LANES, i * LANES : (i + 1) * LANES]
-
+    bias_w = aux_ref[8:16].astype(bf16)
     blocks = []
-    bias_w = bias_w_ref[...]
     for b in range(4):
-        straight = jnp.where(low, piece(0, b), piece(1, b + 4))
-        crossed = jnp.where(low, piece(0, b + 4), piece(1, b))
-        update = (straight + pltpu.roll(crossed, 64, 1)) / div_ref[b : b + 1, :]
-        state = jnp.concatenate([pair_ref[b], pair_ref[b + 4]], axis=0).astype(f32)
-        updated = (state + update.T).astype(bf16)
-        updated_ref[b] = updated[:64]
-        updated_ref[b + 4] = updated[64:]
-        pair_normed = layer_normalize(updated).astype(bf16)
-        blocks.append(dot_nt(bias_w, pair_normed))
+        update = sums[:, b * LANES : (b + 1) * LANES] / aux_ref[b : b + 1, :]
+        before = jnp.concatenate([state[a, b] for a in range(GROUP)], axis=0).astype(f32)
+        updated = (before + update.T).astype(bf16)
+        for a in range(GROUP):
+            after[a, b] = updated[a * 32 : (a + 1) * 32]
+        blocks.append(dot_nt(bias_w, layer_normalize(updated).astype(bf16)))
     lines, _, share, _ = send_ref.shape
     heads = share // 4
     for t in range(GROUP):
         block = jnp.concatenate([rows[t * heads : (t + 1) * heads] for rows in blocks], axis=0).astype(bf16)
         send_ref[:, t] = jnp.broadcast_to(block[None], (lines, share, LANES))
-
-
-def placed_bias(flat, res_ref, heads, h):
-    residues = res_ref.shape[1]
-    sub = lax.broadcasted_iota(jnp.int32, (residues, LANES), 0) % 8
-    keep = (sub < 4) == (lane_index(residues) < 64)
-    raw = flat[pl.ds(h, residues, stride=heads), :]
-    moved = jnp.where(sub < 4, pltpu.roll(raw, residues - 4, 0), pltpu.roll(raw, 4, 0))
-    key_mask = (res_ref[...].astype(f32) - 1.0) * mask_fill
-    return jnp.where(keep, raw, pltpu.roll(moved, 64, 1)) + key_mask
-
-
-def bias_gradient_kernel(bias_ref, res_ref, score_ref, flow_ref, send_ref, full_ref, flat, grads):
+    for step in range(GROUP):
+        updated_refs[step][...] = after[partner(step)]
+
+
+def placed_bias(flat, mask_ref, heads, h):
+    residues = mask_ref.shape[1]
+    row = lax.broadcasted_iota(jnp.int32, (residues, LANES), 0)
+    lane = lane_index(residues)
+    bias = flat[pl.ds(h, residues, stride=heads), :]
+    for rows, lanes in ((8, 64), (4, 32)):
+        first = row % (2 * rows) < rows
+        low = lane % (2 * lanes) < lanes
+        moved = jnp.where(first, pltpu.roll(bias, residues - rows, 0), pltpu.roll(bias, rows, 0))
+        moved = jnp.where(low, pltpu.roll(moved, LANES - lanes, 1), pltpu.roll(moved, lanes, 1))
+        bias = jnp.where(first == low, bias, moved)
+    return bias + mask_ref[4:5, :]
+
+
+def bias_gradient_kernel(bias_ref, mask_ref, score_ref, flow_ref, *refs):
+    part_refs, (pair_ref, send_ref, weights_ref, flat, grads) = refs[:GROUP], refs[GROUP:]
+    columns_each = part_refs[0].shape[1]
+    for step in range(GROUP):
+        first = pl.multiple_of(partner(step) * columns_each, columns_each)
+        pair_ref[:, pl.ds(first, columns_each), :] = part_refs[step][...]
     seqs, rows, residues = score_ref.shape
     heads = rows // residues
     flat[...] = bias_ref[...].reshape(flat.shape).astype(f32)
     ones = jnp.ones((residues, LANES), bf16)
     for h in range(heads):
         at = slice(h * residues, (h + 1) * residues)
-        bias = placed_bias(flat, res_ref, heads, h)
-        full_ref[at, :] = bias
+        bias = placed_bias(flat, mask_ref, heads, h)
         total = jnp.zeros((residues, residues), f32)
         for s in range(seqs):
             scores = score_ref[s, at, :] + bias
             weights = jnp.exp(scores - jnp.max(scores, axis=-1, keepdims=True))
+            rounded = weights.astype(bf16)
+            weights_ref[s, at, :] = rounded
             flow = flow_ref[s, at, :]
-            inverse = 1.0 / dot_nn(weights.astype(bf16), ones)
+            inverse = 1.0 / dot_nn(rounded, ones)
             delta = dot_nn((weights * flow).astype(bf16), ones) * inverse
             total = total + weights * inverse * (flow - delta)
         grads[pl.ds(h, residues, stride=heads), :] = total
     send_ref[...] = grads[...].astype(bf16).reshape(send_ref.shape)
 
 
-def attended_kernel(score_ref, full_ref, *refs):
-    block_refs, out_refs = refs[:GROUP], refs[GROUP:]
-    _, rows, residues = score_ref.shape
-    heads = rows // residues
-    seqs = block_refs[0].shape[0] // 2
-    part_of = lane_index(residues) // 32
+def attended_kernel(weights_ref, value_ref, *out_refs):
+    sequences, _, residues = weights_ref.shape
+    seqs = sequences // GROUP
+    lane = lane_index(residues)
     for step in range(GROUP):
         attended = []
         for s in range(seqs):
-            own = jnp.zeros((residues, LANES), f32)
-            for h in range(heads):
-                at = slice(h * residues, (h + 1) * residues)
-                scores = score_ref[step * seqs + s, at, :] + full_ref[at, :]
-                weights = jnp.exp(scores - jnp.max(scores, axis=-1, keepdims=True))
-                total = jnp.sum(weights, axis=-1, keepdims=True)
-                mixed = dot_nn(weights.astype(bf16), block_refs[step][seqs + s]) / total
-                own = jnp.where(part_of == heads + h, mixed, own)
-            attended.append(own)
-        out_refs[step][...] = jnp.where(
-            part_of < heads, pltpu.roll(attended[0], 64, 1), attended[1]
-        ).astype(bf16)
+            mixed = dot_nn(weights_ref[step * seqs + s], value_ref[step * seqs + s])
+            picked = jnp.where(lane < 96, mixed[:residues], mixed[residues:])
+            totals = jnp.where(lane < 32, mixed[:residues], mixed[residues:])
+            attended.append(picked / pltpu.roll(totals, 64, 1))
+        out_refs[step][...] = jnp.where(lane < 64, pltpu.roll(attended[0], 64, 1), attended[1]).astype(bf16)
 
 
 def output_kernel(gate_ref, wo_ref, *refs):
@@ -447,12 +494,12 @@
         out_ref[s * residues : (s + 1) * residues, :] = sums[s].astype(bf16)
 
 
-def gradient_kernel(shares_ref, bias_w_ref, pair_ref, out_ref):
+def gradient_kernel(shares_ref, aux_ref, pair_ref, out_ref):
     peers, share, _ = shares_ref.shape
     total = jnp.sum(shares_ref[...].astype(f32).reshape(peers // GROUP, GROUP, share, LANES), axis=0)
     rows = pair_ref.shape[0]
     heads = share // rows
-    bias_w = bias_w_ref[...].astype(f32)
+    bias_w = aux_ref[8:16]
     for i in range(rows):
         own = jnp.concatenate([total[t, i * heads : (i + 1) * heads] for t in range(GROUP)], axis=0)
         upstream = lax.dot_general(
@@ -461,7 +508,7 @@
         out_ref[i] = norm_backward(pair_ref[i], upstream)
 
 
-def kernel_call(body, out_shape, in_specs=None, scratch=(), flops=0, moved=0, vmem_mib=24):
+def kernel_call(body, out_shape, in_specs=None, scratch=(), flops=0, moved=0, vmem_mib=12):
     vmem = pl.BlockSpec(memory_space=pltpu.VMEM)
     many = isinstance(out_shape, (list, tuple))
     return pl.pallas_call(
@@ -496,28 +543,39 @@
     head_count = bias_weight.shape[1]
     peers = lax.axis_size("row")
     factor = left_weight.shape[1]
-    chips = peers // 2
+    lines = peers // GROUP
     vmem = pl.BlockSpec(memory_space=pltpu.VMEM)
     smem = pl.BlockSpec(memory_space=pltpu.SMEM)
-    me = lax.axis_index("row")
-    core = me % 2
-    sibling = [(i, i ^ 1) for i in range(peers)]
     token_rows = sequence_wise * residues
-    half = residues // 2
-    block_rows = sequence_wise * 18
-    res_row = residue_mask.reshape(1, residues)
+    columns_each = residues // GROUP
+    block_rows = sequence_wise * 12
     flat_rows = alignment_rows.reshape(token_rows, channel_count)
     shape = jax.ShapeDtypeStruct
 
-    send, normed = kernel_call(
+    send, aux, normed, *pair_blocks = kernel_call(
         factors_kernel,
-        [shape((chips, 2, block_rows, LANES), bf16), shape((token_rows, channel_count), bf16)],
-        [smem, vmem, vmem, vmem, vmem],
+        [
+            shape((lines, GROUP, block_rows, LANES), bf16),
+            shape((16, LANES), f32),
+            shape((token_rows, channel_count), bf16),
+        ]
+        + [shape((rows_here, columns_each, pair_channels), bf16)] * GROUP,
+        [smem] * 2 + [vmem] * 7,
         [pltpu.VMEM((residues, LANES), f32)],
         flops=2 * token_rows * channel_count * LANES,
-        moved=1 << 19,
+        moved=1 << 20,
         vmem_mib=60,
-    )(sequence_mask, res_row, flat_rows, left_weight.T, right_weight.T)
+    )(
+        sequence_mask,
+        residue_mask,
+        sequence_mask.reshape(1, -1),
+        residue_mask.reshape(1, -1),
+        bias_weight.T,
+        flat_rows,
+        left_weight.T,
+        right_weight.T,
+        pair_state,
+    )
     received = lax.all_to_all(
         send.reshape(peers, block_rows, LANES), "row", split_axis=0, concat_axis=0, tiled=True
     )
@@ -525,21 +583,19 @@
     group_heads = head_count // GROUP
     head_rows = group_heads * residues
     scale = (channel_count // head_count) ** (-0.5)
+    normed, *weights = lax.optimization_barrier((normed, query_weight, key_weight, value_weight, gate_weight))
     gate, *blocks = kernel_call(
         projections_kernel,
         [shape((GROUP, residues, LANES), f32)]
         + [shape((2 * sequence_wise, residues, LANES), bf16)] * GROUP,
-        [vmem] * 7,
+        [vmem] * 4,
         [pltpu.VMEM((GROUP, 2 * sequence_wise, residues, LANES), bf16)],
         flops=10 * token_rows * channel_count * channel_count,
         moved=1 << 21,
     )(
         normed,
         update_cotangent.reshape(token_rows, channel_count),
-        query_weight,
-        key_weight,
-        value_weight,
-        gate_weight,
+        jnp.concatenate(weights, axis=1),
         output_weight,
     )
 
@@ -548,77 +604,64 @@
             lax.ppermute(parts[d], "row", [(i, i ^ d) for i in range(peers)]) for d in range(1, GROUP)
         ]
 
+    pair_blocks = trade(pair_blocks)
     blocks = trade(blocks)
-    scores, flow = kernel_call(
+    scores, flow, values = kernel_call(
         lambda *refs: products_kernel(scale, *refs),
-        [shape((GROUP * sequence_wise, head_rows, residues), f32)] * 2,
+        [shape((GROUP * sequence_wise, head_rows, residues), f32)] * 2
+        + [shape((GROUP * sequence_wise, residues, LANES), bf16)],
         [vmem] * GROUP,
         flops=1 << 28,
         moved=1 << 21,
     )(*blocks)
 
-    def trade_columns(tile):
-        kept = lax.dynamic_slice_in_dim(tile, core * half, half, 1)
-        got = lax.ppermute(lax.dynamic_slice_in_dim(tile, (1 - core) * half, half, 1), "row", sibling)
-        return jnp.where(core == 0, jnp.concatenate([kept, got]), jnp.concatenate([got, kept]))
-
-    def trade_rows(tile):
-        kept = lax.dynamic_slice_in_dim(tile, core * rows_here, rows_here, 0)
-        got = lax.ppermute(
-            lax.dynamic_slice_in_dim(tile, (1 - core) * rows_here, rows_here, 0), "row", sibling
-        )
-        return jnp.where(
-            core == 0, jnp.concatenate([kept, got], axis=1), jnp.concatenate([got, kept], axis=1)
-        )
-
-    pair_tile = trade_columns(pair_state)
     weight_t = (
-        outer_weight.reshape(factor, 2, 16, pair_channels)
-        .transpose(1, 3, 2, 0)
-        .reshape(2 * pair_channels, 16 * factor)
-    )
-    seq_live = sequence_mask.astype(f32)
-    res_live = residue_mask.astype(f32)
-    tile_rows = lax.dynamic_slice_in_dim(res_live, (me // 2) * 8, 8).reshape(2, 4)
-    tile_cols = lax.dynamic_slice_in_dim(res_live, core * half, half)
-    divisor = jnp.maximum(
-        jnp.sum(seq_live) * tile_rows.T[:, :, None] * tile_cols[None, None, :], 1.0
-    ).reshape(4, 2 * half)
+        outer_weight.reshape(factor, 4, 8, pair_channels)
+        .transpose(3, 2, 1, 0)
+        .reshape(pair_channels, 32 * factor)
+    )
     share_rows = 4 * group_heads
-    send_bias, updated_tile = kernel_call(
+    part_shape = shape((rows_here, columns_each, pair_channels), bf16)
+    send_bias, *updated = kernel_call(
         pair_kernel,
-        [shape((peers // GROUP, GROUP, share_rows, LANES), bf16), shape((8, half, pair_channels), bf16)],
-        [vmem] * 5,
+        [shape((lines, GROUP, share_rows, LANES), bf16)] + [part_shape] * GROUP,
+        [vmem] * (3 + GROUP),
         [
-            pltpu.VMEM((peers * STRIDE, LANES), f32),
-            pltpu.VMEM((peers * sequence_wise, 16 * LANES), bf16),
-            pltpu.VMEM((peers * sequence_wise, 2 * LANES), bf16),
-            pltpu.VMEM((16 * factor, 8 * LANES), bf16),
+            pltpu.VMEM((peers * block_rows, LANES), f32),
+            pltpu.VMEM((peers * sequence_wise, 8 * LANES), bf16),
+            pltpu.VMEM((peers * sequence_wise, 4 * LANES), f32),
+            pltpu.VMEM((32 * factor, 4 * LANES), bf16),
+            pltpu.VMEM((GROUP, rows_here, columns_each, pair_channels), bf16),
+            pltpu.VMEM((GROUP, rows_here, columns_each, pair_channels), bf16),
         ],
-        flops=1 << 29,
+        flops=1 << 28,
         moved=1 << 20,
-    )(received, weight_t, pair_tile, divisor, bias_weight.T)
+    )(received, weight_t, aux, *pair_blocks)
     bias_all = lax.all_to_all(
         send_bias.reshape(peers, share_rows, LANES), "row", split_axis=0, concat_axis=0, tiled=True
     )
-    pair_updated = trade_rows(updated_tile)
-
-    send_grad, full_bias = kernel_call(
+    updated = trade(updated)
+
+    pair_updated, send_grad, weights = kernel_call(
         bias_gradient_kernel,
-        [shape((peers, rows_here * group_heads, LANES), bf16), shape((head_rows, residues), f32)],
-        [vmem] * 4,
+        [
+            shape((rows_here, residues, pair_channels), bf16),
+            shape((peers, rows_here * group_heads, LANES), bf16),
+            shape((GROUP * sequence_wise, head_rows, residues), bf16),
+        ],
+        [vmem] * (4 + GROUP),
         [pltpu.VMEM((head_rows, LANES), f32), pltpu.VMEM((head_rows, LANES), f32)],
         flops=1 << 28,
         moved=1 << 22,
-    )(bias_all, res_row, scores, flow)
+    )(bias_all, aux, scores, flow, *updated)
     shares = lax.all_to_all(send_grad, "row", split_axis=0, concat_axis=0, tiled=True)
     attended = kernel_call(
         attended_kernel,
         [shape((residues, LANES), bf16)] * GROUP,
-        [vmem] * (2 + GROUP),
+        [vmem] * 2,
         flops=1 << 28,
         moved=1 << 21,
-    )(scores, full_bias, *blocks)
+    )(weights, values)
     update = kernel_call(
         output_kernel,
         shape((token_rows, channel_count), bf16),
@@ -632,7 +675,7 @@
         [vmem] * 3,
         flops=1 << 24,
         moved=1 << 20,
-    )(shares, bias_weight.T, pair_updated)
+    )(shares, aux, pair_updated)
     return (update.reshape(alignment_rows.shape), pair_updated, pair_gradient)
 
 

time: 48.9 us -> 46.2 us (0.945)
  starting transfers between devices: 16.8 us -> 22 us
  waiting for transfers between devices: 14.9 us -> 11 us
  local copies, waits for them, and re-layouts: 4.09 us -> 1.94 us
  other arithmetic: 1.38 us -> 0.06 us
  Pallas kernels: 10.5 us -> 10 us
    all_to_all x1, waiting for transfers between devices: 6.75 us -> 1.87 us  [on_device_paired(): lax.all_to_all(send_bias.reshape(peers, share_rows, LANES), 'row', split_...]
    ppermute x6 -> x12, starting transfers between devices: 3.97 us -> 8.2 us  [trade(): lax.ppermute(parts[d], 'row', [(i, i ^ d) for i in range(peers)])]
    ppermute x6 -> x12, waiting for transfers between devices: 3.35 us -> 5.95 us  [trade(): lax.ppermute(parts[d], 'row', [(i, i ^ d) for i in range(peers)])]
    all_to_all x1, waiting for transfers between devices: 4.83 us -> 2.78 us  [on_device_paired(): lax.all_to_all(send.reshape(peers, block_rows, LANES), 'row', split_axis=...]
    all_to_all x1, starting transfers between devices: 2.57 us -> 3.59 us  [on_device_paired(): lax.all_to_all(send_bias.reshape(peers, share_rows, LANES), 'row', split_...]
    pallas_call x1, Pallas kernels: 1.43 us -> 0.44 us  [on_device_paired(): kernel_call(attended_kernel, [shape((residues, LANES), bf16)] * GROUP, [v...]
    dynamic_slice x3 -> x0, local copies, waits for them, and re-layouts: 0.99 us -> none  [the longest x1 0.89 us: trade_columns(): kept = lax.dynamic_slice_in_dim(tile, core * half, half, 1)]
    mul x1 -> x0, other arithmetic: 0.72 us -> none  [on_device_paired(): jnp.sum(seq_live) * tile_rows.T[:, :, None] * tile_cols[None, None, :]]
  transfers between devices with their start and end apart: 11 -> 15, of which waited for: 4 -> 7; matrix products, arithmetic and copies ran while one was open for 5% -> 1% of each run, Pallas kernels for 19% -> 10%
where the time goes in v6:
time: 46.2 us; the launch traced here: 45.9 us
  starting transfers between devices  22 us (48%)
  waiting for transfers between devices  11 us (24%)
  Pallas kernels  10 us (22%)
  local copies, waits for them, and re-layouts  1.94 us (4%)
  between operations  0.85 us (2%)
    ppermute x12, starting transfers between devices, trade(): lax.ppermute(parts[d], 'row', [(i, i ^ d) for i in range(peers)])  8.2 us
    all_to_all x1, starting transfers between devices, on_device_paired(): lax.all_to_all(send.reshape(peers, block_rows, LANES), 'row', split_axis=...  7.3 us
    ppermute x12, waiting for transfers between devices, trade(): lax.ppermute(parts[d], 'row', [(i, i ^ d) for i in range(peers)])  5.95 us
    all_to_all x1, starting transfers between devices, on_device_paired(): lax.all_to_all(send_bias.reshape(peers, share_rows, LANES), 'row', split_...  3.59 us
    all_to_all x1, starting transfers between devices, on_device_paired(): lax.all_to_all(send_grad, 'row', split_axis=0, concat_axis=0, tiled=True)  2.91 us
    all_to_all x1, waiting for transfers between devices, on_device_paired(): lax.all_to_all(send.reshape(peers, block_rows, LANES), 'row', split_axis=...  2.78 us
    pallas_call x1, Pallas kernels, on_device_paired(): kernel_call(factors_kernel, [shape((lines, GROUP, block_rows, LANES), bf1...  2.39 us
    pallas_call x1, Pallas kernels, on_device_paired(): kernel_call(pair_kernel, [shape((lines, GROUP, share_rows, LANES), bf16)]...  2.24 us
  transfers between devices with their start and end apart: 15, of which 7 were waited for; matrix products, arithmetic and copies ran while one was open for 1% of the time, Pallas kernels for 10%

profile of v6, /device:TPU:0, one launch (start us, length us, event | category | flops | bytes accessed | tf_op | source)
XLA Modules:
  0.0 45.9 jit_solution(14717163146788584460)
XLA Ops:
  0.6 0.0 copy-start.12
  0.6 2.4 %shard_map.157 = (bf16[8,4,24,128]{3,2,1,0:T(8,128)(2,1)}, f32[16,128]{1,0:T(8,128)}, bf16[256,256]{1,0:T(8,128)(2,1)}, bf16[4,32,128]{2,1,0:T(8,128)(2,1)}, bf1...) custom-call(s32[64]{0:T(128)} %seq_smem_ref.1, s32[128]{0:T(128)} %res_smem_ref.1, ...), custom_call_target="tpu_custom_call" | custom-call | flops 16777216 | bytes 1048576 | tf_op jit(solution)/shard_map/pallas_call | solution.py:555
  3.0 0.0 copy-start.9
  3.0 0.0 copy-start.10
  3.1 0.0 copy-start.11
  3.1 7.3 %all-to-all-start = ((bf16[32,24,128]{2,1,0:T(8,128)(2,1)}), bf16[32,24,128]{2,1,0:T(8,128)(2,1)S(1)}, u32[]{:S(2)}, u32[]{:S(2)}) async-start(bf16[32,24,128]{2,1,0:T(8,128)(2,1)} %bitcast.17), calls=%async_computation | async-start | bytes 393216 | tf_op jit(solution)/shard_map/all_to_all | solution.py:579
  10.4 0.3 collective-permute-start
  10.7 1.7 %collective-permute-start.1 = (bf16[4,32,128]{2,1,0:T(8,128)(2,1)}, bf16[4,32,128]{2,1,0:T(8,128)(2,1)S(1)}, u32[]{:S(2)}, u32[]{:S(2)}) collective-permute-start(bf16[4,32,128]{2,1,0:T(8,128)(2,1)} %get-tuple-element.46), channel_id=1, source_target_pairs={{0,2},{1,3},{2,0},{3,1},{4,6},{5,7},{6,4},{7,5},{8,10},{9,11},{10,... | collective-permute-start | bytes 98312 | tf_op jit(solution)/shard_map/ppermute | solution.py:604
  12.4 0.0 collective-permute-start.2
  12.4 0.0 copy-done.12
  12.4 0.0 copy-done.9
  12.4 0.0 copy-done.10
  12.4 0.0 copy-done.11
  12.4 0.0 copy-start
  12.4 0.0 copy-start.1
  12.4 0.0 copy-start.3
  12.4 0.1 pad_maximum_fusion.weights_ref
  12.5 0.8 %copy-done = bf16[256,256]{1,0:T(8,128)(2,1)S(1)} copy-done((bf16[256,256]{1,0:T(8,128)(2,1)S(1)}, bf16[256,256]{1,0:T(8,128)(2,1)}, u32[]{:S(2)}) %copy-start) | copy-done | bytes 131096
  13.3 0.1 copy-done.1
  13.4 0.1 copy-done.3
  13.5 0.5 %shard_map.158 = (f32[4,128,128]{2,1,0:T(8,128)S(1)}, bf16[4,128,128]{2,1,0:T(8,128)(2,1)S(1)}, bf16[4,128,128]{2,1,0:T(8,128)(2,1)S(1)}, bf16[4,128,128]{2,1,0:T(8,128)(2,1)S(1)}, bf16[4,128,128]{2,1,0:T(8,128)(2,1)S(1)}) custom-call(bf16[256,256]{1,0:T(8,128)(2,1)S(1)} %copy-done.3, bf16[256,256]{1,0:T(8,128)(2,1)S(1)} %bitcast.14, ...), custom_call_target="tpu_custom_call" | custom-call | flops 167772160 | bytes 2097152 | tf_op jit(solution)/shard_map/pallas_call | solution.py:587
  14.0 0.5 %collective-permute-start.3 = (bf16[4,128,128]{2,1,0:T(8,128)(2,1)S(1)}, bf16[4,128,128]{2,1,0:T(8,128)(2,1)S(1)}, u32[]{:S(2)}, u32[]{:S(2)}) collective-permute-start(bf16[4,128,128]{2,1,0:T(8,128)(2,1)S(1)} %get-tuple-element.50), channel_id=1, source_target_pairs={{0,1},{1,0},{2,3},{3,2},{4,5},{5,4},{6,7},{7,6},{8,9},{9,8},{10,11... | collective-permute-start | bytes 393224 | tf_op jit(solution)/shard_map/ppermute | solution.py:604
  14.5 1.7 %collective-permute-start.4 = (bf16[4,128,128]{2,1,0:T(8,128)(2,1)S(1)}, bf16[4,128,128]{2,1,0:T(8,128)(2,1)S(1)}, u32[]{:S(2)}, u32[]{:S(2)}) collective-permute-start(bf16[4,128,128]{2,1,0:T(8,128)(2,1)S(1)} %get-tuple-element.51), channel_id=1, source_target_pairs={{0,2},{1,3},{2,0},{3,1},{4,6},{5,7},{6,4},{7,5},{8,10},{9,11},{10,... | collective-permute-start | bytes 393224 | tf_op jit(solution)/shard_map/ppermute | solution.py:604
  16.2 0.0 collective-permute-done.refs_1_
  16.2 0.0 collective-permute-start.5
  16.2 0.0 copy-done.8
  16.2 0.1 copy.19
  16.3 0.0 copy-start.4
  16.3 0.0 copy-start.5
  16.3 0.1 copy.20.weight_ref
  16.5 0.0 collective-permute-done.1.refs_2_
  16.5 0.0 collective-permute-done.2.refs_3_
  16.5 2.8 %all-to-all-done.recv_ref = bf16[32,24,128]{2,1,0:T(8,128)(2,1)S(1)} async-done(((bf16[32,24,128]{2,1,0:T(8,128)(2,1)}), bf16[32,24,128]{2,1,0:T(8,128)(2,1)S(1)}, u32[]{:S(2)}, u32[]{:S(2)}) %all-to-all-start) | async-done | bytes 196640 | tf_op jit(solution)/shard_map/all_to_all | solution.py:579
  19.3 0.0 copy-done.4
  19.3 0.0 copy-done.5
  19.3 2.2 %shard_map.159 = (bf16[8,4,8,128]{3,2,1,0:T(8,128)(2,1)}, bf16[4,32,128]{2,1,0:T(8,128)(2,1)S(1)}, bf16[4,32,128]{2,1,0:T(8,128)(2,1)S(1)}, bf16[4,32,128]{2,1,0:T(8,128)(2,1)S(1)}, bf16[4,32,128]{2,1,0:T(8,128)(2,1)S(1)}) custom-call(bf16[32,24,128]{2,1,0:T(8,128)(2,1)S(1)} %all-to-all-done.recv_ref, bf16[128,1024]{1,0:T(8,128)(2,1)S(1)} %copy.20.weight_ref, ...), custom_call_target="tpu_custom_call" | custom-call | flops 268435456 | bytes 1048576 | tf_op jit(solution)/shard_map/pallas_call | solution.py:625
  21.5 3.6 %all-to-all-start.1 = ((bf16[32,8,128]{2,1,0:T(8,128)(2,1)}), bf16[32,8,128]{2,1,0:T(8,128)(2,1)S(1)}, u32[]{:S(2)}, u32[]{:S(2)}) async-start(bf16[32,8,128]{2,1,0:T(8,128)(2,1)} %bitcast.11), calls=%async_computation.1 | async-start | bytes 131072 | tf_op jit(solution)/shard_map/all_to_all | solution.py:640
  25.1 0.3 collective-permute-start.6
  25.4 1.7 %collective-permute-start.7 = (bf16[4,32,128]{2,1,0:T(8,128)(2,1)S(1)}, bf16[4,32,128]{2,1,0:T(8,128)(2,1)S(1)}, u32[]{:S(2)}, u32[]{:S(2)}) collective-permute-start(bf16[4,32,128]{2,1,0:T(8,128)(2,1)S(1)} %get-tuple-element.57), channel_id=1, source_target_pairs={{0,2},{1,3},{2,0},{3,1},{4,6},{5,7},{6,4},{7,5},{8,10},{9,11},{10,... | collective-permute-start | bytes 98312 | tf_op jit(solution)/shard_map/ppermute | solution.py:604
  27.1 0.0 collective-permute-done.3.refs_1_
  27.1 0.0 collective-permute-start.8
  27.1 0.0 collective-permute-done.4.refs_2_
  27.1 0.0 collective-permute-done.5.refs_3_
  27.1 0.5 shard_map.160
  27.6 0.0 copy-start.6
  27.6 0.7 %copy-done.6 = bf16[8,128,128]{2,1,0:T(8,128)(2,1)} copy-done((bf16[8,128,128]{2,1,0:T(8,128)(2,1)}, bf16[8,128,128]{2,1,0:T(8,128)(2,1)S(1)}, u32[]{:S(2)}) %copy-start.6) | copy-done | bytes 262168
  28.3 0.0 collective-permute-done.6.refs_1_
  28.3 1.1 %collective-permute-done.7.refs_2_ = bf16[4,32,128]{2,1,0:T(8,128)(2,1)S(1)} collective-permute-done((bf16[4,32,128]{2,1,0:T(8,128)(2,1)S(1)}, bf16[4,32,128]{2,1,0:T(8,128)(2,1)S(1)}, u32[]{:S(2)}, u32[]{:S(2)}) %collective-permute-start.7) | collective-permute-done | bytes 32800 | tf_op jit(solution)/shard_map/ppermute | solution.py:604
  29.4 1.3 %collective-permute-done.8.refs_3_ = bf16[4,32,128]{2,1,0:T(8,128)(2,1)S(1)} collective-permute-done((bf16[4,32,128]{2,1,0:T(8,128)(2,1)S(1)}, bf16[4,32,128]{2,1,0:T(8,128)(2,1)S(1)}, u32[]{:S(2)}, u32[]{:S(2)}) %collective-permute-start.8) | collective-permute-done | bytes 32800 | tf_op jit(solution)/shard_map/ppermute | solution.py:604
  30.6 1.9 %all-to-all-done.1.bias_ref = bf16[32,8,128]{2,1,0:T(8,128)(2,1)S(1)} async-done(((bf16[32,8,128]{2,1,0:T(8,128)(2,1)}), bf16[32,8,128]{2,1,0:T(8,128)(2,1)S(1)}, u32[]{:S(2)}, u32[]{:S(2)}) %all-to-all-start.1) | async-done | bytes 65568 | tf_op jit(solution)/shard_map/all_to_all | solution.py:640
  32.5 1.6 %shard_map.161 = (bf16[4,128,128]{2,1,0:T(8,128)(2,1)}, bf16[32,8,128]{2,1,0:T(8,128)(2,1)}, bf16[8,256,128]{2,1,0:T(8,128)(2,1)S(1)}) custom-call(bf16[32,8,128]{2,1,0:T(8,128)(2,1)S(1)} %all-to-all-done.1.bias_ref, f32[16,128]{1,0:T(8,128)S(1)} %copy-done.4, f32[8,256,128]{2,1,0:T(8,128)S(1)} %get-tuple-element.53.score_ref, ...), custom_call_target="tpu_custom_call" | custom-call | flops 268435456 | bytes 4194304 | tf_op jit(solution)/shard_map/pallas_call | solution.py:645
  34.1 2.9 %all-to-all-start.2 = ((bf16[32,8,128]{2,1,0:T(8,128)(2,1)}), bf16[32,8,128]{2,1,0:T(8,128)(2,1)S(1)}, u32[]{:S(2)}, u32[]{:S(2)}) async-start(bf16[32,8,128]{2,1,0:T(8,128)(2,1)} %get-tuple-element.66), calls=%async_computation.2 | async-start | bytes 131072 | tf_op jit(solution)/shard_map/all_to_all | solution.py:657
  37.0 0.0 copy-done.7
  37.0 0.4 shard_map.162
  37.4 0.3 collective-permute-start.9
  37.8 1.7 %collective-permute-start.10 = (bf16[128,128]{1,0:T(8,128)(2,1)S(1)}, bf16[128,128]{1,0:T(8,128)(2,1)S(1)}, u32[]{:S(2)}, u32[]{:S(2)}) collective-permute-start(bf16[128,128]{1,0:T(8,128)(2,1)S(1)} %get-tuple-element.63), channel_id=1, source_target_pairs={{0,2},{1,3},{2,0},{3,1},{4,6},{5,7},{6,4},{7,5},{8,10},{9,11},{10,... | collective-permute-start | bytes 98312 | tf_op jit(solution)/shard_map/ppermute | solution.py:604
  39.4 0.0 collective-permute-start.11
  39.5 0.0 collective-permute-done.9.refs_1_
  39.5 2.4 %collective-permute-done.10.refs_2_ = bf16[128,128]{1,0:T(8,128)(2,1)S(1)} collective-permute-done((bf16[128,128]{1,0:T(8,128)(2,1)S(1)}, bf16[128,128]{1,0:T(8,128)(2,1)S(1)}, u32[]{:S(2)}, u32[]{:S(2)}) %collective-permute-start.10) | collective-permute-done | bytes 32800 | tf_op jit(solution)/shard_map/ppermute | solution.py:604
  41.8 1.2 %collective-permute-done.11.refs_3_ = bf16[128,128]{1,0:T(8,128)(2,1)S(1)} collective-permute-done((bf16[128,128]{1,0:T(8,128)(2,1)S(1)}, bf16[128,128]{1,0:T(8,128)(2,1)S(1)}, u32[]{:S(2)}, u32[]{:S(2)}) %collective-permute-start.11) | collective-permute-done | bytes 32800 | tf_op jit(solution)/shard_map/ppermute | solution.py:604
  43.0 0.9 %shard_map.163 = bf16[256,256]{1,0:T(8,128)(2,1)} custom-call(f32[4,128,128]{2,1,0:T(8,128)S(1)} %get-tuple-element.41.gate_ref, bf16[256,256]{1,0:T(8,128)(2,1)S(1)} %copy-done, bf16[128,128]{1,0:T(8,128)(2,1)S(1)} %get-tuple-element.61.refs_0_, bf16[128,128]{1,0:T(8,128)(2,1)S(1)} %collective-permute-done.9.refs_1_, ...), custom_call_target="tpu_custom_call" | custom-call | flops 33554432 | bytes 1048576 | tf_op jit(solution)/shard_map/pallas_call | solution.py:665
  44.0 0.4 all-to-all-done.2.shares_ref
  44.4 0.0 copy-done.2
  44.4 1.5 %shard_map.164 = f32[4,128,128]{2,1,0:T(8,128)} custom-call(bf16[32,8,128]{2,1,0:T(8,128)(2,1)S(1)} %all-to-all-done.2.shares_ref, f32[16,128]{1,0:T(8,128)S(1)} %copy-done.4, bf16[4,128,128]{2,1,0:T(8,128)(2,1)S(1)} %copy-done.2), custom_call_target="tpu_custom_call" | custom-call | flops 16777216 | bytes 1048576 | tf_op jit(solution)/shard_map/pallas_call | solution.py:672
  (3 shorter events, 0.0 us)
Async XLA Ops:
  0.6 11.8 %copy-start.12 = (bf16[256,256]{1,0:T(8,128)(2,1)S(1)}, bf16[256,256]{1,0:T(8,128)(2,1)}, u32[]{:S(2)}) copy-start(bf16[256,256]{1,0:T(8,128)(2,1)} %param.23) | copy-start | bytes 393220
  3.0 9.4 %copy-start.9 = (bf16[256,256]{1,0:T(8,128)(2,1)S(1)}, bf16[256,256]{1,0:T(8,128)(2,1)}, u32[]{:S(2)}) copy-start(bf16[256,256]{1,0:T(8,128)(2,1)} %param.26) | copy-start | bytes 393220
  3.0 9.3 %copy-start.10 = (bf16[256,256]{1,0:T(8,128)(2,1)S(1)}, bf16[256,256]{1,0:T(8,128)(2,1)}, u32[]{:S(2)}) copy-start(bf16[256,256]{1,0:T(8,128)(2,1)} %param.25) | copy-start | bytes 393220
  3.1 9.3 %copy-start.11 = (bf16[256,256]{1,0:T(8,128)(2,1)S(1)}, bf16[256,256]{1,0:T(8,128)(2,1)}, u32[]{:S(2)}) copy-start(bf16[256,256]{1,0:T(8,128)(2,1)} %param.24) | copy-start | bytes 393220
  3.1 16.2 %all-to-all-start = ((bf16[32,24,128]{2,1,0:T(8,128)(2,1)}), bf16[32,24,128]{2,1,0:T(8,128)(2,1)S(1)}, u32[]{:S(2)}, u32[]{:S(2)}) async-start(bf16[32,24,128]{2,1,0:T(8,128)(2,1)} %bitcast.17), calls=%async_computation | async-start | bytes 393216 | tf_op jit(solution)/shard_map/all_to_all | solution.py:579
  10.4 5.8 %collective-permute-start = (bf16[4,32,128]{2,1,0:T(8,128)(2,1)}, bf16[4,32,128]{2,1,0:T(8,128)(2,1)S(1)}, u32[]{:S(2)}, u32[]{:S(2)}) collective-permute-start(bf16[4,32,128]{2,1,0:T(8,128)(2,1)} %get-tuple-element.45), channel_id=1, source_target_pairs={{0,1},{1,0},{2,3},{3,2},{4,5},{5,4},{6,7},{7,6},{8,9},{9,8},{10,11... | collective-permute-start | bytes 98312 | tf_op jit(solution)/shard_map/ppermute | solution.py:604
  10.7 5.8 %collective-permute-start.1 = (bf16[4,32,128]{2,1,0:T(8,128)(2,1)}, bf16[4,32,128]{2,1,0:T(8,128)(2,1)S(1)}, u32[]{:S(2)}, u32[]{:S(2)}) collective-permute-start(bf16[4,32,128]{2,1,0:T(8,128)(2,1)} %get-tuple-element.46), channel_id=1, source_target_pairs={{0,2},{1,3},{2,0},{3,1},{4,6},{5,7},{6,4},{7,5},{8,10},{9,11},{10,... | collective-permute-start | bytes 98312 | tf_op jit(solution)/shard_map/ppermute | solution.py:604
  12.4 4.1 %collective-permute-start.2 = (bf16[4,32,128]{2,1,0:T(8,128)(2,1)}, bf16[4,32,128]{2,1,0:T(8,128)(2,1)S(1)}, u32[]{:S(2)}, u32[]{:S(2)}) collective-permute-start(bf16[4,32,128]{2,1,0:T(8,128)(2,1)} %get-tuple-element.47), channel_id=1, source_target_pairs={{0,3},{1,2},{2,1},{3,0},{4,7},{5,6},{6,5},{7,4},{8,11},{9,10},{10,... | collective-permute-start | bytes 98312 | tf_op jit(solution)/shard_map/ppermute | solution.py:604
  12.4 0.9 %copy-start = (bf16[256,256]{1,0:T(8,128)(2,1)S(1)}, bf16[256,256]{1,0:T(8,128)(2,1)}, u32[]{:S(2)}) copy-start(bf16[256,256]{1,0:T(8,128)(2,1)} %wo_ref.3) | copy-start | bytes 393220
  12.4 1.0 %copy-start.1 = (bf16[2,128,256]{2,1,0:T(8,128)(2,1)S(1)}, bf16[2,128,256]{2,1,0:T(8,128)(2,1)}, u32[]{:S(2)}) copy-start(bf16[2,128,256]{2,1,0:T(8,128)(2,1)} %param.16) | copy-start | bytes 393220
  12.4 1.0 %copy-start.3 = (bf16[256,256]{1,0:T(8,128)(2,1)S(1)}, bf16[256,256]{1,0:T(8,128)(2,1)}, u32[]{:S(2)}) copy-start(bf16[256,256]{1,0:T(8,128)(2,1)} %get-tuple-element.36.normed_ref) | copy-start | bytes 393220
  13.4 2.7 %copy-start.8 = (bf16[32,32,128]{2,1,0:T(8,128)(2,1)S(1)}, bf16[32,32,128]{2,1,0:T(8,128)(2,1)}, u32[]{:S(2)}) copy-start(bf16[32,32,128]{2,1,0:T(8,128)(2,1)} %param.21) | copy-start | bytes 786436
  14.0 13.1 %collective-permute-start.3 = (bf16[4,128,128]{2,1,0:T(8,128)(2,1)S(1)}, bf16[4,128,128]{2,1,0:T(8,128)(2,1)S(1)}, u32[]{:S(2)}, u32[]{:S(2)}) collective-permute-start(bf16[4,128,128]{2,1,0:T(8,128)(2,1)S(1)} %get-tuple-element.50), channel_id=1, source_target_pairs={{0,1},{1,0},{2,3},{3,2},{4,5},{5,4},{6,7},{7,6},{8,9},{9,8},{10,11... | collective-permute-start | bytes 393224 | tf_op jit(solution)/shard_map/ppermute | solution.py:604
  14.5 12.6 %collective-permute-start.4 = (bf16[4,128,128]{2,1,0:T(8,128)(2,1)S(1)}, bf16[4,128,128]{2,1,0:T(8,128)(2,1)S(1)}, u32[]{:S(2)}, u32[]{:S(2)}) collective-permute-start(bf16[4,128,128]{2,1,0:T(8,128)(2,1)S(1)} %get-tuple-element.51), channel_id=1, source_target_pairs={{0,2},{1,3},{2,0},{3,1},{4,6},{5,7},{6,4},{7,5},{8,10},{9,11},{10,... | collective-permute-start | bytes 393224 | tf_op jit(solution)/shard_map/ppermute | solution.py:604
  16.2 11.0 %collective-permute-start.5 = (bf16[4,128,128]{2,1,0:T(8,128)(2,1)S(1)}, bf16[4,128,128]{2,1,0:T(8,128)(2,1)S(1)}, u32[]{:S(2)}, u32[]{:S(2)}) collective-permute-start(bf16[4,128,128]{2,1,0:T(8,128)(2,1)S(1)} %get-tuple-element.52), channel_id=1, source_target_pairs={{0,3},{1,2},{2,1},{3,0},{4,7},{5,6},{6,5},{7,4},{8,11},{9,10},{10,... | collective-permute-start | bytes 393224 | tf_op jit(solution)/shard_map/ppermute | solution.py:604
  16.3 3.0 %copy-start.4 = (f32[16,128]{1,0:T(8,128)S(1)}, f32[16,128]{1,0:T(8,128)}, u32[]{:S(2)}) copy-start(f32[16,128]{1,0:T(8,128)} %get-tuple-element.43.aux_ref.mask_ref) | copy-start | bytes 24580
  16.3 3.0 %copy-start.5 = (bf16[4,32,128]{2,1,0:T(8,128)(2,1)S(1)}, bf16[4,32,128]{2,1,0:T(8,128)(2,1)}, u32[]{:S(2)}) copy-start(bf16[4,32,128]{2,1,0:T(8,128)(2,1)} %get-tuple-element.44.refs_0_) | copy-start | bytes 98308
  21.5 11.0 %all-to-all-start.1 = ((bf16[32,8,128]{2,1,0:T(8,128)(2,1)}), bf16[32,8,128]{2,1,0:T(8,128)(2,1)S(1)}, u32[]{:S(2)}, u32[]{:S(2)}) async-start(bf16[32,8,128]{2,1,0:T(8,128)(2,1)} %bitcast.11), calls=%async_computation.1 | async-start | bytes 131072 | tf_op jit(solution)/shard_map/all_to_all | solution.py:640
  25.1 3.2 %collective-permute-start.6 = (bf16[4,32,128]{2,1,0:T(8,128)(2,1)S(1)}, bf16[4,32,128]{2,1,0:T(8,128)(2,1)S(1)}, u32[]{:S(2)}, u32[]{:S(2)}) collective-permute-start(bf16[4,32,128]{2,1,0:T(8,128)(2,1)S(1)} %get-tuple-element.56), channel_id=1, source_target_pairs={{0,1},{1,0},{2,3},{3,2},{4,5},{5,4},{6,7},{7,6},{8,9},{9,8},{10,11... | collective-permute-start | bytes 98312 | tf_op jit(solution)/shard_map/ppermute | solution.py:604
  25.4 4.0 %collective-permute-start.7 = (bf16[4,32,128]{2,1,0:T(8,128)(2,1)S(1)}, bf16[4,32,128]{2,1,0:T(8,128)(2,1)S(1)}, u32[]{:S(2)}, u32[]{:S(2)}) collective-permute-start(bf16[4,32,128]{2,1,0:T(8,128)(2,1)S(1)} %get-tuple-element.57), channel_id=1, source_target_pairs={{0,2},{1,3},{2,0},{3,1},{4,6},{5,7},{6,4},{7,5},{8,10},{9,11},{10,... | collective-permute-start | bytes 98312 | tf_op jit(solution)/shard_map/ppermute | solution.py:604
  27.1 3.5 %collective-permute-start.8 = (bf16[4,32,128]{2,1,0:T(8,128)(2,1)S(1)}, bf16[4,32,128]{2,1,0:T(8,128)(2,1)S(1)}, u32[]{:S(2)}, u32[]{:S(2)}) collective-permute-start(bf16[4,32,128]{2,1,0:T(8,128)(2,1)S(1)} %get-tuple-element.58), channel_id=1, source_target_pairs={{0,3},{1,2},{2,1},{3,0},{4,7},{5,6},{6,5},{7,4},{8,11},{9,10},{10,... | collective-permute-start | bytes 98312 | tf_op jit(solution)/shard_map/ppermute | solution.py:604
  27.6 0.7 %copy-start.6 = (bf16[8,128,128]{2,1,0:T(8,128)(2,1)}, bf16[8,128,128]{2,1,0:T(8,128)(2,1)S(1)}, u32[]{:S(2)}) copy-start(bf16[8,128,128]{2,1,0:T(8,128)(2,1)S(1)} %get-tuple-element.60.value_ref) | copy-start | bytes 786436
  32.5 4.5 %copy-start.7 = (bf16[8,128,128]{2,1,0:T(8,128)(2,1)S(1)}, bf16[8,128,128]{2,1,0:T(8,128)(2,1)}, u32[]{:S(2)}) copy-start(bf16[8,128,128]{2,1,0:T(8,128)(2,1)} %copy-done.6) | copy-start | bytes 786436
  34.1 10.3 %all-to-all-start.2 = ((bf16[32,8,128]{2,1,0:T(8,128)(2,1)}), bf16[32,8,128]{2,1,0:T(8,128)(2,1)S(1)}, u32[]{:S(2)}, u32[]{:S(2)}) async-start(bf16[32,8,128]{2,1,0:T(8,128)(2,1)} %get-tuple-element.66), calls=%async_computation.2 | async-start | bytes 131072 | tf_op jit(solution)/shard_map/all_to_all | solution.py:657
  37.4 2.0 %collective-permute-start.9 = (bf16[128,128]{1,0:T(8,128)(2,1)S(1)}, bf16[128,128]{1,0:T(8,128)(2,1)S(1)}, u32[]{:S(2)}, u32[]{:S(2)}) collective-permute-start(bf16[128,128]{1,0:T(8,128)(2,1)S(1)} %get-tuple-element.62), channel_id=1, source_target_pairs={{0,1},{1,0},{2,3},{3,2},{4,5},{5,4},{6,7},{7,6},{8,9},{9,8},{10,11... | collective-permute-start | bytes 98312 | tf_op jit(solution)/shard_map/ppermute | solution.py:604
  37.8 4.0 %collective-permute-start.10 = (bf16[128,128]{1,0:T(8,128)(2,1)S(1)}, bf16[128,128]{1,0:T(8,128)(2,1)S(1)}, u32[]{:S(2)}, u32[]{:S(2)}) collective-permute-start(bf16[128,128]{1,0:T(8,128)(2,1)S(1)} %get-tuple-element.63), channel_id=1, source_target_pairs={{0,2},{1,3},{2,0},{3,1},{4,6},{5,7},{6,4},{7,5},{8,10},{9,11},{10,... | collective-permute-start | bytes 98312 | tf_op jit(solution)/shard_map/ppermute | solution.py:604
  39.4 3.6 %collective-permute-start.11 = (bf16[128,128]{1,0:T(8,128)(2,1)S(1)}, bf16[128,128]{1,0:T(8,128)(2,1)S(1)}, u32[]{:S(2)}, u32[]{:S(2)}) collective-permute-start(bf16[128,128]{1,0:T(8,128)(2,1)S(1)} %get-tuple-element.64), channel_id=1, source_target_pairs={{0,3},{1,2},{2,1},{3,0},{4,7},{5,6},{6,5},{7,4},{8,11},{9,10},{10,... | collective-permute-start | bytes 98312 | tf_op jit(solution)/shard_map/ppermute | solution.py:604
  43.0 1.4 %copy-start.2 = (bf16[4,128,128]{2,1,0:T(8,128)(2,1)S(1)}, bf16[4,128,128]{2,1,0:T(8,128)(2,1)}, u32[]{:S(2)}) copy-start(bf16[4,128,128]{2,1,0:T(8,128)(2,1)} %get-tuple-element.33.pair_ref) | copy-start | bytes 393220

commit v7 on v6

--- a/solution.py
+++ b/solution.py
@@ -224,6 +224,7 @@
 
 LANES = 128
 GROUP = 4
+PIECES = 4
 f32 = jnp.float32
 bf16 = jnp.bfloat16
 
@@ -262,10 +263,9 @@
 
 
 def factors_kernel(
-    seq_smem_ref, res_smem_ref, seq_ref, res_ref, bias_w_ref, rows_ref, left_ref, right_ref, pair_ref,
-    send_ref, aux_ref, normed_ref, *refs
+    seq_smem_ref, res_smem_ref, seq_ref, res_ref, bias_w_ref, left_ref, right_ref, pair_ref, *refs
 ):
-    pair_refs, left_scr = refs[:GROUP], refs[GROUP]
+    row_refs, (send_ref, aux_ref, normed_ref, *pair_refs, left_scr) = refs[:PIECES], refs[PIECES:]
     columns_each = pair_refs[0].shape[1]
     for step in range(GROUP):
         first = pl.multiple_of(partner(step) * columns_each, columns_each)
@@ -274,7 +274,7 @@
     seqs = send_ref.shape[2] // 12
     residues = res_ref.shape[1]
     me = lax.axis_index("row")
-    normed = layer_normalize(rows_ref[...]).astype(bf16)
+    normed = jnp.concatenate([layer_normalize(rows[...]).astype(bf16) for rows in row_refs], axis=0)
     normed_ref[...] = normed
     live = res_ref[...].astype(f32)
     live_rows = jnp.broadcast_to(live, (residues, residues)).T
@@ -341,8 +341,12 @@
     return jnp.concatenate(lines, axis=0)
 
 
-def projections_kernel(normed_ref, cot_ref, weights_ref, wo_ref, gate_ref, *rest):
+def projections_kernel(
+    normed_ref, cot_ref, weights_ref, wo_ref, aux_ref, pair_ref, gate_ref, aux_out_ref, pair_out_ref, *rest
+):
     block_refs, every = rest[:GROUP], rest[GROUP]
+    aux_out_ref[...] = aux_ref[...]
+    pair_out_ref[...] = pair_ref[...]
     normed = normed_ref[...]
     tokens = normed.shape[0]
     residues = gate_ref.shape[1]
@@ -392,18 +396,30 @@
     for s in range(seqs):
         for g in range(8):
             part = flat[pl.ds(s * 8 + g, peers, stride=block_rows), :]
-            rbuf[s * peers : (s + 1) * peers, g * LANES : (g + 1) * LANES] = part.astype(bf16)
+            for a in range(4):
+                turned = part if a == 0 else pltpu.roll(part, 32 * a, 1)
+                rbuf[a, s * peers : (s + 1) * peers, g * LANES : (g + 1) * LANES] = turned.astype(bf16)
         for a in range(4):
             part = flat[pl.ds(8 * seqs + 4 * s + a, peers, stride=block_rows), :]
             lbuf[s * peers : (s + 1) * peers, a * LANES : (a + 1) * LANES] = part
     left_t = lbuf[...].T.astype(bf16)
-    for g in range(8):
-        outer = dot_nn(left_t, rbuf[:, g * LANES : (g + 1) * LANES])
-        for b in range(4):
-            turned = swap_groups([outer[(4 * a + b) * 32 : (4 * a + b + 1) * 32] for a in range(4)])
-            for a in range(4):
-                obuf[(g * 4 + a) * 32 : (g * 4 + a + 1) * 32, b * LANES : (b + 1) * LANES] = turned[a].astype(bf16)
-    sums = dot_nn(weight_ref[...], obuf[...])
+    outer = [dot_nn(left_t[a * LANES : (a + 1) * LANES], rbuf[a]).astype(bf16) for a in range(4)]
+    lane_group = lane_index(LANES) // 32
+    sums = None
+    for q in range(4):
+        for g in range(8):
+            span = slice(g * LANES, (g + 1) * LANES)
+            picked = outer[3][:, span]
+            for a in range(3):
+                picked = jnp.where(lane_group == (q + a) % 4, outer[a][:, span], picked)
+            for b in range(4):
+                obuf[q, g * 32 : (g + 1) * 32, b * LANES : (b + 1) * LANES] = picked[b * 32 : (b + 1) * 32]
+        part = dot_nn(weight_ref[q], obuf[q])
+        if q:
+            part = jnp.concatenate(
+                [pltpu.roll(part[:, b * LANES : (b + 1) * LANES], LANES - 32 * q, 1) for b in range(4)], axis=1
+            )
+        sums = part if sums is None else sums + part
     bias_w = aux_ref[8:16].astype(bf16)
     blocks = []
     for b in range(4):
@@ -412,7 +428,8 @@
         updated = (before + update.T).astype(bf16)
         for a in range(GROUP):
             after[a, b] = updated[a * 32 : (a + 1) * 32]
-        blocks.append(dot_nt(bias_w, layer_normalize(updated).astype(bf16)))
+        line = dot_nt(bias_w, layer_normalize(updated).astype(bf16))
+        blocks.append(pltpu.roll(line, partner(0) * 32, 1))
     lines, _, share, _ = send_ref.shape
     heads = share // 4
     for t in range(GROUP):
@@ -422,22 +439,23 @@
         updated_refs[step][...] = after[partner(step)]
 
 
-def placed_bias(flat, mask_ref, heads, h):
-    residues = mask_ref.shape[1]
-    row = lax.broadcasted_iota(jnp.int32, (residues, LANES), 0)
-    lane = lane_index(residues)
-    bias = flat[pl.ds(h, residues, stride=heads), :]
-    for rows, lanes in ((8, 64), (4, 32)):
-        first = row % (2 * rows) < rows
-        low = lane % (2 * lanes) < lanes
-        moved = jnp.where(first, pltpu.roll(bias, residues - rows, 0), pltpu.roll(bias, rows, 0))
-        moved = jnp.where(low, pltpu.roll(moved, LANES - lanes, 1), pltpu.roll(moved, lanes, 1))
-        bias = jnp.where(first == low, bias, moved)
-    return bias + mask_ref[4:5, :]
+def place_bias(flat, mask_ref, heads, h, bias):
+    lines = bias.shape[0] // 16
+    lane_group = lane_index(lines) // 32
+    mask = mask_ref[4:5, :]
+    for b in range(4):
+        rows = [flat[pl.ds((4 * t + b) * heads + h, lines, stride=16 * heads), :] for t in range(GROUP)]
+        for a in range(4):
+            picked = rows[3]
+            for t in range(3):
+                picked = jnp.where(lane_group == (a + t) % 4, rows[t], picked)
+            if a:
+                picked = pltpu.roll(picked, LANES - 32 * a, 1)
+            bias[pl.ds(4 * a + b, lines, stride=16), :] = picked + mask
 
 
 def bias_gradient_kernel(bias_ref, mask_ref, score_ref, flow_ref, *refs):
-    part_refs, (pair_ref, send_ref, weights_ref, flat, grads) = refs[:GROUP], refs[GROUP:]
+    part_refs, (pair_ref, send_ref, weights_ref, flat, grads, placed) = refs[:GROUP], refs[GROUP:]
     columns_each = part_refs[0].shape[1]
     for step in range(GROUP):
         first = pl.multiple_of(partner(step) * columns_each, columns_each)
@@ -448,7 +466,8 @@
     ones = jnp.ones((residues, LANES), bf16)
     for h in range(heads):
         at = slice(h * residues, (h + 1) * residues)
-        bias = placed_bias(flat, mask_ref, heads, h)
+        place_bias(flat, mask_ref, heads, h, placed.at[h])
+        bias = placed[h]
         total = jnp.zeros((residues, residues), f32)
         for s in range(seqs):
             scores = score_ref[s, at, :] + bias
@@ -494,28 +513,58 @@
         out_ref[s * residues : (s + 1) * residues, :] = sums[s].astype(bf16)
 
 
-def gradient_kernel(shares_ref, aux_ref, pair_ref, out_ref):
+def split_sum(values):
+    high = values.astype(bf16)
+    return high, (values - high.astype(f32)).astype(bf16)
+
+
+def gradient_kernel(shares_ref, aux_ref, pair_ref, out_hbm, result, left_for):
     peers, share, _ = shares_ref.shape
+    rows, _, channels = pair_ref.shape
+    heads = share // rows
     total = jnp.sum(shares_ref[...].astype(f32).reshape(peers // GROUP, GROUP, share, LANES), axis=0)
-    rows = pair_ref.shape[0]
-    heads = share // rows
     bias_w = aux_ref[8:16]
+    mean_high, mean_low = split_sum(
+        jnp.broadcast_to(jnp.mean(bias_w, axis=-1, keepdims=True), bias_w.shape)
+    )
+    exact = bias_w.astype(bf16)
+    none = jnp.zeros(exact.shape, bf16)
+    weights = jnp.concatenate(
+        [
+            jnp.concatenate([exact, mean_high], axis=1),
+            jnp.concatenate([exact, mean_high], axis=1),
+            jnp.concatenate([none, mean_low], axis=1),
+        ],
+        axis=0,
+    )
+    moves = []
     for i in range(rows):
         own = jnp.concatenate([total[t, i * heads : (i + 1) * heads] for t in range(GROUP)], axis=0)
-        upstream = lax.dot_general(
-            own, bias_w, (((0,), (0,)), ((), ())), precision=lax.Precision.HIGHEST, preferred_element_type=f32
+        high, low = split_sum(own)
+        both = dot_tn(jnp.concatenate([high, low, high], axis=0), weights)
+        upstream, mean = both[:, :channels], both[:, channels:]
+        values = pair_ref[i].astype(f32)
+        center = values - jnp.mean(values, axis=-1, keepdims=True)
+        inverse = lax.rsqrt(jnp.mean(center * center, axis=-1, keepdims=True) + norm_eps)
+        normal = center * inverse
+        result[i] = inverse * (
+            upstream - mean - normal * jnp.mean(upstream * normal, axis=-1, keepdims=True)
         )
-        out_ref[i] = norm_backward(pair_ref[i], upstream)
-
-
-def kernel_call(body, out_shape, in_specs=None, scratch=(), flops=0, moved=0, vmem_mib=12):
+        moves.append(pltpu.make_async_copy(result.at[i], out_hbm.at[i], left_for.at[i]))
+        moves[-1].start()
+    for move in moves:
+        move.wait()
+
+
+def kernel_call(body, out_shape, in_specs=None, scratch=(), flops=0, moved=0, vmem_mib=12, out_specs=None, grid=()):
     vmem = pl.BlockSpec(memory_space=pltpu.VMEM)
     many = isinstance(out_shape, (list, tuple))
     return pl.pallas_call(
         body,
+        grid=grid,
         out_shape=out_shape,
         in_specs=in_specs,
-        out_specs=[vmem] * len(out_shape) if many else vmem,
+        out_specs=out_specs or ([vmem] * len(out_shape) if many else vmem),
         scratch_shapes=list(scratch),
         compiler_params=pltpu.CompilerParams(vmem_limit_bytes=vmem_mib * 1024 * 1024),
         cost_estimate=pl.CostEstimate(flops=flops, bytes_accessed=moved, transcendentals=0),
@@ -552,6 +601,9 @@
     flat_rows = alignment_rows.reshape(token_rows, channel_count)
     shape = jax.ShapeDtypeStruct
 
+    pieces = [
+        pl.BlockSpec((token_rows // PIECES, channel_count), lambda step, at=at: (at, 0)) for at in range(PIECES)
+    ]
     send, aux, normed, *pair_blocks = kernel_call(
         factors_kernel,
         [
@@ -560,21 +612,22 @@
             shape((token_rows, channel_count), bf16),
         ]
         + [shape((rows_here, columns_each, pair_channels), bf16)] * GROUP,
-        [smem] * 2 + [vmem] * 7,
+        [smem] * 2 + [vmem] * 6 + pieces,
         [pltpu.VMEM((residues, LANES), f32)],
         flops=2 * token_rows * channel_count * LANES,
         moved=1 << 20,
         vmem_mib=60,
+        grid=(1,),
     )(
         sequence_mask,
         residue_mask,
         sequence_mask.reshape(1, -1),
         residue_mask.reshape(1, -1),
         bias_weight.T,
-        flat_rows,
         left_weight.T,
         right_weight.T,
         pair_state,
+        *[flat_rows] * PIECES,
     )
     received = lax.all_to_all(
         send.reshape(peers, block_rows, LANES), "row", split_axis=0, concat_axis=0, tiled=True
@@ -584,11 +637,12 @@
     head_rows = group_heads * residues
     scale = (channel_count // head_count) ** (-0.5)
     normed, *weights = lax.optimization_barrier((normed, query_weight, key_weight, value_weight, gate_weight))
-    gate, *blocks = kernel_call(
+    part_shape = shape((rows_here, columns_each, pair_channels), bf16)
+    gate, aux, own_block, *blocks = kernel_call(
         projections_kernel,
-        [shape((GROUP, residues, LANES), f32)]
+        [shape((GROUP, residues, LANES), f32), shape((16, LANES), f32), part_shape]
         + [shape((2 * sequence_wise, residues, LANES), bf16)] * GROUP,
-        [vmem] * 4,
+        [vmem] * 6,
         [pltpu.VMEM((GROUP, 2 * sequence_wise, residues, LANES), bf16)],
         flops=10 * token_rows * channel_count * channel_count,
         moved=1 << 21,
@@ -597,6 +651,8 @@
         update_cotangent.reshape(token_rows, channel_count),
         jnp.concatenate(weights, axis=1),
         output_weight,
+        aux,
+        pair_blocks[0],
     )
 
     def trade(parts):
@@ -604,7 +660,7 @@
             lax.ppermute(parts[d], "row", [(i, i ^ d) for i in range(peers)]) for d in range(1, GROUP)
         ]
 
-    pair_blocks = trade(pair_blocks)
+    pair_blocks = [own_block] + trade(pair_blocks)[1:]
     blocks = trade(blocks)
     scores, flow, values = kernel_call(
         lambda *refs: products_kernel(scale, *refs),
@@ -617,20 +673,19 @@
 
     weight_t = (
         outer_weight.reshape(factor, 4, 8, pair_channels)
-        .transpose(3, 2, 1, 0)
-        .reshape(pair_channels, 32 * factor)
+        .transpose(1, 3, 2, 0)
+        .reshape(4, pair_channels, 8 * factor)
     )
     share_rows = 4 * group_heads
-    part_shape = shape((rows_here, columns_each, pair_channels), bf16)
     send_bias, *updated = kernel_call(
         pair_kernel,
         [shape((lines, GROUP, share_rows, LANES), bf16)] + [part_shape] * GROUP,
         [vmem] * (3 + GROUP),
         [
             pltpu.VMEM((peers * block_rows, LANES), f32),
-            pltpu.VMEM((peers * sequence_wise, 8 * LANES), bf16),
+            pltpu.VMEM((4, peers * sequence_wise, 8 * LANES), bf16),
             pltpu.VMEM((peers * sequence_wise, 4 * LANES), f32),
-            pltpu.VMEM((32 * factor, 4 * LANES), bf16),
+            pltpu.VMEM((4, 8 * factor, 4 * LANES), bf16),
             pltpu.VMEM((GROUP, rows_here, columns_each, pair_channels), bf16),
             pltpu.VMEM((GROUP, rows_here, columns_each, pair_channels), bf16),
         ],
@@ -650,7 +705,7 @@
             shape((GROUP * sequence_wise, head_rows, residues), bf16),
         ],
         [vmem] * (4 + GROUP),
-        [pltpu.VMEM((head_rows, LANES), f32), pltpu.VMEM((head_rows, LANES), f32)],
+        [pltpu.VMEM((head_rows, LANES), f32)] * 2 + [pltpu.VMEM((group_heads, residues, LANES), f32)],
         flops=1 << 28,
         moved=1 << 22,
     )(bias_all, aux, scores, flow, *updated)
@@ -673,8 +728,10 @@
         gradient_kernel,
         shape((rows_here, residues, pair_channels), f32),
         [vmem] * 3,
+        [pltpu.VMEM((rows_here, residues, pair_channels), f32), pltpu.SemaphoreType.DMA((rows_here,))],
         flops=1 << 24,
         moved=1 << 20,
+        out_specs=pl.BlockSpec(memory_space=pltpu.HBM),
     )(shares, aux, pair_updated)
     return (update.reshape(alignment_rows.shape), pair_updated, pair_gradient)
 

time: 46.2 us -> 45.1 us (0.976)
  starting transfers between devices: 22 us -> 21.4 us
  Pallas kernels: 10 us -> 9.52 us
    all_to_all x1, starting transfers between devices: 3.59 us -> 3.02 us  [on_device_paired(): lax.all_to_all(send_bias.reshape(peers, share_rows, LANES), 'row', split_...]
    unnamed x26 -> x27, local copies, waits for them, and re-layouts: 1.69 us -> 1.78 us
where the time goes in v7:
time: 45.1 us; the launch traced here: 44.8 us
  starting transfers between devices  21.4 us (47%)
  waiting for transfers between devices  11 us (24%)
  Pallas kernels  9.52 us (21%)
  local copies, waits for them, and re-layouts  1.92 us (4%)
  between operations  0.85 us (2%)
    ppermute x12, starting transfers between devices, trade(): lax.ppermute(parts[d], 'row', [(i, i ^ d) for i in range(peers)])  8.2 us
    all_to_all x1, starting transfers between devices, on_device_paired(): lax.all_to_all(send.reshape(peers, block_rows, LANES), 'row', split_axis=...  7.3 us
    ppermute x12, waiting for transfers between devices, trade(): lax.ppermute(parts[d], 'row', [(i, i ^ d) for i in range(peers)])  5.96 us
    all_to_all x1, starting transfers between devices, on_device_paired(): lax.all_to_all(send_bias.reshape(peers, share_rows, LANES), 'row', split_...  3.02 us
    all_to_all x1, starting transfers between devices, on_device_paired(): lax.all_to_all(send_grad, 'row', split_axis=0, concat_axis=0, tiled=True)  2.9 us
    all_to_all x1, waiting for transfers between devices, on_device_paired(): lax.all_to_all(send.reshape(peers, block_rows, LANES), 'row', split_axis=...  2.8 us
    pallas_call x1, Pallas kernels, on_device_paired(): kernel_call(factors_kernel, [shape((lines, GROUP, block_rows, LANES), bf1...  2.3 us
    pallas_call x1, Pallas kernels, on_device_paired(): kernel_call(pair_kernel, [shape((lines, GROUP, share_rows, LANES), bf16)]...  2.24 us
  transfers between devices with their start and end apart: 15, of which 7 were waited for; matrix products, arithmetic and copies ran while one was open for 1% of the time, Pallas kernels for 10%

profile of v7, /device:TPU:0, one launch (start us, length us, event | category | flops | bytes accessed | tf_op | source)
XLA Modules:
  0.0 44.8 jit_solution(231386525314001579)
XLA Ops:
  0.6 0.0 copy-start.12
  0.6 2.3 %shard_map.157 = (bf16[8,4,24,128]{3,2,1,0:T(8,128)(2,1)}, f32[16,128]{1,0:T(8,128)}, bf16[256,256]{1,0:T(8,128)(2,1)}, bf16[4,32,128]{2,1,0:T(8,128)(2,1)}, bf1...) custom-call(s32[64]{0:T(128)} %seq_smem_ref.1, s32[128]{0:T(128)} %res_smem_ref.1, ...), custom_call_target="tpu_custom_call" | custom-call | flops 16777216 | bytes 1048576 | tf_op jit(solution)/shard_map/pallas_call | solution.py:607
  2.9 0.0 copy-start.9
  3.0 0.0 copy-start.10
  3.0 0.0 copy-start.11
  3.0 7.3 %all-to-all-start = ((bf16[32,24,128]{2,1,0:T(8,128)(2,1)}), bf16[32,24,128]{2,1,0:T(8,128)(2,1)S(1)}, u32[]{:S(2)}, u32[]{:S(2)}) async-start(bf16[32,24,128]{2,1,0:T(8,128)(2,1)} %bitcast.21), calls=%async_computation | async-start | bytes 393216 | tf_op jit(solution)/shard_map/all_to_all | solution.py:632
  10.3 0.3 collective-permute-start
  10.6 1.7 %collective-permute-start.1 = (bf16[4,32,128]{2,1,0:T(8,128)(2,1)}, bf16[4,32,128]{2,1,0:T(8,128)(2,1)S(1)}, u32[]{:S(2)}, u32[]{:S(2)}) collective-permute-start(bf16[4,32,128]{2,1,0:T(8,128)(2,1)} %get-tuple-element.50), channel_id=1, source_target_pairs={{0,2},{1,3},{2,0},{3,1},{4,6},{5,7},{6,4},{7,5},{8,10},{9,11},{10,... | collective-permute-start | bytes 98312 | tf_op jit(solution)/shard_map/ppermute | solution.py:660
  12.3 0.0 collective-permute-start.2
  12.3 0.0 copy-done.12
  12.3 0.0 copy-done.9
  12.3 0.0 copy-done.10
  12.3 0.0 copy-done.11
  12.3 0.0 copy-start
  12.3 0.0 copy-start.2
  12.3 0.0 copy-start.3
  12.4 0.0 copy-start.4
  12.4 0.0 copy-start.5
  12.4 0.1 pad_maximum_fusion.weights_ref
  12.4 0.8 %copy-done = bf16[256,256]{1,0:T(8,128)(2,1)S(1)} copy-done((bf16[256,256]{1,0:T(8,128)(2,1)S(1)}, bf16[256,256]{1,0:T(8,128)(2,1)}, u32[]{:S(2)}) %copy-start) | copy-done | bytes 131096
  13.2 0.1 copy-done.2
  13.3 0.1 copy-done.3
  13.4 0.0 copy-done.4
  13.4 0.0 copy-done.5
  13.4 0.5 %shard_map.158 = (f32[4,128,128]{2,1,0:T(8,128)S(1)}, f32[16,128]{1,0:T(8,128)S(1)}, bf16[4,32,128]{2,1,0:T(8,128)(2,1)S(1)}, bf16[4,128,128]{2,1,0:T(8,128)(2,1...) custom-call(bf16[256,256]{1,0:T(8,128)(2,1)S(1)} %copy-done.3, ...), custom_call_target="tpu_custom_call" | custom-call | flops 167772160 | bytes 2097152 | tf_op jit(solution)/shard_map/pallas_call | solution.py:641
  13.9 0.5 %collective-permute-start.3 = (bf16[4,128,128]{2,1,0:T(8,128)(2,1)S(1)}, bf16[4,128,128]{2,1,0:T(8,128)(2,1)S(1)}, u32[]{:S(2)}, u32[]{:S(2)}) collective-permute-start(bf16[4,128,128]{2,1,0:T(8,128)(2,1)S(1)} %get-tuple-element.54), channel_id=1, source_target_pairs={{0,1},{1,0},{2,3},{3,2},{4,5},{5,4},{6,7},{7,6},{8,9},{9,8},{10,11... | collective-permute-start | bytes 393224 | tf_op jit(solution)/shard_map/ppermute | solution.py:660
  14.4 1.7 %collective-permute-start.4 = (bf16[4,128,128]{2,1,0:T(8,128)(2,1)S(1)}, bf16[4,128,128]{2,1,0:T(8,128)(2,1)S(1)}, u32[]{:S(2)}, u32[]{:S(2)}) collective-permute-start(bf16[4,128,128]{2,1,0:T(8,128)(2,1)S(1)} %get-tuple-element.55), channel_id=1, source_target_pairs={{0,2},{1,3},{2,0},{3,1},{4,6},{5,7},{6,4},{7,5},{8,10},{9,11},{10,... | collective-permute-start | bytes 393224 | tf_op jit(solution)/shard_map/ppermute | solution.py:660
  16.1 0.0 collective-permute-done.refs_1_
  16.1 0.0 collective-permute-start.5
  16.1 0.0 copy-done.8
  16.1 0.1 copy.18
  16.2 0.1 copy.19.weight_ref
  16.4 0.0 collective-permute-done.1.refs_2_
  16.4 0.0 collective-permute-done.2.refs_3_
  16.4 2.8 %all-to-all-done.recv_ref = bf16[32,24,128]{2,1,0:T(8,128)(2,1)S(1)} async-done(((bf16[32,24,128]{2,1,0:T(8,128)(2,1)}), bf16[32,24,128]{2,1,0:T(8,128)(2,1)S(1)}, u32[]{:S(2)}, u32[]{:S(2)}) %all-to-all-start) | async-done | bytes 196640 | tf_op jit(solution)/shard_map/all_to_all | solution.py:632
  19.2 2.2 %shard_map.159 = (bf16[8,4,8,128]{3,2,1,0:T(8,128)(2,1)}, bf16[4,32,128]{2,1,0:T(8,128)(2,1)S(1)}, bf16[4,32,128]{2,1,0:T(8,128)(2,1)S(1)}, bf16[4,32,128]{2,1,0:T(8,128)(2,1)S(1)}, bf16[4,32,128]{2,1,0:T(8,128)(2,1)S(1)}) custom-call(bf16[32,24,128]{2,1,0:T(8,128)(2,1)S(1)} %all-to-all-done.recv_ref, bf16[4,128,256]{2,1,0:T(8,128)(2,1)S(1)} %copy.19.weight_ref, ...), custom_call_target="tpu_custom_call" | custom-call | flops 268435456 | bytes 1048576 | tf_op jit(solution)/shard_map/pallas_call | solution.py:680
  21.4 3.0 %all-to-all-start.1 = ((bf16[32,8,128]{2,1,0:T(8,128)(2,1)}), bf16[32,8,128]{2,1,0:T(8,128)(2,1)S(1)}, u32[]{:S(2)}, u32[]{:S(2)}) async-start(bf16[32,8,128]{2,1,0:T(8,128)(2,1)} %bitcast.11), calls=%async_computation.1 | async-start | bytes 131072 | tf_op jit(solution)/shard_map/all_to_all | solution.py:695
  24.5 0.3 collective-permute-start.6
  24.8 1.7 %collective-permute-start.7 = (bf16[4,32,128]{2,1,0:T(8,128)(2,1)S(1)}, bf16[4,32,128]{2,1,0:T(8,128)(2,1)S(1)}, u32[]{:S(2)}, u32[]{:S(2)}) collective-permute-start(bf16[4,32,128]{2,1,0:T(8,128)(2,1)S(1)} %get-tuple-element.61), channel_id=1, source_target_pairs={{0,2},{1,3},{2,0},{3,1},{4,6},{5,7},{6,4},{7,5},{8,10},{9,11},{10,... | collective-permute-start | bytes 98312 | tf_op jit(solution)/shard_map/ppermute | solution.py:660
  26.5 0.0 collective-permute-done.3.refs_1_
  26.5 0.0 collective-permute-start.8
  26.5 0.0 collective-permute-done.4.refs_2_
  26.5 0.0 collective-permute-done.5.refs_3_
  26.5 0.5 %shard_map.160 = (f32[8,256,128]{2,1,0:T(8,128)S(1)}, f32[8,256,128]{2,1,0:T(8,128)S(1)}, bf16[8,128,128]{2,1,0:T(8,128)(2,1)S(1)}) custom-call(bf16[4,128,128]{2,1,0:T(8,128)(2,1)S(1)} %get-tuple-element.53.refs_0_, bf16[4,128,128]{2,1,0:T(8,128)(2,1)S(1)} %collective-permute-done.3.refs_1_, bf16[4,128,128]{2,1,0:T(8,128)(2,1)S(1)} %collective-permute-done.4.refs_2_, ...), custom_call_target="tpu_custom_call" | custom-call | flops 268435456 | bytes 2097152 | tf_op jit(solution)/shard_map/pallas_call | solution.py:665
  26.9 0.0 copy-start.6
  26.9 0.7 %copy-done.6 = bf16[8,128,128]{2,1,0:T(8,128)(2,1)} copy-done((bf16[8,128,128]{2,1,0:T(8,128)(2,1)}, bf16[8,128,128]{2,1,0:T(8,128)(2,1)S(1)}, u32[]{:S(2)}) %copy-start.6) | copy-done | bytes 262168
  27.6 0.0 collective-permute-done.6.refs_1_
  27.6 1.1 %collective-permute-done.7.refs_2_ = bf16[4,32,128]{2,1,0:T(8,128)(2,1)S(1)} collective-permute-done((bf16[4,32,128]{2,1,0:T(8,128)(2,1)S(1)}, bf16[4,32,128]{2,1,0:T(8,128)(2,1)S(1)}, u32[]{:S(2)}, u32[]{:S(2)}) %collective-permute-start.7) | collective-permute-done | bytes 32800 | tf_op jit(solution)/shard_map/ppermute | solution.py:660
  28.7 1.3 %collective-permute-done.8.refs_3_ = bf16[4,32,128]{2,1,0:T(8,128)(2,1)S(1)} collective-permute-done((bf16[4,32,128]{2,1,0:T(8,128)(2,1)S(1)}, bf16[4,32,128]{2,1,0:T(8,128)(2,1)S(1)}, u32[]{:S(2)}, u32[]{:S(2)}) %collective-permute-start.8) | collective-permute-done | bytes 32800 | tf_op jit(solution)/shard_map/ppermute | solution.py:660
  30.0 1.9 %all-to-all-done.1.bias_ref = bf16[32,8,128]{2,1,0:T(8,128)(2,1)S(1)} async-done(((bf16[32,8,128]{2,1,0:T(8,128)(2,1)}), bf16[32,8,128]{2,1,0:T(8,128)(2,1)S(1)}, u32[]{:S(2)}, u32[]{:S(2)}) %all-to-all-start.1) | async-done | bytes 65568 | tf_op jit(solution)/shard_map/all_to_all | solution.py:695
  31.9 1.4 %shard_map.161 = (bf16[4,128,128]{2,1,0:T(8,128)(2,1)}, bf16[32,8,128]{2,1,0:T(8,128)(2,1)}, bf16[8,256,128]{2,1,0:T(8,128)(2,1)S(1)}) custom-call(bf16[32,8,128]{2,1,0:T(8,128)(2,1)S(1)} %all-to-all-done.1.bias_ref, f32[16,128]{1,0:T(8,128)S(1)} %get-tuple-element.47.aux_ref.mask_ref, f32[8,256,128]{2,1,0:T(8,128)S(1)} %get-tuple-element.57.score_ref, ...), custom_call_target="tpu_custom_call" | custom-call | flops 268435456 | bytes 4194304 | tf_op jit(solution)/shard_map/pallas_call | solution.py:700
  33.3 2.9 %all-to-all-start.2 = ((bf16[32,8,128]{2,1,0:T(8,128)(2,1)}), bf16[32,8,128]{2,1,0:T(8,128)(2,1)S(1)}, u32[]{:S(2)}, u32[]{:S(2)}) async-start(bf16[32,8,128]{2,1,0:T(8,128)(2,1)} %get-tuple-element.70), calls=%async_computation.2 | async-start | bytes 131072 | tf_op jit(solution)/shard_map/all_to_all | solution.py:712
  36.2 0.0 copy-done.7
  36.2 0.4 shard_map.162
  36.6 0.3 collective-permute-start.9
  37.0 1.7 %collective-permute-start.10 = (bf16[128,128]{1,0:T(8,128)(2,1)S(1)}, bf16[128,128]{1,0:T(8,128)(2,1)S(1)}, u32[]{:S(2)}, u32[]{:S(2)}) collective-permute-start(bf16[128,128]{1,0:T(8,128)(2,1)S(1)} %get-tuple-element.67), channel_id=1, source_target_pairs={{0,2},{1,3},{2,0},{3,1},{4,6},{5,7},{6,4},{7,5},{8,10},{9,11},{10,... | collective-permute-start | bytes 98312 | tf_op jit(solution)/shard_map/ppermute | solution.py:660
  38.6 0.0 collective-permute-start.11
  38.6 0.0 collective-permute-done.9.refs_1_
  38.6 2.4 %collective-permute-done.10.refs_2_ = bf16[128,128]{1,0:T(8,128)(2,1)S(1)} collective-permute-done((bf16[128,128]{1,0:T(8,128)(2,1)S(1)}, bf16[128,128]{1,0:T(8,128)(2,1)S(1)}, u32[]{:S(2)}, u32[]{:S(2)}) %collective-permute-start.10) | collective-permute-done | bytes 32800 | tf_op jit(solution)/shard_map/ppermute | solution.py:660
  41.0 1.2 %collective-permute-done.11.refs_3_ = bf16[128,128]{1,0:T(8,128)(2,1)S(1)} collective-permute-done((bf16[128,128]{1,0:T(8,128)(2,1)S(1)}, bf16[128,128]{1,0:T(8,128)(2,1)S(1)}, u32[]{:S(2)}, u32[]{:S(2)}) %collective-permute-start.11) | collective-permute-done | bytes 32800 | tf_op jit(solution)/shard_map/ppermute | solution.py:660
  42.2 0.9 %shard_map.163 = bf16[256,256]{1,0:T(8,128)(2,1)} custom-call(f32[4,128,128]{2,1,0:T(8,128)S(1)} %get-tuple-element.45.gate_ref, bf16[256,256]{1,0:T(8,128)(2,1)S(1)} %copy-done, bf16[128,128]{1,0:T(8,128)(2,1)S(1)} %get-tuple-element.65.refs_0_, bf16[128,128]{1,0:T(8,128)(2,1)S(1)} %collective-permute-done.9.refs_1_, ...), custom_call_target="tpu_custom_call" | custom-call | flops 33554432 | bytes 1048576 | tf_op jit(solution)/shard_map/pallas_call | solution.py:720
  43.2 0.4 all-to-all-done.2.shares_ref
  43.6 0.0 copy-done.1
  43.6 1.2 %shard_map.164 = f32[4,128,128]{2,1,0:T(8,128)} custom-call(bf16[32,8,128]{2,1,0:T(8,128)(2,1)S(1)} %all-to-all-done.2.shares_ref, f32[16,128]{1,0:T(8,128)S(1)} %get-tuple-element.47.aux_ref.mask_ref, bf16[4,128,128]{2,1,0:T(8,128)(2,1)S(1)} %copy-done.1), custom_call_target="tpu_custom_call" | custom-call | flops 16777216 | bytes 1048576 | tf_op jit(solution)/shard_map/pallas_call | solution.py:727
  (3 shorter events, 0.0 us)
Async XLA Ops:
  0.6 11.7 %copy-start.12 = (bf16[256,256]{1,0:T(8,128)(2,1)S(1)}, bf16[256,256]{1,0:T(8,128)(2,1)}, u32[]{:S(2)}) copy-start(bf16[256,256]{1,0:T(8,128)(2,1)} %param.23) | copy-start | bytes 393220
  2.9 9.4 %copy-start.9 = (bf16[256,256]{1,0:T(8,128)(2,1)S(1)}, bf16[256,256]{1,0:T(8,128)(2,1)}, u32[]{:S(2)}) copy-start(bf16[256,256]{1,0:T(8,128)(2,1)} %param.26) | copy-start | bytes 393220
  3.0 9.3 %copy-start.10 = (bf16[256,256]{1,0:T(8,128)(2,1)S(1)}, bf16[256,256]{1,0:T(8,128)(2,1)}, u32[]{:S(2)}) copy-start(bf16[256,256]{1,0:T(8,128)(2,1)} %param.25) | copy-start | bytes 393220
  3.0 9.3 %copy-start.11 = (bf16[256,256]{1,0:T(8,128)(2,1)S(1)}, bf16[256,256]{1,0:T(8,128)(2,1)}, u32[]{:S(2)}) copy-start(bf16[256,256]{1,0:T(8,128)(2,1)} %param.24) | copy-start | bytes 393220
  3.0 16.2 %all-to-all-start = ((bf16[32,24,128]{2,1,0:T(8,128)(2,1)}), bf16[32,24,128]{2,1,0:T(8,128)(2,1)S(1)}, u32[]{:S(2)}, u32[]{:S(2)}) async-start(bf16[32,24,128]{2,1,0:T(8,128)(2,1)} %bitcast.21), calls=%async_computation | async-start | bytes 393216 | tf_op jit(solution)/shard_map/all_to_all | solution.py:632
  10.3 5.8 %collective-permute-start = (bf16[4,32,128]{2,1,0:T(8,128)(2,1)}, bf16[4,32,128]{2,1,0:T(8,128)(2,1)S(1)}, u32[]{:S(2)}, u32[]{:S(2)}) collective-permute-start(bf16[4,32,128]{2,1,0:T(8,128)(2,1)} %get-tuple-element.49), channel_id=1, source_target_pairs={{0,1},{1,0},{2,3},{3,2},{4,5},{5,4},{6,7},{7,6},{8,9},{9,8},{10,11... | collective-permute-start | bytes 98312 | tf_op jit(solution)/shard_map/ppermute | solution.py:660
  10.6 5.8 %collective-permute-start.1 = (bf16[4,32,128]{2,1,0:T(8,128)(2,1)}, bf16[4,32,128]{2,1,0:T(8,128)(2,1)S(1)}, u32[]{:S(2)}, u32[]{:S(2)}) collective-permute-start(bf16[4,32,128]{2,1,0:T(8,128)(2,1)} %get-tuple-element.50), channel_id=1, source_target_pairs={{0,2},{1,3},{2,0},{3,1},{4,6},{5,7},{6,4},{7,5},{8,10},{9,11},{10,... | collective-permute-start | bytes 98312 | tf_op jit(solution)/shard_map/ppermute | solution.py:660
  12.3 4.1 %collective-permute-start.2 = (bf16[4,32,128]{2,1,0:T(8,128)(2,1)}, bf16[4,32,128]{2,1,0:T(8,128)(2,1)S(1)}, u32[]{:S(2)}, u32[]{:S(2)}) collective-permute-start(bf16[4,32,128]{2,1,0:T(8,128)(2,1)} %get-tuple-element.51), channel_id=1, source_target_pairs={{0,3},{1,2},{2,1},{3,0},{4,7},{5,6},{6,5},{7,4},{8,11},{9,10},{10,... | collective-permute-start | bytes 98312 | tf_op jit(solution)/shard_map/ppermute | solution.py:660
  12.3 0.9 %copy-start = (bf16[256,256]{1,0:T(8,128)(2,1)S(1)}, bf16[256,256]{1,0:T(8,128)(2,1)}, u32[]{:S(2)}) copy-start(bf16[256,256]{1,0:T(8,128)(2,1)} %wo_ref.3) | copy-start | bytes 393220
  12.3 1.0 %copy-start.2 = (bf16[2,128,256]{2,1,0:T(8,128)(2,1)S(1)}, bf16[2,128,256]{2,1,0:T(8,128)(2,1)}, u32[]{:S(2)}) copy-start(bf16[2,128,256]{2,1,0:T(8,128)(2,1)} %param.16) | copy-start | bytes 393220
  12.3 1.0 %copy-start.3 = (bf16[256,256]{1,0:T(8,128)(2,1)S(1)}, bf16[256,256]{1,0:T(8,128)(2,1)}, u32[]{:S(2)}) copy-start(bf16[256,256]{1,0:T(8,128)(2,1)} %get-tuple-element.38.normed_ref) | copy-start | bytes 393220
  12.4 1.0 %copy-start.4 = (bf16[4,32,128]{2,1,0:T(8,128)(2,1)S(1)}, bf16[4,32,128]{2,1,0:T(8,128)(2,1)}, u32[]{:S(2)}) copy-start(bf16[4,32,128]{2,1,0:T(8,128)(2,1)} %get-tuple-element.44.pair_ref) | copy-start | bytes 98308
  12.4 1.0 %copy-start.5 = (f32[16,128]{1,0:T(8,128)S(1)}, f32[16,128]{1,0:T(8,128)}, u32[]{:S(2)}) copy-start(f32[16,128]{1,0:T(8,128)} %get-tuple-element.43.aux_ref) | copy-start | bytes 24580
  13.4 2.7 %copy-start.8 = (bf16[32,32,128]{2,1,0:T(8,128)(2,1)S(1)}, bf16[32,32,128]{2,1,0:T(8,128)(2,1)}, u32[]{:S(2)}) copy-start(bf16[32,32,128]{2,1,0:T(8,128)(2,1)} %param.21) | copy-start | bytes 786436
  13.9 12.6 %collective-permute-start.3 = (bf16[4,128,128]{2,1,0:T(8,128)(2,1)S(1)}, bf16[4,128,128]{2,1,0:T(8,128)(2,1)S(1)}, u32[]{:S(2)}, u32[]{:S(2)}) collective-permute-start(bf16[4,128,128]{2,1,0:T(8,128)(2,1)S(1)} %get-tuple-element.54), channel_id=1, source_target_pairs={{0,1},{1,0},{2,3},{3,2},{4,5},{5,4},{6,7},{7,6},{8,9},{9,8},{10,11... | collective-permute-start | bytes 393224 | tf_op jit(solution)/shard_map/ppermute | solution.py:660
  14.4 12.1 %collective-permute-start.4 = (bf16[4,128,128]{2,1,0:T(8,128)(2,1)S(1)}, bf16[4,128,128]{2,1,0:T(8,128)(2,1)S(1)}, u32[]{:S(2)}, u32[]{:S(2)}) collective-permute-start(bf16[4,128,128]{2,1,0:T(8,128)(2,1)S(1)} %get-tuple-element.55), channel_id=1, source_target_pairs={{0,2},{1,3},{2,0},{3,1},{4,6},{5,7},{6,4},{7,5},{8,10},{9,11},{10,... | collective-permute-start | bytes 393224 | tf_op jit(solution)/shard_map/ppermute | solution.py:660
  16.1 10.4 %collective-permute-start.5 = (bf16[4,128,128]{2,1,0:T(8,128)(2,1)S(1)}, bf16[4,128,128]{2,1,0:T(8,128)(2,1)S(1)}, u32[]{:S(2)}, u32[]{:S(2)}) collective-permute-start(bf16[4,128,128]{2,1,0:T(8,128)(2,1)S(1)} %get-tuple-element.56), channel_id=1, source_target_pairs={{0,3},{1,2},{2,1},{3,0},{4,7},{5,6},{6,5},{7,4},{8,11},{9,10},{10,... | collective-permute-start | bytes 393224 | tf_op jit(solution)/shard_map/ppermute | solution.py:660
  21.4 10.4 %all-to-all-start.1 = ((bf16[32,8,128]{2,1,0:T(8,128)(2,1)}), bf16[32,8,128]{2,1,0:T(8,128)(2,1)S(1)}, u32[]{:S(2)}, u32[]{:S(2)}) async-start(bf16[32,8,128]{2,1,0:T(8,128)(2,1)} %bitcast.11), calls=%async_computation.1 | async-start | bytes 131072 | tf_op jit(solution)/shard_map/all_to_all | solution.py:695
  24.5 3.2 %collective-permute-start.6 = (bf16[4,32,128]{2,1,0:T(8,128)(2,1)S(1)}, bf16[4,32,128]{2,1,0:T(8,128)(2,1)S(1)}, u32[]{:S(2)}, u32[]{:S(2)}) collective-permute-start(bf16[4,32,128]{2,1,0:T(8,128)(2,1)S(1)} %get-tuple-element.60), channel_id=1, source_target_pairs={{0,1},{1,0},{2,3},{3,2},{4,5},{5,4},{6,7},{7,6},{8,9},{9,8},{10,11... | collective-permute-start | bytes 98312 | tf_op jit(solution)/shard_map/ppermute | solution.py:660
  24.8 4.0 %collective-permute-start.7 = (bf16[4,32,128]{2,1,0:T(8,128)(2,1)S(1)}, bf16[4,32,128]{2,1,0:T(8,128)(2,1)S(1)}, u32[]{:S(2)}, u32[]{:S(2)}) collective-permute-start(bf16[4,32,128]{2,1,0:T(8,128)(2,1)S(1)} %get-tuple-element.61), channel_id=1, source_target_pairs={{0,2},{1,3},{2,0},{3,1},{4,6},{5,7},{6,4},{7,5},{8,10},{9,11},{10,... | collective-permute-start | bytes 98312 | tf_op jit(solution)/shard_map/ppermute | solution.py:660
  26.5 3.5 %collective-permute-start.8 = (bf16[4,32,128]{2,1,0:T(8,128)(2,1)S(1)}, bf16[4,32,128]{2,1,0:T(8,128)(2,1)S(1)}, u32[]{:S(2)}, u32[]{:S(2)}) collective-permute-start(bf16[4,32,128]{2,1,0:T(8,128)(2,1)S(1)} %get-tuple-element.62), channel_id=1, source_target_pairs={{0,3},{1,2},{2,1},{3,0},{4,7},{5,6},{6,5},{7,4},{8,11},{9,10},{10,... | collective-permute-start | bytes 98312 | tf_op jit(solution)/shard_map/ppermute | solution.py:660
  26.9 0.7 %copy-start.6 = (bf16[8,128,128]{2,1,0:T(8,128)(2,1)}, bf16[8,128,128]{2,1,0:T(8,128)(2,1)S(1)}, u32[]{:S(2)}) copy-start(bf16[8,128,128]{2,1,0:T(8,128)(2,1)S(1)} %get-tuple-element.64.value_ref) | copy-start | bytes 786436
  31.9 4.3 %copy-start.7 = (bf16[8,128,128]{2,1,0:T(8,128)(2,1)S(1)}, bf16[8,128,128]{2,1,0:T(8,128)(2,1)}, u32[]{:S(2)}) copy-start(bf16[8,128,128]{2,1,0:T(8,128)(2,1)} %copy-done.6) | copy-start | bytes 786436
  33.3 10.3 %all-to-all-start.2 = ((bf16[32,8,128]{2,1,0:T(8,128)(2,1)}), bf16[32,8,128]{2,1,0:T(8,128)(2,1)S(1)}, u32[]{:S(2)}, u32[]{:S(2)}) async-start(bf16[32,8,128]{2,1,0:T(8,128)(2,1)} %get-tuple-element.70), calls=%async_computation.2 | async-start | bytes 131072 | tf_op jit(solution)/shard_map/all_to_all | solution.py:712
  36.6 2.0 %collective-permute-start.9 = (bf16[128,128]{1,0:T(8,128)(2,1)S(1)}, bf16[128,128]{1,0:T(8,128)(2,1)S(1)}, u32[]{:S(2)}, u32[]{:S(2)}) collective-permute-start(bf16[128,128]{1,0:T(8,128)(2,1)S(1)} %get-tuple-element.66), channel_id=1, source_target_pairs={{0,1},{1,0},{2,3},{3,2},{4,5},{5,4},{6,7},{7,6},{8,9},{9,8},{10,11... | collective-permute-start | bytes 98312 | tf_op jit(solution)/shard_map/ppermute | solution.py:660
  37.0 4.0 %collective-permute-start.10 = (bf16[128,128]{1,0:T(8,128)(2,1)S(1)}, bf16[128,128]{1,0:T(8,128)(2,1)S(1)}, u32[]{:S(2)}, u32[]{:S(2)}) collective-permute-start(bf16[128,128]{1,0:T(8,128)(2,1)S(1)} %get-tuple-element.67), channel_id=1, source_target_pairs={{0,2},{1,3},{2,0},{3,1},{4,6},{5,7},{6,4},{7,5},{8,10},{9,11},{10,... | collective-permute-start | bytes 98312 | tf_op jit(solution)/shard_map/ppermute | solution.py:660
  38.6 3.6 %collective-permute-start.11 = (bf16[128,128]{1,0:T(8,128)(2,1)S(1)}, bf16[128,128]{1,0:T(8,128)(2,1)S(1)}, u32[]{:S(2)}, u32[]{:S(2)}) collective-permute-start(bf16[128,128]{1,0:T(8,128)(2,1)S(1)} %get-tuple-element.68), channel_id=1, source_target_pairs={{0,3},{1,2},{2,1},{3,0},{4,7},{5,6},{6,5},{7,4},{8,11},{9,10},{10,... | collective-permute-start | bytes 98312 | tf_op jit(solution)/shard_map/ppermute | solution.py:660
  42.2 1.4 %copy-start.1 = (bf16[4,128,128]{2,1,0:T(8,128)(2,1)S(1)}, bf16[4,128,128]{2,1,0:T(8,128)(2,1)}, u32[]{:S(2)}) copy-start(bf16[4,128,128]{2,1,0:T(8,128)(2,1)} %get-tuple-element.35.pair_ref) | copy-start | bytes 393220

commit v8 on v7

--- a/solution.py
+++ b/solution.py
@@ -288,7 +288,7 @@
         own = normed[s * residues : (s + 1) * residues]
         factor = dot_nt(right_t, own) * (live * seq_live)
         quarters.append(swap_groups([factor[a * 8 : (a + 1) * 8] for a in range(4)]))
-        left_scr[...] = dot_nt(own, left_wide) * (live_rows * seq_live)
+        left_scr[:residues] = dot_nt(own, left_wide) * (live_rows * seq_live)
         for a in range(4):
             row = jnp.zeros((lines, LANES), f32)
             for b in range(4):
@@ -392,7 +392,10 @@
     seqs = block_rows // 12
     for step in range(GROUP):
         state[partner(step)] = pair_refs[step][...]
-    flat[...] = recv_ref[...].astype(f32).reshape(flat.shape)
+    before = [
+        jnp.concatenate([state[a, b] for a in range(GROUP)], axis=0).astype(f32).T for b in range(4)
+    ]
+    flat[: peers * block_rows] = recv_ref[...].astype(f32).reshape(peers * block_rows, LANES)
     for s in range(seqs):
         for g in range(8):
             part = flat[pl.ds(s * 8 + g, peers, stride=block_rows), :]
@@ -424,12 +427,15 @@
     blocks = []
     for b in range(4):
         update = sums[:, b * LANES : (b + 1) * LANES] / aux_ref[b : b + 1, :]
-        before = jnp.concatenate([state[a, b] for a in range(GROUP)], axis=0).astype(f32)
-        updated = (before + update.T).astype(bf16)
+        updated = (before[b] + update).astype(bf16)
+        values = updated.astype(f32)
+        center = values - jnp.mean(values, axis=0, keepdims=True)
+        spread = jnp.mean(center * center, axis=0, keepdims=True)
+        line = dot_nn(bias_w, (center * lax.rsqrt(spread + norm_eps)).astype(bf16))
+        blocks.append(pltpu.roll(line, partner(0) * 32, 1))
+        values = values.T.astype(bf16)
         for a in range(GROUP):
-            after[a, b] = updated[a * 32 : (a + 1) * 32]
-        line = dot_nt(bias_w, layer_normalize(updated).astype(bf16))
-        blocks.append(pltpu.roll(line, partner(0) * 32, 1))
+            after[a, b] = values[a * 32 : (a + 1) * 32]
     lines, _, share, _ = send_ref.shape
     heads = share // 4
     for t in range(GROUP):
@@ -440,7 +446,7 @@
 
 
 def place_bias(flat, mask_ref, heads, h, bias):
-    lines = bias.shape[0] // 16
+    lines = bias.shape[0] // 16 - 1
     lane_group = lane_index(lines) // 32
     mask = mask_ref[4:5, :]
     for b in range(4):
@@ -462,12 +468,12 @@
         pair_ref[:, pl.ds(first, columns_each), :] = part_refs[step][...]
     seqs, rows, residues = score_ref.shape
     heads = rows // residues
-    flat[...] = bias_ref[...].reshape(flat.shape).astype(f32)
+    flat[:rows] = bias_ref[...].reshape(rows, LANES).astype(f32)
     ones = jnp.ones((residues, LANES), bf16)
     for h in range(heads):
         at = slice(h * residues, (h + 1) * residues)
         place_bias(flat, mask_ref, heads, h, placed.at[h])
-        bias = placed[h]
+        bias = placed[h, :residues]
         total = jnp.zeros((residues, residues), f32)
         for s in range(seqs):
             scores = score_ref[s, at, :] + bias
@@ -479,7 +485,7 @@
             delta = dot_nn((weights * flow).astype(bf16), ones) * inverse
             total = total + weights * inverse * (flow - delta)
         grads[pl.ds(h, residues, stride=heads), :] = total
-    send_ref[...] = grads[...].astype(bf16).reshape(send_ref.shape)
+    send_ref[...] = grads[:rows].astype(bf16).reshape(send_ref.shape)
 
 
 def attended_kernel(weights_ref, value_ref, *out_refs):
@@ -518,9 +524,17 @@
     return high, (values - high.astype(f32)).astype(bf16)
 
 
-def gradient_kernel(shares_ref, aux_ref, pair_ref, out_hbm, result, left_for):
+def normal_kernel(pair_ref, normal_ref, inverse_ref):
+    values = pair_ref[...].astype(f32)
+    center = values - jnp.mean(values, axis=-1, keepdims=True)
+    inverse = lax.rsqrt(jnp.mean(center * center, axis=-1, keepdims=True) + norm_eps)
+    normal_ref[...] = center * inverse
+    inverse_ref[...] = jnp.broadcast_to(inverse, values.shape)
+
+
+def gradient_kernel(shares_ref, aux_ref, normal_ref, inverse_ref, out_hbm, result, left_for):
     peers, share, _ = shares_ref.shape
-    rows, _, channels = pair_ref.shape
+    rows, _, channels = normal_ref.shape
     heads = share // rows
     total = jnp.sum(shares_ref[...].astype(f32).reshape(peers // GROUP, GROUP, share, LANES), axis=0)
     bias_w = aux_ref[8:16]
@@ -543,11 +557,8 @@
         high, low = split_sum(own)
         both = dot_tn(jnp.concatenate([high, low, high], axis=0), weights)
         upstream, mean = both[:, :channels], both[:, channels:]
-        values = pair_ref[i].astype(f32)
-        center = values - jnp.mean(values, axis=-1, keepdims=True)
-        inverse = lax.rsqrt(jnp.mean(center * center, axis=-1, keepdims=True) + norm_eps)
-        normal = center * inverse
-        result[i] = inverse * (
+        normal = normal_ref[i]
+        result[i] = inverse_ref[i] * (
             upstream - mean - normal * jnp.mean(upstream * normal, axis=-1, keepdims=True)
         )
         moves.append(pltpu.make_async_copy(result.at[i], out_hbm.at[i], left_for.at[i]))
@@ -613,7 +624,7 @@
         ]
         + [shape((rows_here, columns_each, pair_channels), bf16)] * GROUP,
         [smem] * 2 + [vmem] * 6 + pieces,
-        [pltpu.VMEM((residues, LANES), f32)],
+        [pltpu.VMEM((residues + 4 * GROUP, LANES), f32)],
         flops=2 * token_rows * channel_count * LANES,
         moved=1 << 20,
         vmem_mib=60,
@@ -682,7 +693,7 @@
         [shape((lines, GROUP, share_rows, LANES), bf16)] + [part_shape] * GROUP,
         [vmem] * (3 + GROUP),
         [
-            pltpu.VMEM((peers * block_rows, LANES), f32),
+            pltpu.VMEM(((peers + 1) * block_rows, LANES), f32),
             pltpu.VMEM((4, peers * sequence_wise, 8 * LANES), bf16),
             pltpu.VMEM((peers * sequence_wise, 4 * LANES), f32),
             pltpu.VMEM((4, 8 * factor, 4 * LANES), bf16),
@@ -705,7 +716,8 @@
             shape((GROUP * sequence_wise, head_rows, residues), bf16),
         ],
         [vmem] * (4 + GROUP),
-        [pltpu.VMEM((head_rows, LANES), f32)] * 2 + [pltpu.VMEM((group_heads, residues, LANES), f32)],
+        [pltpu.VMEM((head_rows + 16 * group_heads, LANES), f32)] * 2
+        + [pltpu.VMEM((group_heads, residues + 16, LANES), f32)],
         flops=1 << 28,
         moved=1 << 22,
     )(bias_all, aux, scores, flow, *updated)
@@ -724,15 +736,22 @@
         flops=2 * token_rows * channel_count * channel_count,
         moved=1 << 20,
     )(gate, output_weight, *trade(list(attended)))
+    normal, inverse = kernel_call(
+        normal_kernel,
+        [shape((rows_here, residues, pair_channels), f32)] * 2,
+        [vmem],
+        flops=1 << 22,
+        moved=1 << 20,
+    )(pair_updated)
     pair_gradient = kernel_call(
         gradient_kernel,
         shape((rows_here, residues, pair_channels), f32),
-        [vmem] * 3,
+        [vmem] * 4,
         [pltpu.VMEM((rows_here, residues, pair_channels), f32), pltpu.SemaphoreType.DMA((rows_here,))],
         flops=1 << 24,
         moved=1 << 20,
         out_specs=pl.BlockSpec(memory_space=pltpu.HBM),
-    )(shares, aux, pair_updated)
+    )(shares, aux, normal, inverse)
     return (update.reshape(alignment_rows.shape), pair_updated, pair_gradient)
 
 

time: 45.1 us -> 44.7 us (level)
  no operation moved by 1% of the time
where the time goes in v8:
time: 44.7 us; the launch traced here: 44.4 us
  starting transfers between devices  21.4 us (48%)
  waiting for transfers between devices  10.8 us (24%)
  Pallas kernels  9.35 us (21%)
  local copies, waits for them, and re-layouts  1.92 us (4%)
  between operations  0.88 us (2%)
    ppermute x12, starting transfers between devices, trade(): lax.ppermute(parts[d], 'row', [(i, i ^ d) for i in range(peers)])  8.2 us
    all_to_all x1, starting transfers between devices, on_device_paired(): lax.all_to_all(send.reshape(peers, block_rows, LANES), 'row', split_axis=...  7.3 us
    ppermute x12, waiting for transfers between devices, trade(): lax.ppermute(parts[d], 'row', [(i, i ^ d) for i in range(peers)])  5.71 us
    all_to_all x1, starting transfers between devices, on_device_paired(): lax.all_to_all(send_bias.reshape(peers, share_rows, LANES), 'row', split_...  3.01 us
    all_to_all x1, starting transfers between devices, on_device_paired(): lax.all_to_all(send_grad, 'row', split_axis=0, concat_axis=0, tiled=True)  2.91 us
    all_to_all x1, waiting for transfers between devices, on_device_paired(): lax.all_to_all(send.reshape(peers, block_rows, LANES), 'row', split_axis=...  2.8 us
    pallas_call x1, Pallas kernels, on_device_paired(): kernel_call(factors_kernel, [shape((lines, GROUP, block_rows, LANES), bf1...  2.3 us
    pallas_call x1, Pallas kernels, on_device_paired(): kernel_call(pair_kernel, [shape((lines, GROUP, share_rows, LANES), bf16)]...  2.01 us
  transfers between devices with their start and end apart: 15, of which 7 were waited for; matrix products, arithmetic and copies ran while one was open for 1% of the time, Pallas kernels for 10%

profile of v8, /device:TPU:0, one launch (start us, length us, event | category | flops | bytes accessed | tf_op | source)
XLA Modules:
  0.0 44.4 jit_solution(13283419988807042056)
XLA Ops:
  0.6 0.0 copy-start.12
  0.6 2.3 %shard_map.157 = (bf16[8,4,24,128]{3,2,1,0:T(8,128)(2,1)}, f32[16,128]{1,0:T(8,128)}, bf16[256,256]{1,0:T(8,128)(2,1)}, bf16[4,32,128]{2,1,0:T(8,128)(2,1)}, bf1...) custom-call(s32[64]{0:T(128)} %seq_smem_ref.1, s32[128]{0:T(128)} %res_smem_ref.1, ...), custom_call_target="tpu_custom_call" | custom-call | flops 16777216 | bytes 1048576 | tf_op jit(solution)/shard_map/pallas_call | solution.py:618
  2.9 0.0 copy-start.9
  3.0 0.0 copy-start.10
  3.0 0.0 copy-start.11
  3.0 7.3 %all-to-all-start = ((bf16[32,24,128]{2,1,0:T(8,128)(2,1)}), bf16[32,24,128]{2,1,0:T(8,128)(2,1)S(1)}, u32[]{:S(2)}, u32[]{:S(2)}) async-start(bf16[32,24,128]{2,1,0:T(8,128)(2,1)} %bitcast.21), calls=%async_computation | async-start | bytes 393216 | tf_op jit(solution)/shard_map/all_to_all | solution.py:643
  10.3 0.3 collective-permute-start
  10.6 1.7 %collective-permute-start.1 = (bf16[4,32,128]{2,1,0:T(8,128)(2,1)}, bf16[4,32,128]{2,1,0:T(8,128)(2,1)S(1)}, u32[]{:S(2)}, u32[]{:S(2)}) collective-permute-start(bf16[4,32,128]{2,1,0:T(8,128)(2,1)} %get-tuple-element.52), channel_id=1, source_target_pairs={{0,2},{1,3},{2,0},{3,1},{4,6},{5,7},{6,4},{7,5},{8,10},{9,11},{10,... | collective-permute-start | bytes 98312 | tf_op jit(solution)/shard_map/ppermute | solution.py:671
  12.3 0.0 collective-permute-start.2
  12.3 0.0 copy-done.12
  12.3 0.0 copy-done.9
  12.3 0.0 copy-done.10
  12.3 0.0 copy-done.11
  12.3 0.0 copy-start
  12.3 0.0 copy-start.2
  12.3 0.0 copy-start.3
  12.4 0.0 copy-start.4
  12.4 0.0 copy-start.5
  12.4 0.1 pad_maximum_fusion.weights_ref
  12.4 0.8 %copy-done = bf16[256,256]{1,0:T(8,128)(2,1)S(1)} copy-done((bf16[256,256]{1,0:T(8,128)(2,1)S(1)}, bf16[256,256]{1,0:T(8,128)(2,1)}, u32[]{:S(2)}) %copy-start) | copy-done | bytes 131096
  13.2 0.1 copy-done.2
  13.3 0.1 copy-done.3
  13.4 0.0 copy-done.4
  13.4 0.0 copy-done.5
  13.4 0.5 %shard_map.158 = (f32[4,128,128]{2,1,0:T(8,128)S(1)}, f32[16,128]{1,0:T(8,128)S(1)}, bf16[4,32,128]{2,1,0:T(8,128)(2,1)S(1)}, bf16[4,128,128]{2,1,0:T(8,128)(2,1...) custom-call(bf16[256,256]{1,0:T(8,128)(2,1)S(1)} %copy-done.3, ...), custom_call_target="tpu_custom_call" | custom-call | flops 167772160 | bytes 2097152 | tf_op jit(solution)/shard_map/pallas_call | solution.py:652
  13.9 0.5 %collective-permute-start.3 = (bf16[4,128,128]{2,1,0:T(8,128)(2,1)S(1)}, bf16[4,128,128]{2,1,0:T(8,128)(2,1)S(1)}, u32[]{:S(2)}, u32[]{:S(2)}) collective-permute-start(bf16[4,128,128]{2,1,0:T(8,128)(2,1)S(1)} %get-tuple-element.56), channel_id=1, source_target_pairs={{0,1},{1,0},{2,3},{3,2},{4,5},{5,4},{6,7},{7,6},{8,9},{9,8},{10,11... | collective-permute-start | bytes 393224 | tf_op jit(solution)/shard_map/ppermute | solution.py:671
  14.4 1.7 %collective-permute-start.4 = (bf16[4,128,128]{2,1,0:T(8,128)(2,1)S(1)}, bf16[4,128,128]{2,1,0:T(8,128)(2,1)S(1)}, u32[]{:S(2)}, u32[]{:S(2)}) collective-permute-start(bf16[4,128,128]{2,1,0:T(8,128)(2,1)S(1)} %get-tuple-element.57), channel_id=1, source_target_pairs={{0,2},{1,3},{2,0},{3,1},{4,6},{5,7},{6,4},{7,5},{8,10},{9,11},{10,... | collective-permute-start | bytes 393224 | tf_op jit(solution)/shard_map/ppermute | solution.py:671
  16.1 0.0 collective-permute-done.refs_1_
  16.1 0.0 collective-permute-start.5
  16.1 0.1 copy.18
  16.2 0.1 copy.19.weight_ref
  16.4 0.0 collective-permute-done.1.refs_2_
  16.4 0.0 collective-permute-done.2.refs_3_
  16.4 2.8 %all-to-all-done.recv_ref = bf16[32,24,128]{2,1,0:T(8,128)(2,1)S(1)} async-done(((bf16[32,24,128]{2,1,0:T(8,128)(2,1)}), bf16[32,24,128]{2,1,0:T(8,128)(2,1)S(1)}, u32[]{:S(2)}, u32[]{:S(2)}) %all-to-all-start) | async-done | bytes 196640 | tf_op jit(solution)/shard_map/all_to_all | solution.py:643
  19.2 2.0 %shard_map.159 = (bf16[8,4,8,128]{3,2,1,0:T(8,128)(2,1)}, bf16[4,32,128]{2,1,0:T(8,128)(2,1)S(1)}, bf16[4,32,128]{2,1,0:T(8,128)(2,1)S(1)}, bf16[4,32,128]{2,1,0:T(8,128)(2,1)S(1)}, bf16[4,32,128]{2,1,0:T(8,128)(2,1)S(1)}) custom-call(bf16[32,24,128]{2,1,0:T(8,128)(2,1)S(1)} %all-to-all-done.recv_ref, bf16[4,128,256]{2,1,0:T(8,128)(2,1)S(1)} %copy.19.weight_ref, ...), custom_call_target="tpu_custom_call" | custom-call | flops 268435456 | bytes 1048576 | tf_op jit(solution)/shard_map/pallas_call | solution.py:691
  21.2 3.0 %all-to-all-start.1 = ((bf16[32,8,128]{2,1,0:T(8,128)(2,1)}), bf16[32,8,128]{2,1,0:T(8,128)(2,1)S(1)}, u32[]{:S(2)}, u32[]{:S(2)}) async-start(bf16[32,8,128]{2,1,0:T(8,128)(2,1)} %bitcast.11), calls=%async_computation.1 | async-start | bytes 131072 | tf_op jit(solution)/shard_map/all_to_all | solution.py:706
  24.2 0.3 collective-permute-start.6
  24.5 1.7 %collective-permute-start.7 = (bf16[4,32,128]{2,1,0:T(8,128)(2,1)S(1)}, bf16[4,32,128]{2,1,0:T(8,128)(2,1)S(1)}, u32[]{:S(2)}, u32[]{:S(2)}) collective-permute-start(bf16[4,32,128]{2,1,0:T(8,128)(2,1)S(1)} %get-tuple-element.63), channel_id=1, source_target_pairs={{0,2},{1,3},{2,0},{3,1},{4,6},{5,7},{6,4},{7,5},{8,10},{9,11},{10,... | collective-permute-start | bytes 98312 | tf_op jit(solution)/shard_map/ppermute | solution.py:671
  26.2 0.0 collective-permute-done.3.refs_1_
  26.2 0.0 collective-permute-start.8
  26.2 0.0 collective-permute-done.4.refs_2_
  26.2 0.0 collective-permute-done.5.refs_3_
  26.2 0.5 %shard_map.160 = (f32[8,256,128]{2,1,0:T(8,128)S(1)}, f32[8,256,128]{2,1,0:T(8,128)S(1)}, bf16[8,128,128]{2,1,0:T(8,128)(2,1)S(1)}) custom-call(bf16[4,128,128]{2,1,0:T(8,128)(2,1)S(1)} %get-tuple-element.55.refs_0_, bf16[4,128,128]{2,1,0:T(8,128)(2,1)S(1)} %collective-permute-done.3.refs_1_, bf16[4,128,128]{2,1,0:T(8,128)(2,1)S(1)} %collective-permute-done.4.refs_2_, ...), custom_call_target="tpu_custom_call" | custom-call | flops 268435456 | bytes 2097152 | tf_op jit(solution)/shard_map/pallas_call | solution.py:676
  26.7 0.0 copy-start.6
  26.7 0.7 %copy-done.6 = bf16[8,128,128]{2,1,0:T(8,128)(2,1)} copy-done((bf16[8,128,128]{2,1,0:T(8,128)(2,1)}, bf16[8,128,128]{2,1,0:T(8,128)(2,1)S(1)}, u32[]{:S(2)}) %copy-start.6) | copy-done | bytes 262168
  27.4 0.0 collective-permute-done.6.refs_1_
  27.4 1.1 %collective-permute-done.7.refs_2_ = bf16[4,32,128]{2,1,0:T(8,128)(2,1)S(1)} collective-permute-done((bf16[4,32,128]{2,1,0:T(8,128)(2,1)S(1)}, bf16[4,32,128]{2,1,0:T(8,128)(2,1)S(1)}, u32[]{:S(2)}, u32[]{:S(2)}) %collective-permute-start.7) | collective-permute-done | bytes 32800 | tf_op jit(solution)/shard_map/ppermute | solution.py:671
  28.5 1.3 %collective-permute-done.8.refs_3_ = bf16[4,32,128]{2,1,0:T(8,128)(2,1)S(1)} collective-permute-done((bf16[4,32,128]{2,1,0:T(8,128)(2,1)S(1)}, bf16[4,32,128]{2,1,0:T(8,128)(2,1)S(1)}, u32[]{:S(2)}, u32[]{:S(2)}) %collective-permute-start.8) | collective-permute-done | bytes 32800 | tf_op jit(solution)/shard_map/ppermute | solution.py:671
  29.7 1.9 %all-to-all-done.1.bias_ref = bf16[32,8,128]{2,1,0:T(8,128)(2,1)S(1)} async-done(((bf16[32,8,128]{2,1,0:T(8,128)(2,1)}), bf16[32,8,128]{2,1,0:T(8,128)(2,1)S(1)}, u32[]{:S(2)}, u32[]{:S(2)}) %all-to-all-start.1) | async-done | bytes 65568 | tf_op jit(solution)/shard_map/all_to_all | solution.py:706
  31.6 1.4 %shard_map.161 = (bf16[4,128,128]{2,1,0:T(8,128)(2,1)}, bf16[32,8,128]{2,1,0:T(8,128)(2,1)}, bf16[8,256,128]{2,1,0:T(8,128)(2,1)S(1)}) custom-call(bf16[32,8,128]{2,1,0:T(8,128)(2,1)S(1)} %all-to-all-done.1.bias_ref, f32[16,128]{1,0:T(8,128)S(1)} %get-tuple-element.49.aux_ref.mask_ref, f32[8,256,128]{2,1,0:T(8,128)S(1)} %get-tuple-element.59.score_ref, ...), custom_call_target="tpu_custom_call" | custom-call | flops 268435456 | bytes 4194304 | tf_op jit(solution)/shard_map/pallas_call | solution.py:711
  33.0 2.9 %all-to-all-start.2 = ((bf16[32,8,128]{2,1,0:T(8,128)(2,1)}), bf16[32,8,128]{2,1,0:T(8,128)(2,1)S(1)}, u32[]{:S(2)}, u32[]{:S(2)}) async-start(bf16[32,8,128]{2,1,0:T(8,128)(2,1)} %get-tuple-element.72), calls=%async_computation.2 | async-start | bytes 131072 | tf_op jit(solution)/shard_map/all_to_all | solution.py:724
  35.9 0.0 copy-done.7
  35.9 0.0 copy-start.1
  36.0 0.4 shard_map.162
  36.4 0.3 collective-permute-start.9
  36.7 1.7 %collective-permute-start.10 = (bf16[128,128]{1,0:T(8,128)(2,1)S(1)}, bf16[128,128]{1,0:T(8,128)(2,1)S(1)}, u32[]{:S(2)}, u32[]{:S(2)}) collective-permute-start(bf16[128,128]{1,0:T(8,128)(2,1)S(1)} %get-tuple-element.69), channel_id=1, source_target_pairs={{0,2},{1,3},{2,0},{3,1},{4,6},{5,7},{6,4},{7,5},{8,10},{9,11},{10,... | collective-permute-start | bytes 98312 | tf_op jit(solution)/shard_map/ppermute | solution.py:671
  38.4 0.0 collective-permute-start.11
  38.4 0.2 shard_map.164
  38.6 0.0 collective-permute-done.9.refs_1_
  38.6 2.1 %collective-permute-done.10.refs_2_ = bf16[128,128]{1,0:T(8,128)(2,1)S(1)} collective-permute-done((bf16[128,128]{1,0:T(8,128)(2,1)S(1)}, bf16[128,128]{1,0:T(8,128)(2,1)S(1)}, u32[]{:S(2)}, u32[]{:S(2)}) %collective-permute-start.10) | collective-permute-done | bytes 32800 | tf_op jit(solution)/shard_map/ppermute | solution.py:671
  40.8 1.2 %collective-permute-done.11.refs_3_ = bf16[128,128]{1,0:T(8,128)(2,1)S(1)} collective-permute-done((bf16[128,128]{1,0:T(8,128)(2,1)S(1)}, bf16[128,128]{1,0:T(8,128)(2,1)S(1)}, u32[]{:S(2)}, u32[]{:S(2)}) %collective-permute-start.11) | collective-permute-done | bytes 32800 | tf_op jit(solution)/shard_map/ppermute | solution.py:671
  42.0 1.0 %shard_map.163 = bf16[256,256]{1,0:T(8,128)(2,1)} custom-call(f32[4,128,128]{2,1,0:T(8,128)S(1)} %get-tuple-element.47.gate_ref, bf16[256,256]{1,0:T(8,128)(2,1)S(1)} %copy-done, bf16[128,128]{1,0:T(8,128)(2,1)S(1)} %get-tuple-element.67.refs_0_, bf16[128,128]{1,0:T(8,128)(2,1)S(1)} %collective-permute-done.9.refs_1_, ...), custom_call_target="tpu_custom_call" | custom-call | flops 33554432 | bytes 1048576 | tf_op jit(solution)/shard_map/pallas_call | solution.py:732
  43.0 0.4 all-to-all-done.2.shares_ref
  43.3 1.1 %shard_map.165 = f32[4,128,128]{2,1,0:T(8,128)} custom-call(bf16[32,8,128]{2,1,0:T(8,128)(2,1)S(1)} %all-to-all-done.2.shares_ref, f32[16,128]{1,0:T(8,128)S(1)} %get-tuple-element.49.aux_ref.mask_ref, f32[4,128,128]{2,1,0:T(8,128)S(1)} %get-tuple-element.73.normal_ref, f32[4,128,128]{2,1,0:T(8,128)S(1)} %get-tuple-element.74.inverse_ref), custom_call_target="tpu_custom_call" | custom-call | flops 16777216 | bytes 1048576 | tf_op jit(solution)/shard_map/pallas_call | solution.py:746
  (4 shorter events, 0.0 us)
Async XLA Ops:
  0.6 11.7 %copy-start.12 = (bf16[256,256]{1,0:T(8,128)(2,1)S(1)}, bf16[256,256]{1,0:T(8,128)(2,1)}, u32[]{:S(2)}) copy-start(bf16[256,256]{1,0:T(8,128)(2,1)} %param.23) | copy-start | bytes 393220
  2.9 9.4 %copy-start.9 = (bf16[256,256]{1,0:T(8,128)(2,1)S(1)}, bf16[256,256]{1,0:T(8,128)(2,1)}, u32[]{:S(2)}) copy-start(bf16[256,256]{1,0:T(8,128)(2,1)} %param.26) | copy-start | bytes 393220
  3.0 9.3 %copy-start.10 = (bf16[256,256]{1,0:T(8,128)(2,1)S(1)}, bf16[256,256]{1,0:T(8,128)(2,1)}, u32[]{:S(2)}) copy-start(bf16[256,256]{1,0:T(8,128)(2,1)} %param.25) | copy-start | bytes 393220
  3.0 9.3 %copy-start.11 = (bf16[256,256]{1,0:T(8,128)(2,1)S(1)}, bf16[256,256]{1,0:T(8,128)(2,1)}, u32[]{:S(2)}) copy-start(bf16[256,256]{1,0:T(8,128)(2,1)} %param.24) | copy-start | bytes 393220
  3.0 16.2 %all-to-all-start = ((bf16[32,24,128]{2,1,0:T(8,128)(2,1)}), bf16[32,24,128]{2,1,0:T(8,128)(2,1)S(1)}, u32[]{:S(2)}, u32[]{:S(2)}) async-start(bf16[32,24,128]{2,1,0:T(8,128)(2,1)} %bitcast.21), calls=%async_computation | async-start | bytes 393216 | tf_op jit(solution)/shard_map/all_to_all | solution.py:643
  10.3 5.8 %collective-permute-start = (bf16[4,32,128]{2,1,0:T(8,128)(2,1)}, bf16[4,32,128]{2,1,0:T(8,128)(2,1)S(1)}, u32[]{:S(2)}, u32[]{:S(2)}) collective-permute-start(bf16[4,32,128]{2,1,0:T(8,128)(2,1)} %get-tuple-element.51), channel_id=1, source_target_pairs={{0,1},{1,0},{2,3},{3,2},{4,5},{5,4},{6,7},{7,6},{8,9},{9,8},{10,11... | collective-permute-start | bytes 98312 | tf_op jit(solution)/shard_map/ppermute | solution.py:671
  10.6 5.8 %collective-permute-start.1 = (bf16[4,32,128]{2,1,0:T(8,128)(2,1)}, bf16[4,32,128]{2,1,0:T(8,128)(2,1)S(1)}, u32[]{:S(2)}, u32[]{:S(2)}) collective-permute-start(bf16[4,32,128]{2,1,0:T(8,128)(2,1)} %get-tuple-element.52), channel_id=1, source_target_pairs={{0,2},{1,3},{2,0},{3,1},{4,6},{5,7},{6,4},{7,5},{8,10},{9,11},{10,... | collective-permute-start | bytes 98312 | tf_op jit(solution)/shard_map/ppermute | solution.py:671
  12.3 4.1 %collective-permute-start.2 = (bf16[4,32,128]{2,1,0:T(8,128)(2,1)}, bf16[4,32,128]{2,1,0:T(8,128)(2,1)S(1)}, u32[]{:S(2)}, u32[]{:S(2)}) collective-permute-start(bf16[4,32,128]{2,1,0:T(8,128)(2,1)} %get-tuple-element.53), channel_id=1, source_target_pairs={{0,3},{1,2},{2,1},{3,0},{4,7},{5,6},{6,5},{7,4},{8,11},{9,10},{10,... | collective-permute-start | bytes 98312 | tf_op jit(solution)/shard_map/ppermute | solution.py:671
  12.3 0.9 %copy-start = (bf16[256,256]{1,0:T(8,128)(2,1)S(1)}, bf16[256,256]{1,0:T(8,128)(2,1)}, u32[]{:S(2)}) copy-start(bf16[256,256]{1,0:T(8,128)(2,1)} %wo_ref.3) | copy-start | bytes 393220
  12.3 1.0 %copy-start.2 = (bf16[2,128,256]{2,1,0:T(8,128)(2,1)S(1)}, bf16[2,128,256]{2,1,0:T(8,128)(2,1)}, u32[]{:S(2)}) copy-start(bf16[2,128,256]{2,1,0:T(8,128)(2,1)} %param.16) | copy-start | bytes 393220
  12.3 1.0 %copy-start.3 = (bf16[256,256]{1,0:T(8,128)(2,1)S(1)}, bf16[256,256]{1,0:T(8,128)(2,1)}, u32[]{:S(2)}) copy-start(bf16[256,256]{1,0:T(8,128)(2,1)} %get-tuple-element.40.normed_ref) | copy-start | bytes 393220
  12.4 1.0 %copy-start.4 = (bf16[4,32,128]{2,1,0:T(8,128)(2,1)S(1)}, bf16[4,32,128]{2,1,0:T(8,128)(2,1)}, u32[]{:S(2)}) copy-start(bf16[4,32,128]{2,1,0:T(8,128)(2,1)} %get-tuple-element.46.pair_ref) | copy-start | bytes 98308
  12.4 1.0 %copy-start.5 = (f32[16,128]{1,0:T(8,128)S(1)}, f32[16,128]{1,0:T(8,128)}, u32[]{:S(2)}) copy-start(f32[16,128]{1,0:T(8,128)} %get-tuple-element.45.aux_ref) | copy-start | bytes 24580
  13.4 2.7 %copy-start.8 = (bf16[32,32,128]{2,1,0:T(8,128)(2,1)S(1)}, bf16[32,32,128]{2,1,0:T(8,128)(2,1)}, u32[]{:S(2)}) copy-start(bf16[32,32,128]{2,1,0:T(8,128)(2,1)} %param.21) | copy-start | bytes 786436
  13.9 12.3 %collective-permute-start.3 = (bf16[4,128,128]{2,1,0:T(8,128)(2,1)S(1)}, bf16[4,128,128]{2,1,0:T(8,128)(2,1)S(1)}, u32[]{:S(2)}, u32[]{:S(2)}) collective-permute-start(bf16[4,128,128]{2,1,0:T(8,128)(2,1)S(1)} %get-tuple-element.56), channel_id=1, source_target_pairs={{0,1},{1,0},{2,3},{3,2},{4,5},{5,4},{6,7},{7,6},{8,9},{9,8},{10,11... | collective-permute-start | bytes 393224 | tf_op jit(solution)/shard_map/ppermute | solution.py:671
  14.4 11.8 %collective-permute-start.4 = (bf16[4,128,128]{2,1,0:T(8,128)(2,1)S(1)}, bf16[4,128,128]{2,1,0:T(8,128)(2,1)S(1)}, u32[]{:S(2)}, u32[]{:S(2)}) collective-permute-start(bf16[4,128,128]{2,1,0:T(8,128)(2,1)S(1)} %get-tuple-element.57), channel_id=1, source_target_pairs={{0,2},{1,3},{2,0},{3,1},{4,6},{5,7},{6,4},{7,5},{8,10},{9,11},{10,... | collective-permute-start | bytes 393224 | tf_op jit(solution)/shard_map/ppermute | solution.py:671
  16.1 10.1 %collective-permute-start.5 = (bf16[4,128,128]{2,1,0:T(8,128)(2,1)S(1)}, bf16[4,128,128]{2,1,0:T(8,128)(2,1)S(1)}, u32[]{:S(2)}, u32[]{:S(2)}) collective-permute-start(bf16[4,128,128]{2,1,0:T(8,128)(2,1)S(1)} %get-tuple-element.58), channel_id=1, source_target_pairs={{0,3},{1,2},{2,1},{3,0},{4,7},{5,6},{6,5},{7,4},{8,11},{9,10},{10,... | collective-permute-start | bytes 393224 | tf_op jit(solution)/shard_map/ppermute | solution.py:671
  21.2 10.4 %all-to-all-start.1 = ((bf16[32,8,128]{2,1,0:T(8,128)(2,1)}), bf16[32,8,128]{2,1,0:T(8,128)(2,1)S(1)}, u32[]{:S(2)}, u32[]{:S(2)}) async-start(bf16[32,8,128]{2,1,0:T(8,128)(2,1)} %bitcast.11), calls=%async_computation.1 | async-start | bytes 131072 | tf_op jit(solution)/shard_map/all_to_all | solution.py:706
  24.2 3.2 %collective-permute-start.6 = (bf16[4,32,128]{2,1,0:T(8,128)(2,1)S(1)}, bf16[4,32,128]{2,1,0:T(8,128)(2,1)S(1)}, u32[]{:S(2)}, u32[]{:S(2)}) collective-permute-start(bf16[4,32,128]{2,1,0:T(8,128)(2,1)S(1)} %get-tuple-element.62), channel_id=1, source_target_pairs={{0,1},{1,0},{2,3},{3,2},{4,5},{5,4},{6,7},{7,6},{8,9},{9,8},{10,11... | collective-permute-start | bytes 98312 | tf_op jit(solution)/shard_map/ppermute | solution.py:671
  24.5 4.0 %collective-permute-start.7 = (bf16[4,32,128]{2,1,0:T(8,128)(2,1)S(1)}, bf16[4,32,128]{2,1,0:T(8,128)(2,1)S(1)}, u32[]{:S(2)}, u32[]{:S(2)}) collective-permute-start(bf16[4,32,128]{2,1,0:T(8,128)(2,1)S(1)} %get-tuple-element.63), channel_id=1, source_target_pairs={{0,2},{1,3},{2,0},{3,1},{4,6},{5,7},{6,4},{7,5},{8,10},{9,11},{10,... | collective-permute-start | bytes 98312 | tf_op jit(solution)/shard_map/ppermute | solution.py:671
  26.2 3.5 %collective-permute-start.8 = (bf16[4,32,128]{2,1,0:T(8,128)(2,1)S(1)}, bf16[4,32,128]{2,1,0:T(8,128)(2,1)S(1)}, u32[]{:S(2)}, u32[]{:S(2)}) collective-permute-start(bf16[4,32,128]{2,1,0:T(8,128)(2,1)S(1)} %get-tuple-element.64), channel_id=1, source_target_pairs={{0,3},{1,2},{2,1},{3,0},{4,7},{5,6},{6,5},{7,4},{8,11},{9,10},{10,... | collective-permute-start | bytes 98312 | tf_op jit(solution)/shard_map/ppermute | solution.py:671
  26.7 0.7 %copy-start.6 = (bf16[8,128,128]{2,1,0:T(8,128)(2,1)}, bf16[8,128,128]{2,1,0:T(8,128)(2,1)S(1)}, u32[]{:S(2)}) copy-start(bf16[8,128,128]{2,1,0:T(8,128)(2,1)S(1)} %get-tuple-element.66.value_ref) | copy-start | bytes 786436
  31.6 4.3 %copy-start.7 = (bf16[8,128,128]{2,1,0:T(8,128)(2,1)S(1)}, bf16[8,128,128]{2,1,0:T(8,128)(2,1)}, u32[]{:S(2)}) copy-start(bf16[8,128,128]{2,1,0:T(8,128)(2,1)} %copy-done.6) | copy-start | bytes 786436
  33.0 10.3 %all-to-all-start.2 = ((bf16[32,8,128]{2,1,0:T(8,128)(2,1)}), bf16[32,8,128]{2,1,0:T(8,128)(2,1)S(1)}, u32[]{:S(2)}, u32[]{:S(2)}) async-start(bf16[32,8,128]{2,1,0:T(8,128)(2,1)} %get-tuple-element.72), calls=%async_computation.2 | async-start | bytes 131072 | tf_op jit(solution)/shard_map/all_to_all | solution.py:724
  35.9 2.5 %copy-start.1 = (bf16[4,128,128]{2,1,0:T(8,128)(2,1)S(1)}, bf16[4,128,128]{2,1,0:T(8,128)(2,1)}, u32[]{:S(2)}) copy-start(bf16[4,128,128]{2,1,0:T(8,128)(2,1)} %get-tuple-element.37.pair_ref) | copy-start | bytes 393220
  36.4 2.2 %collective-permute-start.9 = (bf16[128,128]{1,0:T(8,128)(2,1)S(1)}, bf16[128,128]{1,0:T(8,128)(2,1)S(1)}, u32[]{:S(2)}, u32[]{:S(2)}) collective-permute-start(bf16[128,128]{1,0:T(8,128)(2,1)S(1)} %get-tuple-element.68), channel_id=1, source_target_pairs={{0,1},{1,0},{2,3},{3,2},{4,5},{5,4},{6,7},{7,6},{8,9},{9,8},{10,11... | collective-permute-start | bytes 98312 | tf_op jit(solution)/shard_map/ppermute | solution.py:671
  36.7 4.0 %collective-permute-start.10 = (bf16[128,128]{1,0:T(8,128)(2,1)S(1)}, bf16[128,128]{1,0:T(8,128)(2,1)S(1)}, u32[]{:S(2)}, u32[]{:S(2)}) collective-permute-start(bf16[128,128]{1,0:T(8,128)(2,1)S(1)} %get-tuple-element.69), channel_id=1, source_target_pairs={{0,2},{1,3},{2,0},{3,1},{4,6},{5,7},{6,4},{7,5},{8,10},{9,11},{10,... | collective-permute-start | bytes 98312 | tf_op jit(solution)/shard_map/ppermute | solution.py:671
  38.4 3.6 %collective-permute-start.11 = (bf16[128,128]{1,0:T(8,128)(2,1)S(1)}, bf16[128,128]{1,0:T(8,128)(2,1)S(1)}, u32[]{:S(2)}, u32[]{:S(2)}) collective-permute-start(bf16[128,128]{1,0:T(8,128)(2,1)S(1)} %get-tuple-element.70), channel_id=1, source_target_pairs={{0,3},{1,2},{2,1},{3,0},{4,7},{5,6},{6,5},{7,4},{8,11},{9,10},{10,... | collective-permute-start | bytes 98312 | tf_op jit(solution)/shard_map/ppermute | solution.py:671

commit v9 on v8

--- a/solution.py
+++ b/solution.py
@@ -366,23 +366,6 @@
             every[t, seqs + s] = columns[s * residues : (s + 1) * residues]
     for step in range(GROUP):
         block_refs[step][...] = every[partner(step)]
-
-
-def products_kernel(scale, *refs):
-    block_refs, (score_ref, flow_ref, value_ref) = refs[:GROUP], refs[GROUP:]
-    rows = score_ref.shape[1]
-    residues = score_ref.shape[2]
-    part_of = lane_index(residues) // 32
-    seqs = block_refs[0].shape[0] // 2
-    for step, block in enumerate(block_refs):
-        for s in range(seqs):
-            wide = jnp.concatenate(
-                [jnp.where(part_of == g, block[s], jnp.zeros((), bf16)) for g in range(4)], axis=0
-            )
-            both = dot_nt(wide, block[seqs + s])
-            score_ref[step * seqs + s] = both[:rows] * scale
-            flow_ref[step * seqs + s] = both[rows:]
-            value_ref[step * seqs + s] = jnp.where(part_of < 2, jnp.ones((), bf16), block[seqs + s])
 
 
 def pair_kernel(recv_ref, weight_ref, aux_ref, *refs):
@@ -460,35 +443,48 @@
             bias[pl.ds(4 * a + b, lines, stride=16), :] = picked + mask
 
 
-def bias_gradient_kernel(bias_ref, mask_ref, score_ref, flow_ref, *refs):
-    part_refs, (pair_ref, send_ref, weights_ref, flat, grads, placed) = refs[:GROUP], refs[GROUP:]
-    columns_each = part_refs[0].shape[1]
-    for step in range(GROUP):
-        first = pl.multiple_of(partner(step) * columns_each, columns_each)
-        pair_ref[:, pl.ds(first, columns_each), :] = part_refs[step][...]
-    seqs, rows, residues = score_ref.shape
+def place_kernel(bias_ref, mask_ref, placed, flat):
+    heads = placed.shape[0]
+    rows = bias_ref.shape[0] * bias_ref.shape[1]
+    flat[:rows] = bias_ref[...].reshape(rows, LANES).astype(f32)
+    for h in range(heads):
+        place_bias(flat, mask_ref, heads, h, placed.at[h])
+
+
+def bias_gradient_kernel(scale, *refs):
+    block_refs, (placed, send_ref, weights_ref, value_ref, grads) = refs[:GROUP], refs[GROUP:]
+    sequences, rows, residues = weights_ref.shape
     heads = rows // residues
-    flat[:rows] = bias_ref[...].reshape(rows, LANES).astype(f32)
+    seqs = sequences // GROUP
     ones = jnp.ones((residues, LANES), bf16)
+    part_of = lane_index(residues) // 32
+    totals = [jnp.zeros((residues, residues), f32) for _ in range(heads)]
+    for step, block in enumerate(block_refs):
+        for s in range(seqs):
+            at = step * seqs + s
+            columns = block[seqs + s]
+            value_ref[at] = jnp.where(part_of < heads, jnp.ones((), bf16), columns)
+            wide = jnp.concatenate(
+                [jnp.where(part_of == g, block[s], jnp.zeros((), bf16)) for g in range(2 * heads)], axis=0
+            )
+            both = dot_nt(wide, columns)
+            for h in range(heads):
+                own = slice(h * residues, (h + 1) * residues)
+                scores = both[own] * scale + placed[h, :residues]
+                weights = jnp.exp(scores - jnp.max(scores, axis=-1, keepdims=True))
+                rounded = weights.astype(bf16)
+                weights_ref[at, own, :] = rounded
+                flow = both[(heads + h) * residues : (heads + h + 1) * residues]
+                inverse = 1.0 / dot_nn(rounded, ones)
+                delta = dot_nn((weights * flow).astype(bf16), ones) * inverse
+                totals[h] = totals[h] + weights * inverse * (flow - delta)
     for h in range(heads):
-        at = slice(h * residues, (h + 1) * residues)
-        place_bias(flat, mask_ref, heads, h, placed.at[h])
-        bias = placed[h, :residues]
-        total = jnp.zeros((residues, residues), f32)
-        for s in range(seqs):
-            scores = score_ref[s, at, :] + bias
-            weights = jnp.exp(scores - jnp.max(scores, axis=-1, keepdims=True))
-            rounded = weights.astype(bf16)
-            weights_ref[s, at, :] = rounded
-            flow = flow_ref[s, at, :]
-            inverse = 1.0 / dot_nn(rounded, ones)
-            delta = dot_nn((weights * flow).astype(bf16), ones) * inverse
-            total = total + weights * inverse * (flow - delta)
-        grads[pl.ds(h, residues, stride=heads), :] = total
+        grads[pl.ds(h, residues, stride=heads), :] = totals[h]
     send_ref[...] = grads[:rows].astype(bf16).reshape(send_ref.shape)
 
 
-def attended_kernel(weights_ref, value_ref, *out_refs):
+def attended_kernel(weights_ref, value_ref, *refs):
+    part_refs, out_refs = refs[:GROUP], refs[GROUP:]
     sequences, _, residues = weights_ref.shape
     seqs = sequences // GROUP
     lane = lane_index(residues)
@@ -499,22 +495,32 @@
             picked = jnp.where(lane < 96, mixed[:residues], mixed[residues:])
             totals = jnp.where(lane < 32, mixed[:residues], mixed[residues:])
             attended.append(picked / pltpu.roll(totals, 64, 1))
-        out_refs[step][...] = jnp.where(lane < 64, pltpu.roll(attended[0], 64, 1), attended[1]).astype(bf16)
+        out_refs[step][0] = jnp.where(lane < 64, pltpu.roll(attended[0], 64, 1), attended[1]).astype(bf16)
+        out_refs[step][1] = part_refs[step][...].reshape(residues, LANES)
 
 
 def output_kernel(gate_ref, wo_ref, *refs):
-    in_refs, out_ref = refs[:GROUP], refs[GROUP]
+    in_refs, (out_ref, pair_ref, normal_ref, inverse_ref) = refs[:GROUP], refs[GROUP:]
     residues = gate_ref.shape[1]
+    rows = pair_ref.shape[0]
+    columns_each = residues // GROUP
     low = lane_index(residues) < 64
     zero = jnp.zeros((), bf16)
     sums = [jnp.zeros((residues, out_ref.shape[1]), f32) for _ in range(2)]
     for step in range(GROUP):
         at = partner(step)
-        gated = (gate_ref[at] * in_refs[step][...].astype(f32)).astype(bf16)
+        gated = (gate_ref[at] * in_refs[step][0].astype(f32)).astype(bf16)
         weight = wo_ref[pl.ds(pl.multiple_of(at * 64, 64), 64), :]
         weight = jnp.concatenate([weight, weight], axis=0)
         sums[0] = sums[0] + dot_nn(jnp.where(low, gated, zero), weight)
         sums[1] = sums[1] + dot_nn(jnp.where(low, zero, gated), weight)
+        columns = pl.ds(pl.multiple_of(at * columns_each, columns_each), columns_each)
+        pair_ref[:, columns, :] = in_refs[step][1].reshape(rows, columns_each, LANES)
+        values = in_refs[step][1].astype(f32)
+        center = values - jnp.mean(values, axis=-1, keepdims=True)
+        inverse = lax.rsqrt(jnp.mean(center * center, axis=-1, keepdims=True) + norm_eps)
+        normal_ref[:, columns, :] = (center * inverse).reshape(rows, columns_each, LANES)
+        inverse_ref[:, columns, :] = jnp.broadcast_to(inverse, values.shape).reshape(rows, columns_each, LANES)
     for s in range(2):
         out_ref[s * residues : (s + 1) * residues, :] = sums[s].astype(bf16)
 
@@ -524,15 +530,15 @@
     return high, (values - high.astype(f32)).astype(bf16)
 
 
-def normal_kernel(pair_ref, normal_ref, inverse_ref):
-    values = pair_ref[...].astype(f32)
-    center = values - jnp.mean(values, axis=-1, keepdims=True)
-    inverse = lax.rsqrt(jnp.mean(center * center, axis=-1, keepdims=True) + norm_eps)
-    normal_ref[...] = center * inverse
-    inverse_ref[...] = jnp.broadcast_to(inverse, values.shape)
-
-
-def gradient_kernel(shares_ref, aux_ref, normal_ref, inverse_ref, out_hbm, result, left_for):
+def gradient_kernel(
+    shares_ref, aux_ref, normal_ref, inverse_ref, update_ref, pair_ref, update_hbm, pair_hbm, out_hbm, result, left_for
+):
+    moves = [
+        pltpu.make_async_copy(update_ref, update_hbm, left_for.at[0]),
+        pltpu.make_async_copy(pair_ref, pair_hbm, left_for.at[1]),
+    ]
+    for move in moves:
+        move.start()
     peers, share, _ = shares_ref.shape
     rows, _, channels = normal_ref.shape
     heads = share // rows
@@ -551,7 +557,6 @@
         ],
         axis=0,
     )
-    moves = []
     for i in range(rows):
         own = jnp.concatenate([total[t, i * heads : (i + 1) * heads] for t in range(GROUP)], axis=0)
         high, low = split_sum(own)
@@ -561,7 +566,7 @@
         result[i] = inverse_ref[i] * (
             upstream - mean - normal * jnp.mean(upstream * normal, axis=-1, keepdims=True)
         )
-        moves.append(pltpu.make_async_copy(result.at[i], out_hbm.at[i], left_for.at[i]))
+        moves.append(pltpu.make_async_copy(result.at[i], out_hbm.at[i], left_for.at[2 + i]))
         moves[-1].start()
     for move in moves:
         move.wait()
@@ -648,6 +653,8 @@
     head_rows = group_heads * residues
     scale = (channel_count // head_count) ** (-0.5)
     normed, *weights = lax.optimization_barrier((normed, query_weight, key_weight, value_weight, gate_weight))
+    joined = jnp.concatenate(weights, axis=1)
+    joined, *pair_blocks = lax.optimization_barrier((joined, *pair_blocks))
     part_shape = shape((rows_here, columns_each, pair_channels), bf16)
     gate, aux, own_block, *blocks = kernel_call(
         projections_kernel,
@@ -660,7 +667,7 @@
     )(
         normed,
         update_cotangent.reshape(token_rows, channel_count),
-        jnp.concatenate(weights, axis=1),
+        joined,
         output_weight,
         aux,
         pair_blocks[0],
@@ -673,15 +680,6 @@
 
     pair_blocks = [own_block] + trade(pair_blocks)[1:]
     blocks = trade(blocks)
-    scores, flow, values = kernel_call(
-        lambda *refs: products_kernel(scale, *refs),
-        [shape((GROUP * sequence_wise, head_rows, residues), f32)] * 2
-        + [shape((GROUP * sequence_wise, residues, LANES), bf16)],
-        [vmem] * GROUP,
-        flops=1 << 28,
-        moved=1 << 21,
-    )(*blocks)
-
     weight_t = (
         outer_weight.reshape(factor, 4, 8, pair_channels)
         .transpose(1, 3, 2, 0)
@@ -706,52 +704,60 @@
     bias_all = lax.all_to_all(
         send_bias.reshape(peers, share_rows, LANES), "row", split_axis=0, concat_axis=0, tiled=True
     )
-    updated = trade(updated)
-
-    pair_updated, send_grad, weights = kernel_call(
-        bias_gradient_kernel,
+
+    placed = kernel_call(
+        place_kernel,
+        shape((group_heads, residues + 16, LANES), f32),
+        [vmem] * 2,
+        [pltpu.VMEM((head_rows + 16 * group_heads, LANES), f32)],
+        flops=1 << 22,
+        moved=1 << 18,
+    )(bias_all, aux)
+    send_grad, weights, values = kernel_call(
+        lambda *refs: bias_gradient_kernel(scale, *refs),
         [
-            shape((rows_here, residues, pair_channels), bf16),
             shape((peers, rows_here * group_heads, LANES), bf16),
             shape((GROUP * sequence_wise, head_rows, residues), bf16),
+            shape((GROUP * sequence_wise, residues, LANES), bf16),
         ],
-        [vmem] * (4 + GROUP),
-        [pltpu.VMEM((head_rows + 16 * group_heads, LANES), f32)] * 2
-        + [pltpu.VMEM((group_heads, residues + 16, LANES), f32)],
+        [vmem] * (1 + GROUP),
+        [pltpu.VMEM((head_rows + 16 * group_heads, LANES), f32)],
         flops=1 << 28,
         moved=1 << 22,
-    )(bias_all, aux, scores, flow, *updated)
+    )(*blocks, placed)
     shares = lax.all_to_all(send_grad, "row", split_axis=0, concat_axis=0, tiled=True)
     attended = kernel_call(
         attended_kernel,
-        [shape((residues, LANES), bf16)] * GROUP,
-        [vmem] * 2,
+        [shape((2, residues, LANES), bf16)] * GROUP,
+        [vmem] * (2 + GROUP),
         flops=1 << 28,
         moved=1 << 21,
-    )(weights, values)
-    update = kernel_call(
+    )(weights, values, *updated)
+    update, pair_updated, normal, inverse = kernel_call(
         output_kernel,
-        shape((token_rows, channel_count), bf16),
+        [
+            shape((token_rows, channel_count), bf16),
+            shape((rows_here, residues, pair_channels), bf16),
+            shape((rows_here, residues, pair_channels), f32),
+            shape((rows_here, residues, pair_channels), f32),
+        ],
         [vmem] * (2 + GROUP),
         flops=2 * token_rows * channel_count * channel_count,
         moved=1 << 20,
     )(gate, output_weight, *trade(list(attended)))
-    normal, inverse = kernel_call(
-        normal_kernel,
-        [shape((rows_here, residues, pair_channels), f32)] * 2,
-        [vmem],
-        flops=1 << 22,
-        moved=1 << 20,
-    )(pair_updated)
-    pair_gradient = kernel_call(
+    update, pair_updated, pair_gradient = kernel_call(
         gradient_kernel,
-        shape((rows_here, residues, pair_channels), f32),
-        [vmem] * 4,
-        [pltpu.VMEM((rows_here, residues, pair_channels), f32), pltpu.SemaphoreType.DMA((rows_here,))],
+        [
+            shape((token_rows, channel_count), bf16),
+            shape((rows_here, residues, pair_channels), bf16),
+            shape((rows_here, residues, pair_channels), f32),
+        ],
+        [vmem] * 6,
+        [pltpu.VMEM((rows_here, residues, pair_channels), f32), pltpu.SemaphoreType.DMA((2 + rows_here,))],
         flops=1 << 24,
         moved=1 << 20,
-        out_specs=pl.BlockSpec(memory_space=pltpu.HBM),
-    )(shares, aux, normal, inverse)
+        out_specs=[pl.BlockSpec(memory_space=pltpu.HBM)] * 3,
+    )(shares, aux, normal, inverse, update, pair_updated)
     return (update.reshape(alignment_rows.shape), pair_updated, pair_gradient)
 
 

time: 44.7 us -> 43.7 us (0.978)
  blocking collectives: 0 us -> 10 us
  starting transfers between devices: 21.4 us -> 16 us
  waiting for transfers between devices: 10.8 us -> 7.7 us
  Pallas kernels: 9.35 us -> 7.82 us
  local copies, waits for them, and re-layouts: 1.92 us -> 0.93 us
    all_to_all x0 -> x1, blocking collectives: none -> 10 us  [on_device_paired(): lax.all_to_all(send_bias.reshape(peers, share_rows, LANES), 'row', split_...]
    all_to_all x1 -> x0, starting transfers between devices: 3.01 us -> none  [on_device_paired(): lax.all_to_all(send_bias.reshape(peers, share_rows, LANES), 'row', split_...]
    ppermute x12 -> x9, starting transfers between devices: 8.2 us -> 6.16 us  [trade(): lax.ppermute(parts[d], 'row', [(i, i ^ d) for i in range(peers)])]
    all_to_all x1 -> x0, waiting for transfers between devices: 1.87 us -> none  [on_device_paired(): lax.all_to_all(send_bias.reshape(peers, share_rows, LANES), 'row', split_...]
    unnamed x27, local copies, waits for them, and re-layouts: 1.78 us -> 0.78 us
    pallas_call x6 -> x5, Pallas kernels: 4.52 us -> 3.61 us  [the longest x1 1.62 us: on_device_paired(): kernel_call(lambda *refs: bias_gradient_kernel(scale, *refs), [shape((pee...]
    pallas_call x1, Pallas kernels: 2.01 us -> 1.38 us  [on_device_paired(): kernel_call(pair_kernel, [shape((lines, GROUP, share_rows, LANES), bf16)]...]
    ppermute x12 -> x9, waiting for transfers between devices: 5.71 us -> 5.14 us  [trade(): lax.ppermute(parts[d], 'row', [(i, i ^ d) for i in range(peers)])]
  transfers between devices with their start and end apart: 15 -> 11, of which waited for: 7 -> 5; matrix products, arithmetic and copies ran while one was open for 1% -> 1% of each run, Pallas kernels for 10% -> 6%
where the time goes in v9:
time: 43.7 us; the launch traced here: 43.5 us
  starting transfers between devices  16 us (37%)
  blocking collectives  10 us (23%)
  Pallas kernels  7.82 us (18%)
  waiting for transfers between devices  7.7 us (18%)
  local copies, waits for them, and re-layouts  0.93 us (2%)
  between operations  0.9 us (2%)
    all_to_all x1, blocking collectives, on_device_paired(): lax.all_to_all(send_bias.reshape(peers, share_rows, LANES), 'row', split_...  10 us
    all_to_all x1, starting transfers between devices, on_device_paired(): lax.all_to_all(send.reshape(peers, block_rows, LANES), 'row', split_axis=...  7.3 us
    ppermute x9, starting transfers between devices, trade(): lax.ppermute(parts[d], 'row', [(i, i ^ d) for i in range(peers)])  6.16 us
    ppermute x9, waiting for transfers between devices, trade(): lax.ppermute(parts[d], 'row', [(i, i ^ d) for i in range(peers)])  5.14 us
    all_to_all x1, starting transfers between devices, on_device_paired(): lax.all_to_all(send_grad, 'row', split_axis=0, concat_axis=0, tiled=True)  2.57 us
    all_to_all x1, waiting for transfers between devices, on_device_paired(): lax.all_to_all(send.reshape(peers, block_rows, LANES), 'row', split_axis=...  2.31 us
    pallas_call x1, Pallas kernels, on_device_paired(): kernel_call(factors_kernel, [shape((lines, GROUP, block_rows, LANES), bf1...  2.3 us
    pallas_call x1, Pallas kernels, on_device_paired(): kernel_call(lambda *refs: bias_gradient_kernel(scale, *refs), [shape((pee...  1.62 us
  transfers between devices with their start and end apart: 11, of which 5 were waited for; matrix products, arithmetic and copies ran while one was open for 1% of the time, Pallas kernels for 6%

profile of v9, /device:TPU:0, one launch (start us, length us, event | category | flops | bytes accessed | tf_op | source)
XLA Modules:
  0.0 43.5 jit_solution(15841461172827415496)
XLA Ops:
  0.6 0.0 copy-start.9
  0.6 2.3 %shard_map.157 = (bf16[8,4,24,128]{3,2,1,0:T(8,128)(2,1)}, f32[16,128]{1,0:T(8,128)}, bf16[256,256]{1,0:T(8,128)(2,1)}, bf16[4,32,128]{2,1,0:T(8,128)(2,1)}, bf1...) custom-call(s32[64]{0:T(128)} %seq_smem_ref.1, s32[128]{0:T(128)} %res_smem_ref.1, ...), custom_call_target="tpu_custom_call" | custom-call | flops 16777216 | bytes 1048576 | tf_op jit(solution)/shard_map/pallas_call | solution.py:623
  2.9 0.0 copy-start.6
  3.0 0.0 copy-start.7
  3.0 0.0 copy-start.8
  3.0 7.3 %all-to-all-start = ((bf16[32,24,128]{2,1,0:T(8,128)(2,1)}), bf16[32,24,128]{2,1,0:T(8,128)(2,1)S(1)}, u32[]{:S(2)}, u32[]{:S(2)}) async-start(bf16[32,24,128]{2,1,0:T(8,128)(2,1)} %bitcast.22), calls=%async_computation | async-start | bytes 393216 | tf_op jit(solution)/shard_map/all_to_all | solution.py:648
  10.3 0.0 copy-done.9
  10.3 0.0 copy-done.6
  10.3 0.0 copy-done.7
  10.3 0.0 copy-done.8
  10.3 0.0 copy-start.12
  10.3 0.0 copy-start.11
  10.4 0.0 copy-start.10
  10.4 0.0 copy-start
  10.4 0.0 copy-start.1
  10.4 0.0 copy-start.2
  10.4 0.0 copy-start.3
  10.4 0.1 pad_maximum_fusion.weights_ref
  10.5 0.0 copy-start.4
  10.5 0.6 %copy-done.12 = bf16[4,32,128]{2,1,0:T(8,128)(2,1)S(1)} copy-done((bf16[4,32,128]{2,1,0:T(8,128)(2,1)S(1)}, bf16[4,32,128]{2,1,0:T(8,128)(2,1)}, u32[]{:S(2)}) %copy-start.12) | copy-done | bytes 32792
  11.1 0.3 collective-permute-start.3
  11.3 0.0 copy-done.11
  11.3 1.7 %collective-permute-start.4 = (bf16[4,32,128]{2,1,0:T(8,128)(2,1)S(1)}, bf16[4,32,128]{2,1,0:T(8,128)(2,1)S(1)}, u32[]{:S(2)}, u32[]{:S(2)}) collective-permute-start(bf16[4,32,128]{2,1,0:T(8,128)(2,1)S(1)} %copy-done.11), channel_id=1, source_target_pairs={{0,2},{1,3},{2,0},{3,1},{4,6},{5,7},{6,4},{7,5},{8,10},{9,11},{10,... | collective-permute-start | bytes 98312 | tf_op jit(solution)/shard_map/ppermute | solution.py:678
  13.0 0.0 copy-done.10
  13.0 0.0 collective-permute-start.5
  13.1 0.0 copy-done
  13.1 0.0 copy-done.1
  13.1 0.0 copy-done.2
  13.1 0.0 copy-done.3
  13.1 0.0 copy-done.4
  13.1 0.0 copy-start.5
  13.1 0.5 %shard_map.158 = (f32[4,128,128]{2,1,0:T(8,128)S(1)}, f32[16,128]{1,0:T(8,128)S(1)}, bf16[4,32,128]{2,1,0:T(8,128)(2,1)S(1)}, bf16[4,128,128]{2,1,0:T(8,128)(2,1...) custom-call(bf16[256,256]{1,0:T(8,128)(2,1)S(1)} %copy-done.2, ...), custom_call_target="tpu_custom_call" | custom-call | flops 167772160 | bytes 2097152 | tf_op jit(solution)/shard_map/pallas_call | solution.py:659
  13.6 0.5 %collective-permute-start = (bf16[4,128,128]{2,1,0:T(8,128)(2,1)S(1)}, bf16[4,128,128]{2,1,0:T(8,128)(2,1)S(1)}, u32[]{:S(2)}, u32[]{:S(2)}) collective-permute-start(bf16[4,128,128]{2,1,0:T(8,128)(2,1)S(1)} %get-tuple-element.60), channel_id=1, source_target_pairs={{0,1},{1,0},{2,3},{3,2},{4,5},{5,4},{6,7},{7,6},{8,9},{9,8},{10,11... | collective-permute-start | bytes 393224 | tf_op jit(solution)/shard_map/ppermute | solution.py:678
  14.1 1.7 %collective-permute-start.1 = (bf16[4,128,128]{2,1,0:T(8,128)(2,1)S(1)}, bf16[4,128,128]{2,1,0:T(8,128)(2,1)S(1)}, u32[]{:S(2)}, u32[]{:S(2)}) collective-permute-start(bf16[4,128,128]{2,1,0:T(8,128)(2,1)S(1)} %get-tuple-element.61), channel_id=1, source_target_pairs={{0,2},{1,3},{2,0},{3,1},{4,6},{5,7},{6,4},{7,5},{8,10},{9,11},{10,... | collective-permute-start | bytes 393224 | tf_op jit(solution)/shard_map/ppermute | solution.py:678
  15.8 0.0 copy-done.5
  15.8 0.1 copy.18
  15.9 0.1 copy.19.weight_ref
  16.1 0.0 collective-permute-done.3.refs_1_
  16.1 0.1 collective-permute-start.2
  16.2 0.0 collective-permute-done.4.refs_2_
  16.2 0.7 %collective-permute-done.5.refs_3_ = bf16[4,32,128]{2,1,0:T(8,128)(2,1)S(1)} collective-permute-done((bf16[4,32,128]{2,1,0:T(8,128)(2,1)S(1)}, bf16[4,32,128]{2,1,0:T(8,128)(2,1)S(1)}, u32[]{:S(2)}, u32[]{:S(2)}) %collective-permute-start.5) | collective-permute-done | bytes 32800 | tf_op jit(solution)/shard_map/ppermute | solution.py:678
  16.9 2.3 %all-to-all-done.recv_ref = bf16[32,24,128]{2,1,0:T(8,128)(2,1)S(1)} async-done(((bf16[32,24,128]{2,1,0:T(8,128)(2,1)}), bf16[32,24,128]{2,1,0:T(8,128)(2,1)S(1)}, u32[]{:S(2)}, u32[]{:S(2)}) %all-to-all-start) | async-done | bytes 196640 | tf_op jit(solution)/shard_map/all_to_all | solution.py:648
  19.2 1.4 %shard_map.159 = (bf16[8,4,8,128]{3,2,1,0:T(8,128)(2,1)S(1)}, bf16[4,32,128]{2,1,0:T(8,128)(2,1)S(1)}, bf16[4,32,128]{2,1,0:T(8,128)(2,1)S(1)}, bf16[4,32,128]{2,1,0:T(8,128)(2,1)S(1)}, bf16[4,32,128]{2,1,0:T(8,128)(2,1)S(1)}) custom-call(bf16[32,24,128]{2,1,0:T(8,128)(2,1)S(1)} %all-to-all-done.recv_ref, bf16[4,128,256]{2,1,0:T(8,128)(2,1)S(1)} %copy.19.weight_ref, ...), custom_call_target="tpu_custom_call" | custom-call | flops 268435456 | bytes 1048576 | tf_op jit(solution)/shard_map/pallas_call | solution.py:689
  20.6 10.0 %all_to_all.15.bias_ref = bf16[32,8,128]{2,1,0:T(8,128)(2,1)S(1)} all-to-all(bf16[32,8,128]{2,1,0:T(8,128)(2,1)S(1)} %bitcast.16), channel_id=1, replica_groups=mesh['grp'=1,'row'=32,'col'=1] {'row'}, dimensions={0} | all-to-all | bytes 131072 | tf_op jit(solution)/shard_map/all_to_all | solution.py:704
  30.6 0.2 shard_map.160.refs_4_
  30.8 0.0 collective-permute-done.refs_1_
  30.8 0.0 collective-permute-done.1.refs_2_
  30.8 0.0 collective-permute-done.2.refs_3_
  30.8 1.6 %shard_map.161 = (bf16[32,8,128]{2,1,0:T(8,128)(2,1)}, bf16[8,256,128]{2,1,0:T(8,128)(2,1)S(1)}, bf16[8,128,128]{2,1,0:T(8,128)(2,1)S(1)}) custom-call(bf16[4,128,128]{2,1,0:T(8,128)(2,1)S(1)} %get-tuple-element.59.refs_0_, bf16[4,128,128]{2,1,0:T(8,128)(2,1)S(1)} %collective-permute-done.refs_1_, bf16[4,128,128]{2,1,0:T(8,128)(2,1)S(1)} %collective-permute-done.1.refs_2_, ...), custom_call_target="tpu_custom_call" | custom-call | flops 268435456 | bytes 4194304 | tf_op jit(solution)/shard_map/pallas_call | solution.py:716
  32.4 2.6 %all-to-all-start.2 = ((bf16[32,8,128]{2,1,0:T(8,128)(2,1)}), bf16[32,8,128]{2,1,0:T(8,128)(2,1)S(1)}, u32[]{:S(2)}, u32[]{:S(2)}) async-start(bf16[32,8,128]{2,1,0:T(8,128)(2,1)} %get-tuple-element.70), calls=%async_computation.2 | async-start | bytes 131072 | tf_op jit(solution)/shard_map/all_to_all | solution.py:728
  35.0 0.4 %shard_map.162 = (bf16[2,128,128]{2,1,0:T(8,128)(2,1)S(1)}, bf16[2,128,128]{2,1,0:T(8,128)(2,1)S(1)}, bf16[2,128,128]{2,1,0:T(8,128)(2,1)S(1)}, bf16[2,128,128]{2,1,0:T(8,128)(2,1)S(1)}) custom-call(bf16[8,256,128]{2,1,0:T(8,128)(2,1)S(1)} %get-tuple-element.72.weights_ref, bf16[8,128,128]{2,1,0:T(8,128)(2,1)S(1)} %get-tuple-element.73.value_ref, ...), custom_call_target="tpu_custom_call" | custom-call | flops 268435456 | bytes 2097152 | tf_op jit(solution)/shard_map/pallas_call | solution.py:729
  35.4 0.2 collective-permute-start.6
  35.6 1.7 %collective-permute-start.7 = (bf16[2,128,128]{2,1,0:T(8,128)(2,1)S(1)}, bf16[2,128,128]{2,1,0:T(8,128)(2,1)S(1)}, u32[]{:S(2)}, u32[]{:S(2)}) collective-permute-start(bf16[2,128,128]{2,1,0:T(8,128)(2,1)S(1)} %get-tuple-element.80), channel_id=1, source_target_pairs={{0,2},{1,3},{2,0},{3,1},{4,6},{5,7},{6,4},{7,5},{8,10},{9,11},{10,... | collective-permute-start | bytes 196616 | tf_op jit(solution)/shard_map/ppermute | solution.py:678
  37.3 0.1 collective-permute-start.8
  37.4 0.0 collective-permute-done.6.refs_1_
  37.4 3.0 %collective-permute-done.7.refs_2_ = bf16[2,128,128]{2,1,0:T(8,128)(2,1)S(1)} collective-permute-done((bf16[2,128,128]{2,1,0:T(8,128)(2,1)S(1)}, bf16[2,128,128]{2,1,0:T(8,128)(2,1)S(1)}, u32[]{:S(2)}, u32[]{:S(2)}) %collective-permute-start.7) | collective-permute-done | bytes 65568 | tf_op jit(solution)/shard_map/ppermute | solution.py:678
  40.4 1.4 %collective-permute-done.8.refs_3_ = bf16[2,128,128]{2,1,0:T(8,128)(2,1)S(1)} collective-permute-done((bf16[2,128,128]{2,1,0:T(8,128)(2,1)S(1)}, bf16[2,128,128]{2,1,0:T(8,128)(2,1)S(1)}, u32[]{:S(2)}, u32[]{:S(2)}) %collective-permute-start.8) | collective-permute-done | bytes 65568 | tf_op jit(solution)/shard_map/ppermute | solution.py:678
  41.8 0.3 shard_map.163
  42.1 0.3 all-to-all-done.2.shares_ref
  42.4 1.1 %shard_map.164 = (bf16[256,256]{1,0:T(8,128)(2,1)}, bf16[4,128,128]{2,1,0:T(8,128)(2,1)}, f32[4,128,128]{2,1,0:T(8,128)}) custom-call(bf16[32,8,128]{2,1,0:T(8,128)(2,1)S(1)} %all-to-all-done.2.shares_ref, f32[16,128]{1,0:T(8,128)S(1)} %get-tuple-element.64.aux_ref.mask_ref, f32[4,128,128]{2,1,0:T(8,128)S(1)} %get-tuple-element.82.normal_ref, ...), custom_call_target="tpu_custom_call" | custom-call | flops 16777216 | bytes 1048576 | tf_op jit(solution)/shard_map/pallas_call | solution.py:748
Async XLA Ops:
  0.6 9.7 %copy-start.9 = (bf16[256,256]{1,0:T(8,128)(2,1)S(1)}, bf16[256,256]{1,0:T(8,128)(2,1)}, u32[]{:S(2)}) copy-start(bf16[256,256]{1,0:T(8,128)(2,1)} %param.23) | copy-start | bytes 393220
  2.9 7.4 %copy-start.6 = (bf16[256,256]{1,0:T(8,128)(2,1)S(1)}, bf16[256,256]{1,0:T(8,128)(2,1)}, u32[]{:S(2)}) copy-start(bf16[256,256]{1,0:T(8,128)(2,1)} %param.26) | copy-start | bytes 393220
  3.0 7.4 %copy-start.7 = (bf16[256,256]{1,0:T(8,128)(2,1)S(1)}, bf16[256,256]{1,0:T(8,128)(2,1)}, u32[]{:S(2)}) copy-start(bf16[256,256]{1,0:T(8,128)(2,1)} %param.25) | copy-start | bytes 393220
  3.0 7.4 %copy-start.8 = (bf16[256,256]{1,0:T(8,128)(2,1)S(1)}, bf16[256,256]{1,0:T(8,128)(2,1)}, u32[]{:S(2)}) copy-start(bf16[256,256]{1,0:T(8,128)(2,1)} %param.24) | copy-start | bytes 393220
  3.0 16.2 %all-to-all-start = ((bf16[32,24,128]{2,1,0:T(8,128)(2,1)}), bf16[32,24,128]{2,1,0:T(8,128)(2,1)S(1)}, u32[]{:S(2)}, u32[]{:S(2)}) async-start(bf16[32,24,128]{2,1,0:T(8,128)(2,1)} %bitcast.22), calls=%async_computation | async-start | bytes 393216 | tf_op jit(solution)/shard_map/all_to_all | solution.py:648
  10.3 0.8 %copy-start.12 = (bf16[4,32,128]{2,1,0:T(8,128)(2,1)S(1)}, bf16[4,32,128]{2,1,0:T(8,128)(2,1)}, u32[]{:S(2)}) copy-start(bf16[4,32,128]{2,1,0:T(8,128)(2,1)} %get-tuple-element.66) | copy-start | bytes 98308
  10.3 1.0 %copy-start.11 = (bf16[4,32,128]{2,1,0:T(8,128)(2,1)S(1)}, bf16[4,32,128]{2,1,0:T(8,128)(2,1)}, u32[]{:S(2)}) copy-start(bf16[4,32,128]{2,1,0:T(8,128)(2,1)} %get-tuple-element.67) | copy-start | bytes 98308
  10.4 2.7 %copy-start.10 = (bf16[4,32,128]{2,1,0:T(8,128)(2,1)S(1)}, bf16[4,32,128]{2,1,0:T(8,128)(2,1)}, u32[]{:S(2)}) copy-start(bf16[4,32,128]{2,1,0:T(8,128)(2,1)} %get-tuple-element.68) | copy-start | bytes 98308
  10.4 2.7 %copy-start = (bf16[256,256]{1,0:T(8,128)(2,1)S(1)}, bf16[256,256]{1,0:T(8,128)(2,1)}, u32[]{:S(2)}) copy-start(bf16[256,256]{1,0:T(8,128)(2,1)} %wo_ref.3) | copy-start | bytes 393220
  10.4 2.7 %copy-start.1 = (bf16[2,128,256]{2,1,0:T(8,128)(2,1)S(1)}, bf16[2,128,256]{2,1,0:T(8,128)(2,1)}, u32[]{:S(2)}) copy-start(bf16[2,128,256]{2,1,0:T(8,128)(2,1)} %param.16) | copy-start | bytes 393220
  10.4 2.7 %copy-start.2 = (bf16[256,256]{1,0:T(8,128)(2,1)S(1)}, bf16[256,256]{1,0:T(8,128)(2,1)}, u32[]{:S(2)}) copy-start(bf16[256,256]{1,0:T(8,128)(2,1)} %get-tuple-element.47.normed_ref) | copy-start | bytes 393220
  10.4 2.7 %copy-start.3 = (bf16[4,32,128]{2,1,0:T(8,128)(2,1)S(1)}, bf16[4,32,128]{2,1,0:T(8,128)(2,1)}, u32[]{:S(2)}) copy-start(bf16[4,32,128]{2,1,0:T(8,128)(2,1)} %get-tuple-element.58.pair_ref) | copy-start | bytes 98308
  10.5 2.6 %copy-start.4 = (f32[16,128]{1,0:T(8,128)S(1)}, f32[16,128]{1,0:T(8,128)}, u32[]{:S(2)}) copy-start(f32[16,128]{1,0:T(8,128)} %get-tuple-element.57.aux_ref) | copy-start | bytes 24580
  11.1 5.0 %collective-permute-start.3 = (bf16[4,32,128]{2,1,0:T(8,128)(2,1)S(1)}, bf16[4,32,128]{2,1,0:T(8,128)(2,1)S(1)}, u32[]{:S(2)}, u32[]{:S(2)}) collective-permute-start(bf16[4,32,128]{2,1,0:T(8,128)(2,1)S(1)} %copy-done.12), channel_id=1, source_target_pairs={{0,1},{1,0},{2,3},{3,2},{4,5},{5,4},{6,7},{7,6},{8,9},{9,8},{10,11... | collective-permute-start | bytes 98312 | tf_op jit(solution)/shard_map/ppermute | solution.py:678
  11.3 4.8 %collective-permute-start.4 = (bf16[4,32,128]{2,1,0:T(8,128)(2,1)S(1)}, bf16[4,32,128]{2,1,0:T(8,128)(2,1)S(1)}, u32[]{:S(2)}, u32[]{:S(2)}) collective-permute-start(bf16[4,32,128]{2,1,0:T(8,128)(2,1)S(1)} %copy-done.11), channel_id=1, source_target_pairs={{0,2},{1,3},{2,0},{3,1},{4,6},{5,7},{6,4},{7,5},{8,10},{9,11},{10,... | collective-permute-start | bytes 98312 | tf_op jit(solution)/shard_map/ppermute | solution.py:678
  13.0 3.8 %collective-permute-start.5 = (bf16[4,32,128]{2,1,0:T(8,128)(2,1)S(1)}, bf16[4,32,128]{2,1,0:T(8,128)(2,1)S(1)}, u32[]{:S(2)}, u32[]{:S(2)}) collective-permute-start(bf16[4,32,128]{2,1,0:T(8,128)(2,1)S(1)} %copy-done.10), channel_id=1, source_target_pairs={{0,3},{1,2},{2,1},{3,0},{4,7},{5,6},{6,5},{7,4},{8,11},{9,10},{10,... | collective-permute-start | bytes 98312 | tf_op jit(solution)/shard_map/ppermute | solution.py:678
  13.1 2.7 %copy-start.5 = (bf16[32,32,128]{2,1,0:T(8,128)(2,1)S(1)}, bf16[32,32,128]{2,1,0:T(8,128)(2,1)}, u32[]{:S(2)}) copy-start(bf16[32,32,128]{2,1,0:T(8,128)(2,1)} %param.21) | copy-start | bytes 786436
  13.6 17.1 %collective-permute-start = (bf16[4,128,128]{2,1,0:T(8,128)(2,1)S(1)}, bf16[4,128,128]{2,1,0:T(8,128)(2,1)S(1)}, u32[]{:S(2)}, u32[]{:S(2)}) collective-permute-start(bf16[4,128,128]{2,1,0:T(8,128)(2,1)S(1)} %get-tuple-element.60), channel_id=1, source_target_pairs={{0,1},{1,0},{2,3},{3,2},{4,5},{5,4},{6,7},{7,6},{8,9},{9,8},{10,11... | collective-permute-start | bytes 393224 | tf_op jit(solution)/shard_map/ppermute | solution.py:678
  14.1 16.6 %collective-permute-start.1 = (bf16[4,128,128]{2,1,0:T(8,128)(2,1)S(1)}, bf16[4,128,128]{2,1,0:T(8,128)(2,1)S(1)}, u32[]{:S(2)}, u32[]{:S(2)}) collective-permute-start(bf16[4,128,128]{2,1,0:T(8,128)(2,1)S(1)} %get-tuple-element.61), channel_id=1, source_target_pairs={{0,2},{1,3},{2,0},{3,1},{4,6},{5,7},{6,4},{7,5},{8,10},{9,11},{10,... | collective-permute-start | bytes 393224 | tf_op jit(solution)/shard_map/ppermute | solution.py:678
  16.1 14.7 %collective-permute-start.2 = (bf16[4,128,128]{2,1,0:T(8,128)(2,1)S(1)}, bf16[4,128,128]{2,1,0:T(8,128)(2,1)S(1)}, u32[]{:S(2)}, u32[]{:S(2)}) collective-permute-start(bf16[4,128,128]{2,1,0:T(8,128)(2,1)S(1)} %get-tuple-element.62), channel_id=1, source_target_pairs={{0,3},{1,2},{2,1},{3,0},{4,7},{5,6},{6,5},{7,4},{8,11},{9,10},{10,... | collective-permute-start | bytes 393224 | tf_op jit(solution)/shard_map/ppermute | solution.py:678
  32.4 10.0 %all-to-all-start.2 = ((bf16[32,8,128]{2,1,0:T(8,128)(2,1)}), bf16[32,8,128]{2,1,0:T(8,128)(2,1)S(1)}, u32[]{:S(2)}, u32[]{:S(2)}) async-start(bf16[32,8,128]{2,1,0:T(8,128)(2,1)} %get-tuple-element.70), calls=%async_computation.2 | async-start | bytes 131072 | tf_op jit(solution)/shard_map/all_to_all | solution.py:728
  35.4 2.0 %collective-permute-start.6 = (bf16[2,128,128]{2,1,0:T(8,128)(2,1)S(1)}, bf16[2,128,128]{2,1,0:T(8,128)(2,1)S(1)}, u32[]{:S(2)}, u32[]{:S(2)}) collective-permute-start(bf16[2,128,128]{2,1,0:T(8,128)(2,1)S(1)} %get-tuple-element.79), channel_id=1, source_target_pairs={{0,1},{1,0},{2,3},{3,2},{4,5},{5,4},{6,7},{7,6},{8,9},{9,8},{10,11... | collective-permute-start | bytes 196616 | tf_op jit(solution)/shard_map/ppermute | solution.py:678
  35.6 4.8 %collective-permute-start.7 = (bf16[2,128,128]{2,1,0:T(8,128)(2,1)S(1)}, bf16[2,128,128]{2,1,0:T(8,128)(2,1)S(1)}, u32[]{:S(2)}, u32[]{:S(2)}) collective-permute-start(bf16[2,128,128]{2,1,0:T(8,128)(2,1)S(1)} %get-tuple-element.80), channel_id=1, source_target_pairs={{0,2},{1,3},{2,0},{3,1},{4,6},{5,7},{6,4},{7,5},{8,10},{9,11},{10,... | collective-permute-start | bytes 196616 | tf_op jit(solution)/shard_map/ppermute | solution.py:678
  37.3 4.5 %collective-permute-start.8 = (bf16[2,128,128]{2,1,0:T(8,128)(2,1)S(1)}, bf16[2,128,128]{2,1,0:T(8,128)(2,1)S(1)}, u32[]{:S(2)}, u32[]{:S(2)}) collective-permute-start(bf16[2,128,128]{2,1,0:T(8,128)(2,1)S(1)} %get-tuple-element.81), channel_id=1, source_target_pairs={{0,3},{1,2},{2,1},{3,0},{4,7},{5,6},{6,5},{7,4},{8,11},{9,10},{10,... | collective-permute-start | bytes 196616 | tf_op jit(solution)/shard_map/ppermute | solution.py:678

commit v10 on v9

--- a/solution.py
+++ b/solution.py
@@ -263,13 +263,9 @@
 
 
 def factors_kernel(
-    seq_smem_ref, res_smem_ref, seq_ref, res_ref, bias_w_ref, left_ref, right_ref, pair_ref, *refs
+    seq_smem_ref, res_smem_ref, seq_ref, res_ref, bias_w_ref, left_ref, right_ref, *refs
 ):
-    row_refs, (send_ref, aux_ref, normed_ref, *pair_refs, left_scr) = refs[:PIECES], refs[PIECES:]
-    columns_each = pair_refs[0].shape[1]
-    for step in range(GROUP):
-        first = pl.multiple_of(partner(step) * columns_each, columns_each)
-        pair_refs[step][...] = pair_ref[:, pl.ds(first, columns_each), :]
+    row_refs, (send_ref, aux_ref, normed_ref, left_scr) = refs[:PIECES], refs[PIECES:]
     lines = send_ref.shape[0]
     seqs = send_ref.shape[2] // 12
     residues = res_ref.shape[1]
@@ -428,10 +424,9 @@
         updated_refs[step][...] = after[partner(step)]
 
 
-def place_bias(flat, mask_ref, heads, h, bias):
+def place_bias(flat, heads, h, bias):
     lines = bias.shape[0] // 16 - 1
     lane_group = lane_index(lines) // 32
-    mask = mask_ref[4:5, :]
     for b in range(4):
         rows = [flat[pl.ds((4 * t + b) * heads + h, lines, stride=16 * heads), :] for t in range(GROUP)]
         for a in range(4):
@@ -440,7 +435,7 @@
                 picked = jnp.where(lane_group == (a + t) % 4, rows[t], picked)
             if a:
                 picked = pltpu.roll(picked, LANES - 32 * a, 1)
-            bias[pl.ds(4 * a + b, lines, stride=16), :] = picked + mask
+            bias[pl.ds(4 * a + b, lines, stride=16), :] = picked
 
 
 def place_kernel(bias_ref, mask_ref, placed, flat):
@@ -448,7 +443,8 @@
     rows = bias_ref.shape[0] * bias_ref.shape[1]
     flat[:rows] = bias_ref[...].reshape(rows, LANES).astype(f32)
     for h in range(heads):
-        place_bias(flat, mask_ref, heads, h, placed.at[h])
+        place_bias(flat, heads, h, placed.at[h])
+    placed[0, placed.shape[1] - 16 : placed.shape[1] - 12] = mask_ref[4:8]
 
 
 def bias_gradient_kernel(scale, *refs):
@@ -458,6 +454,7 @@
     seqs = sequences // GROUP
     ones = jnp.ones((residues, LANES), bf16)
     part_of = lane_index(residues) // 32
+    key_mask = placed[0, residues : residues + 1]
     totals = [jnp.zeros((residues, residues), f32) for _ in range(heads)]
     for step, block in enumerate(block_refs):
         for s in range(seqs):
@@ -470,7 +467,7 @@
             both = dot_nt(wide, columns)
             for h in range(heads):
                 own = slice(h * residues, (h + 1) * residues)
-                scores = both[own] * scale + placed[h, :residues]
+                scores = both[own] * scale + placed[h, :residues] + key_mask
                 weights = jnp.exp(scores - jnp.max(scores, axis=-1, keepdims=True))
                 rounded = weights.astype(bf16)
                 weights_ref[at, own, :] = rounded
@@ -620,15 +617,14 @@
     pieces = [
         pl.BlockSpec((token_rows // PIECES, channel_count), lambda step, at=at: (at, 0)) for at in range(PIECES)
     ]
-    send, aux, normed, *pair_blocks = kernel_call(
+    send, aux, normed = kernel_call(
         factors_kernel,
         [
             shape((lines, GROUP, block_rows, LANES), bf16),
             shape((16, LANES), f32),
             shape((token_rows, channel_count), bf16),
-        ]
-        + [shape((rows_here, columns_each, pair_channels), bf16)] * GROUP,
-        [smem] * 2 + [vmem] * 6 + pieces,
+        ],
+        [smem] * 2 + [vmem] * 5 + pieces,
         [pltpu.VMEM((residues + 4 * GROUP, LANES), f32)],
         flops=2 * token_rows * channel_count * LANES,
         moved=1 << 20,
@@ -642,7 +638,6 @@
         bias_weight.T,
         left_weight.T,
         right_weight.T,
-        pair_state,
         *[flat_rows] * PIECES,
     )
     received = lax.all_to_all(
@@ -654,7 +649,11 @@
     scale = (channel_count // head_count) ** (-0.5)
     normed, *weights = lax.optimization_barrier((normed, query_weight, key_weight, value_weight, gate_weight))
     joined = jnp.concatenate(weights, axis=1)
-    joined, *pair_blocks = lax.optimization_barrier((joined, *pair_blocks))
+    joined, pair_rows = lax.optimization_barrier((joined, pair_state))
+    own = lax.axis_index("row") % GROUP
+    pair_blocks = [
+        lax.dynamic_slice_in_dim(pair_rows, (own ^ step) * columns_each, columns_each, 1) for step in range(GROUP)
+    ]
     part_shape = shape((rows_here, columns_each, pair_channels), bf16)
     gate, aux, own_block, *blocks = kernel_call(
         projections_kernel,

time: 43.7 us -> 43.8 us (level)
    unnamed x27 -> x21, local copies, waits for them, and re-layouts: 0.78 us -> 0.95 us
where the time goes in v10:
time: 43.8 us; the launch traced here: 43.6 us
  starting transfers between devices  16.1 us (37%)
  blocking collectives  10.3 us (24%)
  Pallas kernels  7.7 us (18%)
  waiting for transfers between devices  7.44 us (17%)
  local copies, waits for them, and re-layouts  1.11 us (3%)
  between operations  0.9 us (2%)
    all_to_all x1, blocking collectives, on_device_paired(): lax.all_to_all(send_bias.reshape(peers, share_rows, LANES), 'row', split_...  10.3 us
    all_to_all x1, starting transfers between devices, on_device_paired(): lax.all_to_all(send.reshape(peers, block_rows, LANES), 'row', split_axis=...  7.3 us
    ppermute x9, starting transfers between devices, trade(): lax.ppermute(parts[d], 'row', [(i, i ^ d) for i in range(peers)])  6.23 us
    ppermute x9, waiting for transfers between devices, trade(): lax.ppermute(parts[d], 'row', [(i, i ^ d) for i in range(peers)])  5.18 us
    all_to_all x1, starting transfers between devices, on_device_paired(): lax.all_to_all(send_grad, 'row', split_axis=0, concat_axis=0, tiled=True)  2.57 us
    pallas_call x1, Pallas kernels, on_device_paired(): kernel_call(factors_kernel, [shape((lines, GROUP, block_rows, LANES), bf1...  2.2 us
    all_to_all x1, waiting for transfers between devices, on_device_paired(): lax.all_to_all(send.reshape(peers, block_rows, LANES), 'row', split_axis=...  2 us
    pallas_call x1, Pallas kernels, on_device_paired(): kernel_call(lambda *refs: bias_gradient_kernel(scale, *refs), [shape((pee...  1.61 us
  transfers between devices with their start and end apart: 11, of which 5 were waited for; matrix products, arithmetic and copies ran while one was open for 1% of the time, Pallas kernels for 6%

profile of v10, /device:TPU:0, one launch (start us, length us, event | category | flops | bytes accessed | tf_op | source)
XLA Modules:
  0.0 43.6 jit_solution(11640730577251349536)
XLA Ops:
  0.6 0.0 copy-start.9
  0.6 2.2 %shard_map.157 = (bf16[8,4,24,128]{3,2,1,0:T(8,128)(2,1)}, f32[16,128]{1,0:T(8,128)}, bf16[256,256]{1,0:T(8,128)(2,1)}) custom-call(s32[64]{0:T(128)} %seq_smem_ref.1, s32[128]{0:T(128)} %res_smem_ref.1, s32[1,64]{1,0:T(1,128)} %bitcast.26, s32[1,128]{1,0:T(1,128)} %bitcast.27, bf16[8,128]{1,0:T(8,128)(2,1)} %bitcast.25, bf16[32,256]{1,0:T(8,128)(2,1)} %bitcast.23, ...), custom_call_target="tpu_custom_call" | custom-call | flops 16777216 | bytes 1048576 | tf_op jit(solution)/shard_map/pallas_call | solution.py:620
  2.8 0.0 copy-start.6
  2.8 0.0 copy-start.7
  2.9 0.0 copy-start.8
  2.9 7.3 %all-to-all-start = ((bf16[32,24,128]{2,1,0:T(8,128)(2,1)}), bf16[32,24,128]{2,1,0:T(8,128)(2,1)S(1)}, u32[]{:S(2)}, u32[]{:S(2)}) async-start(bf16[32,24,128]{2,1,0:T(8,128)(2,1)} %bitcast.22), calls=%async_computation | async-start | bytes 393216 | tf_op jit(solution)/shard_map/all_to_all | solution.py:643
  10.2 0.0 copy-done.9
  10.2 0.0 copy-done.6
  10.2 0.0 copy-done.7
  10.2 0.0 copy-done.8
  10.2 0.0 copy-start.5
  10.3 0.0 copy-start.2
  10.3 0.1 pad_maximum_fusion.weights_ref
  10.4 0.8 %copy-done.5 = bf16[4,128,128]{2,1,0:T(8,128)(2,1)S(1)} copy-done((bf16[4,128,128]{2,1,0:T(8,128)(2,1)S(1)}, bf16[4,128,128]{2,1,0:T(8,128)(2,1)}, u32[]{:S(2)}) %copy-start.5) | copy-done | bytes 131096
  11.2 0.0 copy-start
  11.2 0.0 copy-start.1
  11.2 0.0 copy-start.3
  11.2 0.3 collective-permute-start.3
  11.5 1.7 %collective-permute-start.4 = (bf16[4,32,128]{2,1,0:T(8,128)(2,1)S(1)}, bf16[4,32,128]{2,1,0:T(8,128)(2,1)S(1)}, u32[]{:S(2)}, u32[]{:S(2)}) collective-permute-start(bf16[4,32,128]{2,1,0:T(8,128)(2,1)S(1)} %get-tuple-element.76), channel_id=1, source_target_pairs={{0,2},{1,3},{2,0},{3,1},{4,6},{5,7},{6,4},{7,5},{8,10},{9,11},{10,... | collective-permute-start | bytes 98312 | tf_op jit(solution)/shard_map/ppermute | solution.py:677
  13.2 0.0 collective-permute-start.5
  13.2 0.0 copy-done.2
  13.2 0.0 copy-done
  13.2 0.0 copy-done.1
  13.2 0.0 copy-done.3
  13.2 0.0 copy-start.4
  13.2 0.5 %shard_map.158 = (f32[4,128,128]{2,1,0:T(8,128)S(1)}, f32[16,128]{1,0:T(8,128)S(1)}, bf16[4,32,128]{2,1,0:T(8,128)(2,1)S(1)}, bf16[4,128,128]{2,1,0:T(8,128)(2,1...) custom-call(bf16[256,256]{1,0:T(8,128)(2,1)S(1)} %copy-done.2, ...), custom_call_target="tpu_custom_call" | custom-call | flops 167772160 | bytes 2097152 | tf_op jit(solution)/shard_map/pallas_call | solution.py:658
  13.8 0.5 %collective-permute-start = (bf16[4,128,128]{2,1,0:T(8,128)(2,1)S(1)}, bf16[4,128,128]{2,1,0:T(8,128)(2,1)S(1)}, u32[]{:S(2)}, u32[]{:S(2)}) collective-permute-start(bf16[4,128,128]{2,1,0:T(8,128)(2,1)S(1)} %get-tuple-element.49), channel_id=1, source_target_pairs={{0,1},{1,0},{2,3},{3,2},{4,5},{5,4},{6,7},{7,6},{8,9},{9,8},{10,11... | collective-permute-start | bytes 393224 | tf_op jit(solution)/shard_map/ppermute | solution.py:677
  14.3 1.7 %collective-permute-start.1 = (bf16[4,128,128]{2,1,0:T(8,128)(2,1)S(1)}, bf16[4,128,128]{2,1,0:T(8,128)(2,1)S(1)}, u32[]{:S(2)}, u32[]{:S(2)}) collective-permute-start(bf16[4,128,128]{2,1,0:T(8,128)(2,1)S(1)} %get-tuple-element.50), channel_id=1, source_target_pairs={{0,2},{1,3},{2,0},{3,1},{4,6},{5,7},{6,4},{7,5},{8,10},{9,11},{10,... | collective-permute-start | bytes 393224 | tf_op jit(solution)/shard_map/ppermute | solution.py:677
  16.0 0.0 copy-done.4
  16.0 0.1 copy.18
  16.1 0.1 copy.19.weight_ref
  16.2 0.0 collective-permute-done.3.refs_1_
  16.2 0.1 collective-permute-start.2
  16.3 0.0 collective-permute-done.4.refs_2_
  16.3 0.7 %collective-permute-done.5.refs_3_ = bf16[4,32,128]{2,1,0:T(8,128)(2,1)S(1)} collective-permute-done((bf16[4,32,128]{2,1,0:T(8,128)(2,1)S(1)}, bf16[4,32,128]{2,1,0:T(8,128)(2,1)S(1)}, u32[]{:S(2)}, u32[]{:S(2)}) %collective-permute-start.5) | collective-permute-done | bytes 32800 | tf_op jit(solution)/shard_map/ppermute | solution.py:677
  17.1 2.0 %all-to-all-done.recv_ref = bf16[32,24,128]{2,1,0:T(8,128)(2,1)S(1)} async-done(((bf16[32,24,128]{2,1,0:T(8,128)(2,1)}), bf16[32,24,128]{2,1,0:T(8,128)(2,1)S(1)}, u32[]{:S(2)}, u32[]{:S(2)}) %all-to-all-start) | async-done | bytes 196640 | tf_op jit(solution)/shard_map/all_to_all | solution.py:643
  19.1 1.4 %shard_map.159 = (bf16[8,4,8,128]{3,2,1,0:T(8,128)(2,1)S(1)}, bf16[4,32,128]{2,1,0:T(8,128)(2,1)S(1)}, bf16[4,32,128]{2,1,0:T(8,128)(2,1)S(1)}, bf16[4,32,128]{2,1,0:T(8,128)(2,1)S(1)}, bf16[4,32,128]{2,1,0:T(8,128)(2,1)S(1)}) custom-call(bf16[32,24,128]{2,1,0:T(8,128)(2,1)S(1)} %all-to-all-done.recv_ref, bf16[4,128,256]{2,1,0:T(8,128)(2,1)S(1)} %copy.19.weight_ref, ...), custom_call_target="tpu_custom_call" | custom-call | flops 268435456 | bytes 1048576 | tf_op jit(solution)/shard_map/pallas_call | solution.py:688
  20.5 10.3 %all_to_all.15.bias_ref = bf16[32,8,128]{2,1,0:T(8,128)(2,1)S(1)} all-to-all(bf16[32,8,128]{2,1,0:T(8,128)(2,1)S(1)} %bitcast.16), channel_id=1, replica_groups=mesh['grp'=1,'row'=32,'col'=1] {'row'}, dimensions={0} | all-to-all | bytes 131072 | tf_op jit(solution)/shard_map/all_to_all | solution.py:703
  30.7 0.2 shard_map.160.refs_4_
  30.9 0.0 collective-permute-done.refs_1_
  30.9 0.0 collective-permute-done.1.refs_2_
  30.9 0.0 collective-permute-done.2.refs_3_
  30.9 1.6 %shard_map.161 = (bf16[32,8,128]{2,1,0:T(8,128)(2,1)}, bf16[8,256,128]{2,1,0:T(8,128)(2,1)S(1)}, bf16[8,128,128]{2,1,0:T(8,128)(2,1)S(1)}) custom-call(bf16[4,128,128]{2,1,0:T(8,128)(2,1)S(1)} %get-tuple-element.48.refs_0_, bf16[4,128,128]{2,1,0:T(8,128)(2,1)S(1)} %collective-permute-done.refs_1_, bf16[4,128,128]{2,1,0:T(8,128)(2,1)S(1)} %collective-permute-done.1.refs_2_, ...), custom_call_target="tpu_custom_call" | custom-call | flops 268435456 | bytes 4194304 | tf_op jit(solution)/shard_map/pallas_call | solution.py:715
  32.5 2.6 %all-to-all-start.2 = ((bf16[32,8,128]{2,1,0:T(8,128)(2,1)}), bf16[32,8,128]{2,1,0:T(8,128)(2,1)S(1)}, u32[]{:S(2)}, u32[]{:S(2)}) async-start(bf16[32,8,128]{2,1,0:T(8,128)(2,1)} %get-tuple-element.56), calls=%async_computation.2 | async-start | bytes 131072 | tf_op jit(solution)/shard_map/all_to_all | solution.py:727
  35.1 0.4 %shard_map.162 = (bf16[2,128,128]{2,1,0:T(8,128)(2,1)S(1)}, bf16[2,128,128]{2,1,0:T(8,128)(2,1)S(1)}, bf16[2,128,128]{2,1,0:T(8,128)(2,1)S(1)}, bf16[2,128,128]{2,1,0:T(8,128)(2,1)S(1)}) custom-call(bf16[8,256,128]{2,1,0:T(8,128)(2,1)S(1)} %get-tuple-element.58.weights_ref, bf16[8,128,128]{2,1,0:T(8,128)(2,1)S(1)} %get-tuple-element.59.value_ref, ...), custom_call_target="tpu_custom_call" | custom-call | flops 268435456 | bytes 2097152 | tf_op jit(solution)/shard_map/pallas_call | solution.py:728
  35.5 0.2 collective-permute-start.6
  35.7 1.7 %collective-permute-start.7 = (bf16[2,128,128]{2,1,0:T(8,128)(2,1)S(1)}, bf16[2,128,128]{2,1,0:T(8,128)(2,1)S(1)}, u32[]{:S(2)}, u32[]{:S(2)}) collective-permute-start(bf16[2,128,128]{2,1,0:T(8,128)(2,1)S(1)} %get-tuple-element.66), channel_id=1, source_target_pairs={{0,2},{1,3},{2,0},{3,1},{4,6},{5,7},{6,4},{7,5},{8,10},{9,11},{10,... | collective-permute-start | bytes 196616 | tf_op jit(solution)/shard_map/ppermute | solution.py:677
  37.4 0.1 collective-permute-start.8
  37.5 0.0 collective-permute-done.6.refs_1_
  37.5 3.0 %collective-permute-done.7.refs_2_ = bf16[2,128,128]{2,1,0:T(8,128)(2,1)S(1)} collective-permute-done((bf16[2,128,128]{2,1,0:T(8,128)(2,1)S(1)}, bf16[2,128,128]{2,1,0:T(8,128)(2,1)S(1)}, u32[]{:S(2)}, u32[]{:S(2)}) %collective-permute-start.7) | collective-permute-done | bytes 65568 | tf_op jit(solution)/shard_map/ppermute | solution.py:677
  40.5 1.4 %collective-permute-done.8.refs_3_ = bf16[2,128,128]{2,1,0:T(8,128)(2,1)S(1)} collective-permute-done((bf16[2,128,128]{2,1,0:T(8,128)(2,1)S(1)}, bf16[2,128,128]{2,1,0:T(8,128)(2,1)S(1)}, u32[]{:S(2)}, u32[]{:S(2)}) %collective-permute-start.8) | collective-permute-done | bytes 65568 | tf_op jit(solution)/shard_map/ppermute | solution.py:677
  41.9 0.3 shard_map.163
  42.2 0.3 all-to-all-done.2.shares_ref
  42.5 1.1 %shard_map.164 = (bf16[256,256]{1,0:T(8,128)(2,1)}, bf16[4,128,128]{2,1,0:T(8,128)(2,1)}, f32[4,128,128]{2,1,0:T(8,128)}) custom-call(bf16[32,8,128]{2,1,0:T(8,128)(2,1)S(1)} %all-to-all-done.2.shares_ref, f32[16,128]{1,0:T(8,128)S(1)} %get-tuple-element.53.aux_ref.mask_ref, f32[4,128,128]{2,1,0:T(8,128)S(1)} %get-tuple-element.68.normal_ref, ...), custom_call_target="tpu_custom_call" | custom-call | flops 16777216 | bytes 1048576 | tf_op jit(solution)/shard_map/pallas_call | solution.py:747
  (1 shorter events, 0.0 us)
Async XLA Ops:
  0.6 9.6 %copy-start.9 = (bf16[256,256]{1,0:T(8,128)(2,1)S(1)}, bf16[256,256]{1,0:T(8,128)(2,1)}, u32[]{:S(2)}) copy-start(bf16[256,256]{1,0:T(8,128)(2,1)} %param.23) | copy-start | bytes 393220
  2.8 7.4 %copy-start.6 = (bf16[256,256]{1,0:T(8,128)(2,1)S(1)}, bf16[256,256]{1,0:T(8,128)(2,1)}, u32[]{:S(2)}) copy-start(bf16[256,256]{1,0:T(8,128)(2,1)} %param.26) | copy-start | bytes 393220
  2.8 7.4 %copy-start.7 = (bf16[256,256]{1,0:T(8,128)(2,1)S(1)}, bf16[256,256]{1,0:T(8,128)(2,1)}, u32[]{:S(2)}) copy-start(bf16[256,256]{1,0:T(8,128)(2,1)} %param.25) | copy-start | bytes 393220
  2.9 7.4 %copy-start.8 = (bf16[256,256]{1,0:T(8,128)(2,1)S(1)}, bf16[256,256]{1,0:T(8,128)(2,1)}, u32[]{:S(2)}) copy-start(bf16[256,256]{1,0:T(8,128)(2,1)} %param.24) | copy-start | bytes 393220
  2.9 16.2 %all-to-all-start = ((bf16[32,24,128]{2,1,0:T(8,128)(2,1)}), bf16[32,24,128]{2,1,0:T(8,128)(2,1)S(1)}, u32[]{:S(2)}, u32[]{:S(2)}) async-start(bf16[32,24,128]{2,1,0:T(8,128)(2,1)} %bitcast.22), calls=%async_computation | async-start | bytes 393216 | tf_op jit(solution)/shard_map/all_to_all | solution.py:643
  10.2 0.9 %copy-start.5 = (bf16[4,128,128]{2,1,0:T(8,128)(2,1)S(1)}, bf16[4,128,128]{2,1,0:T(8,128)(2,1)}, u32[]{:S(2)}) copy-start(bf16[4,128,128]{2,1,0:T(8,128)(2,1)} %param.15) | copy-start | bytes 393220
  10.3 2.9 %copy-start.2 = (bf16[256,256]{1,0:T(8,128)(2,1)S(1)}, bf16[256,256]{1,0:T(8,128)(2,1)}, u32[]{:S(2)}) copy-start(bf16[256,256]{1,0:T(8,128)(2,1)} %get-tuple-element.40.normed_ref) | copy-start | bytes 393220
  11.2 2.0 %copy-start = (bf16[256,256]{1,0:T(8,128)(2,1)S(1)}, bf16[256,256]{1,0:T(8,128)(2,1)}, u32[]{:S(2)}) copy-start(bf16[256,256]{1,0:T(8,128)(2,1)} %wo_ref.3) | copy-start | bytes 393220
  11.2 2.0 %copy-start.1 = (bf16[2,128,256]{2,1,0:T(8,128)(2,1)S(1)}, bf16[2,128,256]{2,1,0:T(8,128)(2,1)}, u32[]{:S(2)}) copy-start(bf16[2,128,256]{2,1,0:T(8,128)(2,1)} %param.16) | copy-start | bytes 393220
  11.2 2.0 %copy-start.3 = (f32[16,128]{1,0:T(8,128)S(1)}, f32[16,128]{1,0:T(8,128)}, u32[]{:S(2)}) copy-start(f32[16,128]{1,0:T(8,128)} %get-tuple-element.46.aux_ref) | copy-start | bytes 24580
  11.2 5.0 %collective-permute-start.3 = (bf16[4,32,128]{2,1,0:T(8,128)(2,1)S(1)}, bf16[4,32,128]{2,1,0:T(8,128)(2,1)S(1)}, u32[]{:S(2)}, u32[]{:S(2)}) collective-permute-start(bf16[4,32,128]{2,1,0:T(8,128)(2,1)S(1)} %get-tuple-element.77), channel_id=1, source_target_pairs={{0,1},{1,0},{2,3},{3,2},{4,5},{5,4},{6,7},{7,6},{8,9},{9,8},{10,11... | collective-permute-start | bytes 98312 | tf_op jit(solution)/shard_map/ppermute | solution.py:677
  11.5 4.8 %collective-permute-start.4 = (bf16[4,32,128]{2,1,0:T(8,128)(2,1)S(1)}, bf16[4,32,128]{2,1,0:T(8,128)(2,1)S(1)}, u32[]{:S(2)}, u32[]{:S(2)}) collective-permute-start(bf16[4,32,128]{2,1,0:T(8,128)(2,1)S(1)} %get-tuple-element.76), channel_id=1, source_target_pairs={{0,2},{1,3},{2,0},{3,1},{4,6},{5,7},{6,4},{7,5},{8,10},{9,11},{10,... | collective-permute-start | bytes 98312 | tf_op jit(solution)/shard_map/ppermute | solution.py:677
  13.2 3.9 %collective-permute-start.5 = (bf16[4,32,128]{2,1,0:T(8,128)(2,1)S(1)}, bf16[4,32,128]{2,1,0:T(8,128)(2,1)S(1)}, u32[]{:S(2)}, u32[]{:S(2)}) collective-permute-start(bf16[4,32,128]{2,1,0:T(8,128)(2,1)S(1)} %get-tuple-element.75), channel_id=1, source_target_pairs={{0,3},{1,2},{2,1},{3,0},{4,7},{5,6},{6,5},{7,4},{8,11},{9,10},{10,... | collective-permute-start | bytes 98312 | tf_op jit(solution)/shard_map/ppermute | solution.py:677
  13.2 2.7 %copy-start.4 = (bf16[32,32,128]{2,1,0:T(8,128)(2,1)S(1)}, bf16[32,32,128]{2,1,0:T(8,128)(2,1)}, u32[]{:S(2)}) copy-start(bf16[32,32,128]{2,1,0:T(8,128)(2,1)} %param.21) | copy-start | bytes 786436
  13.8 17.1 %collective-permute-start = (bf16[4,128,128]{2,1,0:T(8,128)(2,1)S(1)}, bf16[4,128,128]{2,1,0:T(8,128)(2,1)S(1)}, u32[]{:S(2)}, u32[]{:S(2)}) collective-permute-start(bf16[4,128,128]{2,1,0:T(8,128)(2,1)S(1)} %get-tuple-element.49), channel_id=1, source_target_pairs={{0,1},{1,0},{2,3},{3,2},{4,5},{5,4},{6,7},{7,6},{8,9},{9,8},{10,11... | collective-permute-start | bytes 393224 | tf_op jit(solution)/shard_map/ppermute | solution.py:677
  14.3 16.6 %collective-permute-start.1 = (bf16[4,128,128]{2,1,0:T(8,128)(2,1)S(1)}, bf16[4,128,128]{2,1,0:T(8,128)(2,1)S(1)}, u32[]{:S(2)}, u32[]{:S(2)}) collective-permute-start(bf16[4,128,128]{2,1,0:T(8,128)(2,1)S(1)} %get-tuple-element.50), channel_id=1, source_target_pairs={{0,2},{1,3},{2,0},{3,1},{4,6},{5,7},{6,4},{7,5},{8,10},{9,11},{10,... | collective-permute-start | bytes 393224 | tf_op jit(solution)/shard_map/ppermute | solution.py:677
  16.2 14.7 %collective-permute-start.2 = (bf16[4,128,128]{2,1,0:T(8,128)(2,1)S(1)}, bf16[4,128,128]{2,1,0:T(8,128)(2,1)S(1)}, u32[]{:S(2)}, u32[]{:S(2)}) collective-permute-start(bf16[4,128,128]{2,1,0:T(8,128)(2,1)S(1)} %get-tuple-element.51), channel_id=1, source_target_pairs={{0,3},{1,2},{2,1},{3,0},{4,7},{5,6},{6,5},{7,4},{8,11},{9,10},{10,... | collective-permute-start | bytes 393224 | tf_op jit(solution)/shard_map/ppermute | solution.py:677
  32.5 10.0 %all-to-all-start.2 = ((bf16[32,8,128]{2,1,0:T(8,128)(2,1)}), bf16[32,8,128]{2,1,0:T(8,128)(2,1)S(1)}, u32[]{:S(2)}, u32[]{:S(2)}) async-start(bf16[32,8,128]{2,1,0:T(8,128)(2,1)} %get-tuple-element.56), calls=%async_computation.2 | async-start | bytes 131072 | tf_op jit(solution)/shard_map/all_to_all | solution.py:727
  35.5 2.0 %collective-permute-start.6 = (bf16[2,128,128]{2,1,0:T(8,128)(2,1)S(1)}, bf16[2,128,128]{2,1,0:T(8,128)(2,1)S(1)}, u32[]{:S(2)}, u32[]{:S(2)}) collective-permute-start(bf16[2,128,128]{2,1,0:T(8,128)(2,1)S(1)} %get-tuple-element.65), channel_id=1, source_target_pairs={{0,1},{1,0},{2,3},{3,2},{4,5},{5,4},{6,7},{7,6},{8,9},{9,8},{10,11... | collective-permute-start | bytes 196616 | tf_op jit(solution)/shard_map/ppermute | solution.py:677
  35.7 4.8 %collective-permute-start.7 = (bf16[2,128,128]{2,1,0:T(8,128)(2,1)S(1)}, bf16[2,128,128]{2,1,0:T(8,128)(2,1)S(1)}, u32[]{:S(2)}, u32[]{:S(2)}) collective-permute-start(bf16[2,128,128]{2,1,0:T(8,128)(2,1)S(1)} %get-tuple-element.66), channel_id=1, source_target_pairs={{0,2},{1,3},{2,0},{3,1},{4,6},{5,7},{6,4},{7,5},{8,10},{9,11},{10,... | collective-permute-start | bytes 196616 | tf_op jit(solution)/shard_map/ppermute | solution.py:677
  37.4 4.5 %collective-permute-start.8 = (bf16[2,128,128]{2,1,0:T(8,128)(2,1)S(1)}, bf16[2,128,128]{2,1,0:T(8,128)(2,1)S(1)}, u32[]{:S(2)}, u32[]{:S(2)}) collective-permute-start(bf16[2,128,128]{2,1,0:T(8,128)(2,1)S(1)} %get-tuple-element.67), channel_id=1, source_target_pairs={{0,3},{1,2},{2,1},{3,0},{4,7},{5,6},{6,5},{7,4},{8,11},{9,10},{10,... | collective-permute-start | bytes 196616 | tf_op jit(solution)/shard_map/ppermute | solution.py:677

commit v11 on v10

--- a/solution.py
+++ b/solution.py
@@ -297,7 +297,7 @@
         block = jnp.concatenate([own[t] for own in quarters], axis=0).astype(bf16)
         send_ref[:, t, :right_rows, :] = jnp.broadcast_to(block[None], (lines, right_rows, LANES))
         send_ref[:, t, right_rows:, :] = tail
-    aux_ref[0:4] = tile_divisor(res_smem_ref, res_ref, seq_ref)
+    aux_ref[0:4] = tile_inverse(res_smem_ref, res_ref, seq_ref)
     aux_ref[4:8] = jnp.broadcast_to((live - 1.0) * mask_fill, (4, LANES))
     aux_ref[8:16] = bias_w_ref[...].astype(f32)
 
@@ -315,7 +315,7 @@
     return lax.bitwise_xor(lax.rem(lax.axis_index("row"), GROUP), step)
 
 
-def tile_divisor(res_smem_ref, res_ref, seq_ref):
+def tile_inverse(res_smem_ref, res_ref, seq_ref):
     own = partner(0)
     rows = lax.div(lax.axis_index("row"), GROUP) * 16
     lane = lane_index(1)
@@ -333,12 +333,12 @@
         line = jnp.zeros((1, LANES), f32)
         for a in range(4):
             line = jnp.where(lane // 32 == a, res_smem_ref[rows + 4 * a + b].astype(f32), line)
-        lines.append(jnp.maximum(total * line * columns, 1.0))
+        lines.append(1.0 / jnp.maximum(total * line * columns, 1.0))
     return jnp.concatenate(lines, axis=0)
 
 
 def projections_kernel(
-    normed_ref, cot_ref, weights_ref, wo_ref, aux_ref, pair_ref, gate_ref, aux_out_ref, pair_out_ref, *rest
+    normed_ref, cot_ref, weights_ref, wg_ref, wo_ref, aux_ref, pair_ref, gate_ref, aux_out_ref, pair_out_ref, *rest
 ):
     block_refs, every = rest[:GROUP], rest[GROUP]
     aux_out_ref[...] = aux_ref[...]
@@ -348,10 +348,10 @@
     residues = gate_ref.shape[1]
     seqs = tokens // residues
     channels = normed.shape[1]
-    queries, keys, values, gate = [
-        dot_nn(normed, weights_ref[:, at * channels : (at + 1) * channels]) for at in range(4)
+    queries, keys, values = [
+        dot_nn(normed, weights_ref[:, at * channels : (at + 1) * channels]) for at in range(3)
     ]
-    gate = jax.nn.sigmoid(gate)
+    gate = jax.nn.sigmoid(dot_nn(normed, wg_ref[...]))
     d_attended = dot_nt(cot_ref[...], wo_ref[...]) * gate
     for t in range(GROUP):
         rows = side_by_side(queries, d_attended, t).astype(bf16)
@@ -405,7 +405,7 @@
     bias_w = aux_ref[8:16].astype(bf16)
     blocks = []
     for b in range(4):
-        update = sums[:, b * LANES : (b + 1) * LANES] / aux_ref[b : b + 1, :]
+        update = sums[:, b * LANES : (b + 1) * LANES] * aux_ref[b : b + 1, :]
         updated = (before[b] + update).astype(bf16)
         values = updated.astype(f32)
         center = values - jnp.mean(values, axis=0, keepdims=True)
@@ -647,7 +647,7 @@
     group_heads = head_count // GROUP
     head_rows = group_heads * residues
     scale = (channel_count // head_count) ** (-0.5)
-    normed, *weights = lax.optimization_barrier((normed, query_weight, key_weight, value_weight, gate_weight))
+    normed, *weights = lax.optimization_barrier((normed, query_weight, key_weight, value_weight))
     joined = jnp.concatenate(weights, axis=1)
     joined, pair_rows = lax.optimization_barrier((joined, pair_state))
     own = lax.axis_index("row") % GROUP
@@ -659,7 +659,7 @@
         projections_kernel,
         [shape((GROUP, residues, LANES), f32), shape((16, LANES), f32), part_shape]
         + [shape((2 * sequence_wise, residues, LANES), bf16)] * GROUP,
-        [vmem] * 6,
+        [vmem] * 7,
         [pltpu.VMEM((GROUP, 2 * sequence_wise, residues, LANES), bf16)],
         flops=10 * token_rows * channel_count * channel_count,
         moved=1 << 21,
@@ -667,6 +667,7 @@
         normed,
         update_cotangent.reshape(token_rows, channel_count),
         joined,
+        gate_weight,
         output_weight,
         aux,
         pair_blocks[0],

time: 43.8 us -> 43.9 us (level)
  no operation moved by 1% of the time
where the time goes in v11:
time: 43.9 us; the launch traced here: 43.5 us
  starting transfers between devices  16.1 us (37%)
  blocking collectives  10.3 us (23%)
  Pallas kernels  7.68 us (17%)
  waiting for transfers between devices  7.45 us (17%)
  local copies, waits for them, and re-layouts  1.13 us (3%)
  between operations  0.9 us (2%)
    all_to_all x1, blocking collectives, on_device_paired(): lax.all_to_all(send_bias.reshape(peers, share_rows, LANES), 'row', split_...  10.3 us
    all_to_all x1, starting transfers between devices, on_device_paired(): lax.all_to_all(send.reshape(peers, block_rows, LANES), 'row', split_axis=...  7.3 us
    ppermute x9, starting transfers between devices, trade(): lax.ppermute(parts[d], 'row', [(i, i ^ d) for i in range(peers)])  6.21 us
    ppermute x9, waiting for transfers between devices, trade(): lax.ppermute(parts[d], 'row', [(i, i ^ d) for i in range(peers)])  5.18 us
    all_to_all x1, starting transfers between devices, on_device_paired(): lax.all_to_all(send_grad, 'row', split_axis=0, concat_axis=0, tiled=True)  2.57 us
    pallas_call x1, Pallas kernels, on_device_paired(): kernel_call(factors_kernel, [shape((lines, GROUP, block_rows, LANES), bf1...  2.17 us
    all_to_all x1, waiting for transfers between devices, on_device_paired(): lax.all_to_all(send.reshape(peers, block_rows, LANES), 'row', split_axis=...  2.02 us
    pallas_call x1, Pallas kernels, on_device_paired(): kernel_call(lambda *refs: bias_gradient_kernel(scale, *refs), [shape((pee...  1.61 us
  transfers between devices with their start and end apart: 11, of which 5 were waited for; matrix products, arithmetic and copies ran while one was open for 1% of the time, Pallas kernels for 6%

profile of v11, /device:TPU:0, one launch (start us, length us, event | category | flops | bytes accessed | tf_op | source)
XLA Modules:
  0.0 43.5 jit_solution(13847116697732869245)
XLA Ops:
  0.6 2.2 %shard_map.157 = (bf16[8,4,24,128]{3,2,1,0:T(8,128)(2,1)}, f32[16,128]{1,0:T(8,128)}, bf16[256,256]{1,0:T(8,128)(2,1)}) custom-call(s32[64]{0:T(128)} %seq_smem_ref.1, s32[128]{0:T(128)} %res_smem_ref.1, s32[1,64]{1,0:T(1,128)} %bitcast.26, s32[1,128]{1,0:T(1,128)} %bitcast.27, bf16[8,128]{1,0:T(8,128)(2,1)} %bitcast.25, bf16[32,256]{1,0:T(8,128)(2,1)} %bitcast.23, ...), custom_call_target="tpu_custom_call" | custom-call | flops 16777216 | bytes 1048576 | tf_op jit(solution)/shard_map/pallas_call | solution.py:620
  2.8 0.0 copy-start.7
  2.8 0.0 copy-start.8
  2.8 0.0 copy-start.9
  2.8 7.3 %all-to-all-start = ((bf16[32,24,128]{2,1,0:T(8,128)(2,1)}), bf16[32,24,128]{2,1,0:T(8,128)(2,1)S(1)}, u32[]{:S(2)}, u32[]{:S(2)}) async-start(bf16[32,24,128]{2,1,0:T(8,128)(2,1)} %bitcast.22), calls=%async_computation | async-start | bytes 393216 | tf_op jit(solution)/shard_map/all_to_all | solution.py:643
  10.2 0.0 copy-done.7
  10.2 0.0 copy-done.8
  10.2 0.0 copy-done.9
  10.2 0.0 copy-start.6
  10.2 0.0 copy-start.2
  10.2 0.0 copy-start.3
  10.3 0.8 %copy-done.6 = bf16[4,128,128]{2,1,0:T(8,128)(2,1)S(1)} copy-done((bf16[4,128,128]{2,1,0:T(8,128)(2,1)S(1)}, bf16[4,128,128]{2,1,0:T(8,128)(2,1)}, u32[]{:S(2)}) %copy-start.6) | copy-done | bytes 131096
  11.1 0.0 copy-start
  11.1 0.0 copy-start.1
  11.1 0.0 copy-start.4
  11.1 0.3 collective-permute-start.3
  11.4 1.7 %collective-permute-start.4 = (bf16[4,32,128]{2,1,0:T(8,128)(2,1)S(1)}, bf16[4,32,128]{2,1,0:T(8,128)(2,1)S(1)}, u32[]{:S(2)}, u32[]{:S(2)}) collective-permute-start(bf16[4,32,128]{2,1,0:T(8,128)(2,1)S(1)} %get-tuple-element.74), channel_id=1, source_target_pairs={{0,2},{1,3},{2,0},{3,1},{4,6},{5,7},{6,4},{7,5},{8,10},{9,11},{10,... | collective-permute-start | bytes 98312 | tf_op jit(solution)/shard_map/ppermute | solution.py:678
  13.1 0.0 collective-permute-start.5
  13.1 0.0 copy-done.2
  13.1 0.0 copy-done.3
  13.1 0.0 copy-done
  13.2 0.0 copy-done.1
  13.2 0.0 copy-done.4
  13.2 0.0 copy-start.5
  13.2 0.5 %shard_map.158 = (f32[4,128,128]{2,1,0:T(8,128)S(1)}, f32[16,128]{1,0:T(8,128)S(1)}, bf16[4,32,128]{2,1,0:T(8,128)(2,1)S(1)}, bf16[4,128,128]{2,1,0:T(8,128)(2,1...) custom-call(bf16[256,256]{1,0:T(8,128)(2,1)S(1)} %copy-done.3, ...), custom_call_target="tpu_custom_call" | custom-call | flops 167772160 | bytes 2097152 | tf_op jit(solution)/shard_map/pallas_call | solution.py:658
  13.7 0.5 %collective-permute-start = (bf16[4,128,128]{2,1,0:T(8,128)(2,1)S(1)}, bf16[4,128,128]{2,1,0:T(8,128)(2,1)S(1)}, u32[]{:S(2)}, u32[]{:S(2)}) collective-permute-start(bf16[4,128,128]{2,1,0:T(8,128)(2,1)S(1)} %get-tuple-element.47), channel_id=1, source_target_pairs={{0,1},{1,0},{2,3},{3,2},{4,5},{5,4},{6,7},{7,6},{8,9},{9,8},{10,11... | collective-permute-start | bytes 393224 | tf_op jit(solution)/shard_map/ppermute | solution.py:678
  14.2 1.7 %collective-permute-start.1 = (bf16[4,128,128]{2,1,0:T(8,128)(2,1)S(1)}, bf16[4,128,128]{2,1,0:T(8,128)(2,1)S(1)}, u32[]{:S(2)}, u32[]{:S(2)}) collective-permute-start(bf16[4,128,128]{2,1,0:T(8,128)(2,1)S(1)} %get-tuple-element.48), channel_id=1, source_target_pairs={{0,2},{1,3},{2,0},{3,1},{4,6},{5,7},{6,4},{7,5},{8,10},{9,11},{10,... | collective-permute-start | bytes 393224 | tf_op jit(solution)/shard_map/ppermute | solution.py:678
  15.9 0.0 copy-done.5
  15.9 0.1 copy.18
  16.0 0.1 copy.19.weight_ref
  16.2 0.0 collective-permute-done.3.refs_1_
  16.2 0.1 collective-permute-start.2
  16.3 0.0 collective-permute-done.4.refs_2_
  16.3 0.7 %collective-permute-done.5.refs_3_ = bf16[4,32,128]{2,1,0:T(8,128)(2,1)S(1)} collective-permute-done((bf16[4,32,128]{2,1,0:T(8,128)(2,1)S(1)}, bf16[4,32,128]{2,1,0:T(8,128)(2,1)S(1)}, u32[]{:S(2)}, u32[]{:S(2)}) %collective-permute-start.5) | collective-permute-done | bytes 32800 | tf_op jit(solution)/shard_map/ppermute | solution.py:678
  17.0 2.0 %all-to-all-done.recv_ref = bf16[32,24,128]{2,1,0:T(8,128)(2,1)S(1)} async-done(((bf16[32,24,128]{2,1,0:T(8,128)(2,1)}), bf16[32,24,128]{2,1,0:T(8,128)(2,1)S(1)}, u32[]{:S(2)}, u32[]{:S(2)}) %all-to-all-start) | async-done | bytes 196640 | tf_op jit(solution)/shard_map/all_to_all | solution.py:643
  19.0 1.4 %shard_map.159 = (bf16[8,4,8,128]{3,2,1,0:T(8,128)(2,1)S(1)}, bf16[4,32,128]{2,1,0:T(8,128)(2,1)S(1)}, bf16[4,32,128]{2,1,0:T(8,128)(2,1)S(1)}, bf16[4,32,128]{2,1,0:T(8,128)(2,1)S(1)}, bf16[4,32,128]{2,1,0:T(8,128)(2,1)S(1)}) custom-call(bf16[32,24,128]{2,1,0:T(8,128)(2,1)S(1)} %all-to-all-done.recv_ref, bf16[4,128,256]{2,1,0:T(8,128)(2,1)S(1)} %copy.19.weight_ref, ...), custom_call_target="tpu_custom_call" | custom-call | flops 268435456 | bytes 1048576 | tf_op jit(solution)/shard_map/pallas_call | solution.py:689
  20.4 10.3 %all_to_all.15.bias_ref = bf16[32,8,128]{2,1,0:T(8,128)(2,1)S(1)} all-to-all(bf16[32,8,128]{2,1,0:T(8,128)(2,1)S(1)} %bitcast.16), channel_id=1, replica_groups=mesh['grp'=1,'row'=32,'col'=1] {'row'}, dimensions={0} | all-to-all | bytes 131072 | tf_op jit(solution)/shard_map/all_to_all | solution.py:704
  30.7 0.2 shard_map.160.refs_4_
  30.8 0.0 collective-permute-done.refs_1_
  30.8 0.0 collective-permute-done.1.refs_2_
  30.9 0.0 collective-permute-done.2.refs_3_
  30.9 1.6 %shard_map.161 = (bf16[32,8,128]{2,1,0:T(8,128)(2,1)}, bf16[8,256,128]{2,1,0:T(8,128)(2,1)S(1)}, bf16[8,128,128]{2,1,0:T(8,128)(2,1)S(1)}) custom-call(bf16[4,128,128]{2,1,0:T(8,128)(2,1)S(1)} %get-tuple-element.46.refs_0_, bf16[4,128,128]{2,1,0:T(8,128)(2,1)S(1)} %collective-permute-done.refs_1_, bf16[4,128,128]{2,1,0:T(8,128)(2,1)S(1)} %collective-permute-done.1.refs_2_, ...), custom_call_target="tpu_custom_call" | custom-call | flops 268435456 | bytes 4194304 | tf_op jit(solution)/shard_map/pallas_call | solution.py:716
  32.5 2.6 %all-to-all-start.2 = ((bf16[32,8,128]{2,1,0:T(8,128)(2,1)}), bf16[32,8,128]{2,1,0:T(8,128)(2,1)S(1)}, u32[]{:S(2)}, u32[]{:S(2)}) async-start(bf16[32,8,128]{2,1,0:T(8,128)(2,1)} %get-tuple-element.54), calls=%async_computation.2 | async-start | bytes 131072 | tf_op jit(solution)/shard_map/all_to_all | solution.py:728
  35.0 0.4 %shard_map.162 = (bf16[2,128,128]{2,1,0:T(8,128)(2,1)S(1)}, bf16[2,128,128]{2,1,0:T(8,128)(2,1)S(1)}, bf16[2,128,128]{2,1,0:T(8,128)(2,1)S(1)}, bf16[2,128,128]{2,1,0:T(8,128)(2,1)S(1)}) custom-call(bf16[8,256,128]{2,1,0:T(8,128)(2,1)S(1)} %get-tuple-element.56.weights_ref, bf16[8,128,128]{2,1,0:T(8,128)(2,1)S(1)} %get-tuple-element.57.value_ref, ...), custom_call_target="tpu_custom_call" | custom-call | flops 268435456 | bytes 2097152 | tf_op jit(solution)/shard_map/pallas_call | solution.py:729
  35.5 0.2 collective-permute-start.6
  35.7 1.7 %collective-permute-start.7 = (bf16[2,128,128]{2,1,0:T(8,128)(2,1)S(1)}, bf16[2,128,128]{2,1,0:T(8,128)(2,1)S(1)}, u32[]{:S(2)}, u32[]{:S(2)}) collective-permute-start(bf16[2,128,128]{2,1,0:T(8,128)(2,1)S(1)} %get-tuple-element.64), channel_id=1, source_target_pairs={{0,2},{1,3},{2,0},{3,1},{4,6},{5,7},{6,4},{7,5},{8,10},{9,11},{10,... | collective-permute-start | bytes 196616 | tf_op jit(solution)/shard_map/ppermute | solution.py:678
  37.4 0.1 collective-permute-start.8
  37.5 0.0 collective-permute-done.6.refs_1_
  37.5 3.0 %collective-permute-done.7.refs_2_ = bf16[2,128,128]{2,1,0:T(8,128)(2,1)S(1)} collective-permute-done((bf16[2,128,128]{2,1,0:T(8,128)(2,1)S(1)}, bf16[2,128,128]{2,1,0:T(8,128)(2,1)S(1)}, u32[]{:S(2)}, u32[]{:S(2)}) %collective-permute-start.7) | collective-permute-done | bytes 65568 | tf_op jit(solution)/shard_map/ppermute | solution.py:678
  40.5 1.4 %collective-permute-done.8.refs_3_ = bf16[2,128,128]{2,1,0:T(8,128)(2,1)S(1)} collective-permute-done((bf16[2,128,128]{2,1,0:T(8,128)(2,1)S(1)}, bf16[2,128,128]{2,1,0:T(8,128)(2,1)S(1)}, u32[]{:S(2)}, u32[]{:S(2)}) %collective-permute-start.8) | collective-permute-done | bytes 65568 | tf_op jit(solution)/shard_map/ppermute | solution.py:678
  41.9 0.3 shard_map.163
  42.2 0.3 all-to-all-done.2.shares_ref
  42.5 1.1 %shard_map.164 = (bf16[256,256]{1,0:T(8,128)(2,1)}, bf16[4,128,128]{2,1,0:T(8,128)(2,1)}, f32[4,128,128]{2,1,0:T(8,128)}) custom-call(bf16[32,8,128]{2,1,0:T(8,128)(2,1)S(1)} %all-to-all-done.2.shares_ref, f32[16,128]{1,0:T(8,128)S(1)} %get-tuple-element.51.aux_ref.mask_ref, f32[4,128,128]{2,1,0:T(8,128)S(1)} %get-tuple-element.66.normal_ref, ...), custom_call_target="tpu_custom_call" | custom-call | flops 16777216 | bytes 1048576 | tf_op jit(solution)/shard_map/pallas_call | solution.py:748
  (2 shorter events, 0.0 us)
Async XLA Ops:
  2.8 7.4 %copy-start.7 = (bf16[256,256]{1,0:T(8,128)(2,1)S(1)}, bf16[256,256]{1,0:T(8,128)(2,1)}, u32[]{:S(2)}) copy-start(bf16[256,256]{1,0:T(8,128)(2,1)} %param.25) | copy-start | bytes 393220
  2.8 7.4 %copy-start.8 = (bf16[256,256]{1,0:T(8,128)(2,1)S(1)}, bf16[256,256]{1,0:T(8,128)(2,1)}, u32[]{:S(2)}) copy-start(bf16[256,256]{1,0:T(8,128)(2,1)} %param.24) | copy-start | bytes 393220
  2.8 7.4 %copy-start.9 = (bf16[256,256]{1,0:T(8,128)(2,1)S(1)}, bf16[256,256]{1,0:T(8,128)(2,1)}, u32[]{:S(2)}) copy-start(bf16[256,256]{1,0:T(8,128)(2,1)} %param.23) | copy-start | bytes 393220
  2.8 16.2 %all-to-all-start = ((bf16[32,24,128]{2,1,0:T(8,128)(2,1)}), bf16[32,24,128]{2,1,0:T(8,128)(2,1)S(1)}, u32[]{:S(2)}, u32[]{:S(2)}) async-start(bf16[32,24,128]{2,1,0:T(8,128)(2,1)} %bitcast.22), calls=%async_computation | async-start | bytes 393216 | tf_op jit(solution)/shard_map/all_to_all | solution.py:643
  10.2 0.9 %copy-start.6 = (bf16[4,128,128]{2,1,0:T(8,128)(2,1)S(1)}, bf16[4,128,128]{2,1,0:T(8,128)(2,1)}, u32[]{:S(2)}) copy-start(bf16[4,128,128]{2,1,0:T(8,128)(2,1)} %param.15) | copy-start | bytes 393220
  10.2 2.9 %copy-start.2 = (bf16[256,256]{1,0:T(8,128)(2,1)S(1)}, bf16[256,256]{1,0:T(8,128)(2,1)}, u32[]{:S(2)}) copy-start(bf16[256,256]{1,0:T(8,128)(2,1)} %wg_ref.1) | copy-start | bytes 393220
  10.2 2.9 %copy-start.3 = (bf16[256,256]{1,0:T(8,128)(2,1)S(1)}, bf16[256,256]{1,0:T(8,128)(2,1)}, u32[]{:S(2)}) copy-start(bf16[256,256]{1,0:T(8,128)(2,1)} %get-tuple-element.39.normed_ref) | copy-start | bytes 393220
  11.1 2.0 %copy-start = (bf16[256,256]{1,0:T(8,128)(2,1)S(1)}, bf16[256,256]{1,0:T(8,128)(2,1)}, u32[]{:S(2)}) copy-start(bf16[256,256]{1,0:T(8,128)(2,1)} %wo_ref.3) | copy-start | bytes 393220
  11.1 2.1 %copy-start.1 = (bf16[2,128,256]{2,1,0:T(8,128)(2,1)S(1)}, bf16[2,128,256]{2,1,0:T(8,128)(2,1)}, u32[]{:S(2)}) copy-start(bf16[2,128,256]{2,1,0:T(8,128)(2,1)} %param.16) | copy-start | bytes 393220
  11.1 2.0 %copy-start.4 = (f32[16,128]{1,0:T(8,128)S(1)}, f32[16,128]{1,0:T(8,128)}, u32[]{:S(2)}) copy-start(f32[16,128]{1,0:T(8,128)} %get-tuple-element.44.aux_ref) | copy-start | bytes 24580
  11.1 5.0 %collective-permute-start.3 = (bf16[4,32,128]{2,1,0:T(8,128)(2,1)S(1)}, bf16[4,32,128]{2,1,0:T(8,128)(2,1)S(1)}, u32[]{:S(2)}, u32[]{:S(2)}) collective-permute-start(bf16[4,32,128]{2,1,0:T(8,128)(2,1)S(1)} %get-tuple-element.75), channel_id=1, source_target_pairs={{0,1},{1,0},{2,3},{3,2},{4,5},{5,4},{6,7},{7,6},{8,9},{9,8},{10,11... | collective-permute-start | bytes 98312 | tf_op jit(solution)/shard_map/ppermute | solution.py:678
  11.4 4.8 %collective-permute-start.4 = (bf16[4,32,128]{2,1,0:T(8,128)(2,1)S(1)}, bf16[4,32,128]{2,1,0:T(8,128)(2,1)S(1)}, u32[]{:S(2)}, u32[]{:S(2)}) collective-permute-start(bf16[4,32,128]{2,1,0:T(8,128)(2,1)S(1)} %get-tuple-element.74), channel_id=1, source_target_pairs={{0,2},{1,3},{2,0},{3,1},{4,6},{5,7},{6,4},{7,5},{8,10},{9,11},{10,... | collective-permute-start | bytes 98312 | tf_op jit(solution)/shard_map/ppermute | solution.py:678
  13.1 3.9 %collective-permute-start.5 = (bf16[4,32,128]{2,1,0:T(8,128)(2,1)S(1)}, bf16[4,32,128]{2,1,0:T(8,128)(2,1)S(1)}, u32[]{:S(2)}, u32[]{:S(2)}) collective-permute-start(bf16[4,32,128]{2,1,0:T(8,128)(2,1)S(1)} %get-tuple-element.73), channel_id=1, source_target_pairs={{0,3},{1,2},{2,1},{3,0},{4,7},{5,6},{6,5},{7,4},{8,11},{9,10},{10,... | collective-permute-start | bytes 98312 | tf_op jit(solution)/shard_map/ppermute | solution.py:678
  13.2 2.7 %copy-start.5 = (bf16[32,32,128]{2,1,0:T(8,128)(2,1)S(1)}, bf16[32,32,128]{2,1,0:T(8,128)(2,1)}, u32[]{:S(2)}) copy-start(bf16[32,32,128]{2,1,0:T(8,128)(2,1)} %param.21) | copy-start | bytes 786436
  13.7 17.1 %collective-permute-start = (bf16[4,128,128]{2,1,0:T(8,128)(2,1)S(1)}, bf16[4,128,128]{2,1,0:T(8,128)(2,1)S(1)}, u32[]{:S(2)}, u32[]{:S(2)}) collective-permute-start(bf16[4,128,128]{2,1,0:T(8,128)(2,1)S(1)} %get-tuple-element.47), channel_id=1, source_target_pairs={{0,1},{1,0},{2,3},{3,2},{4,5},{5,4},{6,7},{7,6},{8,9},{9,8},{10,11... | collective-permute-start | bytes 393224 | tf_op jit(solution)/shard_map/ppermute | solution.py:678
  14.2 16.6 %collective-permute-start.1 = (bf16[4,128,128]{2,1,0:T(8,128)(2,1)S(1)}, bf16[4,128,128]{2,1,0:T(8,128)(2,1)S(1)}, u32[]{:S(2)}, u32[]{:S(2)}) collective-permute-start(bf16[4,128,128]{2,1,0:T(8,128)(2,1)S(1)} %get-tuple-element.48), channel_id=1, source_target_pairs={{0,2},{1,3},{2,0},{3,1},{4,6},{5,7},{6,4},{7,5},{8,10},{9,11},{10,... | collective-permute-start | bytes 393224 | tf_op jit(solution)/shard_map/ppermute | solution.py:678
  16.2 14.7 %collective-permute-start.2 = (bf16[4,128,128]{2,1,0:T(8,128)(2,1)S(1)}, bf16[4,128,128]{2,1,0:T(8,128)(2,1)S(1)}, u32[]{:S(2)}, u32[]{:S(2)}) collective-permute-start(bf16[4,128,128]{2,1,0:T(8,128)(2,1)S(1)} %get-tuple-element.49), channel_id=1, source_target_pairs={{0,3},{1,2},{2,1},{3,0},{4,7},{5,6},{6,5},{7,4},{8,11},{9,10},{10,... | collective-permute-start | bytes 393224 | tf_op jit(solution)/shard_map/ppermute | solution.py:678
  32.5 10.0 %all-to-all-start.2 = ((bf16[32,8,128]{2,1,0:T(8,128)(2,1)}), bf16[32,8,128]{2,1,0:T(8,128)(2,1)S(1)}, u32[]{:S(2)}, u32[]{:S(2)}) async-start(bf16[32,8,128]{2,1,0:T(8,128)(2,1)} %get-tuple-element.54), calls=%async_computation.2 | async-start | bytes 131072 | tf_op jit(solution)/shard_map/all_to_all | solution.py:728
  35.5 2.0 %collective-permute-start.6 = (bf16[2,128,128]{2,1,0:T(8,128)(2,1)S(1)}, bf16[2,128,128]{2,1,0:T(8,128)(2,1)S(1)}, u32[]{:S(2)}, u32[]{:S(2)}) collective-permute-start(bf16[2,128,128]{2,1,0:T(8,128)(2,1)S(1)} %get-tuple-element.63), channel_id=1, source_target_pairs={{0,1},{1,0},{2,3},{3,2},{4,5},{5,4},{6,7},{7,6},{8,9},{9,8},{10,11... | collective-permute-start | bytes 196616 | tf_op jit(solution)/shard_map/ppermute | solution.py:678
  35.7 4.8 %collective-permute-start.7 = (bf16[2,128,128]{2,1,0:T(8,128)(2,1)S(1)}, bf16[2,128,128]{2,1,0:T(8,128)(2,1)S(1)}, u32[]{:S(2)}, u32[]{:S(2)}) collective-permute-start(bf16[2,128,128]{2,1,0:T(8,128)(2,1)S(1)} %get-tuple-element.64), channel_id=1, source_target_pairs={{0,2},{1,3},{2,0},{3,1},{4,6},{5,7},{6,4},{7,5},{8,10},{9,11},{10,... | collective-permute-start | bytes 196616 | tf_op jit(solution)/shard_map/ppermute | solution.py:678
  37.4 4.5 %collective-permute-start.8 = (bf16[2,128,128]{2,1,0:T(8,128)(2,1)S(1)}, bf16[2,128,128]{2,1,0:T(8,128)(2,1)S(1)}, u32[]{:S(2)}, u32[]{:S(2)}) collective-permute-start(bf16[2,128,128]{2,1,0:T(8,128)(2,1)S(1)} %get-tuple-element.65), channel_id=1, source_target_pairs={{0,3},{1,2},{2,1},{3,0},{4,7},{5,6},{6,5},{7,4},{8,11},{9,10},{10,... | collective-permute-start | bytes 196616 | tf_op jit(solution)/shard_map/ppermute | solution.py:678

commit v12 on v11

--- a/solution.py
+++ b/solution.py
@@ -396,7 +396,7 @@
                 picked = jnp.where(lane_group == (q + a) % 4, outer[a][:, span], picked)
             for b in range(4):
                 obuf[q, g * 32 : (g + 1) * 32, b * LANES : (b + 1) * LANES] = picked[b * 32 : (b + 1) * 32]
-        part = dot_nn(weight_ref[q], obuf[q])
+        part = dot_tn(weight_ref[q], obuf[q])
         if q:
             part = jnp.concatenate(
                 [pltpu.roll(part[:, b * LANES : (b + 1) * LANES], LANES - 32 * q, 1) for b in range(4)], axis=1
@@ -682,8 +682,8 @@
     blocks = trade(blocks)
     weight_t = (
         outer_weight.reshape(factor, 4, 8, pair_channels)
-        .transpose(1, 3, 2, 0)
-        .reshape(4, pair_channels, 8 * factor)
+        .transpose(1, 2, 0, 3)
+        .reshape(4, 8 * factor, pair_channels)
     )
     share_rows = 4 * group_heads
     send_bias, *updated = kernel_call(

time: 43.9 us -> 43.8 us (level)
    unnamed x21 -> x20, local copies, waits for them, and re-layouts: 0.97 us -> 0.86 us
  transfers between devices with their start and end apart: 11 -> 11, of which waited for: 5 -> 5; matrix products, arithmetic and copies ran while one was open for 1% -> 0% of each run, Pallas kernels for 6% -> 7%
where the time goes in v12:
time: 43.8 us; the launch traced here: 43.4 us
  starting transfers between devices  16.1 us (37%)
  blocking collectives  10.1 us (23%)
  Pallas kernels  7.72 us (18%)
  waiting for transfers between devices  7.61 us (17%)
  local copies, waits for them, and re-layouts  0.98 us (2%)
  between operations  0.9 us (2%)
    all_to_all x1, blocking collectives, on_device_paired(): lax.all_to_all(send_bias.reshape(peers, share_rows, LANES), 'row', split_...  10.1 us
    all_to_all x1, starting transfers between devices, on_device_paired(): lax.all_to_all(send.reshape(peers, block_rows, LANES), 'row', split_axis=...  7.3 us
    ppermute x9, starting transfers between devices, trade(): lax.ppermute(parts[d], 'row', [(i, i ^ d) for i in range(peers)])  6.21 us
    ppermute x9, waiting for transfers between devices, trade(): lax.ppermute(parts[d], 'row', [(i, i ^ d) for i in range(peers)])  5.33 us
    all_to_all x1, starting transfers between devices, on_device_paired(): lax.all_to_all(send_grad, 'row', split_axis=0, concat_axis=0, tiled=True)  2.57 us
    pallas_call x1, Pallas kernels, on_device_paired(): kernel_call(factors_kernel, [shape((lines, GROUP, block_rows, LANES), bf1...  2.17 us
    all_to_all x1, waiting for transfers between devices, on_device_paired(): lax.all_to_all(send.reshape(peers, block_rows, LANES), 'row', split_axis=...  2.02 us
    pallas_call x1, Pallas kernels, on_device_paired(): kernel_call(lambda *refs: bias_gradient_kernel(scale, *refs), [shape((pee...  1.61 us
  transfers between devices with their start and end apart: 11, of which 5 were waited for; matrix products, arithmetic and copies ran while one was open for 0% of the time, Pallas kernels for 7%

profile of v12, /device:TPU:0, one launch (start us, length us, event | category | flops | bytes accessed | tf_op | source)
XLA Modules:
  0.0 43.4 jit_solution(13785980240110614584)
XLA Ops:
  0.6 2.2 %shard_map.157 = (bf16[8,4,24,128]{3,2,1,0:T(8,128)(2,1)}, f32[16,128]{1,0:T(8,128)}, bf16[256,256]{1,0:T(8,128)(2,1)}) custom-call(s32[64]{0:T(128)} %seq_smem_ref.1, s32[128]{0:T(128)} %res_smem_ref.1, s32[1,64]{1,0:T(1,128)} %bitcast.26, s32[1,128]{1,0:T(1,128)} %bitcast.27, bf16[8,128]{1,0:T(8,128)(2,1)} %bitcast.25, bf16[32,256]{1,0:T(8,128)(2,1)} %bitcast.23, ...), custom_call_target="tpu_custom_call" | custom-call | flops 16777216 | bytes 1048576 | tf_op jit(solution)/shard_map/pallas_call | solution.py:620
  2.8 0.0 copy-start.7
  2.8 0.0 copy-start.8
  2.8 0.0 copy-start.9
  2.8 7.3 %all-to-all-start = ((bf16[32,24,128]{2,1,0:T(8,128)(2,1)}), bf16[32,24,128]{2,1,0:T(8,128)(2,1)S(1)}, u32[]{:S(2)}, u32[]{:S(2)}) async-start(bf16[32,24,128]{2,1,0:T(8,128)(2,1)} %bitcast.22), calls=%async_computation | async-start | bytes 393216 | tf_op jit(solution)/shard_map/all_to_all | solution.py:643
  10.2 0.0 copy-done.7
  10.2 0.0 copy-done.8
  10.2 0.0 copy-done.9
  10.2 0.0 copy-start.6
  10.2 0.0 copy-start.2
  10.2 0.0 copy-start.3
  10.3 0.8 %copy-done.6 = bf16[4,128,128]{2,1,0:T(8,128)(2,1)S(1)} copy-done((bf16[4,128,128]{2,1,0:T(8,128)(2,1)S(1)}, bf16[4,128,128]{2,1,0:T(8,128)(2,1)}, u32[]{:S(2)}) %copy-start.6) | copy-done | bytes 131096
  11.1 0.0 copy-start
  11.1 0.0 copy-start.1
  11.1 0.0 copy-start.4
  11.1 0.3 collective-permute-start.3
  11.4 1.7 %collective-permute-start.4 = (bf16[4,32,128]{2,1,0:T(8,128)(2,1)S(1)}, bf16[4,32,128]{2,1,0:T(8,128)(2,1)S(1)}, u32[]{:S(2)}, u32[]{:S(2)}) collective-permute-start(bf16[4,32,128]{2,1,0:T(8,128)(2,1)S(1)} %get-tuple-element.74), channel_id=1, source_target_pairs={{0,2},{1,3},{2,0},{3,1},{4,6},{5,7},{6,4},{7,5},{8,10},{9,11},{10,... | collective-permute-start | bytes 98312 | tf_op jit(solution)/shard_map/ppermute | solution.py:678
  13.1 0.0 collective-permute-start.5
  13.1 0.0 copy-done.2
  13.1 0.0 copy-done.3
  13.1 0.0 copy-done
  13.2 0.0 copy-done.1
  13.2 0.0 copy-done.4
  13.2 0.0 copy-start.5
  13.2 0.5 %shard_map.158 = (f32[4,128,128]{2,1,0:T(8,128)S(1)}, f32[16,128]{1,0:T(8,128)S(1)}, bf16[4,32,128]{2,1,0:T(8,128)(2,1)S(1)}, bf16[4,128,128]{2,1,0:T(8,128)(2,1...) custom-call(bf16[256,256]{1,0:T(8,128)(2,1)S(1)} %copy-done.3, ...), custom_call_target="tpu_custom_call" | custom-call | flops 167772160 | bytes 2097152 | tf_op jit(solution)/shard_map/pallas_call | solution.py:658
  13.7 0.5 %collective-permute-start = (bf16[4,128,128]{2,1,0:T(8,128)(2,1)S(1)}, bf16[4,128,128]{2,1,0:T(8,128)(2,1)S(1)}, u32[]{:S(2)}, u32[]{:S(2)}) collective-permute-start(bf16[4,128,128]{2,1,0:T(8,128)(2,1)S(1)} %get-tuple-element.47), channel_id=1, source_target_pairs={{0,1},{1,0},{2,3},{3,2},{4,5},{5,4},{6,7},{7,6},{8,9},{9,8},{10,11... | collective-permute-start | bytes 393224 | tf_op jit(solution)/shard_map/ppermute | solution.py:678
  14.2 1.7 %collective-permute-start.1 = (bf16[4,128,128]{2,1,0:T(8,128)(2,1)S(1)}, bf16[4,128,128]{2,1,0:T(8,128)(2,1)S(1)}, u32[]{:S(2)}, u32[]{:S(2)}) collective-permute-start(bf16[4,128,128]{2,1,0:T(8,128)(2,1)S(1)} %get-tuple-element.48), channel_id=1, source_target_pairs={{0,2},{1,3},{2,0},{3,1},{4,6},{5,7},{6,4},{7,5},{8,10},{9,11},{10,... | collective-permute-start | bytes 393224 | tf_op jit(solution)/shard_map/ppermute | solution.py:678
  15.9 0.0 copy-done.5
  15.9 0.1 copy.17
  16.0 0.0 collective-permute-done.3.refs_1_
  16.0 0.1 collective-permute-start.2
  16.1 0.0 collective-permute-done.4.refs_2_
  16.1 0.9 %collective-permute-done.5.refs_3_ = bf16[4,32,128]{2,1,0:T(8,128)(2,1)S(1)} collective-permute-done((bf16[4,32,128]{2,1,0:T(8,128)(2,1)S(1)}, bf16[4,32,128]{2,1,0:T(8,128)(2,1)S(1)}, u32[]{:S(2)}, u32[]{:S(2)}) %collective-permute-start.5) | collective-permute-done | bytes 32800 | tf_op jit(solution)/shard_map/ppermute | solution.py:678
  17.0 2.0 %all-to-all-done.recv_ref = bf16[32,24,128]{2,1,0:T(8,128)(2,1)S(1)} async-done(((bf16[32,24,128]{2,1,0:T(8,128)(2,1)}), bf16[32,24,128]{2,1,0:T(8,128)(2,1)S(1)}, u32[]{:S(2)}, u32[]{:S(2)}) %all-to-all-start) | async-done | bytes 196640 | tf_op jit(solution)/shard_map/all_to_all | solution.py:643
  19.0 1.4 %shard_map.159 = (bf16[8,4,8,128]{3,2,1,0:T(8,128)(2,1)S(1)}, bf16[4,32,128]{2,1,0:T(8,128)(2,1)S(1)}, bf16[4,32,128]{2,1,0:T(8,128)(2,1)S(1)}, bf16[4,32,128]{2,1,0:T(8,128)(2,1)S(1)}, bf16[4,32,128]{2,1,0:T(8,128)(2,1)S(1)}) custom-call(bf16[32,24,128]{2,1,0:T(8,128)(2,1)S(1)} %all-to-all-done.recv_ref, bf16[4,256,128]{2,1,0:T(8,128)(2,1)S(1)} %bitcast.14, ...), custom_call_target="tpu_custom_call" | custom-call | flops 268435456 | bytes 1048576 | tf_op jit(solution)/shard_map/pallas_call | solution.py:689
  20.4 10.1 %all_to_all.15.bias_ref = bf16[32,8,128]{2,1,0:T(8,128)(2,1)S(1)} all-to-all(bf16[32,8,128]{2,1,0:T(8,128)(2,1)S(1)} %bitcast.16), channel_id=1, replica_groups=mesh['grp'=1,'row'=32,'col'=1] {'row'}, dimensions={0} | all-to-all | bytes 131072 | tf_op jit(solution)/shard_map/all_to_all | solution.py:704
  30.6 0.2 shard_map.160.refs_4_
  30.7 0.0 collective-permute-done.refs_1_
  30.7 0.0 collective-permute-done.1.refs_2_
  30.7 0.0 collective-permute-done.2.refs_3_
  30.8 1.6 %shard_map.161 = (bf16[32,8,128]{2,1,0:T(8,128)(2,1)}, bf16[8,256,128]{2,1,0:T(8,128)(2,1)S(1)}, bf16[8,128,128]{2,1,0:T(8,128)(2,1)S(1)}) custom-call(bf16[4,128,128]{2,1,0:T(8,128)(2,1)S(1)} %get-tuple-element.46.refs_0_, bf16[4,128,128]{2,1,0:T(8,128)(2,1)S(1)} %collective-permute-done.refs_1_, bf16[4,128,128]{2,1,0:T(8,128)(2,1)S(1)} %collective-permute-done.1.refs_2_, ...), custom_call_target="tpu_custom_call" | custom-call | flops 268435456 | bytes 4194304 | tf_op jit(solution)/shard_map/pallas_call | solution.py:716
  32.4 2.6 %all-to-all-start.2 = ((bf16[32,8,128]{2,1,0:T(8,128)(2,1)}), bf16[32,8,128]{2,1,0:T(8,128)(2,1)S(1)}, u32[]{:S(2)}, u32[]{:S(2)}) async-start(bf16[32,8,128]{2,1,0:T(8,128)(2,1)} %get-tuple-element.54), calls=%async_computation.2 | async-start | bytes 131072 | tf_op jit(solution)/shard_map/all_to_all | solution.py:728
  34.9 0.4 %shard_map.162 = (bf16[2,128,128]{2,1,0:T(8,128)(2,1)S(1)}, bf16[2,128,128]{2,1,0:T(8,128)(2,1)S(1)}, bf16[2,128,128]{2,1,0:T(8,128)(2,1)S(1)}, bf16[2,128,128]{2,1,0:T(8,128)(2,1)S(1)}) custom-call(bf16[8,256,128]{2,1,0:T(8,128)(2,1)S(1)} %get-tuple-element.56.weights_ref, bf16[8,128,128]{2,1,0:T(8,128)(2,1)S(1)} %get-tuple-element.57.value_ref, ...), custom_call_target="tpu_custom_call" | custom-call | flops 268435456 | bytes 2097152 | tf_op jit(solution)/shard_map/pallas_call | solution.py:729
  35.4 0.2 collective-permute-start.6
  35.6 1.7 %collective-permute-start.7 = (bf16[2,128,128]{2,1,0:T(8,128)(2,1)S(1)}, bf16[2,128,128]{2,1,0:T(8,128)(2,1)S(1)}, u32[]{:S(2)}, u32[]{:S(2)}) collective-permute-start(bf16[2,128,128]{2,1,0:T(8,128)(2,1)S(1)} %get-tuple-element.64), channel_id=1, source_target_pairs={{0,2},{1,3},{2,0},{3,1},{4,6},{5,7},{6,4},{7,5},{8,10},{9,11},{10,... | collective-permute-start | bytes 196616 | tf_op jit(solution)/shard_map/ppermute | solution.py:678
  37.3 0.1 collective-permute-start.8
  37.3 0.0 collective-permute-done.6.refs_1_
  37.3 3.0 %collective-permute-done.7.refs_2_ = bf16[2,128,128]{2,1,0:T(8,128)(2,1)S(1)} collective-permute-done((bf16[2,128,128]{2,1,0:T(8,128)(2,1)S(1)}, bf16[2,128,128]{2,1,0:T(8,128)(2,1)S(1)}, u32[]{:S(2)}, u32[]{:S(2)}) %collective-permute-start.7) | collective-permute-done | bytes 65568 | tf_op jit(solution)/shard_map/ppermute | solution.py:678
  40.3 1.4 %collective-permute-done.8.refs_3_ = bf16[2,128,128]{2,1,0:T(8,128)(2,1)S(1)} collective-permute-done((bf16[2,128,128]{2,1,0:T(8,128)(2,1)S(1)}, bf16[2,128,128]{2,1,0:T(8,128)(2,1)S(1)}, u32[]{:S(2)}, u32[]{:S(2)}) %collective-permute-start.8) | collective-permute-done | bytes 65568 | tf_op jit(solution)/shard_map/ppermute | solution.py:678
  41.8 0.3 shard_map.163
  42.1 0.3 all-to-all-done.2.shares_ref
  42.3 1.1 %shard_map.164 = (bf16[256,256]{1,0:T(8,128)(2,1)}, bf16[4,128,128]{2,1,0:T(8,128)(2,1)}, f32[4,128,128]{2,1,0:T(8,128)}) custom-call(bf16[32,8,128]{2,1,0:T(8,128)(2,1)S(1)} %all-to-all-done.2.shares_ref, f32[16,128]{1,0:T(8,128)S(1)} %get-tuple-element.51.aux_ref.mask_ref, f32[4,128,128]{2,1,0:T(8,128)S(1)} %get-tuple-element.66.normal_ref, ...), custom_call_target="tpu_custom_call" | custom-call | flops 16777216 | bytes 1048576 | tf_op jit(solution)/shard_map/pallas_call | solution.py:748
  (2 shorter events, 0.0 us)
Async XLA Ops:
  2.8 7.4 %copy-start.7 = (bf16[256,256]{1,0:T(8,128)(2,1)S(1)}, bf16[256,256]{1,0:T(8,128)(2,1)}, u32[]{:S(2)}) copy-start(bf16[256,256]{1,0:T(8,128)(2,1)} %param.25) | copy-start | bytes 393220
  2.8 7.4 %copy-start.8 = (bf16[256,256]{1,0:T(8,128)(2,1)S(1)}, bf16[256,256]{1,0:T(8,128)(2,1)}, u32[]{:S(2)}) copy-start(bf16[256,256]{1,0:T(8,128)(2,1)} %param.24) | copy-start | bytes 393220
  2.8 7.4 %copy-start.9 = (bf16[256,256]{1,0:T(8,128)(2,1)S(1)}, bf16[256,256]{1,0:T(8,128)(2,1)}, u32[]{:S(2)}) copy-start(bf16[256,256]{1,0:T(8,128)(2,1)} %param.23) | copy-start | bytes 393220
  2.8 16.2 %all-to-all-start = ((bf16[32,24,128]{2,1,0:T(8,128)(2,1)}), bf16[32,24,128]{2,1,0:T(8,128)(2,1)S(1)}, u32[]{:S(2)}, u32[]{:S(2)}) async-start(bf16[32,24,128]{2,1,0:T(8,128)(2,1)} %bitcast.22), calls=%async_computation | async-start | bytes 393216 | tf_op jit(solution)/shard_map/all_to_all | solution.py:643
  10.2 0.9 %copy-start.6 = (bf16[4,128,128]{2,1,0:T(8,128)(2,1)S(1)}, bf16[4,128,128]{2,1,0:T(8,128)(2,1)}, u32[]{:S(2)}) copy-start(bf16[4,128,128]{2,1,0:T(8,128)(2,1)} %param.15) | copy-start | bytes 393220
  10.2 2.9 %copy-start.2 = (bf16[256,256]{1,0:T(8,128)(2,1)S(1)}, bf16[256,256]{1,0:T(8,128)(2,1)}, u32[]{:S(2)}) copy-start(bf16[256,256]{1,0:T(8,128)(2,1)} %wg_ref.1) | copy-start | bytes 393220
  10.2 2.9 %copy-start.3 = (bf16[256,256]{1,0:T(8,128)(2,1)S(1)}, bf16[256,256]{1,0:T(8,128)(2,1)}, u32[]{:S(2)}) copy-start(bf16[256,256]{1,0:T(8,128)(2,1)} %get-tuple-element.39.normed_ref) | copy-start | bytes 393220
  11.1 2.0 %copy-start = (bf16[256,256]{1,0:T(8,128)(2,1)S(1)}, bf16[256,256]{1,0:T(8,128)(2,1)}, u32[]{:S(2)}) copy-start(bf16[256,256]{1,0:T(8,128)(2,1)} %wo_ref.3) | copy-start | bytes 393220
  11.1 2.1 %copy-start.1 = (bf16[2,128,256]{2,1,0:T(8,128)(2,1)S(1)}, bf16[2,128,256]{2,1,0:T(8,128)(2,1)}, u32[]{:S(2)}) copy-start(bf16[2,128,256]{2,1,0:T(8,128)(2,1)} %param.16) | copy-start | bytes 393220
  11.1 2.0 %copy-start.4 = (f32[16,128]{1,0:T(8,128)S(1)}, f32[16,128]{1,0:T(8,128)}, u32[]{:S(2)}) copy-start(f32[16,128]{1,0:T(8,128)} %get-tuple-element.44.aux_ref) | copy-start | bytes 24580
  11.1 4.9 %collective-permute-start.3 = (bf16[4,32,128]{2,1,0:T(8,128)(2,1)S(1)}, bf16[4,32,128]{2,1,0:T(8,128)(2,1)S(1)}, u32[]{:S(2)}, u32[]{:S(2)}) collective-permute-start(bf16[4,32,128]{2,1,0:T(8,128)(2,1)S(1)} %get-tuple-element.75), channel_id=1, source_target_pairs={{0,1},{1,0},{2,3},{3,2},{4,5},{5,4},{6,7},{7,6},{8,9},{9,8},{10,11... | collective-permute-start | bytes 98312 | tf_op jit(solution)/shard_map/ppermute | solution.py:678
  11.4 4.7 %collective-permute-start.4 = (bf16[4,32,128]{2,1,0:T(8,128)(2,1)S(1)}, bf16[4,32,128]{2,1,0:T(8,128)(2,1)S(1)}, u32[]{:S(2)}, u32[]{:S(2)}) collective-permute-start(bf16[4,32,128]{2,1,0:T(8,128)(2,1)S(1)} %get-tuple-element.74), channel_id=1, source_target_pairs={{0,2},{1,3},{2,0},{3,1},{4,6},{5,7},{6,4},{7,5},{8,10},{9,11},{10,... | collective-permute-start | bytes 98312 | tf_op jit(solution)/shard_map/ppermute | solution.py:678
  13.1 3.9 %collective-permute-start.5 = (bf16[4,32,128]{2,1,0:T(8,128)(2,1)S(1)}, bf16[4,32,128]{2,1,0:T(8,128)(2,1)S(1)}, u32[]{:S(2)}, u32[]{:S(2)}) collective-permute-start(bf16[4,32,128]{2,1,0:T(8,128)(2,1)S(1)} %get-tuple-element.73), channel_id=1, source_target_pairs={{0,3},{1,2},{2,1},{3,0},{4,7},{5,6},{6,5},{7,4},{8,11},{9,10},{10,... | collective-permute-start | bytes 98312 | tf_op jit(solution)/shard_map/ppermute | solution.py:678
  13.2 2.7 %copy-start.5 = (bf16[32,32,128]{2,1,0:T(8,128)(2,1)S(1)}, bf16[32,32,128]{2,1,0:T(8,128)(2,1)}, u32[]{:S(2)}) copy-start(bf16[32,32,128]{2,1,0:T(8,128)(2,1)} %param.21) | copy-start | bytes 786436
  13.7 17.0 %collective-permute-start = (bf16[4,128,128]{2,1,0:T(8,128)(2,1)S(1)}, bf16[4,128,128]{2,1,0:T(8,128)(2,1)S(1)}, u32[]{:S(2)}, u32[]{:S(2)}) collective-permute-start(bf16[4,128,128]{2,1,0:T(8,128)(2,1)S(1)} %get-tuple-element.47), channel_id=1, source_target_pairs={{0,1},{1,0},{2,3},{3,2},{4,5},{5,4},{6,7},{7,6},{8,9},{9,8},{10,11... | collective-permute-start | bytes 393224 | tf_op jit(solution)/shard_map/ppermute | solution.py:678
  14.2 16.5 %collective-permute-start.1 = (bf16[4,128,128]{2,1,0:T(8,128)(2,1)S(1)}, bf16[4,128,128]{2,1,0:T(8,128)(2,1)S(1)}, u32[]{:S(2)}, u32[]{:S(2)}) collective-permute-start(bf16[4,128,128]{2,1,0:T(8,128)(2,1)S(1)} %get-tuple-element.48), channel_id=1, source_target_pairs={{0,2},{1,3},{2,0},{3,1},{4,6},{5,7},{6,4},{7,5},{8,10},{9,11},{10,... | collective-permute-start | bytes 393224 | tf_op jit(solution)/shard_map/ppermute | solution.py:678
  16.0 14.7 %collective-permute-start.2 = (bf16[4,128,128]{2,1,0:T(8,128)(2,1)S(1)}, bf16[4,128,128]{2,1,0:T(8,128)(2,1)S(1)}, u32[]{:S(2)}, u32[]{:S(2)}) collective-permute-start(bf16[4,128,128]{2,1,0:T(8,128)(2,1)S(1)} %get-tuple-element.49), channel_id=1, source_target_pairs={{0,3},{1,2},{2,1},{3,0},{4,7},{5,6},{6,5},{7,4},{8,11},{9,10},{10,... | collective-permute-start | bytes 393224 | tf_op jit(solution)/shard_map/ppermute | solution.py:678
  32.4 10.0 %all-to-all-start.2 = ((bf16[32,8,128]{2,1,0:T(8,128)(2,1)}), bf16[32,8,128]{2,1,0:T(8,128)(2,1)S(1)}, u32[]{:S(2)}, u32[]{:S(2)}) async-start(bf16[32,8,128]{2,1,0:T(8,128)(2,1)} %get-tuple-element.54), calls=%async_computation.2 | async-start | bytes 131072 | tf_op jit(solution)/shard_map/all_to_all | solution.py:728
  35.4 2.0 %collective-permute-start.6 = (bf16[2,128,128]{2,1,0:T(8,128)(2,1)S(1)}, bf16[2,128,128]{2,1,0:T(8,128)(2,1)S(1)}, u32[]{:S(2)}, u32[]{:S(2)}) collective-permute-start(bf16[2,128,128]{2,1,0:T(8,128)(2,1)S(1)} %get-tuple-element.63), channel_id=1, source_target_pairs={{0,1},{1,0},{2,3},{3,2},{4,5},{5,4},{6,7},{7,6},{8,9},{9,8},{10,11... | collective-permute-start | bytes 196616 | tf_op jit(solution)/shard_map/ppermute | solution.py:678
  35.6 4.8 %collective-permute-start.7 = (bf16[2,128,128]{2,1,0:T(8,128)(2,1)S(1)}, bf16[2,128,128]{2,1,0:T(8,128)(2,1)S(1)}, u32[]{:S(2)}, u32[]{:S(2)}) collective-permute-start(bf16[2,128,128]{2,1,0:T(8,128)(2,1)S(1)} %get-tuple-element.64), channel_id=1, source_target_pairs={{0,2},{1,3},{2,0},{3,1},{4,6},{5,7},{6,4},{7,5},{8,10},{9,11},{10,... | collective-permute-start | bytes 196616 | tf_op jit(solution)/shard_map/ppermute | solution.py:678
  37.3 4.5 %collective-permute-start.8 = (bf16[2,128,128]{2,1,0:T(8,128)(2,1)S(1)}, bf16[2,128,128]{2,1,0:T(8,128)(2,1)S(1)}, u32[]{:S(2)}, u32[]{:S(2)}) collective-permute-start(bf16[2,128,128]{2,1,0:T(8,128)(2,1)S(1)} %get-tuple-element.65), channel_id=1, source_target_pairs={{0,3},{1,2},{2,1},{3,0},{4,7},{5,6},{6,5},{7,4},{8,11},{9,10},{10,... | collective-permute-start | bytes 196616 | tf_op jit(solution)/shard_map/ppermute | solution.py:678

commit v13 on v12

--- a/solution.py
+++ b/solution.py
@@ -496,8 +496,22 @@
         out_refs[step][1] = part_refs[step][...].reshape(residues, LANES)
 
 
-def output_kernel(gate_ref, wo_ref, *refs):
-    in_refs, (out_ref, pair_ref, normal_ref, inverse_ref) = refs[:GROUP], refs[GROUP:]
+def output_kernel(aux_ref, gate_ref, wo_ref, *refs):
+    in_refs, (out_ref, pair_ref, normal_ref, inverse_ref, both_ref) = refs[:GROUP], refs[GROUP:]
+    bias_w = aux_ref[8:16]
+    mean_high, mean_low = split_sum(
+        jnp.broadcast_to(jnp.mean(bias_w, axis=-1, keepdims=True), bias_w.shape)
+    )
+    exact = bias_w.astype(bf16)
+    none = jnp.zeros(exact.shape, bf16)
+    both_ref[...] = jnp.concatenate(
+        [
+            jnp.concatenate([exact, mean_high], axis=1),
+            jnp.concatenate([exact, mean_high], axis=1),
+            jnp.concatenate([none, mean_low], axis=1),
+        ],
+        axis=0,
+    )
     residues = gate_ref.shape[1]
     rows = pair_ref.shape[0]
     columns_each = residues // GROUP
@@ -528,7 +542,7 @@
 
 
 def gradient_kernel(
-    shares_ref, aux_ref, normal_ref, inverse_ref, update_ref, pair_ref, update_hbm, pair_hbm, out_hbm, result, left_for
+    shares_ref, both_ref, normal_ref, inverse_ref, update_ref, pair_ref, update_hbm, pair_hbm, out_hbm, result, left_for
 ):
     moves = [
         pltpu.make_async_copy(update_ref, update_hbm, left_for.at[0]),
@@ -540,20 +554,7 @@
     rows, _, channels = normal_ref.shape
     heads = share // rows
     total = jnp.sum(shares_ref[...].astype(f32).reshape(peers // GROUP, GROUP, share, LANES), axis=0)
-    bias_w = aux_ref[8:16]
-    mean_high, mean_low = split_sum(
-        jnp.broadcast_to(jnp.mean(bias_w, axis=-1, keepdims=True), bias_w.shape)
-    )
-    exact = bias_w.astype(bf16)
-    none = jnp.zeros(exact.shape, bf16)
-    weights = jnp.concatenate(
-        [
-            jnp.concatenate([exact, mean_high], axis=1),
-            jnp.concatenate([exact, mean_high], axis=1),
-            jnp.concatenate([none, mean_low], axis=1),
-        ],
-        axis=0,
-    )
+    weights = both_ref[...]
     for i in range(rows):
         own = jnp.concatenate([total[t, i * heads : (i + 1) * heads] for t in range(GROUP)], axis=0)
         high, low = split_sum(own)
@@ -733,18 +734,19 @@
         flops=1 << 28,
         moved=1 << 21,
     )(weights, values, *updated)
-    update, pair_updated, normal, inverse = kernel_call(
+    update, pair_updated, normal, inverse, both = kernel_call(
         output_kernel,
         [
             shape((token_rows, channel_count), bf16),
             shape((rows_here, residues, pair_channels), bf16),
             shape((rows_here, residues, pair_channels), f32),
             shape((rows_here, residues, pair_channels), f32),
+            shape((3 * head_count, 2 * pair_channels), bf16),
         ],
-        [vmem] * (2 + GROUP),
+        [vmem] * (3 + GROUP),
         flops=2 * token_rows * channel_count * channel_count,
         moved=1 << 20,
-    )(gate, output_weight, *trade(list(attended)))
+    )(aux, gate, output_weight, *trade(list(attended)))
     update, pair_updated, pair_gradient = kernel_call(
         gradient_kernel,
         [
@@ -757,7 +759,7 @@
         flops=1 << 24,
         moved=1 << 20,
         out_specs=[pl.BlockSpec(memory_space=pltpu.HBM)] * 3,
-    )(shares, aux, normal, inverse, update, pair_updated)
+    )(shares, both, normal, inverse, update, pair_updated)
     return (update.reshape(alignment_rows.shape), pair_updated, pair_gradient)
 
 

time: 43.8 us -> 43.7 us (level)
  no operation moved by 1% of the time
where the time goes in v13:
time: 43.7 us; the launch traced here: 43.4 us
  starting transfers between devices  16.1 us (37%)
  blocking collectives  10.1 us (23%)
  Pallas kernels  7.7 us (18%)
  waiting for transfers between devices  7.62 us (17%)
  local copies, waits for them, and re-layouts  0.98 us (2%)
  between operations  0.9 us (2%)
    all_to_all x1, blocking collectives, on_device_paired(): lax.all_to_all(send_bias.reshape(peers, share_rows, LANES), 'row', split_...  10.1 us
    all_to_all x1, starting transfers between devices, on_device_paired(): lax.all_to_all(send.reshape(peers, block_rows, LANES), 'row', split_axis=...  7.3 us
    ppermute x9, starting transfers between devices, trade(): lax.ppermute(parts[d], 'row', [(i, i ^ d) for i in range(peers)])  6.21 us
    ppermute x9, waiting for transfers between devices, trade(): lax.ppermute(parts[d], 'row', [(i, i ^ d) for i in range(peers)])  5.33 us
    all_to_all x1, starting transfers between devices, on_device_paired(): lax.all_to_all(send_grad, 'row', split_axis=0, concat_axis=0, tiled=True)  2.57 us
    pallas_call x1, Pallas kernels, on_device_paired(): kernel_call(factors_kernel, [shape((lines, GROUP, block_rows, LANES), bf1...  2.17 us
    all_to_all x1, waiting for transfers between devices, on_device_paired(): lax.all_to_all(send.reshape(peers, block_rows, LANES), 'row', split_axis=...  2.02 us
    pallas_call x1, Pallas kernels, on_device_paired(): kernel_call(lambda *refs: bias_gradient_kernel(scale, *refs), [shape((pee...  1.61 us
  transfers between devices with their start and end apart: 11, of which 5 were waited for; matrix products, arithmetic and copies ran while one was open for 0% of the time, Pallas kernels for 7%

profile of v13, /device:TPU:0, one launch (start us, length us, event | category | flops | bytes accessed | tf_op | source)
XLA Modules:
  0.0 43.4 jit_solution(10821753556183086807)
XLA Ops:
  0.6 2.2 %shard_map.157 = (bf16[8,4,24,128]{3,2,1,0:T(8,128)(2,1)}, f32[16,128]{1,0:T(8,128)}, bf16[256,256]{1,0:T(8,128)(2,1)}) custom-call(s32[64]{0:T(128)} %seq_smem_ref.1, s32[128]{0:T(128)} %res_smem_ref.1, s32[1,64]{1,0:T(1,128)} %bitcast.26, s32[1,128]{1,0:T(1,128)} %bitcast.27, bf16[8,128]{1,0:T(8,128)(2,1)} %bitcast.25, bf16[32,256]{1,0:T(8,128)(2,1)} %bitcast.23, ...), custom_call_target="tpu_custom_call" | custom-call | flops 16777216 | bytes 1048576 | tf_op jit(solution)/shard_map/pallas_call | solution.py:621
  2.8 0.0 copy-start.7
  2.8 0.0 copy-start.8
  2.8 0.0 copy-start.9
  2.8 7.3 %all-to-all-start = ((bf16[32,24,128]{2,1,0:T(8,128)(2,1)}), bf16[32,24,128]{2,1,0:T(8,128)(2,1)S(1)}, u32[]{:S(2)}, u32[]{:S(2)}) async-start(bf16[32,24,128]{2,1,0:T(8,128)(2,1)} %bitcast.22), calls=%async_computation | async-start | bytes 393216 | tf_op jit(solution)/shard_map/all_to_all | solution.py:644
  10.2 0.0 copy-done.7
  10.2 0.0 copy-done.8
  10.2 0.0 copy-done.9
  10.2 0.0 copy-start.6
  10.2 0.0 copy-start.2
  10.2 0.0 copy-start.3
  10.3 0.8 %copy-done.6 = bf16[4,128,128]{2,1,0:T(8,128)(2,1)S(1)} copy-done((bf16[4,128,128]{2,1,0:T(8,128)(2,1)S(1)}, bf16[4,128,128]{2,1,0:T(8,128)(2,1)}, u32[]{:S(2)}) %copy-start.6) | copy-done | bytes 131096
  11.1 0.0 copy-start
  11.1 0.0 copy-start.1
  11.1 0.0 copy-start.4
  11.1 0.3 collective-permute-start.3
  11.4 1.7 %collective-permute-start.4 = (bf16[4,32,128]{2,1,0:T(8,128)(2,1)S(1)}, bf16[4,32,128]{2,1,0:T(8,128)(2,1)S(1)}, u32[]{:S(2)}, u32[]{:S(2)}) collective-permute-start(bf16[4,32,128]{2,1,0:T(8,128)(2,1)S(1)} %get-tuple-element.76), channel_id=1, source_target_pairs={{0,2},{1,3},{2,0},{3,1},{4,6},{5,7},{6,4},{7,5},{8,10},{9,11},{10,... | collective-permute-start | bytes 98312 | tf_op jit(solution)/shard_map/ppermute | solution.py:679
  13.1 0.0 collective-permute-start.5
  13.1 0.0 copy-done.2
  13.1 0.0 copy-done.3
  13.1 0.0 copy-done
  13.2 0.0 copy-done.1
  13.2 0.0 copy-done.4
  13.2 0.0 copy-start.5
  13.2 0.5 %shard_map.158 = (f32[4,128,128]{2,1,0:T(8,128)S(1)}, f32[16,128]{1,0:T(8,128)S(1)}, bf16[4,32,128]{2,1,0:T(8,128)(2,1)S(1)}, bf16[4,128,128]{2,1,0:T(8,128)(2,1...) custom-call(bf16[256,256]{1,0:T(8,128)(2,1)S(1)} %copy-done.3, ...), custom_call_target="tpu_custom_call" | custom-call | flops 167772160 | bytes 2097152 | tf_op jit(solution)/shard_map/pallas_call | solution.py:659
  13.7 0.5 %collective-permute-start = (bf16[4,128,128]{2,1,0:T(8,128)(2,1)S(1)}, bf16[4,128,128]{2,1,0:T(8,128)(2,1)S(1)}, u32[]{:S(2)}, u32[]{:S(2)}) collective-permute-start(bf16[4,128,128]{2,1,0:T(8,128)(2,1)S(1)} %get-tuple-element.48), channel_id=1, source_target_pairs={{0,1},{1,0},{2,3},{3,2},{4,5},{5,4},{6,7},{7,6},{8,9},{9,8},{10,11... | collective-permute-start | bytes 393224 | tf_op jit(solution)/shard_map/ppermute | solution.py:679
  14.2 1.7 %collective-permute-start.1 = (bf16[4,128,128]{2,1,0:T(8,128)(2,1)S(1)}, bf16[4,128,128]{2,1,0:T(8,128)(2,1)S(1)}, u32[]{:S(2)}, u32[]{:S(2)}) collective-permute-start(bf16[4,128,128]{2,1,0:T(8,128)(2,1)S(1)} %get-tuple-element.49), channel_id=1, source_target_pairs={{0,2},{1,3},{2,0},{3,1},{4,6},{5,7},{6,4},{7,5},{8,10},{9,11},{10,... | collective-permute-start | bytes 393224 | tf_op jit(solution)/shard_map/ppermute | solution.py:679
  15.9 0.0 copy-done.5
  15.9 0.1 copy.17
  16.0 0.0 collective-permute-done.3.refs_1_
  16.0 0.1 collective-permute-start.2
  16.1 0.0 collective-permute-done.4.refs_2_
  16.1 0.9 %collective-permute-done.5.refs_3_ = bf16[4,32,128]{2,1,0:T(8,128)(2,1)S(1)} collective-permute-done((bf16[4,32,128]{2,1,0:T(8,128)(2,1)S(1)}, bf16[4,32,128]{2,1,0:T(8,128)(2,1)S(1)}, u32[]{:S(2)}, u32[]{:S(2)}) %collective-permute-start.5) | collective-permute-done | bytes 32800 | tf_op jit(solution)/shard_map/ppermute | solution.py:679
  17.0 2.0 %all-to-all-done.recv_ref = bf16[32,24,128]{2,1,0:T(8,128)(2,1)S(1)} async-done(((bf16[32,24,128]{2,1,0:T(8,128)(2,1)}), bf16[32,24,128]{2,1,0:T(8,128)(2,1)S(1)}, u32[]{:S(2)}, u32[]{:S(2)}) %all-to-all-start) | async-done | bytes 196640 | tf_op jit(solution)/shard_map/all_to_all | solution.py:644
  19.0 1.4 %shard_map.159 = (bf16[8,4,8,128]{3,2,1,0:T(8,128)(2,1)S(1)}, bf16[4,32,128]{2,1,0:T(8,128)(2,1)S(1)}, bf16[4,32,128]{2,1,0:T(8,128)(2,1)S(1)}, bf16[4,32,128]{2,1,0:T(8,128)(2,1)S(1)}, bf16[4,32,128]{2,1,0:T(8,128)(2,1)S(1)}) custom-call(bf16[32,24,128]{2,1,0:T(8,128)(2,1)S(1)} %all-to-all-done.recv_ref, bf16[4,256,128]{2,1,0:T(8,128)(2,1)S(1)} %bitcast.14, ...), custom_call_target="tpu_custom_call" | custom-call | flops 268435456 | bytes 1048576 | tf_op jit(solution)/shard_map/pallas_call | solution.py:690
  20.4 10.1 %all_to_all.15.bias_ref = bf16[32,8,128]{2,1,0:T(8,128)(2,1)S(1)} all-to-all(bf16[32,8,128]{2,1,0:T(8,128)(2,1)S(1)} %bitcast.16), channel_id=1, replica_groups=mesh['grp'=1,'row'=32,'col'=1] {'row'}, dimensions={0} | all-to-all | bytes 131072 | tf_op jit(solution)/shard_map/all_to_all | solution.py:705
  30.6 0.2 shard_map.160.refs_4_
  30.7 0.0 collective-permute-done.refs_1_
  30.7 0.0 collective-permute-done.1.refs_2_
  30.7 0.0 collective-permute-done.2.refs_3_
  30.8 1.6 %shard_map.161 = (bf16[32,8,128]{2,1,0:T(8,128)(2,1)}, bf16[8,256,128]{2,1,0:T(8,128)(2,1)S(1)}, bf16[8,128,128]{2,1,0:T(8,128)(2,1)S(1)}) custom-call(bf16[4,128,128]{2,1,0:T(8,128)(2,1)S(1)} %get-tuple-element.47.refs_0_, bf16[4,128,128]{2,1,0:T(8,128)(2,1)S(1)} %collective-permute-done.refs_1_, bf16[4,128,128]{2,1,0:T(8,128)(2,1)S(1)} %collective-permute-done.1.refs_2_, ...), custom_call_target="tpu_custom_call" | custom-call | flops 268435456 | bytes 4194304 | tf_op jit(solution)/shard_map/pallas_call | solution.py:717
  32.4 2.6 %all-to-all-start.2 = ((bf16[32,8,128]{2,1,0:T(8,128)(2,1)}), bf16[32,8,128]{2,1,0:T(8,128)(2,1)S(1)}, u32[]{:S(2)}, u32[]{:S(2)}) async-start(bf16[32,8,128]{2,1,0:T(8,128)(2,1)} %get-tuple-element.55), calls=%async_computation.2 | async-start | bytes 131072 | tf_op jit(solution)/shard_map/all_to_all | solution.py:729
  34.9 0.4 %shard_map.162 = (bf16[2,128,128]{2,1,0:T(8,128)(2,1)S(1)}, bf16[2,128,128]{2,1,0:T(8,128)(2,1)S(1)}, bf16[2,128,128]{2,1,0:T(8,128)(2,1)S(1)}, bf16[2,128,128]{2,1,0:T(8,128)(2,1)S(1)}) custom-call(bf16[8,256,128]{2,1,0:T(8,128)(2,1)S(1)} %get-tuple-element.57.weights_ref, bf16[8,128,128]{2,1,0:T(8,128)(2,1)S(1)} %get-tuple-element.58.value_ref, ...), custom_call_target="tpu_custom_call" | custom-call | flops 268435456 | bytes 2097152 | tf_op jit(solution)/shard_map/pallas_call | solution.py:730
  35.4 0.2 collective-permute-start.6
  35.6 1.7 %collective-permute-start.7 = (bf16[2,128,128]{2,1,0:T(8,128)(2,1)S(1)}, bf16[2,128,128]{2,1,0:T(8,128)(2,1)S(1)}, u32[]{:S(2)}, u32[]{:S(2)}) collective-permute-start(bf16[2,128,128]{2,1,0:T(8,128)(2,1)S(1)} %get-tuple-element.65), channel_id=1, source_target_pairs={{0,2},{1,3},{2,0},{3,1},{4,6},{5,7},{6,4},{7,5},{8,10},{9,11},{10,... | collective-permute-start | bytes 196616 | tf_op jit(solution)/shard_map/ppermute | solution.py:679
  37.3 0.1 collective-permute-start.8
  37.3 0.0 collective-permute-done.6.refs_1_
  37.3 3.0 %collective-permute-done.7.refs_2_ = bf16[2,128,128]{2,1,0:T(8,128)(2,1)S(1)} collective-permute-done((bf16[2,128,128]{2,1,0:T(8,128)(2,1)S(1)}, bf16[2,128,128]{2,1,0:T(8,128)(2,1)S(1)}, u32[]{:S(2)}, u32[]{:S(2)}) %collective-permute-start.7) | collective-permute-done | bytes 65568 | tf_op jit(solution)/shard_map/ppermute | solution.py:679
  40.3 1.4 %collective-permute-done.8.refs_3_ = bf16[2,128,128]{2,1,0:T(8,128)(2,1)S(1)} collective-permute-done((bf16[2,128,128]{2,1,0:T(8,128)(2,1)S(1)}, bf16[2,128,128]{2,1,0:T(8,128)(2,1)S(1)}, u32[]{:S(2)}, u32[]{:S(2)}) %collective-permute-start.8) | collective-permute-done | bytes 65568 | tf_op jit(solution)/shard_map/ppermute | solution.py:679
  41.8 0.3 shard_map.163
  42.1 0.3 all-to-all-done.2.shares_ref
  42.3 1.1 %shard_map.164 = (bf16[256,256]{1,0:T(8,128)(2,1)}, bf16[4,128,128]{2,1,0:T(8,128)(2,1)}, f32[4,128,128]{2,1,0:T(8,128)}) custom-call(bf16[32,8,128]{2,1,0:T(8,128)(2,1)S(1)} %all-to-all-done.2.shares_ref, bf16[24,256]{1,0:T(8,128)(2,1)S(1)} %get-tuple-element.67.both_ref, f32[4,128,128]{2,1,0:T(8,128)S(1)} %get-tuple-element.68.normal_ref, ...), custom_call_target="tpu_custom_call" | custom-call | flops 16777216 | bytes 1048576 | tf_op jit(solution)/shard_map/pallas_call | solution.py:750
  (2 shorter events, 0.0 us)
Async XLA Ops:
  2.8 7.4 %copy-start.7 = (bf16[256,256]{1,0:T(8,128)(2,1)S(1)}, bf16[256,256]{1,0:T(8,128)(2,1)}, u32[]{:S(2)}) copy-start(bf16[256,256]{1,0:T(8,128)(2,1)} %param.25) | copy-start | bytes 393220
  2.8 7.4 %copy-start.8 = (bf16[256,256]{1,0:T(8,128)(2,1)S(1)}, bf16[256,256]{1,0:T(8,128)(2,1)}, u32[]{:S(2)}) copy-start(bf16[256,256]{1,0:T(8,128)(2,1)} %param.24) | copy-start | bytes 393220
  2.8 7.4 %copy-start.9 = (bf16[256,256]{1,0:T(8,128)(2,1)S(1)}, bf16[256,256]{1,0:T(8,128)(2,1)}, u32[]{:S(2)}) copy-start(bf16[256,256]{1,0:T(8,128)(2,1)} %param.23) | copy-start | bytes 393220
  2.8 16.2 %all-to-all-start = ((bf16[32,24,128]{2,1,0:T(8,128)(2,1)}), bf16[32,24,128]{2,1,0:T(8,128)(2,1)S(1)}, u32[]{:S(2)}, u32[]{:S(2)}) async-start(bf16[32,24,128]{2,1,0:T(8,128)(2,1)} %bitcast.22), calls=%async_computation | async-start | bytes 393216 | tf_op jit(solution)/shard_map/all_to_all | solution.py:644
  10.2 0.9 %copy-start.6 = (bf16[4,128,128]{2,1,0:T(8,128)(2,1)S(1)}, bf16[4,128,128]{2,1,0:T(8,128)(2,1)}, u32[]{:S(2)}) copy-start(bf16[4,128,128]{2,1,0:T(8,128)(2,1)} %param.15) | copy-start | bytes 393220
  10.2 2.9 %copy-start.2 = (bf16[256,256]{1,0:T(8,128)(2,1)S(1)}, bf16[256,256]{1,0:T(8,128)(2,1)}, u32[]{:S(2)}) copy-start(bf16[256,256]{1,0:T(8,128)(2,1)} %wg_ref.1) | copy-start | bytes 393220
  10.2 2.9 %copy-start.3 = (bf16[256,256]{1,0:T(8,128)(2,1)S(1)}, bf16[256,256]{1,0:T(8,128)(2,1)}, u32[]{:S(2)}) copy-start(bf16[256,256]{1,0:T(8,128)(2,1)} %get-tuple-element.40.normed_ref) | copy-start | bytes 393220
  11.1 2.0 %copy-start = (bf16[256,256]{1,0:T(8,128)(2,1)S(1)}, bf16[256,256]{1,0:T(8,128)(2,1)}, u32[]{:S(2)}) copy-start(bf16[256,256]{1,0:T(8,128)(2,1)} %wo_ref.3) | copy-start | bytes 393220
  11.1 2.1 %copy-start.1 = (bf16[2,128,256]{2,1,0:T(8,128)(2,1)S(1)}, bf16[2,128,256]{2,1,0:T(8,128)(2,1)}, u32[]{:S(2)}) copy-start(bf16[2,128,256]{2,1,0:T(8,128)(2,1)} %param.16) | copy-start | bytes 393220
  11.1 2.0 %copy-start.4 = (f32[16,128]{1,0:T(8,128)S(1)}, f32[16,128]{1,0:T(8,128)}, u32[]{:S(2)}) copy-start(f32[16,128]{1,0:T(8,128)} %get-tuple-element.45.aux_ref) | copy-start | bytes 24580
  11.1 4.9 %collective-permute-start.3 = (bf16[4,32,128]{2,1,0:T(8,128)(2,1)S(1)}, bf16[4,32,128]{2,1,0:T(8,128)(2,1)S(1)}, u32[]{:S(2)}, u32[]{:S(2)}) collective-permute-start(bf16[4,32,128]{2,1,0:T(8,128)(2,1)S(1)} %get-tuple-element.77), channel_id=1, source_target_pairs={{0,1},{1,0},{2,3},{3,2},{4,5},{5,4},{6,7},{7,6},{8,9},{9,8},{10,11... | collective-permute-start | bytes 98312 | tf_op jit(solution)/shard_map/ppermute | solution.py:679
  11.4 4.7 %collective-permute-start.4 = (bf16[4,32,128]{2,1,0:T(8,128)(2,1)S(1)}, bf16[4,32,128]{2,1,0:T(8,128)(2,1)S(1)}, u32[]{:S(2)}, u32[]{:S(2)}) collective-permute-start(bf16[4,32,128]{2,1,0:T(8,128)(2,1)S(1)} %get-tuple-element.76), channel_id=1, source_target_pairs={{0,2},{1,3},{2,0},{3,1},{4,6},{5,7},{6,4},{7,5},{8,10},{9,11},{10,... | collective-permute-start | bytes 98312 | tf_op jit(solution)/shard_map/ppermute | solution.py:679
  13.1 3.9 %collective-permute-start.5 = (bf16[4,32,128]{2,1,0:T(8,128)(2,1)S(1)}, bf16[4,32,128]{2,1,0:T(8,128)(2,1)S(1)}, u32[]{:S(2)}, u32[]{:S(2)}) collective-permute-start(bf16[4,32,128]{2,1,0:T(8,128)(2,1)S(1)} %get-tuple-element.75), channel_id=1, source_target_pairs={{0,3},{1,2},{2,1},{3,0},{4,7},{5,6},{6,5},{7,4},{8,11},{9,10},{10,... | collective-permute-start | bytes 98312 | tf_op jit(solution)/shard_map/ppermute | solution.py:679
  13.2 2.7 %copy-start.5 = (bf16[32,32,128]{2,1,0:T(8,128)(2,1)S(1)}, bf16[32,32,128]{2,1,0:T(8,128)(2,1)}, u32[]{:S(2)}) copy-start(bf16[32,32,128]{2,1,0:T(8,128)(2,1)} %param.21) | copy-start | bytes 786436
  13.7 17.0 %collective-permute-start = (bf16[4,128,128]{2,1,0:T(8,128)(2,1)S(1)}, bf16[4,128,128]{2,1,0:T(8,128)(2,1)S(1)}, u32[]{:S(2)}, u32[]{:S(2)}) collective-permute-start(bf16[4,128,128]{2,1,0:T(8,128)(2,1)S(1)} %get-tuple-element.48), channel_id=1, source_target_pairs={{0,1},{1,0},{2,3},{3,2},{4,5},{5,4},{6,7},{7,6},{8,9},{9,8},{10,11... | collective-permute-start | bytes 393224 | tf_op jit(solution)/shard_map/ppermute | solution.py:679
  14.2 16.5 %collective-permute-start.1 = (bf16[4,128,128]{2,1,0:T(8,128)(2,1)S(1)}, bf16[4,128,128]{2,1,0:T(8,128)(2,1)S(1)}, u32[]{:S(2)}, u32[]{:S(2)}) collective-permute-start(bf16[4,128,128]{2,1,0:T(8,128)(2,1)S(1)} %get-tuple-element.49), channel_id=1, source_target_pairs={{0,2},{1,3},{2,0},{3,1},{4,6},{5,7},{6,4},{7,5},{8,10},{9,11},{10,... | collective-permute-start | bytes 393224 | tf_op jit(solution)/shard_map/ppermute | solution.py:679
  16.0 14.7 %collective-permute-start.2 = (bf16[4,128,128]{2,1,0:T(8,128)(2,1)S(1)}, bf16[4,128,128]{2,1,0:T(8,128)(2,1)S(1)}, u32[]{:S(2)}, u32[]{:S(2)}) collective-permute-start(bf16[4,128,128]{2,1,0:T(8,128)(2,1)S(1)} %get-tuple-element.50), channel_id=1, source_target_pairs={{0,3},{1,2},{2,1},{3,0},{4,7},{5,6},{6,5},{7,4},{8,11},{9,10},{10,... | collective-permute-start | bytes 393224 | tf_op jit(solution)/shard_map/ppermute | solution.py:679
  32.4 10.0 %all-to-all-start.2 = ((bf16[32,8,128]{2,1,0:T(8,128)(2,1)}), bf16[32,8,128]{2,1,0:T(8,128)(2,1)S(1)}, u32[]{:S(2)}, u32[]{:S(2)}) async-start(bf16[32,8,128]{2,1,0:T(8,128)(2,1)} %get-tuple-element.55), calls=%async_computation.2 | async-start | bytes 131072 | tf_op jit(solution)/shard_map/all_to_all | solution.py:729
  35.4 2.0 %collective-permute-start.6 = (bf16[2,128,128]{2,1,0:T(8,128)(2,1)S(1)}, bf16[2,128,128]{2,1,0:T(8,128)(2,1)S(1)}, u32[]{:S(2)}, u32[]{:S(2)}) collective-permute-start(bf16[2,128,128]{2,1,0:T(8,128)(2,1)S(1)} %get-tuple-element.64), channel_id=1, source_target_pairs={{0,1},{1,0},{2,3},{3,2},{4,5},{5,4},{6,7},{7,6},{8,9},{9,8},{10,11... | collective-permute-start | bytes 196616 | tf_op jit(solution)/shard_map/ppermute | solution.py:679
  35.6 4.8 %collective-permute-start.7 = (bf16[2,128,128]{2,1,0:T(8,128)(2,1)S(1)}, bf16[2,128,128]{2,1,0:T(8,128)(2,1)S(1)}, u32[]{:S(2)}, u32[]{:S(2)}) collective-permute-start(bf16[2,128,128]{2,1,0:T(8,128)(2,1)S(1)} %get-tuple-element.65), channel_id=1, source_target_pairs={{0,2},{1,3},{2,0},{3,1},{4,6},{5,7},{6,4},{7,5},{8,10},{9,11},{10,... | collective-permute-start | bytes 196616 | tf_op jit(solution)/shard_map/ppermute | solution.py:679
  37.3 4.5 %collective-permute-start.8 = (bf16[2,128,128]{2,1,0:T(8,128)(2,1)S(1)}, bf16[2,128,128]{2,1,0:T(8,128)(2,1)S(1)}, u32[]{:S(2)}, u32[]{:S(2)}) collective-permute-start(bf16[2,128,128]{2,1,0:T(8,128)(2,1)S(1)} %get-tuple-element.66), channel_id=1, source_target_pairs={{0,3},{1,2},{2,1},{3,0},{4,7},{5,6},{6,5},{7,4},{8,11},{9,10},{10,... | collective-permute-start | bytes 196616 | tf_op jit(solution)/shard_map/ppermute | solution.py:679

commit v14 on v12

--- a/solution.py
+++ b/solution.py
@@ -284,11 +284,11 @@
         own = normed[s * residues : (s + 1) * residues]
         factor = dot_nt(right_t, own) * (live * seq_live)
         quarters.append(swap_groups([factor[a * 8 : (a + 1) * 8] for a in range(4)]))
-        left_scr[:residues] = dot_nt(own, left_wide) * (live_rows * seq_live)
+        left_scr[s, :residues] = dot_nt(own, left_wide) * (live_rows * seq_live)
         for a in range(4):
             row = jnp.zeros((lines, LANES), f32)
             for b in range(4):
-                part = left_scr[pl.ds(4 * a + b, lines, stride=4 * GROUP), :]
+                part = left_scr[s, pl.ds(4 * a + b, lines, stride=4 * GROUP), :]
                 row = jnp.where(lane_group == b, part, row)
             tail.append(row)
     tail = jnp.stack(tail, axis=1).astype(bf16)
@@ -625,7 +625,7 @@
             shape((token_rows, channel_count), bf16),
         ],
         [smem] * 2 + [vmem] * 5 + pieces,
-        [pltpu.VMEM((residues + 4 * GROUP, LANES), f32)],
+        [pltpu.VMEM((sequence_wise, residues + 4 * GROUP, LANES), f32)],
         flops=2 * token_rows * channel_count * LANES,
         moved=1 << 20,
         vmem_mib=60,

time: 43.8 us -> 43.8 us (level)
  no operation moved by 1% of the time
where the time goes in v14:
time: 43.8 us; the launch traced here: 43.5 us
  starting transfers between devices  16.1 us (37%)
  blocking collectives  10.1 us (23%)
  Pallas kernels  7.76 us (18%)
  waiting for transfers between devices  7.61 us (17%)
  local copies, waits for them, and re-layouts  0.98 us (2%)
  between operations  0.89 us (2%)
    all_to_all x1, blocking collectives, on_device_paired(): lax.all_to_all(send_bias.reshape(peers, share_rows, LANES), 'row', split_...  10.1 us
    all_to_all x1, starting transfers between devices, on_device_paired(): lax.all_to_all(send.reshape(peers, block_rows, LANES), 'row', split_axis=...  7.3 us
    ppermute x9, starting transfers between devices, trade(): lax.ppermute(parts[d], 'row', [(i, i ^ d) for i in range(peers)])  6.22 us
    ppermute x9, waiting for transfers between devices, trade(): lax.ppermute(parts[d], 'row', [(i, i ^ d) for i in range(peers)])  5.33 us
    all_to_all x1, starting transfers between devices, on_device_paired(): lax.all_to_all(send_grad, 'row', split_axis=0, concat_axis=0, tiled=True)  2.57 us
    pallas_call x1, Pallas kernels, on_device_paired(): kernel_call(factors_kernel, [shape((lines, GROUP, block_rows, LANES), bf1...  2.21 us
    all_to_all x1, waiting for transfers between devices, on_device_paired(): lax.all_to_all(send.reshape(peers, block_rows, LANES), 'row', split_axis=...  2.02 us
    pallas_call x1, Pallas kernels, on_device_paired(): kernel_call(lambda *refs: bias_gradient_kernel(scale, *refs), [shape((pee...  1.61 us
  transfers between devices with their start and end apart: 11, of which 5 were waited for; matrix products, arithmetic and copies ran while one was open for 0% of the time, Pallas kernels for 7%

profile of v14, /device:TPU:0, one launch (start us, length us, event | category | flops | bytes accessed | tf_op | source)
XLA Modules:
  0.0 43.5 jit_solution(9228358661950684735)
XLA Ops:
  0.6 2.2 %shard_map.157 = (bf16[8,4,24,128]{3,2,1,0:T(8,128)(2,1)}, f32[16,128]{1,0:T(8,128)}, bf16[256,256]{1,0:T(8,128)(2,1)}) custom-call(s32[64]{0:T(128)} %seq_smem_ref.1, s32[128]{0:T(128)} %res_smem_ref.1, s32[1,64]{1,0:T(1,128)} %bitcast.26, s32[1,128]{1,0:T(1,128)} %bitcast.27, bf16[8,128]{1,0:T(8,128)(2,1)} %bitcast.25, bf16[32,256]{1,0:T(8,128)(2,1)} %bitcast.23, ...), custom_call_target="tpu_custom_call" | custom-call | flops 16777216 | bytes 1048576 | tf_op jit(solution)/shard_map/pallas_call | solution.py:620
  2.8 0.0 copy-start.7
  2.8 0.0 copy-start.8
  2.9 0.0 copy-start.9
  2.9 7.3 %all-to-all-start = ((bf16[32,24,128]{2,1,0:T(8,128)(2,1)}), bf16[32,24,128]{2,1,0:T(8,128)(2,1)S(1)}, u32[]{:S(2)}, u32[]{:S(2)}) async-start(bf16[32,24,128]{2,1,0:T(8,128)(2,1)} %bitcast.22), calls=%async_computation | async-start | bytes 393216 | tf_op jit(solution)/shard_map/all_to_all | solution.py:643
  10.2 0.0 copy-done.7
  10.2 0.0 copy-done.8
  10.2 0.0 copy-done.9
  10.2 0.0 copy-start.6
  10.2 0.0 copy-start.2
  10.3 0.0 copy-start.3
  10.3 0.8 %copy-done.6 = bf16[4,128,128]{2,1,0:T(8,128)(2,1)S(1)} copy-done((bf16[4,128,128]{2,1,0:T(8,128)(2,1)S(1)}, bf16[4,128,128]{2,1,0:T(8,128)(2,1)}, u32[]{:S(2)}) %copy-start.6) | copy-done | bytes 131096
  11.1 0.0 copy-start
  11.1 0.0 copy-start.1
  11.2 0.0 copy-start.4
  11.2 0.3 collective-permute-start.3
  11.5 1.7 %collective-permute-start.4 = (bf16[4,32,128]{2,1,0:T(8,128)(2,1)S(1)}, bf16[4,32,128]{2,1,0:T(8,128)(2,1)S(1)}, u32[]{:S(2)}, u32[]{:S(2)}) collective-permute-start(bf16[4,32,128]{2,1,0:T(8,128)(2,1)S(1)} %get-tuple-element.74), channel_id=1, source_target_pairs={{0,2},{1,3},{2,0},{3,1},{4,6},{5,7},{6,4},{7,5},{8,10},{9,11},{10,... | collective-permute-start | bytes 98312 | tf_op jit(solution)/shard_map/ppermute | solution.py:678
  13.2 0.0 collective-permute-start.5
  13.2 0.0 copy-done.2
  13.2 0.0 copy-done.3
  13.2 0.0 copy-done
  13.2 0.0 copy-done.1
  13.2 0.0 copy-done.4
  13.2 0.0 copy-start.5
  13.2 0.5 %shard_map.158 = (f32[4,128,128]{2,1,0:T(8,128)S(1)}, f32[16,128]{1,0:T(8,128)S(1)}, bf16[4,32,128]{2,1,0:T(8,128)(2,1)S(1)}, bf16[4,128,128]{2,1,0:T(8,128)(2,1...) custom-call(bf16[256,256]{1,0:T(8,128)(2,1)S(1)} %copy-done.3, ...), custom_call_target="tpu_custom_call" | custom-call | flops 167772160 | bytes 2097152 | tf_op jit(solution)/shard_map/pallas_call | solution.py:658
  13.8 0.5 %collective-permute-start = (bf16[4,128,128]{2,1,0:T(8,128)(2,1)S(1)}, bf16[4,128,128]{2,1,0:T(8,128)(2,1)S(1)}, u32[]{:S(2)}, u32[]{:S(2)}) collective-permute-start(bf16[4,128,128]{2,1,0:T(8,128)(2,1)S(1)} %get-tuple-element.47), channel_id=1, source_target_pairs={{0,1},{1,0},{2,3},{3,2},{4,5},{5,4},{6,7},{7,6},{8,9},{9,8},{10,11... | collective-permute-start | bytes 393224 | tf_op jit(solution)/shard_map/ppermute | solution.py:678
  14.3 1.7 %collective-permute-start.1 = (bf16[4,128,128]{2,1,0:T(8,128)(2,1)S(1)}, bf16[4,128,128]{2,1,0:T(8,128)(2,1)S(1)}, u32[]{:S(2)}, u32[]{:S(2)}) collective-permute-start(bf16[4,128,128]{2,1,0:T(8,128)(2,1)S(1)} %get-tuple-element.48), channel_id=1, source_target_pairs={{0,2},{1,3},{2,0},{3,1},{4,6},{5,7},{6,4},{7,5},{8,10},{9,11},{10,... | collective-permute-start | bytes 393224 | tf_op jit(solution)/shard_map/ppermute | solution.py:678
  15.9 0.0 copy-done.5
  15.9 0.1 copy.17
  16.1 0.0 collective-permute-done.3.refs_1_
  16.1 0.1 collective-permute-start.2
  16.1 0.0 collective-permute-done.4.refs_2_
  16.2 0.9 %collective-permute-done.5.refs_3_ = bf16[4,32,128]{2,1,0:T(8,128)(2,1)S(1)} collective-permute-done((bf16[4,32,128]{2,1,0:T(8,128)(2,1)S(1)}, bf16[4,32,128]{2,1,0:T(8,128)(2,1)S(1)}, u32[]{:S(2)}, u32[]{:S(2)}) %collective-permute-start.5) | collective-permute-done | bytes 32800 | tf_op jit(solution)/shard_map/ppermute | solution.py:678
  17.0 2.0 %all-to-all-done.recv_ref = bf16[32,24,128]{2,1,0:T(8,128)(2,1)S(1)} async-done(((bf16[32,24,128]{2,1,0:T(8,128)(2,1)}), bf16[32,24,128]{2,1,0:T(8,128)(2,1)S(1)}, u32[]{:S(2)}, u32[]{:S(2)}) %all-to-all-start) | async-done | bytes 196640 | tf_op jit(solution)/shard_map/all_to_all | solution.py:643
  19.1 1.4 %shard_map.159 = (bf16[8,4,8,128]{3,2,1,0:T(8,128)(2,1)S(1)}, bf16[4,32,128]{2,1,0:T(8,128)(2,1)S(1)}, bf16[4,32,128]{2,1,0:T(8,128)(2,1)S(1)}, bf16[4,32,128]{2,1,0:T(8,128)(2,1)S(1)}, bf16[4,32,128]{2,1,0:T(8,128)(2,1)S(1)}) custom-call(bf16[32,24,128]{2,1,0:T(8,128)(2,1)S(1)} %all-to-all-done.recv_ref, bf16[4,256,128]{2,1,0:T(8,128)(2,1)S(1)} %bitcast.14, ...), custom_call_target="tpu_custom_call" | custom-call | flops 268435456 | bytes 1048576 | tf_op jit(solution)/shard_map/pallas_call | solution.py:689
  20.5 10.1 %all_to_all.15.bias_ref = bf16[32,8,128]{2,1,0:T(8,128)(2,1)S(1)} all-to-all(bf16[32,8,128]{2,1,0:T(8,128)(2,1)S(1)} %bitcast.16), channel_id=1, replica_groups=mesh['grp'=1,'row'=32,'col'=1] {'row'}, dimensions={0} | all-to-all | bytes 131072 | tf_op jit(solution)/shard_map/all_to_all | solution.py:704
  30.6 0.2 shard_map.160.refs_4_
  30.8 0.0 collective-permute-done.refs_1_
  30.8 0.0 collective-permute-done.1.refs_2_
  30.8 0.0 collective-permute-done.2.refs_3_
  30.8 1.6 %shard_map.161 = (bf16[32,8,128]{2,1,0:T(8,128)(2,1)}, bf16[8,256,128]{2,1,0:T(8,128)(2,1)S(1)}, bf16[8,128,128]{2,1,0:T(8,128)(2,1)S(1)}) custom-call(bf16[4,128,128]{2,1,0:T(8,128)(2,1)S(1)} %get-tuple-element.46.refs_0_, bf16[4,128,128]{2,1,0:T(8,128)(2,1)S(1)} %collective-permute-done.refs_1_, bf16[4,128,128]{2,1,0:T(8,128)(2,1)S(1)} %collective-permute-done.1.refs_2_, ...), custom_call_target="tpu_custom_call" | custom-call | flops 268435456 | bytes 4194304 | tf_op jit(solution)/shard_map/pallas_call | solution.py:716
  32.4 2.6 %all-to-all-start.2 = ((bf16[32,8,128]{2,1,0:T(8,128)(2,1)}), bf16[32,8,128]{2,1,0:T(8,128)(2,1)S(1)}, u32[]{:S(2)}, u32[]{:S(2)}) async-start(bf16[32,8,128]{2,1,0:T(8,128)(2,1)} %get-tuple-element.54), calls=%async_computation.2 | async-start | bytes 131072 | tf_op jit(solution)/shard_map/all_to_all | solution.py:728
  35.0 0.4 %shard_map.162 = (bf16[2,128,128]{2,1,0:T(8,128)(2,1)S(1)}, bf16[2,128,128]{2,1,0:T(8,128)(2,1)S(1)}, bf16[2,128,128]{2,1,0:T(8,128)(2,1)S(1)}, bf16[2,128,128]{2,1,0:T(8,128)(2,1)S(1)}) custom-call(bf16[8,256,128]{2,1,0:T(8,128)(2,1)S(1)} %get-tuple-element.56.weights_ref, bf16[8,128,128]{2,1,0:T(8,128)(2,1)S(1)} %get-tuple-element.57.value_ref, ...), custom_call_target="tpu_custom_call" | custom-call | flops 268435456 | bytes 2097152 | tf_op jit(solution)/shard_map/pallas_call | solution.py:729
  35.4 0.2 collective-permute-start.6
  35.6 1.7 %collective-permute-start.7 = (bf16[2,128,128]{2,1,0:T(8,128)(2,1)S(1)}, bf16[2,128,128]{2,1,0:T(8,128)(2,1)S(1)}, u32[]{:S(2)}, u32[]{:S(2)}) collective-permute-start(bf16[2,128,128]{2,1,0:T(8,128)(2,1)S(1)} %get-tuple-element.64), channel_id=1, source_target_pairs={{0,2},{1,3},{2,0},{3,1},{4,6},{5,7},{6,4},{7,5},{8,10},{9,11},{10,... | collective-permute-start | bytes 196616 | tf_op jit(solution)/shard_map/ppermute | solution.py:678
  37.3 0.1 collective-permute-start.8
  37.4 0.0 collective-permute-done.6.refs_1_
  37.4 3.0 %collective-permute-done.7.refs_2_ = bf16[2,128,128]{2,1,0:T(8,128)(2,1)S(1)} collective-permute-done((bf16[2,128,128]{2,1,0:T(8,128)(2,1)S(1)}, bf16[2,128,128]{2,1,0:T(8,128)(2,1)S(1)}, u32[]{:S(2)}, u32[]{:S(2)}) %collective-permute-start.7) | collective-permute-done | bytes 65568 | tf_op jit(solution)/shard_map/ppermute | solution.py:678
  40.4 1.4 %collective-permute-done.8.refs_3_ = bf16[2,128,128]{2,1,0:T(8,128)(2,1)S(1)} collective-permute-done((bf16[2,128,128]{2,1,0:T(8,128)(2,1)S(1)}, bf16[2,128,128]{2,1,0:T(8,128)(2,1)S(1)}, u32[]{:S(2)}, u32[]{:S(2)}) %collective-permute-start.8) | collective-permute-done | bytes 65568 | tf_op jit(solution)/shard_map/ppermute | solution.py:678
  41.8 0.3 shard_map.163
  42.1 0.3 all-to-all-done.2.shares_ref
  42.4 1.1 %shard_map.164 = (bf16[256,256]{1,0:T(8,128)(2,1)}, bf16[4,128,128]{2,1,0:T(8,128)(2,1)}, f32[4,128,128]{2,1,0:T(8,128)}) custom-call(bf16[32,8,128]{2,1,0:T(8,128)(2,1)S(1)} %all-to-all-done.2.shares_ref, f32[16,128]{1,0:T(8,128)S(1)} %get-tuple-element.51.aux_ref.mask_ref, f32[4,128,128]{2,1,0:T(8,128)S(1)} %get-tuple-element.66.normal_ref, ...), custom_call_target="tpu_custom_call" | custom-call | flops 16777216 | bytes 1048576 | tf_op jit(solution)/shard_map/pallas_call | solution.py:748
  (2 shorter events, 0.0 us)
Async XLA Ops:
  2.8 7.4 %copy-start.7 = (bf16[256,256]{1,0:T(8,128)(2,1)S(1)}, bf16[256,256]{1,0:T(8,128)(2,1)}, u32[]{:S(2)}) copy-start(bf16[256,256]{1,0:T(8,128)(2,1)} %param.25) | copy-start | bytes 393220
  2.8 7.4 %copy-start.8 = (bf16[256,256]{1,0:T(8,128)(2,1)S(1)}, bf16[256,256]{1,0:T(8,128)(2,1)}, u32[]{:S(2)}) copy-start(bf16[256,256]{1,0:T(8,128)(2,1)} %param.24) | copy-start | bytes 393220
  2.9 7.4 %copy-start.9 = (bf16[256,256]{1,0:T(8,128)(2,1)S(1)}, bf16[256,256]{1,0:T(8,128)(2,1)}, u32[]{:S(2)}) copy-start(bf16[256,256]{1,0:T(8,128)(2,1)} %param.23) | copy-start | bytes 393220
  2.9 16.2 %all-to-all-start = ((bf16[32,24,128]{2,1,0:T(8,128)(2,1)}), bf16[32,24,128]{2,1,0:T(8,128)(2,1)S(1)}, u32[]{:S(2)}, u32[]{:S(2)}) async-start(bf16[32,24,128]{2,1,0:T(8,128)(2,1)} %bitcast.22), calls=%async_computation | async-start | bytes 393216 | tf_op jit(solution)/shard_map/all_to_all | solution.py:643
  10.2 0.9 %copy-start.6 = (bf16[4,128,128]{2,1,0:T(8,128)(2,1)S(1)}, bf16[4,128,128]{2,1,0:T(8,128)(2,1)}, u32[]{:S(2)}) copy-start(bf16[4,128,128]{2,1,0:T(8,128)(2,1)} %param.15) | copy-start | bytes 393220
  10.2 2.9 %copy-start.2 = (bf16[256,256]{1,0:T(8,128)(2,1)S(1)}, bf16[256,256]{1,0:T(8,128)(2,1)}, u32[]{:S(2)}) copy-start(bf16[256,256]{1,0:T(8,128)(2,1)} %wg_ref.1) | copy-start | bytes 393220
  10.3 2.9 %copy-start.3 = (bf16[256,256]{1,0:T(8,128)(2,1)S(1)}, bf16[256,256]{1,0:T(8,128)(2,1)}, u32[]{:S(2)}) copy-start(bf16[256,256]{1,0:T(8,128)(2,1)} %get-tuple-element.39.normed_ref) | copy-start | bytes 393220
  11.1 2.0 %copy-start = (bf16[256,256]{1,0:T(8,128)(2,1)S(1)}, bf16[256,256]{1,0:T(8,128)(2,1)}, u32[]{:S(2)}) copy-start(bf16[256,256]{1,0:T(8,128)(2,1)} %wo_ref.3) | copy-start | bytes 393220
  11.1 2.1 %copy-start.1 = (bf16[2,128,256]{2,1,0:T(8,128)(2,1)S(1)}, bf16[2,128,256]{2,1,0:T(8,128)(2,1)}, u32[]{:S(2)}) copy-start(bf16[2,128,256]{2,1,0:T(8,128)(2,1)} %param.16) | copy-start | bytes 393220
  11.2 2.0 %copy-start.4 = (f32[16,128]{1,0:T(8,128)S(1)}, f32[16,128]{1,0:T(8,128)}, u32[]{:S(2)}) copy-start(f32[16,128]{1,0:T(8,128)} %get-tuple-element.44.aux_ref) | copy-start | bytes 24580
  11.2 4.9 %collective-permute-start.3 = (bf16[4,32,128]{2,1,0:T(8,128)(2,1)S(1)}, bf16[4,32,128]{2,1,0:T(8,128)(2,1)S(1)}, u32[]{:S(2)}, u32[]{:S(2)}) collective-permute-start(bf16[4,32,128]{2,1,0:T(8,128)(2,1)S(1)} %get-tuple-element.75), channel_id=1, source_target_pairs={{0,1},{1,0},{2,3},{3,2},{4,5},{5,4},{6,7},{7,6},{8,9},{9,8},{10,11... | collective-permute-start | bytes 98312 | tf_op jit(solution)/shard_map/ppermute | solution.py:678
  11.5 4.7 %collective-permute-start.4 = (bf16[4,32,128]{2,1,0:T(8,128)(2,1)S(1)}, bf16[4,32,128]{2,1,0:T(8,128)(2,1)S(1)}, u32[]{:S(2)}, u32[]{:S(2)}) collective-permute-start(bf16[4,32,128]{2,1,0:T(8,128)(2,1)S(1)} %get-tuple-element.74), channel_id=1, source_target_pairs={{0,2},{1,3},{2,0},{3,1},{4,6},{5,7},{6,4},{7,5},{8,10},{9,11},{10,... | collective-permute-start | bytes 98312 | tf_op jit(solution)/shard_map/ppermute | solution.py:678
  13.2 3.9 %collective-permute-start.5 = (bf16[4,32,128]{2,1,0:T(8,128)(2,1)S(1)}, bf16[4,32,128]{2,1,0:T(8,128)(2,1)S(1)}, u32[]{:S(2)}, u32[]{:S(2)}) collective-permute-start(bf16[4,32,128]{2,1,0:T(8,128)(2,1)S(1)} %get-tuple-element.73), channel_id=1, source_target_pairs={{0,3},{1,2},{2,1},{3,0},{4,7},{5,6},{6,5},{7,4},{8,11},{9,10},{10,... | collective-permute-start | bytes 98312 | tf_op jit(solution)/shard_map/ppermute | solution.py:678
  13.2 2.7 %copy-start.5 = (bf16[32,32,128]{2,1,0:T(8,128)(2,1)S(1)}, bf16[32,32,128]{2,1,0:T(8,128)(2,1)}, u32[]{:S(2)}) copy-start(bf16[32,32,128]{2,1,0:T(8,128)(2,1)} %param.21) | copy-start | bytes 786436
  13.8 17.0 %collective-permute-start = (bf16[4,128,128]{2,1,0:T(8,128)(2,1)S(1)}, bf16[4,128,128]{2,1,0:T(8,128)(2,1)S(1)}, u32[]{:S(2)}, u32[]{:S(2)}) collective-permute-start(bf16[4,128,128]{2,1,0:T(8,128)(2,1)S(1)} %get-tuple-element.47), channel_id=1, source_target_pairs={{0,1},{1,0},{2,3},{3,2},{4,5},{5,4},{6,7},{7,6},{8,9},{9,8},{10,11... | collective-permute-start | bytes 393224 | tf_op jit(solution)/shard_map/ppermute | solution.py:678
  14.3 16.5 %collective-permute-start.1 = (bf16[4,128,128]{2,1,0:T(8,128)(2,1)S(1)}, bf16[4,128,128]{2,1,0:T(8,128)(2,1)S(1)}, u32[]{:S(2)}, u32[]{:S(2)}) collective-permute-start(bf16[4,128,128]{2,1,0:T(8,128)(2,1)S(1)} %get-tuple-element.48), channel_id=1, source_target_pairs={{0,2},{1,3},{2,0},{3,1},{4,6},{5,7},{6,4},{7,5},{8,10},{9,11},{10,... | collective-permute-start | bytes 393224 | tf_op jit(solution)/shard_map/ppermute | solution.py:678
  16.1 14.7 %collective-permute-start.2 = (bf16[4,128,128]{2,1,0:T(8,128)(2,1)S(1)}, bf16[4,128,128]{2,1,0:T(8,128)(2,1)S(1)}, u32[]{:S(2)}, u32[]{:S(2)}) collective-permute-start(bf16[4,128,128]{2,1,0:T(8,128)(2,1)S(1)} %get-tuple-element.49), channel_id=1, source_target_pairs={{0,3},{1,2},{2,1},{3,0},{4,7},{5,6},{6,5},{7,4},{8,11},{9,10},{10,... | collective-permute-start | bytes 393224 | tf_op jit(solution)/shard_map/ppermute | solution.py:678
  32.4 10.0 %all-to-all-start.2 = ((bf16[32,8,128]{2,1,0:T(8,128)(2,1)}), bf16[32,8,128]{2,1,0:T(8,128)(2,1)S(1)}, u32[]{:S(2)}, u32[]{:S(2)}) async-start(bf16[32,8,128]{2,1,0:T(8,128)(2,1)} %get-tuple-element.54), calls=%async_computation.2 | async-start | bytes 131072 | tf_op jit(solution)/shard_map/all_to_all | solution.py:728
  35.4 2.0 %collective-permute-start.6 = (bf16[2,128,128]{2,1,0:T(8,128)(2,1)S(1)}, bf16[2,128,128]{2,1,0:T(8,128)(2,1)S(1)}, u32[]{:S(2)}, u32[]{:S(2)}) collective-permute-start(bf16[2,128,128]{2,1,0:T(8,128)(2,1)S(1)} %get-tuple-element.63), channel_id=1, source_target_pairs={{0,1},{1,0},{2,3},{3,2},{4,5},{5,4},{6,7},{7,6},{8,9},{9,8},{10,11... | collective-permute-start | bytes 196616 | tf_op jit(solution)/shard_map/ppermute | solution.py:678
  35.6 4.8 %collective-permute-start.7 = (bf16[2,128,128]{2,1,0:T(8,128)(2,1)S(1)}, bf16[2,128,128]{2,1,0:T(8,128)(2,1)S(1)}, u32[]{:S(2)}, u32[]{:S(2)}) collective-permute-start(bf16[2,128,128]{2,1,0:T(8,128)(2,1)S(1)} %get-tuple-element.64), channel_id=1, source_target_pairs={{0,2},{1,3},{2,0},{3,1},{4,6},{5,7},{6,4},{7,5},{8,10},{9,11},{10,... | collective-permute-start | bytes 196616 | tf_op jit(solution)/shard_map/ppermute | solution.py:678
  37.3 4.5 %collective-permute-start.8 = (bf16[2,128,128]{2,1,0:T(8,128)(2,1)S(1)}, bf16[2,128,128]{2,1,0:T(8,128)(2,1)S(1)}, u32[]{:S(2)}, u32[]{:S(2)}) collective-permute-start(bf16[2,128,128]{2,1,0:T(8,128)(2,1)S(1)} %get-tuple-element.65), channel_id=1, source_target_pairs={{0,3},{1,2},{2,1},{3,0},{4,7},{5,6},{6,5},{7,4},{8,11},{9,10},{10,... | collective-permute-start | bytes 196616 | tf_op jit(solution)/shard_map/ppermute | solution.py:678

commit v15 on v12

--- a/solution.py
+++ b/solution.py
@@ -386,14 +386,15 @@
             lbuf[s * peers : (s + 1) * peers, a * LANES : (a + 1) * LANES] = part
     left_t = lbuf[...].T.astype(bf16)
     outer = [dot_nn(left_t[a * LANES : (a + 1) * LANES], rbuf[a]).astype(bf16) for a in range(4)]
-    lane_group = lane_index(LANES) // 32
+    low, even = lane_index(LANES) < 64, lane_index(LANES) % 64 < 32
     sums = None
     for q in range(4):
         for g in range(8):
             span = slice(g * LANES, (g + 1) * LANES)
-            picked = outer[3][:, span]
-            for a in range(3):
-                picked = jnp.where(lane_group == (q + a) % 4, outer[a][:, span], picked)
+            turned = [outer[(group - q) % 4][:, span] for group in range(4)]
+            picked = jnp.where(
+                low, jnp.where(even, turned[0], turned[1]), jnp.where(even, turned[2], turned[3])
+            )
             for b in range(4):
                 obuf[q, g * 32 : (g + 1) * 32, b * LANES : (b + 1) * LANES] = picked[b * 32 : (b + 1) * 32]
         part = dot_tn(weight_ref[q], obuf[q])

time: 43.8 us -> 43.7 us (level)
  no operation moved by 1% of the time
where the time goes in v15:
time: 43.7 us; the launch traced here: 43.4 us
  starting transfers between devices  16.1 us (37%)
  blocking collectives  10.1 us (23%)
  Pallas kernels  7.68 us (18%)
  waiting for transfers between devices  7.61 us (17%)
  local copies, waits for them, and re-layouts  0.98 us (2%)
  between operations  0.9 us (2%)
    all_to_all x1, blocking collectives, on_device_paired(): lax.all_to_all(send_bias.reshape(peers, share_rows, LANES), 'row', split_...  10.1 us
    all_to_all x1, starting transfers between devices, on_device_paired(): lax.all_to_all(send.reshape(peers, block_rows, LANES), 'row', split_axis=...  7.3 us
    ppermute x9, starting transfers between devices, trade(): lax.ppermute(parts[d], 'row', [(i, i ^ d) for i in range(peers)])  6.21 us
    ppermute x9, waiting for transfers between devices, trade(): lax.ppermute(parts[d], 'row', [(i, i ^ d) for i in range(peers)])  5.33 us
    all_to_all x1, starting transfers between devices, on_device_paired(): lax.all_to_all(send_grad, 'row', split_axis=0, concat_axis=0, tiled=True)  2.57 us
    pallas_call x1, Pallas kernels, on_device_paired(): kernel_call(factors_kernel, [shape((lines, GROUP, block_rows, LANES), bf1...  2.17 us
    all_to_all x1, waiting for transfers between devices, on_device_paired(): lax.all_to_all(send.reshape(peers, block_rows, LANES), 'row', split_axis=...  2.02 us
    pallas_call x1, Pallas kernels, on_device_paired(): kernel_call(lambda *refs: bias_gradient_kernel(scale, *refs), [shape((pee...  1.61 us
  transfers between devices with their start and end apart: 11, of which 5 were waited for; matrix products, arithmetic and copies ran while one was open for 0% of the time, Pallas kernels for 7%

profile of v15, /device:TPU:0, one launch (start us, length us, event | category | flops | bytes accessed | tf_op | source)
XLA Modules:
  0.0 43.4 jit_solution(8813975990067855170)
XLA Ops:
  0.6 2.2 %shard_map.157 = (bf16[8,4,24,128]{3,2,1,0:T(8,128)(2,1)}, f32[16,128]{1,0:T(8,128)}, bf16[256,256]{1,0:T(8,128)(2,1)}) custom-call(s32[64]{0:T(128)} %seq_smem_ref.1, s32[128]{0:T(128)} %res_smem_ref.1, s32[1,64]{1,0:T(1,128)} %bitcast.26, s32[1,128]{1,0:T(1,128)} %bitcast.27, bf16[8,128]{1,0:T(8,128)(2,1)} %bitcast.25, bf16[32,256]{1,0:T(8,128)(2,1)} %bitcast.23, ...), custom_call_target="tpu_custom_call" | custom-call | flops 16777216 | bytes 1048576 | tf_op jit(solution)/shard_map/pallas_call | solution.py:621
  2.8 0.0 copy-start.7
  2.8 0.0 copy-start.8
  2.8 0.0 copy-start.9
  2.8 7.3 %all-to-all-start = ((bf16[32,24,128]{2,1,0:T(8,128)(2,1)}), bf16[32,24,128]{2,1,0:T(8,128)(2,1)S(1)}, u32[]{:S(2)}, u32[]{:S(2)}) async-start(bf16[32,24,128]{2,1,0:T(8,128)(2,1)} %bitcast.22), calls=%async_computation | async-start | bytes 393216 | tf_op jit(solution)/shard_map/all_to_all | solution.py:644
  10.2 0.0 copy-done.7
  10.2 0.0 copy-done.8
  10.2 0.0 copy-done.9
  10.2 0.0 copy-start.6
  10.2 0.0 copy-start.2
  10.2 0.0 copy-start.3
  10.3 0.8 %copy-done.6 = bf16[4,128,128]{2,1,0:T(8,128)(2,1)S(1)} copy-done((bf16[4,128,128]{2,1,0:T(8,128)(2,1)S(1)}, bf16[4,128,128]{2,1,0:T(8,128)(2,1)}, u32[]{:S(2)}) %copy-start.6) | copy-done | bytes 131096
  11.1 0.0 copy-start
  11.1 0.0 copy-start.1
  11.1 0.0 copy-start.4
  11.1 0.3 collective-permute-start.3
  11.4 1.7 %collective-permute-start.4 = (bf16[4,32,128]{2,1,0:T(8,128)(2,1)S(1)}, bf16[4,32,128]{2,1,0:T(8,128)(2,1)S(1)}, u32[]{:S(2)}, u32[]{:S(2)}) collective-permute-start(bf16[4,32,128]{2,1,0:T(8,128)(2,1)S(1)} %get-tuple-element.74), channel_id=1, source_target_pairs={{0,2},{1,3},{2,0},{3,1},{4,6},{5,7},{6,4},{7,5},{8,10},{9,11},{10,... | collective-permute-start | bytes 98312 | tf_op jit(solution)/shard_map/ppermute | solution.py:679
  13.1 0.0 collective-permute-start.5
  13.1 0.0 copy-done.2
  13.1 0.0 copy-done.3
  13.1 0.0 copy-done
  13.2 0.0 copy-done.1
  13.2 0.0 copy-done.4
  13.2 0.0 copy-start.5
  13.2 0.5 %shard_map.158 = (f32[4,128,128]{2,1,0:T(8,128)S(1)}, f32[16,128]{1,0:T(8,128)S(1)}, bf16[4,32,128]{2,1,0:T(8,128)(2,1)S(1)}, bf16[4,128,128]{2,1,0:T(8,128)(2,1...) custom-call(bf16[256,256]{1,0:T(8,128)(2,1)S(1)} %copy-done.3, ...), custom_call_target="tpu_custom_call" | custom-call | flops 167772160 | bytes 2097152 | tf_op jit(solution)/shard_map/pallas_call | solution.py:659
  13.7 0.5 %collective-permute-start = (bf16[4,128,128]{2,1,0:T(8,128)(2,1)S(1)}, bf16[4,128,128]{2,1,0:T(8,128)(2,1)S(1)}, u32[]{:S(2)}, u32[]{:S(2)}) collective-permute-start(bf16[4,128,128]{2,1,0:T(8,128)(2,1)S(1)} %get-tuple-element.47), channel_id=1, source_target_pairs={{0,1},{1,0},{2,3},{3,2},{4,5},{5,4},{6,7},{7,6},{8,9},{9,8},{10,11... | collective-permute-start | bytes 393224 | tf_op jit(solution)/shard_map/ppermute | solution.py:679
  14.2 1.7 %collective-permute-start.1 = (bf16[4,128,128]{2,1,0:T(8,128)(2,1)S(1)}, bf16[4,128,128]{2,1,0:T(8,128)(2,1)S(1)}, u32[]{:S(2)}, u32[]{:S(2)}) collective-permute-start(bf16[4,128,128]{2,1,0:T(8,128)(2,1)S(1)} %get-tuple-element.48), channel_id=1, source_target_pairs={{0,2},{1,3},{2,0},{3,1},{4,6},{5,7},{6,4},{7,5},{8,10},{9,11},{10,... | collective-permute-start | bytes 393224 | tf_op jit(solution)/shard_map/ppermute | solution.py:679
  15.9 0.0 copy-done.5
  15.9 0.1 copy.17
  16.0 0.0 collective-permute-done.3.refs_1_
  16.0 0.1 collective-permute-start.2
  16.1 0.0 collective-permute-done.4.refs_2_
  16.1 0.9 %collective-permute-done.5.refs_3_ = bf16[4,32,128]{2,1,0:T(8,128)(2,1)S(1)} collective-permute-done((bf16[4,32,128]{2,1,0:T(8,128)(2,1)S(1)}, bf16[4,32,128]{2,1,0:T(8,128)(2,1)S(1)}, u32[]{:S(2)}, u32[]{:S(2)}) %collective-permute-start.5) | collective-permute-done | bytes 32800 | tf_op jit(solution)/shard_map/ppermute | solution.py:679
  17.0 2.0 %all-to-all-done.recv_ref = bf16[32,24,128]{2,1,0:T(8,128)(2,1)S(1)} async-done(((bf16[32,24,128]{2,1,0:T(8,128)(2,1)}), bf16[32,24,128]{2,1,0:T(8,128)(2,1)S(1)}, u32[]{:S(2)}, u32[]{:S(2)}) %all-to-all-start) | async-done | bytes 196640 | tf_op jit(solution)/shard_map/all_to_all | solution.py:644
  19.0 1.4 %shard_map.159 = (bf16[8,4,8,128]{3,2,1,0:T(8,128)(2,1)S(1)}, bf16[4,32,128]{2,1,0:T(8,128)(2,1)S(1)}, bf16[4,32,128]{2,1,0:T(8,128)(2,1)S(1)}, bf16[4,32,128]{2,1,0:T(8,128)(2,1)S(1)}, bf16[4,32,128]{2,1,0:T(8,128)(2,1)S(1)}) custom-call(bf16[32,24,128]{2,1,0:T(8,128)(2,1)S(1)} %all-to-all-done.recv_ref, bf16[4,256,128]{2,1,0:T(8,128)(2,1)S(1)} %bitcast.14, ...), custom_call_target="tpu_custom_call" | custom-call | flops 268435456 | bytes 1048576 | tf_op jit(solution)/shard_map/pallas_call | solution.py:690
  20.4 10.1 %all_to_all.15.bias_ref = bf16[32,8,128]{2,1,0:T(8,128)(2,1)S(1)} all-to-all(bf16[32,8,128]{2,1,0:T(8,128)(2,1)S(1)} %bitcast.16), channel_id=1, replica_groups=mesh['grp'=1,'row'=32,'col'=1] {'row'}, dimensions={0} | all-to-all | bytes 131072 | tf_op jit(solution)/shard_map/all_to_all | solution.py:705
  30.5 0.2 shard_map.160.refs_4_
  30.7 0.0 collective-permute-done.refs_1_
  30.7 0.0 collective-permute-done.1.refs_2_
  30.7 0.0 collective-permute-done.2.refs_3_
  30.7 1.6 %shard_map.161 = (bf16[32,8,128]{2,1,0:T(8,128)(2,1)}, bf16[8,256,128]{2,1,0:T(8,128)(2,1)S(1)}, bf16[8,128,128]{2,1,0:T(8,128)(2,1)S(1)}) custom-call(bf16[4,128,128]{2,1,0:T(8,128)(2,1)S(1)} %get-tuple-element.46.refs_0_, bf16[4,128,128]{2,1,0:T(8,128)(2,1)S(1)} %collective-permute-done.refs_1_, bf16[4,128,128]{2,1,0:T(8,128)(2,1)S(1)} %collective-permute-done.1.refs_2_, ...), custom_call_target="tpu_custom_call" | custom-call | flops 268435456 | bytes 4194304 | tf_op jit(solution)/shard_map/pallas_call | solution.py:717
  32.3 2.6 %all-to-all-start.2 = ((bf16[32,8,128]{2,1,0:T(8,128)(2,1)}), bf16[32,8,128]{2,1,0:T(8,128)(2,1)S(1)}, u32[]{:S(2)}, u32[]{:S(2)}) async-start(bf16[32,8,128]{2,1,0:T(8,128)(2,1)} %get-tuple-element.54), calls=%async_computation.2 | async-start | bytes 131072 | tf_op jit(solution)/shard_map/all_to_all | solution.py:729
  34.9 0.4 %shard_map.162 = (bf16[2,128,128]{2,1,0:T(8,128)(2,1)S(1)}, bf16[2,128,128]{2,1,0:T(8,128)(2,1)S(1)}, bf16[2,128,128]{2,1,0:T(8,128)(2,1)S(1)}, bf16[2,128,128]{2,1,0:T(8,128)(2,1)S(1)}) custom-call(bf16[8,256,128]{2,1,0:T(8,128)(2,1)S(1)} %get-tuple-element.56.weights_ref, bf16[8,128,128]{2,1,0:T(8,128)(2,1)S(1)} %get-tuple-element.57.value_ref, ...), custom_call_target="tpu_custom_call" | custom-call | flops 268435456 | bytes 2097152 | tf_op jit(solution)/shard_map/pallas_call | solution.py:730
  35.4 0.2 collective-permute-start.6
  35.5 1.7 %collective-permute-start.7 = (bf16[2,128,128]{2,1,0:T(8,128)(2,1)S(1)}, bf16[2,128,128]{2,1,0:T(8,128)(2,1)S(1)}, u32[]{:S(2)}, u32[]{:S(2)}) collective-permute-start(bf16[2,128,128]{2,1,0:T(8,128)(2,1)S(1)} %get-tuple-element.64), channel_id=1, source_target_pairs={{0,2},{1,3},{2,0},{3,1},{4,6},{5,7},{6,4},{7,5},{8,10},{9,11},{10,... | collective-permute-start | bytes 196616 | tf_op jit(solution)/shard_map/ppermute | solution.py:679
  37.2 0.1 collective-permute-start.8
  37.3 0.0 collective-permute-done.6.refs_1_
  37.3 3.0 %collective-permute-done.7.refs_2_ = bf16[2,128,128]{2,1,0:T(8,128)(2,1)S(1)} collective-permute-done((bf16[2,128,128]{2,1,0:T(8,128)(2,1)S(1)}, bf16[2,128,128]{2,1,0:T(8,128)(2,1)S(1)}, u32[]{:S(2)}, u32[]{:S(2)}) %collective-permute-start.7) | collective-permute-done | bytes 65568 | tf_op jit(solution)/shard_map/ppermute | solution.py:679
  40.3 1.4 %collective-permute-done.8.refs_3_ = bf16[2,128,128]{2,1,0:T(8,128)(2,1)S(1)} collective-permute-done((bf16[2,128,128]{2,1,0:T(8,128)(2,1)S(1)}, bf16[2,128,128]{2,1,0:T(8,128)(2,1)S(1)}, u32[]{:S(2)}, u32[]{:S(2)}) %collective-permute-start.8) | collective-permute-done | bytes 65568 | tf_op jit(solution)/shard_map/ppermute | solution.py:679
  41.7 0.3 shard_map.163
  42.1 0.3 all-to-all-done.2.shares_ref
  42.3 1.1 %shard_map.164 = (bf16[256,256]{1,0:T(8,128)(2,1)}, bf16[4,128,128]{2,1,0:T(8,128)(2,1)}, f32[4,128,128]{2,1,0:T(8,128)}) custom-call(bf16[32,8,128]{2,1,0:T(8,128)(2,1)S(1)} %all-to-all-done.2.shares_ref, f32[16,128]{1,0:T(8,128)S(1)} %get-tuple-element.51.aux_ref.mask_ref, f32[4,128,128]{2,1,0:T(8,128)S(1)} %get-tuple-element.66.normal_ref, ...), custom_call_target="tpu_custom_call" | custom-call | flops 16777216 | bytes 1048576 | tf_op jit(solution)/shard_map/pallas_call | solution.py:749
  (2 shorter events, 0.0 us)
Async XLA Ops:
  2.8 7.4 %copy-start.7 = (bf16[256,256]{1,0:T(8,128)(2,1)S(1)}, bf16[256,256]{1,0:T(8,128)(2,1)}, u32[]{:S(2)}) copy-start(bf16[256,256]{1,0:T(8,128)(2,1)} %param.25) | copy-start | bytes 393220
  2.8 7.4 %copy-start.8 = (bf16[256,256]{1,0:T(8,128)(2,1)S(1)}, bf16[256,256]{1,0:T(8,128)(2,1)}, u32[]{:S(2)}) copy-start(bf16[256,256]{1,0:T(8,128)(2,1)} %param.24) | copy-start | bytes 393220
  2.8 7.4 %copy-start.9 = (bf16[256,256]{1,0:T(8,128)(2,1)S(1)}, bf16[256,256]{1,0:T(8,128)(2,1)}, u32[]{:S(2)}) copy-start(bf16[256,256]{1,0:T(8,128)(2,1)} %param.23) | copy-start | bytes 393220
  2.8 16.2 %all-to-all-start = ((bf16[32,24,128]{2,1,0:T(8,128)(2,1)}), bf16[32,24,128]{2,1,0:T(8,128)(2,1)S(1)}, u32[]{:S(2)}, u32[]{:S(2)}) async-start(bf16[32,24,128]{2,1,0:T(8,128)(2,1)} %bitcast.22), calls=%async_computation | async-start | bytes 393216 | tf_op jit(solution)/shard_map/all_to_all | solution.py:644
  10.2 0.9 %copy-start.6 = (bf16[4,128,128]{2,1,0:T(8,128)(2,1)S(1)}, bf16[4,128,128]{2,1,0:T(8,128)(2,1)}, u32[]{:S(2)}) copy-start(bf16[4,128,128]{2,1,0:T(8,128)(2,1)} %param.15) | copy-start | bytes 393220
  10.2 2.9 %copy-start.2 = (bf16[256,256]{1,0:T(8,128)(2,1)S(1)}, bf16[256,256]{1,0:T(8,128)(2,1)}, u32[]{:S(2)}) copy-start(bf16[256,256]{1,0:T(8,128)(2,1)} %wg_ref.1) | copy-start | bytes 393220
  10.2 2.9 %copy-start.3 = (bf16[256,256]{1,0:T(8,128)(2,1)S(1)}, bf16[256,256]{1,0:T(8,128)(2,1)}, u32[]{:S(2)}) copy-start(bf16[256,256]{1,0:T(8,128)(2,1)} %get-tuple-element.39.normed_ref) | copy-start | bytes 393220
  11.1 2.0 %copy-start = (bf16[256,256]{1,0:T(8,128)(2,1)S(1)}, bf16[256,256]{1,0:T(8,128)(2,1)}, u32[]{:S(2)}) copy-start(bf16[256,256]{1,0:T(8,128)(2,1)} %wo_ref.3) | copy-start | bytes 393220
  11.1 2.1 %copy-start.1 = (bf16[2,128,256]{2,1,0:T(8,128)(2,1)S(1)}, bf16[2,128,256]{2,1,0:T(8,128)(2,1)}, u32[]{:S(2)}) copy-start(bf16[2,128,256]{2,1,0:T(8,128)(2,1)} %param.16) | copy-start | bytes 393220
  11.1 2.0 %copy-start.4 = (f32[16,128]{1,0:T(8,128)S(1)}, f32[16,128]{1,0:T(8,128)}, u32[]{:S(2)}) copy-start(f32[16,128]{1,0:T(8,128)} %get-tuple-element.44.aux_ref) | copy-start | bytes 24580
  11.1 4.9 %collective-permute-start.3 = (bf16[4,32,128]{2,1,0:T(8,128)(2,1)S(1)}, bf16[4,32,128]{2,1,0:T(8,128)(2,1)S(1)}, u32[]{:S(2)}, u32[]{:S(2)}) collective-permute-start(bf16[4,32,128]{2,1,0:T(8,128)(2,1)S(1)} %get-tuple-element.75), channel_id=1, source_target_pairs={{0,1},{1,0},{2,3},{3,2},{4,5},{5,4},{6,7},{7,6},{8,9},{9,8},{10,11... | collective-permute-start | bytes 98312 | tf_op jit(solution)/shard_map/ppermute | solution.py:679
  11.4 4.7 %collective-permute-start.4 = (bf16[4,32,128]{2,1,0:T(8,128)(2,1)S(1)}, bf16[4,32,128]{2,1,0:T(8,128)(2,1)S(1)}, u32[]{:S(2)}, u32[]{:S(2)}) collective-permute-start(bf16[4,32,128]{2,1,0:T(8,128)(2,1)S(1)} %get-tuple-element.74), channel_id=1, source_target_pairs={{0,2},{1,3},{2,0},{3,1},{4,6},{5,7},{6,4},{7,5},{8,10},{9,11},{10,... | collective-permute-start | bytes 98312 | tf_op jit(solution)/shard_map/ppermute | solution.py:679
  13.1 3.9 %collective-permute-start.5 = (bf16[4,32,128]{2,1,0:T(8,128)(2,1)S(1)}, bf16[4,32,128]{2,1,0:T(8,128)(2,1)S(1)}, u32[]{:S(2)}, u32[]{:S(2)}) collective-permute-start(bf16[4,32,128]{2,1,0:T(8,128)(2,1)S(1)} %get-tuple-element.73), channel_id=1, source_target_pairs={{0,3},{1,2},{2,1},{3,0},{4,7},{5,6},{6,5},{7,4},{8,11},{9,10},{10,... | collective-permute-start | bytes 98312 | tf_op jit(solution)/shard_map/ppermute | solution.py:679
  13.2 2.7 %copy-start.5 = (bf16[32,32,128]{2,1,0:T(8,128)(2,1)S(1)}, bf16[32,32,128]{2,1,0:T(8,128)(2,1)}, u32[]{:S(2)}) copy-start(bf16[32,32,128]{2,1,0:T(8,128)(2,1)} %param.21) | copy-start | bytes 786436
  13.7 17.0 %collective-permute-start = (bf16[4,128,128]{2,1,0:T(8,128)(2,1)S(1)}, bf16[4,128,128]{2,1,0:T(8,128)(2,1)S(1)}, u32[]{:S(2)}, u32[]{:S(2)}) collective-permute-start(bf16[4,128,128]{2,1,0:T(8,128)(2,1)S(1)} %get-tuple-element.47), channel_id=1, source_target_pairs={{0,1},{1,0},{2,3},{3,2},{4,5},{5,4},{6,7},{7,6},{8,9},{9,8},{10,11... | collective-permute-start | bytes 393224 | tf_op jit(solution)/shard_map/ppermute | solution.py:679
  14.2 16.5 %collective-permute-start.1 = (bf16[4,128,128]{2,1,0:T(8,128)(2,1)S(1)}, bf16[4,128,128]{2,1,0:T(8,128)(2,1)S(1)}, u32[]{:S(2)}, u32[]{:S(2)}) collective-permute-start(bf16[4,128,128]{2,1,0:T(8,128)(2,1)S(1)} %get-tuple-element.48), channel_id=1, source_target_pairs={{0,2},{1,3},{2,0},{3,1},{4,6},{5,7},{6,4},{7,5},{8,10},{9,11},{10,... | collective-permute-start | bytes 393224 | tf_op jit(solution)/shard_map/ppermute | solution.py:679
  16.0 14.7 %collective-permute-start.2 = (bf16[4,128,128]{2,1,0:T(8,128)(2,1)S(1)}, bf16[4,128,128]{2,1,0:T(8,128)(2,1)S(1)}, u32[]{:S(2)}, u32[]{:S(2)}) collective-permute-start(bf16[4,128,128]{2,1,0:T(8,128)(2,1)S(1)} %get-tuple-element.49), channel_id=1, source_target_pairs={{0,3},{1,2},{2,1},{3,0},{4,7},{5,6},{6,5},{7,4},{8,11},{9,10},{10,... | collective-permute-start | bytes 393224 | tf_op jit(solution)/shard_map/ppermute | solution.py:679
  32.3 10.0 %all-to-all-start.2 = ((bf16[32,8,128]{2,1,0:T(8,128)(2,1)}), bf16[32,8,128]{2,1,0:T(8,128)(2,1)S(1)}, u32[]{:S(2)}, u32[]{:S(2)}) async-start(bf16[32,8,128]{2,1,0:T(8,128)(2,1)} %get-tuple-element.54), calls=%async_computation.2 | async-start | bytes 131072 | tf_op jit(solution)/shard_map/all_to_all | solution.py:729
  35.4 2.0 %collective-permute-start.6 = (bf16[2,128,128]{2,1,0:T(8,128)(2,1)S(1)}, bf16[2,128,128]{2,1,0:T(8,128)(2,1)S(1)}, u32[]{:S(2)}, u32[]{:S(2)}) collective-permute-start(bf16[2,128,128]{2,1,0:T(8,128)(2,1)S(1)} %get-tuple-element.63), channel_id=1, source_target_pairs={{0,1},{1,0},{2,3},{3,2},{4,5},{5,4},{6,7},{7,6},{8,9},{9,8},{10,11... | collective-permute-start | bytes 196616 | tf_op jit(solution)/shard_map/ppermute | solution.py:679
  35.5 4.8 %collective-permute-start.7 = (bf16[2,128,128]{2,1,0:T(8,128)(2,1)S(1)}, bf16[2,128,128]{2,1,0:T(8,128)(2,1)S(1)}, u32[]{:S(2)}, u32[]{:S(2)}) collective-permute-start(bf16[2,128,128]{2,1,0:T(8,128)(2,1)S(1)} %get-tuple-element.64), channel_id=1, source_target_pairs={{0,2},{1,3},{2,0},{3,1},{4,6},{5,7},{6,4},{7,5},{8,10},{9,11},{10,... | collective-permute-start | bytes 196616 | tf_op jit(solution)/shard_map/ppermute | solution.py:679
  37.2 4.5 %collective-permute-start.8 = (bf16[2,128,128]{2,1,0:T(8,128)(2,1)S(1)}, bf16[2,128,128]{2,1,0:T(8,128)(2,1)S(1)}, u32[]{:S(2)}, u32[]{:S(2)}) collective-permute-start(bf16[2,128,128]{2,1,0:T(8,128)(2,1)S(1)} %get-tuple-element.65), channel_id=1, source_target_pairs={{0,3},{1,2},{2,1},{3,0},{4,7},{5,6},{6,5},{7,4},{8,11},{9,10},{10,... | collective-permute-start | bytes 196616 | tf_op jit(solution)/shard_map/ppermute | solution.py:679
